TPU v7x, 32 devices: a whole 2x2x4 slice. The times are simulated.
32 devices in a mesh: dp: 4 (over y, x), seq: 8 (over z, core).
Axes of the slice: x: 2, y: 2, z: 4, core: 2. Of those that a mesh axis runs over, the one named last changes fastest.
Arguments:
- qkvu: bfloat16 [4096, 4096], P(('dp', 'seq')), may hold values from -6 to 6
- w_out: bfloat16 [1024, 1024], replicated, may hold values from -0.1875 to 0.1875
- head_coef: bfloat16 [4096, 32], P(('dp', 'seq')), may hold values from -1 to 1
- item_table: bfloat16 [4096, 1024], P('seq'), may hold values from -6 to 6
- neg_ids: int32 [32], P('seq'), may hold values from 0 to 511
- send_order: int32 [32, 128], P(('dp', 'seq')), may hold values from 0 to 127, each once within a row
- recv_order: int32 [32, 128], P(('dp', 'seq')), may hold values from 0 to 127, each once within a row
- tile_len: int32 [4, 8], P('dp'), may hold values from 1 to 128, 341 in all within a row
Outputs:
- layer_out: bfloat16 [4096, 1024], P(('dp', 'seq'))
- d_qkvu: bfloat16 [4096, 4096], P(('dp', 'seq'))
- d_w_out: float32 [1024, 1024], P('seq', 'dp')
Inputs may be any that keep to these rules, and one draw needn't show every extreme that they name: Each row of send_order and of recv_order names every number once. `recv_order`: each row names every number once. `tile_len`: in each data group the lengths sum to 341.
All inputs are finite; a program needn't handle non-finite values.
Results may differ from a plain program's by a relative error of at most 0.014.
Values may be sent and summed in bfloat16 or wider, within the bound.
No kernel may reach another device: no remote copies, remote signals or barrier semaphores. Data moves between devices by JAX's collectives and lax.ppermute only.
A program may use at most 64 MiB of HBM per device.

v0:
```python
import math

import jax
import jax.numpy as jnp
from jax import lax
from jax.sharding import PartitionSpec as P

HEADS = 8
SPAN = 3


eps = 1e-05


def shifted(block, axis, distance):
    devices = range(lax.axis_size(axis))
    route = [(i - distance, i) for i in devices if i - distance in devices]
    return lax.ppermute(block, axis, route)


def silu_grad(values):
    sigmoid_val = jax.nn.sigmoid(values)
    return sigmoid_val * (1.0 + values * (1.0 - sigmoid_val))


def pair_mask(count, len_p, len_q, allowed, causal):
    positions = jnp.arange(count, dtype=jnp.int32)
    live = (positions[:, None] < len_p) & (positions[None, :] < len_q) & allowed
    if causal:
        live = live & (positions[None, :] <= positions[:, None])
    return jnp.where(live, 1.0, 0.0).astype(jnp.float32)


def head_major(flat, count, head_dim):
    return flat.reshape(count, HEADS, head_dim).transpose(1, 0, 2)


def row_major(heads_first, count, width):
    return heads_first.transpose(1, 0, 2).reshape(count, width)


def on_device(qkvu, w_out, head_coef, item_table, neg_ids, send_order, recv_order, tile_len):
    row_count = qkvu.shape[0]
    model_width = w_out.shape[0]
    head_dim = model_width // HEADS
    score_scale = 1.0 / math.sqrt(head_dim)
    send_list = send_order[0]
    recv_list = recv_order[0]
    own_index = lax.axis_index("seq")
    lengths_row = tile_len[0]
    own_len = jnp.take(lengths_row, own_index)
    outgoing = jnp.take(qkvu, send_list, axis=0)
    received = lax.all_to_all(outgoing, "seq", split_axis=0, concat_axis=0, tiled=True)
    balanced = jnp.take(received, recv_list, axis=0)
    neg_all = lax.all_gather(jnp.take(item_table, neg_ids, axis=0), "seq", axis=0, tiled=True)
    u_part = balanced[:, :model_width].astype(jnp.float32)
    value_heads = head_major(balanced[:, model_width : 2 * model_width], row_count, head_dim)
    query_heads = head_major(balanced[:, 2 * model_width : 3 * model_width], row_count, head_dim)
    key_heads = head_major(balanced[:, 3 * model_width :], row_count, head_dim)
    lagged = []
    carried = (value_heads, key_heads)
    for lag in range(1, SPAN):
        carried = shifted((carried[0], carried[1]), "seq", 1)
        lagged.append(carried)
    value_list = [value_heads]
    key_list = [key_heads]
    mask_list = [pair_mask(row_count, own_len, own_len, True, True)]
    for lag in range(1, SPAN):
        earlier_len = jnp.take(lengths_row, jnp.maximum(own_index - lag, 0))
        value_list.append(lagged[lag - 1][0])
        key_list.append(lagged[lag - 1][1])
        mask_list.append(pair_mask(row_count, own_len, earlier_len, own_index >= lag, False))
    values_all = jnp.concatenate(value_list, axis=1)
    keys_all = jnp.concatenate(key_list, axis=1)
    mask_all = jnp.concatenate(mask_list, axis=1)
    scores = (
        jnp.einsum("hpd,hqd->hpq", query_heads, keys_all, preferred_element_type=jnp.float32)
        * score_scale
    )
    weights = (jax.nn.silu(scores) * mask_all[None] / row_count).astype(jnp.bfloat16)
    attended_heads = jnp.einsum(
        "hpq,hqd->hpd", weights, values_all, preferred_element_type=jnp.float32
    )
    attended = row_major(attended_heads, row_count, model_width)
    row_mean = jnp.mean(attended, axis=1, keepdims=True)
    centered = attended - row_mean
    variance = jnp.mean(centered * centered, axis=1, keepdims=True)
    inv_std = lax.rsqrt(variance + eps)
    normed = centered * inv_std
    mixed_rows = (normed * u_part).astype(jnp.bfloat16)
    layer_out = jnp.dot(mixed_rows, w_out, preferred_element_type=jnp.float32).astype(jnp.bfloat16)
    positions = jnp.arange(row_count, dtype=jnp.int32)
    live_col = jnp.where(positions < own_len, 1.0, 0.0).astype(jnp.float32)[:, None]
    coef_live = (head_coef * live_col).astype(jnp.bfloat16)
    head_grad = jnp.dot(coef_live, neg_all, preferred_element_type=jnp.float32).astype(jnp.bfloat16)
    d_mixed = lax.dot_general(
        head_grad, w_out, (((1,), (1,)), ((), ())), preferred_element_type=jnp.float32
    )
    d_u_part = d_mixed * normed
    d_normed = d_mixed * u_part
    d_att = (
        d_normed
        - jnp.mean(d_normed, axis=1, keepdims=True)
        - normed * jnp.mean(d_normed * normed, axis=1, keepdims=True)
    ) * inv_std
    d_att_heads = head_major(d_att.astype(jnp.bfloat16), row_count, head_dim)
    d_weights = jnp.einsum(
        "hpd,hqd->hpq", d_att_heads, values_all, preferred_element_type=jnp.float32
    )
    d_scores = (d_weights * mask_all[None] / row_count * silu_grad(scores) * score_scale).astype(
        jnp.bfloat16
    )
    d_query = jnp.einsum("hpq,hqd->hpd", d_scores, keys_all, preferred_element_type=jnp.float32)
    part_keys = jnp.einsum(
        "hpq,hpd->hqd", d_scores, query_heads, preferred_element_type=jnp.float32
    )
    part_values = jnp.einsum(
        "hpq,hpd->hqd", weights, d_att_heads, preferred_element_type=jnp.float32
    )
    key_grad = part_keys[:, :row_count]
    value_grad = part_values[:, :row_count]
    for lag in range(1, SPAN):
        block_keys = part_keys[:, lag * row_count : (lag + 1) * row_count].astype(jnp.bfloat16)
        block_values = part_values[:, lag * row_count : (lag + 1) * row_count].astype(jnp.bfloat16)
        back_values, back_keys = shifted((block_values, block_keys), "seq", -lag)
        key_grad = key_grad + back_keys.astype(jnp.float32)
        value_grad = value_grad + back_values.astype(jnp.float32)
    tile_grads = jnp.concatenate(
        [
            d_u_part,
            row_major(value_grad, row_count, model_width),
            row_major(d_query, row_count, model_width),
            row_major(key_grad, row_count, model_width),
        ],
        axis=1,
    ).astype(jnp.bfloat16)
    slot_grads = jnp.zeros_like(tile_grads).at[recv_list].set(tile_grads)
    returned = lax.all_to_all(slot_grads, "seq", split_axis=0, concat_axis=0, tiled=True)
    d_home = jnp.zeros_like(returned).at[send_list].set(returned)
    coef_sums = lax.psum_scatter(
        lax.dot_general(
            mixed_rows, coef_live, (((0,), (0,)), ((), ())), preferred_element_type=jnp.float32
        ),
        "seq",
        scatter_dimension=0,
        tiled=True,
    )
    row_grad = jnp.dot(coef_sums, neg_all.astype(jnp.float32), precision=lax.Precision.HIGHEST)
    d_w_out = lax.psum_scatter(
        row_grad.astype(jnp.bfloat16), "dp", scatter_dimension=1, tiled=True
    ).astype(jnp.float32)
    return (layer_out, d_home, d_w_out)


def solution(mesh):
    placed = (
        P(("dp", "seq"), None),
        P(),
        P(("dp", "seq"), None),
        P("seq", None),
        P("seq"),
        P(("dp", "seq"), None),
        P(("dp", "seq"), None),
        P("dp", None),
    )
    return jax.shard_map(
        on_device,
        mesh=mesh,
        in_specs=placed,
        out_specs=(P(("dp", "seq"), None), P(("dp", "seq"), None), P("seq", "dp")),
        check_vma=False,
    )
```

profile of v0, /device:TPU:0, one launch (start us, length us, event | category | flops | bytes accessed | tf_op | source)
XLA Modules:
  0.0 203.1 jit_solution(7415320870426287766)
XLA Ops:
  8.7 3.6 %gather_fusion.1 = bf16[128,4096]{1,0:T(8,128)(2,1)S(1)} fusion(bf16[128,4096]{1,0:T(8,128)(2,1)} %param.10, s32[1024]{0:T(1024)S(1)} %pad_clamp_fusion.2), kind=kCustom, calls=%fused_computation.clone | custom fusion | bytes 2097664 | tf_op jit(solution)/shard_map/jit(_take)/gather | solution.py:52
  13.4 6.5 %all-to-all-start = ((bf16[8,16,4096]{2,1,0:T(8,128)(2,1)}), bf16[8,16,4096]{2,1,0:T(8,128)(2,1)S(1)}, u32[]{:S(2)}, u32[]{:S(2)}) async-start(bf16[8,16,4096]{2,1,0:T(8,128)(2,1)} %bitcast.88), calls=%async_computation | async-start | bytes 2097152 | tf_op jit(solution)/shard_map/all_to_all | solution.py:53
  23.4 23.0 %all-to-all-done = bf16[8,16,4096]{2,1,0:T(8,128)(2,1)S(1)} async-done(((bf16[8,16,4096]{2,1,0:T(8,128)(2,1)}), bf16[8,16,4096]{2,1,0:T(8,128)(2,1)S(1)}, u32[]{:S(2)}, u32[]{:S(2)}) %all-to-all-start) | async-done | bytes 1048608 | tf_op jit(solution)/shard_map/all_to_all | solution.py:53
  46.4 2.2 %gather_fusion.2 = bf16[128,4096]{1,0:T(8,128)(2,1)} fusion(bf16[128,4096]{1,0:T(8,128)(2,1)S(1)} %bitcast.87, s32[1024]{0:T(1024)S(1)} %pad_clamp_fusion.1), kind=kCustom, calls=%fused_computation.1.clone | custom fusion | bytes 2097664 | tf_op jit(solution)/shard_map/jit(_take)/gather | solution.py:54
  52.8 2.2 %collective-permute-start = (bf16[8,128,128]{2,1,0:T(8,128)(2,1)}, bf16[8,128,128]{2,1,0:T(8,128)(2,1)}, u32[]{:S(2)}, u32[]{:S(2)}) collective-permute-start(bf16[8,128,128]{2,1,0:T(8,128)(2,1)} %bitcast.98), channel_id=1, source_target_pairs={{0,1},{1,2},{2,3},{3,4},{4,5},{5,6},{6,7},{8,9},{9,10},{10,11},{11... | collective-permute-start | bytes 786440 | tf_op jit(solution)/shard_map/ppermute | solution.py:18
  55.1 1.9 gather_fusion
  57.1 1.8 copy.39
  58.9 2.0 collective-permute-start.2
  60.9 2.0 collective-permute-start.1
  62.9 14.0 %all-gather = bf16[8,4,1024]{2,1,0:T(4,128)(2,1)S(1)} all-gather(bf16[1,4,1024]{2,1,0:T(4,128)(2,1)S(1)} %select_bitcast_fusion), channel_id=1, replica_groups=mesh['dp'=4,'seq'=8] {'seq'}, dimensions={0}, use_global_device_ids=true | all-gather | bytes 73728 | tf_op jit(solution)/shard_map/all_gather | solution.py:55
  78.9 2.2 %collective-permute-start.3 = (bf16[8,128,128]{1,2,0:T(8,128)(2,1)}, bf16[8,128,128]{1,2,0:T(8,128)(2,1)S(1)}, u32[]{:S(2)}, u32[]{:S(2)}) collective-permute-start(bf16[8,128,128]{1,2,0:T(8,128)(2,1)} %collective-permute-done.2), channel_id=1, source_target_pairs={{0,1},{1,2},{2,3},{3,4},{4,5},{5,6},{6,7},{8,9},{9,10},{10,11},{11... | collective-permute-start | bytes 786440 | tf_op jit(solution)/shard_map/ppermute | solution.py:18
  81.1 3.2 %multiply_convert_fusion.1 = (bf16[8,128,384]{2,1,0:T(8,128)(2,1)S(1)}, f32[8,128,384]{2,1,0:T(8,128)}) fusion(f32[128,384]{1,0:T(8,128)} %pad_maximum_fusion.6, bf16[8,128,128]{2,1,0:T(8,128)(2,1)} %collective-permute-done.1, bf16[8,128,128]{2,1,0:T(8,128)(2,1)} %collective-permute-done, bf16[8,128,128]{2,1,0:T(8,128)(2,1)} %bitcast.99, ...), kind=kOutput, calls=%fused_computation.6 | convolution fusion | flops 106168320 | bytes 3604480 | tf_op jit(solution)/shard_map/hpd,hqd->hpq/dot_general | solution.py:77
  85.2 2.3 %fusion.37 = (f32[128]{0:T(128)S(1)}, f32[8,128,128]{1,2,0:T(8,128)}) fusion(bf16[8,128,384]{2,1,0:T(8,128)(2,1)S(1)} %get-tuple-element.55, bf16[8,128,128]{1,2,0:T(8,128)(2,1)S(1)} %collective-permute-done.3, bf16[8,128,128]{1,2,0:T(8,128)(2,1)} %collective-permute-done.2, bf16[8,128,128]{1,2,0:T(8,128)(2,1)} %bitcast.18), kind=kOutput, calls=%fused_computation.92 | convolution fusion | flops 103153536 | bytes 2097664 | tf_op jit(solution)/shard_map/hpq,hqd->hpd/dot_general | solution.py:81
  87.5 2.0 %copy.40 = f32[128,1024]{1,0:T(8,128)} copy(f32[128,1024]{0,1:T(8,128)} %bitcast.91) | data formatting | bytes 1048576 | tf_op jit(solution)/shard_map/reshape | solution.py:39
  90.7 2.8 %fusion.24 = (f32[128]{0:T(128)S(1)}, f32[128]{0:T(128)S(1)}, f32[128,1024]{1,0:T(8,128)}) fusion(bf16[128,4096]{1,0:T(8,128)(2,1)S(1)} %broadcast_select_fusion, f32[128]{0:T(128)S(1)} %add_rsqrt_fusion, f32[128,1024]{1,0:T(8,128)} %copy.40, f32[128]{0:T(128)S(1)} %broadcast_multiply_fusion.2, bf16[1024,1024]{1,0:T(8,128)(2,1)S(1)} %copy-done, ...), kind=kOutput, calls=%fused_computation.52 | convolution fusion | flops 277884672 | bytes 3484160 | tf_op jit(solution)/shard_map/dot_general | solution.py:96
  93.6 2.3 %multiply_convert_fusion.2 = (bf16[128,1024]{1,0:T(8,128)(2,1)S(1)}, bf16[128,1024]{1,0:T(8,128)(2,1)S(1)}, bf16[128,1024]{1,0:T(8,128)(2,1)}) fusion(f32[128,1024]{1,0:T(8,128)} %copy.40, f32[128]{0:T(128)S(1)} %broadcast_multiply_fusion, f32[128]{0:T(128)S(1)} %broadcast_multiply_fusion.1, f32[128]{0:T(128)S(1)} %add_rsqrt_fusion, ...), kind=kLoop, calls=%fused_computation.38 | loop fusion | flops 1703936 | bytes 2099200 | tf_op jit(solution)/shard_map/convert_element_type | solution.py:106
  95.9 1.9 multiply_convert_fusion
  112.7 6.4 %collective-permute-done.5 = bf16[8,128,128]{1,2,0:T(8,128)(2,1)} collective-permute-done((bf16[8,128,128]{1,2,0:T(8,128)(2,1)}, bf16[8,128,128]{1,2,0:T(8,128)(2,1)}, u32[]{:S(2)}, u32[]{:S(2)}) %collective-permute-start.5) | collective-permute-done | bytes 262176 | tf_op jit(solution)/shard_map/ppermute | solution.py:18
  121.3 3.5 %scatter_custom_fusion = bf16[128,4096]{1,0:T(8,128)(2,1)} fusion(s32[128]{0:T(128)S(1)} %fusion.29, bf16[128,1024]{1,0:T(8,128)(2,1)S(1)} %copy.59, bf16[]{:T(256)} %constant.167, bf16[128,1024]{1,0:T(8,128)(2,1)S(1)} %copy.56, bf16[128,1024]{1,0:T(8,128)(2,1)} %copy.55, bf16[128,1024]{1,0:T(8,128)(2,1)S(1)} %copy-done.3, bf16[]{:T(256)} %constant.90.clone.1), kind=kCustom, calls=%fused_computation.14 | custom fusion | flops 4194304 | bytes 2097156 | tf_op jit(solution)/shard_map/scatter | solution.py:137
  124.9 5.5 %all-to-all-start.1 = ((bf16[8,16,4096]{2,1,0:T(8,128)(2,1)}), bf16[8,16,4096]{2,1,0:T(8,128)(2,1)S(1)}, u32[]{:S(2)}, u32[]{:S(2)}) async-start(bf16[8,16,4096]{2,1,0:T(8,128)(2,1)} %bitcast.36), calls=%async_computation.1 | async-start | bytes 2097152 | tf_op jit(solution)/shard_map/all_to_all | solution.py:138
  131.3 35.0 %reduce-scatter.3.cloned.1.call-done = f32[128,32]{0,1:T(8,128)} async-done(((f32[1024,32]{0,1:T(8,128)}), f32[128,32]{0,1:T(8,128)}) %reduce-scatter.3.cloned.1.call-update) | async-done | bytes 16400 | tf_op jit(solution)/shard_map/reduce_scatter | solution.py:140
  166.3 1.8 convolution_convert_fusion
  169.4 22.4 %reduce-scatter.5.cloned.1.call-done = bf16[128,256]{1,0:T(8,128)(2,1)} async-done(((bf16[128,1024]{1,0:T(8,128)(2,1)}), bf16[128,256]{1,0:T(8,128)(2,1)}) %reduce-scatter.5.cloned.1.call-update) | async-done | bytes 65552 | tf_op jit(solution)/shard_map/reduce_scatter | solution.py:149
  193.2 3.0 %scatter_custom_fusion.1 = bf16[128,4096]{1,0:T(8,128)(2,1)} fusion(s32[128]{0:T(128)S(1)} %fusion.28, bf16[128,4096]{1,0:T(8,128)(2,1)S(1)} %bitcast.95, bf16[]{:T(256)} %constant.90.clone.1), kind=kCustom, calls=%fused_computation.41 | custom fusion | bytes 1048578 | tf_op jit(solution)/shard_map/scatter | solution.py:139
  (95 shorter events, 33.1 us)
Async XLA Ops:
  7.2 83.5 %copy-start = (bf16[1024,1024]{1,0:T(8,128)(2,1)S(1)}, bf16[1024,1024]{1,0:T(8,128)(2,1)}, u32[]{:S(2)}) copy-start(bf16[1024,1024]{1,0:T(8,128)(2,1)} %param.11) | copy-start | bytes 6291460
  13.4 6.5 %copy-start.10 = (s32[1,8]{1,0:T(1,128)S(1)}, s32[1,8]{1,0:T(1,128)}, u32[]{:S(2)}) copy-start(s32[1,8]{1,0:T(1,128)} %param.17) | copy-start | bytes 100
  13.4 9.2 %copy-start.14 = (s32[1,128]{1,0:T(1,128)S(1)}, s32[1,128]{1,0:T(1,128)}, u32[]{:S(2)}) copy-start(s32[1,128]{1,0:T(1,128)} %param.16) | copy-start | bytes 1540
  13.4 10.0 %copy-start.13 = (s32[4]{0:T(128)S(1)}, s32[4]{0:T(128)}, u32[]{:S(2)}) copy-start(s32[4]{0:T(128)} %param.14) | copy-start | bytes 52
  13.4 33.1 %all-to-all-start = ((bf16[8,16,4096]{2,1,0:T(8,128)(2,1)}), bf16[8,16,4096]{2,1,0:T(8,128)(2,1)S(1)}, u32[]{:S(2)}, u32[]{:S(2)}) async-start(bf16[8,16,4096]{2,1,0:T(8,128)(2,1)} %bitcast.88), calls=%async_computation | async-start | bytes 2097152 | tf_op jit(solution)/shard_map/all_to_all | solution.py:53
  52.8 8.1 %collective-permute-start = (bf16[8,128,128]{2,1,0:T(8,128)(2,1)}, bf16[8,128,128]{2,1,0:T(8,128)(2,1)}, u32[]{:S(2)}, u32[]{:S(2)}) collective-permute-start(bf16[8,128,128]{2,1,0:T(8,128)(2,1)} %bitcast.98), channel_id=1, source_target_pairs={{0,1},{1,2},{2,3},{3,4},{4,5},{5,6},{6,7},{8,9},{9,10},{10,11},{11... | collective-permute-start | bytes 786440 | tf_op jit(solution)/shard_map/ppermute | solution.py:18
  58.9 20.0 %collective-permute-start.2 = (bf16[8,128,128]{1,2,0:T(8,128)(2,1)}, bf16[8,128,128]{1,2,0:T(8,128)(2,1)}, u32[]{:S(2)}, u32[]{:S(2)}) collective-permute-start(bf16[8,128,128]{1,2,0:T(8,128)(2,1)} %bitcast.18), channel_id=1, source_target_pairs={{0,1},{1,2},{2,3},{3,4},{4,5},{5,6},{6,7},{8,9},{9,10},{10,11},{11... | collective-permute-start | bytes 786440 | tf_op jit(solution)/shard_map/ppermute | solution.py:18
  60.9 20.2 %collective-permute-start.1 = (bf16[8,128,128]{2,1,0:T(8,128)(2,1)}, bf16[8,128,128]{2,1,0:T(8,128)(2,1)}, u32[]{:S(2)}, u32[]{:S(2)}) collective-permute-start(bf16[8,128,128]{2,1,0:T(8,128)(2,1)} %collective-permute-done), channel_id=1, source_target_pairs={{0,1},{1,2},{2,3},{3,4},{4,5},{5,6},{6,7},{8,9},{9,10},{10,11},{11... | collective-permute-start | bytes 786440 | tf_op jit(solution)/shard_map/ppermute | solution.py:18
  78.0 6.3 %copy-start.1 = (bf16[128,1024]{0,1:T(8,128)(2,1)}, bf16[128,1024]{0,1:T(8,128)(2,1)S(1)}, u32[]{:S(2)}) copy-start(bf16[128,1024]{0,1:T(8,128)(2,1)S(1)} %copy.35) | copy-start | bytes 786436
  78.9 5.4 %collective-permute-start.3 = (bf16[8,128,128]{1,2,0:T(8,128)(2,1)}, bf16[8,128,128]{1,2,0:T(8,128)(2,1)S(1)}, u32[]{:S(2)}, u32[]{:S(2)}) collective-permute-start(bf16[8,128,128]{1,2,0:T(8,128)(2,1)} %collective-permute-done.2), channel_id=1, source_target_pairs={{0,1},{1,2},{2,3},{3,4},{4,5},{5,6},{6,7},{8,9},{9,10},{10,11},{11... | collective-permute-start | bytes 786440 | tf_op jit(solution)/shard_map/ppermute | solution.py:18
  84.3 3.2 %copy-start.11 = (bf16[8,128,128]{1,2,0:T(8,128)(2,1)}, bf16[8,128,128]{1,2,0:T(8,128)(2,1)S(1)}, u32[]{:S(2)}) copy-start(bf16[8,128,128]{1,2,0:T(8,128)(2,1)S(1)} %collective-permute-done.3) | copy-start | bytes 786436
  85.1 5.6 %copy-start.9 = (bf16[128,32]{0,1:T(8,128)(2,1)S(1)}, bf16[128,32]{0,1:T(8,128)(2,1)}, u32[]{:S(2)}) copy-start(bf16[128,32]{0,1:T(8,128)(2,1)} %param.12) | copy-start | bytes 24580
  93.5 2.4 %copy-start.16 = (f32[8,128,384]{2,1,0:T(8,128)S(1)}, f32[8,128,384]{2,1,0:T(8,128)}, u32[]{:S(2)}) copy-start(f32[8,128,384]{2,1,0:T(8,128)} %get-tuple-element.56) | copy-start | bytes 4718596
  99.4 3.6 %copy-start.5 = (bf16[8,128,384]{2,1,0:T(8,128)(2,1)S(1)}, bf16[8,128,384]{2,1,0:T(8,128)(2,1)}, u32[]{:S(2)}) copy-start(bf16[8,128,384]{2,1,0:T(8,128)(2,1)} %copy-done.4) | copy-start | bytes 2359300
  100.3 10.3 %collective-permute-start.7 = (bf16[8,128,128]{1,2,0:T(8,128)(2,1)}, bf16[8,128,128]{1,2,0:T(8,128)(2,1)S(1)}, u32[]{:S(2)}, u32[]{:S(2)}) collective-permute-start(bf16[8,128,128]{1,2,0:T(8,128)(2,1)} %get-tuple-element.48), channel_id=1, source_target_pairs={{2,0},{3,1},{4,2},{5,3},{6,4},{7,5},{10,8},{11,9},{12,10},{13,11},... | collective-permute-start | bytes 786440 | tf_op jit(solution)/shard_map/ppermute | solution.py:18
  101.6 9.0 %collective-permute-start.6 = (bf16[8,128,128]{1,2,0:T(8,128)(2,1)}, bf16[8,128,128]{1,2,0:T(8,128)(2,1)S(1)}, u32[]{:S(2)}, u32[]{:S(2)}) collective-permute-start(bf16[8,128,128]{1,2,0:T(8,128)(2,1)} %get-tuple-element.47), channel_id=1, source_target_pairs={{1,0},{2,1},{3,2},{4,3},{5,4},{6,5},{7,6},{9,8},{10,9},{11,10},{12... | collective-permute-start | bytes 786440 | tf_op jit(solution)/shard_map/ppermute | solution.py:18
  103.0 5.3 %copy-start.7 = (bf16[128,8,128]{2,0,1:T(8,128)(2,1)S(1)}, bf16[128,8,128]{2,0,1:T(8,128)(2,1)}, u32[]{:S(2)}) copy-start(bf16[128,8,128]{2,0,1:T(8,128)(2,1)} %copy.38) | copy-start | bytes 786436
  105.5 13.7 %collective-permute-start.5 = (bf16[8,128,128]{1,2,0:T(8,128)(2,1)}, bf16[8,128,128]{1,2,0:T(8,128)(2,1)}, u32[]{:S(2)}, u32[]{:S(2)}) collective-permute-start(bf16[8,128,128]{1,2,0:T(8,128)(2,1)} %get-tuple-element.46), channel_id=1, source_target_pairs={{2,0},{3,1},{4,2},{5,3},{6,4},{7,5},{10,8},{11,9},{12,10},{13,11},... | collective-permute-start | bytes 786440 | tf_op jit(solution)/shard_map/ppermute | solution.py:18
  106.8 12.4 %collective-permute-start.4 = (bf16[8,128,128]{1,2,0:T(8,128)(2,1)}, bf16[8,128,128]{1,2,0:T(8,128)(2,1)}, u32[]{:S(2)}, u32[]{:S(2)}) collective-permute-start(bf16[8,128,128]{1,2,0:T(8,128)(2,1)} %get-tuple-element.45), channel_id=1, source_target_pairs={{1,0},{2,1},{3,2},{4,3},{5,4},{6,5},{7,6},{9,8},{10,9},{11,10},{12... | collective-permute-start | bytes 786440 | tf_op jit(solution)/shard_map/ppermute | solution.py:18
  111.3 10.0 %copy-start.3 = (bf16[128,1024]{1,0:T(8,128)(2,1)S(1)}, bf16[128,1024]{1,0:T(8,128)(2,1)}, u32[]{:S(2)}) copy-start(bf16[128,1024]{1,0:T(8,128)(2,1)} %get-tuple-element.41) | copy-start | bytes 786436
  124.9 43.4 %copy-start.15 = (s32[1,128]{1,0:T(1,128)S(1)}, s32[1,128]{1,0:T(1,128)}, u32[]{:S(2)}) copy-start(s32[1,128]{1,0:T(1,128)} %param.15) | copy-start | bytes 1540
  124.9 68.4 %all-to-all-start.1 = ((bf16[8,16,4096]{2,1,0:T(8,128)(2,1)}), bf16[8,16,4096]{2,1,0:T(8,128)(2,1)S(1)}, u32[]{:S(2)}, u32[]{:S(2)}) async-start(bf16[8,16,4096]{2,1,0:T(8,128)(2,1)} %bitcast.36), calls=%async_computation.1 | async-start | bytes 2097152 | tf_op jit(solution)/shard_map/all_to_all | solution.py:138
  130.4 36.0 %reduce-scatter.3.cloned.1.call-start = ((), (), s32[]{:S(2)}) async-start(), calls=%async_computation.4 | async-start | bytes 147456 | tf_op jit(solution)/shard_map/reduce_scatter | solution.py:140
  131.3 60.5 %reduce-scatter.5.cloned.1.call-start = ((), (), s32[]{:S(2)}) async-start(), calls=%async_computation.5 | async-start | bytes 327680 | tf_op jit(solution)/shard_map/reduce_scatter | solution.py:149
  (5 other events, 8.3 us)
Sparse Core Ops, SparseCore 0:
  134.0 32.2 reduce-scatter.2
  169.3 22.3 reduce-scatter.4
where the time goes:
time: 204 us; the launch traced here: 203 us
  waiting for transfers between devices  87.5 us (43%)
  starting transfers between devices  25.8 us (13%)
  local copies, waits for them, and re-layouts  24.8 us (12%)
  matrix products  18.6 us (9%)
  between operations  16.4 us (8%)
  other arithmetic  16.1 us (8%)
  blocking collectives  14 us (7%)
    reduce_scatter x1, waiting for transfers between devices, on_device(): lax.psum_scatter(lax.dot_general(mixed_rows, coef_live, (((0,), (0,)), ((...  35 us
    all_to_all x1, waiting for transfers between devices, on_device(): lax.all_to_all(outgoing, 'seq', split_axis=0, concat_axis=0, tiled=True)  23 us
    reduce_scatter x1, waiting for transfers between devices, on_device(): lax.psum_scatter(row_grad.astype(jnp.bfloat16), 'dp', scatter_dimension=1...  22.4 us
    all_gather x1, blocking collectives, on_device(): lax.all_gather(jnp.take(item_table, neg_ids, axis=0), 'seq', axis=0, tile...  14 us
    ppermute x8, starting transfers between devices, shifted(): return lax.ppermute(block, axis, route)  13.8 us
    ppermute x8, waiting for transfers between devices, shifted(): return lax.ppermute(block, axis, route)  7.1 us
    all_to_all x1, starting transfers between devices, on_device(): lax.all_to_all(outgoing, 'seq', split_axis=0, concat_axis=0, tiled=True)  6.46 us
    all_to_all x1, starting transfers between devices, on_device(): lax.all_to_all(slot_grads, 'seq', split_axis=0, concat_axis=0, tiled=True)  5.51 us
  transfers between devices with their start and end apart: 12, of which 5 were waited for; matrix products, arithmetic and copies ran while one was open for 11% of the time, Pallas kernels for 0%

commit v1 on v0

--- a/solution.py
+++ b/solution.py
@@ -1,15 +1,26 @@
+import functools
 import math
 
 import jax
 import jax.numpy as jnp
 from jax import lax
+from jax.experimental import pallas as pl
+from jax.experimental.pallas import tpu as pltpu
 from jax.sharding import PartitionSpec as P
 
 HEADS = 8
 SPAN = 3
+PARTS = 4
+SLOTS = 64
+IDX_ROWS = 16
 
 
 eps = 1e-05
+
+VMEM = pl.BlockSpec(memory_space=pltpu.VMEM)
+SMEM = pl.BlockSpec(memory_space=pltpu.SMEM)
+F32 = jnp.float32
+BF16 = jnp.bfloat16
 
 
 def shifted(block, axis, distance):
@@ -39,7 +50,7 @@
     return heads_first.transpose(1, 0, 2).reshape(count, width)
 
 
-def on_device(qkvu, w_out, head_coef, item_table, neg_ids, send_order, recv_order, tile_len):
+def tile_plan(qkvu, w_out, head_coef, item_table, neg_ids, send_order, recv_order, tile_len):
     row_count = qkvu.shape[0]
     model_width = w_out.shape[0]
     head_dim = model_width // HEADS
@@ -152,6 +163,332 @@
     return (layer_out, d_home, d_w_out)
 
 
+def dot(a, b, dims=((1,), (0,))):
+    return lax.dot_general(a, b, (dims, ((), ())), preferred_element_type=F32)
+
+
+def iota(shape, dim):
+    return lax.broadcasted_iota(jnp.int32, shape, dim)
+
+
+def starts_of(len_ref, count):
+    starts = [jnp.int32(0)]
+    for t in range(count):
+        starts.append(starts[-1] + len_ref[t])
+    return starts
+
+
+def tile_of(position, starts):
+    tile = jnp.zeros(position.shape, jnp.int32)
+    for start in starts[1:-1]:
+        tile = tile + jnp.where(position >= start, 1, 0)
+    return tile
+
+
+def one_hot(condition):
+    return jnp.where(condition, 1.0, 0.0).astype(BF16)
+
+
+def index_kernel(sizes, me_ref, len_ref, gathered, w_rows, place, rank, most, coef_c, d_mixed, negatives, neg_rows):
+    n, rows, live_cap, negs, per = sizes
+    cell = rows // n
+    me = me_ref[0]
+    starts = starts_of(len_ref, n)
+    blocks = [gathered[me ^ s].astype(F32) for s in range(n)]
+    order = jnp.concatenate([b[0:8] for b in blocks], axis=0)
+    order = jnp.concatenate([order, jnp.zeros((rows - 8 * n, rows), F32)], axis=0)
+    order_t = jnp.transpose(order)
+    lane = iota((rows, rows), 1)
+    sub = iota((rows, rows), 0)
+    slot_rows = []
+    for t in range(n):
+        recv_col = order_t[:, 8 * t : 8 * t + 1].astype(jnp.int32)
+        target = jnp.where(sub < len_ref[t], sub + starts[t] + 1, 0)
+        hit = jnp.where(recv_col == lane, target, 0)
+        slot_rows.append(jnp.sum(hit.astype(F32), axis=0, keepdims=True))
+    slots = jnp.concatenate(slot_rows + [jnp.zeros((rows - n, rows), F32)], axis=0)
+    slots_t = jnp.transpose(slots)
+    home_rows = []
+    for s in range(n):
+        send_col = order_t[:, 8 * s + 1 : 8 * s + 2].astype(jnp.int32)
+        target = jnp.concatenate([jnp.broadcast_to(slots_t[s * cell : (s + 1) * cell, t : t + 1], (cell, rows)) for t in range(n)], axis=0)
+        home_rows.append(jnp.sum(jnp.where(send_col == lane, target, 0.0), axis=0, keepdims=True))
+    home = jnp.concatenate(home_rows, axis=0)
+    place[...] = home - 1.0
+    live = home > 0.5
+    before = dot(one_hot(live), one_hot(sub < lane))
+    rank[...] = jnp.where(live, before, -1.0)
+    most[...] = jnp.broadcast_to(jnp.max(jnp.sum(jnp.where(live, 1.0, 0.0), axis=1, keepdims=True)), most.shape)
+    total = jnp.zeros((negs, live_cap), F32)
+    wide = iota((live_cap, rows), 0)
+    pos = iota((live_cap, rows), 1)
+    for t in range(n):
+        pick = one_hot((wide == pos + starts[t]) & (pos < len_ref[t]))
+        total = total + dot(blocks[t][IDX_ROWS : IDX_ROWS + negs].astype(BF16), pick, ((1,), (1,)))
+    coef_t = total.astype(BF16)
+    coef_c[...] = coef_t
+    base = IDX_ROWS + negs
+    width = neg_rows.shape[1]
+    for s in range(n):
+        for b in range(width // rows):
+            neg_rows[per * s : per * (s + 1), b * rows : (b + 1) * rows] = blocks[s][base + per * b : base + per * (b + 1)]
+    neg = neg_rows[...].astype(BF16)
+    negatives[...] = neg
+    head_grad = dot(coef_t, neg, ((0,), (0,))).astype(BF16)
+    d_mixed[...] = dot(head_grad, w_rows[...], ((1,), (1,)))
+
+
+def pair_live(live_cap, starts):
+    row = iota((live_cap, 1), 0)
+    col = iota((1, live_cap), 1)
+    return (col <= row) & (tile_of(col, starts) > tile_of(row, starts) - SPAN) & (row < starts[-1])
+
+
+def forward_kernel(sizes, len_ref, received, place, d_mixed, compact, weights, att, stats):
+    n, rows, live_cap = sizes
+    head_dim = att.shape[1]
+    starts = starts_of(len_ref, n)
+    wide = iota((live_cap, rows), 0)
+    home = place[...].astype(jnp.int32)
+    pick = jnp.concatenate([one_hot(wide == home[s : s + 1]) for s in range(n)], axis=1)
+    both = dot(pick, received[...].reshape(n * rows, PARTS * head_dim)).astype(BF16)
+    compact[...] = both
+    u, v, q, k = (both[:, i * head_dim : (i + 1) * head_dim] for i in range(PARTS))
+    scores = dot(q, k, ((1,), (1,))) * (1.0 / math.sqrt(head_dim))
+    sig = jax.nn.sigmoid(scores)
+    w = jnp.where(pair_live(live_cap, starts), scores * sig * (1.0 / rows), 0.0).astype(BF16)
+    weights[...] = w
+    a = dot(w, v)
+    att[...] = a
+    dn = d_mixed[...] * u.astype(F32)
+    mean = jnp.sum(a, axis=1, keepdims=True) * (1.0 / head_dim)
+    cen = a - mean
+    lane = iota((live_cap, 128), 1)
+    cols = jnp.where(lane == 0, mean, 0.0)
+    cols = jnp.where(lane == 1, jnp.sum(cen * cen, axis=1, keepdims=True), cols)
+    cols = jnp.where(lane == 2, jnp.sum(dn, axis=1, keepdims=True), cols)
+    cols = jnp.where(lane == 3, jnp.sum(dn * cen, axis=1, keepdims=True), cols)
+    stats[...] = jnp.transpose(cols)[0:8]
+
+
+def merge_stats(a, b, count):
+    gap = b[0] - a[0]
+    return (
+        (a[0] + b[0]) * 0.5,
+        a[1] + b[1] + gap * gap * (0.5 * count),
+        a[2] + b[2],
+        a[3] + b[3] + (b[2] - a[2]) * gap * 0.5,
+    )
+
+
+def backward_kernel(sizes, len_ref, compact, weights, att, d_mixed, st0, st1, st2, st3, place, rank, coef_c, message, grads, d_sums):
+    n, rows, live_cap, slots = sizes
+    head_dim = att.shape[1]
+    width = head_dim * n
+    starts = starts_of(len_ref, n)
+    quad = [[st[i : i + 1] for i in range(4)] for st in (st0, st1, st2, st3)]
+    ab = merge_stats(quad[0], quad[1], 2 * head_dim)
+    cd = merge_stats(quad[2], quad[3], 2 * head_dim)
+    mean, m2, s_dn, s_dna = merge_stats(ab, cd, 4 * head_dim)
+    inv = lax.rsqrt(m2 * (1.0 / width) + eps)
+    table = jnp.concatenate([mean, inv, s_dn * (1.0 / width), s_dna * inv * (1.0 / width), jnp.zeros((124, live_cap), F32)], axis=0)
+    table = jnp.transpose(table)
+    mean, inv, mean_dn, mean_dnn = (table[:, i : i + 1] for i in range(4))
+    both = compact[...]
+    u, v, q, k = (both[:, i * head_dim : (i + 1) * head_dim] for i in range(PARTS))
+    u = u.astype(F32)
+    dm = d_mixed[...]
+    normed = (att[...] - mean) * inv
+    mixed = (normed * u).astype(BF16)
+    dn = dm * u
+    d_att = ((dn - mean_dn - normed * mean_dnn) * inv).astype(BF16)
+    scale = 1.0 / math.sqrt(head_dim)
+    scores = dot(q, k, ((1,), (1,))) * scale
+    sig = jax.nn.sigmoid(scores)
+    slope = sig * (1.0 + scores * (1.0 - sig)) * (scale / rows)
+    ds = jnp.where(pair_live(live_cap, starts), dot(d_att, v, ((1,), (1,))) * slope, 0.0).astype(BF16)
+    grad = jnp.concatenate(
+        [dm * normed, dot(weights[...], d_att, ((0,), (0,))), dot(ds, k), dot(ds, q, ((0,), (0,)))], axis=1
+    ).astype(BF16)
+    grads[...] = grad
+    d_sums[...] = dot(coef_c[...], mixed)
+    fill_slots(n, rows, slots, 0, place, rank, grad, message)
+    quarter = rows // PARTS
+    col = iota((rows, live_cap), 1)
+    row = iota((rows, live_cap), 0)
+    for t in range(n):
+        tile = dot(one_hot((col == row + starts[t]) & (row < len_ref[t])), mixed).astype(BF16)
+        for b in range(PARTS):
+            message[t, slots : slots + quarter, b * head_dim : (b + 1) * head_dim] = tile[b * quarter : (b + 1) * quarter]
+
+
+def fill_slots(n, rows, slots, first, place, rank, grad, message):
+    live_cap = grad.shape[0]
+    slot = iota((slots, rows), 0) + first
+    col = iota((slots, live_cap), 1)
+    for s in range(n):
+        hit = rank[s : s + 1].astype(jnp.int32) == slot
+        source = jnp.sum(jnp.where(hit, place[s : s + 1] + 1.0, 0.0), axis=1, keepdims=True) - 1.0
+        message[s, 0:slots] = dot(one_hot(source.astype(jnp.int32) == col), grad).astype(BF16)
+
+
+def rest_kernel(sizes, place, rank, grad, message):
+    n, rows, slots = sizes
+    fill_slots(n, rows, slots, slots, place, rank, grad[...], message)
+
+
+def finish_kernel(sizes, extra, me_ref, *refs):
+    n, rows, slots = sizes
+    rank, w_out, message = refs[:3]
+    d_home, layer_out = refs[-2:]
+    head_dim = message.shape[2] // PARTS
+    width = head_dim * n
+    quarter = rows // PARTS
+    own = rank[pl.ds(me_ref[0], 1), :].astype(jnp.int32)
+    total = slots * (1 + extra)
+    pick = one_hot(own == iota((total, rows), 0))
+    mixed = []
+    for h in range(n):
+        block = message[h, 0:slots]
+        if extra:
+            block = jnp.concatenate([block, refs[3][h]], axis=0)
+        full = dot(pick, block, ((0,), (0,))).astype(BF16)
+        for i in range(PARTS):
+            d_home[:, i * width + h * head_dim : i * width + (h + 1) * head_dim] = full[:, i * head_dim : (i + 1) * head_dim]
+        mixed.append(
+            jnp.concatenate([message[h, slots : slots + quarter, b * head_dim : (b + 1) * head_dim] for b in range(PARTS)], axis=0)
+        )
+    layer_out[...] = dot(jnp.concatenate(mixed, axis=1), w_out[...]).astype(BF16)
+
+
+def kernel_call(body, shapes, specs, scratch=(), cost=None):
+    return pl.pallas_call(
+        body,
+        out_shape=shapes,
+        in_specs=specs,
+        out_specs=jax.tree.map(lambda _: VMEM, shapes),
+        scratch_shapes=scratch,
+        compiler_params=pltpu.CompilerParams(vmem_limit_bytes=40 * 1024 * 1024),
+        cost_estimate=cost,
+    )
+
+
+def swap(block, axis, distance):
+    return lax.ppermute(block, axis, [(i, i ^ distance) for i in range(lax.axis_size(axis))])
+
+
+def head_plan(qkvu, w_out, head_coef, item_table, neg_ids, send_order, recv_order, tile_len):
+    n = lax.axis_size("seq")
+    groups = lax.axis_size("dp")
+    rows = qkvu.shape[0]
+    width = w_out.shape[0]
+    head_dim = width // HEADS
+    negs = head_coef.shape[1]
+    per = neg_ids.shape[0]
+    live_cap = -(-(n * rows // 3) // 128) * 128
+    sds = jax.ShapeDtypeStruct
+    me = lax.axis_index("seq")
+    me_arr = me.astype(jnp.int32).reshape(1)
+    lens = tile_len[0]
+    outgoing = qkvu.reshape(rows, PARTS, n, head_dim).transpose(2, 0, 1, 3).reshape(n, rows, PARTS * head_dim)
+    received = lax.all_to_all(outgoing, "seq", split_axis=0, concat_axis=0, tiled=True)
+
+    negatives = jnp.take(item_table, neg_ids, axis=0)
+    small = jnp.concatenate(
+        [
+            recv_order.astype(BF16),
+            send_order.astype(BF16),
+            jnp.zeros((IDX_ROWS - 2, rows), BF16),
+            head_coef.T,
+            negatives.reshape(per, width // rows, rows).transpose(1, 0, 2).reshape(-1, rows),
+        ],
+        axis=0,
+    )[None]
+    distance = 1
+    while distance < n:
+        small = jnp.concatenate([small, swap(small, "seq", distance)], axis=0)
+        distance *= 2
+    w_rows = lax.dynamic_slice_in_dim(w_out, me * head_dim, head_dim, axis=0)
+    place, rank, most, coef_c, d_mixed, neg_all = kernel_call(
+        functools.partial(index_kernel, (n, rows, live_cap, negs, per)),
+        (
+            sds((n, rows), F32),
+            sds((n, rows), F32),
+            sds((8, 128), F32),
+            sds((negs, live_cap), BF16),
+            sds((live_cap, head_dim), F32),
+            sds((negs, width), BF16),
+        ),
+        [SMEM, SMEM, VMEM, VMEM],
+        [pltpu.VMEM((negs, width), F32)],
+    )(me_arr, lens, small, w_rows)
+    distance = 1
+    while distance < groups:
+        most = jnp.maximum(most, swap(most, "dp", distance))
+        distance *= 2
+
+    compact, weights, att, stats = kernel_call(
+        functools.partial(forward_kernel, (n, rows, live_cap)),
+        (
+            sds((live_cap, PARTS * head_dim), BF16),
+            sds((live_cap, live_cap), BF16),
+            sds((live_cap, head_dim), F32),
+            sds((8, live_cap), F32),
+        ),
+        [SMEM, VMEM, VMEM, VMEM],
+    )(lens, received, place, d_mixed)
+    other = swap(stats, "seq", 1)
+    first = jnp.where(me % 2 == 0, 1.0, 0.0)
+    low, high = (stats, other)
+    gap = high[0] - low[0]
+    paired = jnp.stack(
+        [
+            (low[0] + high[0]) * 0.5,
+            low[1] + high[1] + gap * gap * (0.5 * head_dim),
+            low[2] + high[2],
+            low[3] + high[3] + (high[2] - low[2]) * gap * 0.5,
+        ]
+        + [jnp.zeros_like(gap)] * 4
+    )
+    far = [swap(paired, "seq", d) for d in (2, 4, 6)]
+    message, grads, d_sums = kernel_call(
+        functools.partial(backward_kernel, (n, rows, live_cap, SLOTS)),
+        (
+            sds((n, SLOTS + rows // PARTS, PARTS * head_dim), BF16),
+            sds((live_cap, PARTS * head_dim), BF16),
+            sds((negs, head_dim), F32),
+        ),
+        [SMEM] + [VMEM] * 11,
+    )(lens, compact, weights, att, d_mixed, paired, *far, place, rank, coef_c)
+    returned = lax.all_to_all(message, "seq", split_axis=0, concat_axis=0, tiled=True)
+    total = d_sums
+    for d in range(1, groups):
+        total = total + swap(d_sums, "dp", d)
+    neg_cols = lax.dynamic_slice_in_dim(neg_all, lax.axis_index("dp") * (width // groups), width // groups, axis=1)
+    d_w_out = lax.dot_general(
+        total, neg_cols.astype(F32), (((0,), (0,)), ((), ())), precision=lax.Precision.HIGHEST
+    )
+
+    out_shapes = (sds((rows, PARTS * width), BF16), sds((rows, width), BF16))
+
+    def finish_one(message, place, rank, grads):
+        return kernel_call(functools.partial(finish_kernel, (n, rows, SLOTS), 0), out_shapes, [SMEM] + [VMEM] * 3)(
+            me_arr, rank, w_out, message
+        )
+
+    def finish_two(message, place, rank, grads):
+        rest = kernel_call(
+            functools.partial(rest_kernel, (n, rows, SLOTS)), sds((n, SLOTS, PARTS * head_dim), BF16), [VMEM] * 3
+        )(place, rank, grads)
+        rest = lax.all_to_all(rest, "seq", split_axis=0, concat_axis=0, tiled=True)
+        return kernel_call(functools.partial(finish_kernel, (n, rows, SLOTS), 1), out_shapes, [SMEM] + [VMEM] * 4)(
+            me_arr, rank, w_out, message, rest
+        )
+
+    d_home, layer_out = lax.cond(most[0, 0] > SLOTS, finish_two, finish_one, returned, place, rank, grads)
+    return (layer_out, d_home, d_w_out)
+
+
 def solution(mesh):
     placed = (
         P(("dp", "seq"), None),
@@ -164,7 +501,7 @@
         P("dp", None),
     )
     return jax.shard_map(
-        on_device,
+        head_plan if mesh.shape["seq"] == HEADS else tile_plan,
         mesh=mesh,
         in_specs=placed,
         out_specs=(P(("dp", "seq"), None), P(("dp", "seq"), None), P("seq", "dp")),

time: 204 us -> 85.1 us (0.42)
  waiting for transfers between devices: 87.5 us -> 37.6 us
  local copies, waits for them, and re-layouts: 24.8 us -> 5.44 us
  matrix products: 18.6 us -> 0.93 us
  other arithmetic: 16.1 us -> 0.16 us
  between operations: 16.4 us -> 1.51 us
  blocking collectives: 14 us -> 0 us
  Pallas kernels: 0 us -> 10.8 us
  starting transfers between devices: 25.8 us -> 28.3 us
    reduce_scatter x2 -> x0, waiting for transfers between devices: 57.4 us -> none  [the longest x1 35 us: on_device(): lax.psum_scatter(lax.dot_general(mixed_rows, coef_live, (((0,), (0,)), ((...]
    ppermute x8 -> x12, waiting for transfers between devices: 7.1 us -> 29.5 us  [swap(): lax.ppermute(block, axis, [(i, i ^ distance) for i in range(lax.axis_size...]
    dot_general x10 -> x1, matrix products: 18.6 us -> 0.93 us  [head_plan(): lax.dot_general(total, neg_cols.astype(F32), (((0,), (0,)), ((), ())), pr...]
    all_to_all x2, waiting for transfers between devices: 23 us -> 8.13 us  [the longest x1 8.13 us: head_plan(): lax.all_to_all(message, 'seq', split_axis=0, concat_axis=0, tiled=True)]
    all_gather x1 -> x0, blocking collectives: 14 us -> none  [on_device(): lax.all_gather(jnp.take(item_table, neg_ids, axis=0), 'seq', axis=0, tile...]
    pallas_call x0 -> x4, Pallas kernels: none -> 10.8 us  [the longest x1 3.38 us: head_plan(): kernel_call(functools.partial(backward_kernel, (n, rows, live_cap, SLOTS)...]
    gather x3 -> x1, local copies, waits for them, and re-layouts: 7.66 us -> 0.57 us  [head_plan(): negatives = jnp.take(item_table, neg_ids, axis=0)]
    slice x6 -> x1, local copies, waits for them, and re-layouts: 6.82 us -> 0.51 us  [head_plan(): most[0, 0] > SLOTS]
  transfers between devices with their start and end apart: 12 -> 14, of which waited for: 5 -> 9; matrix products, arithmetic and copies ran while one was open for 11% -> 4% of each run, Pallas kernels for 0% -> 3%
where the time goes in v1:
time: 85.1 us; the launch traced here: 84.8 us
  waiting for transfers between devices  37.6 us (44%)
  starting transfers between devices  28.3 us (33%)
  Pallas kernels  10.8 us (13%)
  local copies, waits for them, and re-layouts  5.44 us (6%)
  between operations  1.51 us (2%)
  matrix products  0.93 us (1%)
    ppermute x12, waiting for transfers between devices, swap(): lax.ppermute(block, axis, [(i, i ^ distance) for i in range(lax.axis_size...  29.5 us
    ppermute x12, starting transfers between devices, swap(): lax.ppermute(block, axis, [(i, i ^ distance) for i in range(lax.axis_size...  18 us
    all_to_all x1, waiting for transfers between devices, head_plan(): lax.all_to_all(message, 'seq', split_axis=0, concat_axis=0, tiled=True)  8.13 us
    all_to_all x1, starting transfers between devices, head_plan(): lax.all_to_all(outgoing, 'seq', split_axis=0, concat_axis=0, tiled=True)  6.46 us
    all_to_all x1, starting transfers between devices, head_plan(): lax.all_to_all(message, 'seq', split_axis=0, concat_axis=0, tiled=True)  3.85 us
    pallas_call x1, Pallas kernels, head_plan(): kernel_call(functools.partial(backward_kernel, (n, rows, live_cap, SLOTS)...  3.38 us
    pallas_call x1, Pallas kernels, finish_one(): kernel_call(functools.partial(finish_kernel, (n, rows, SLOTS), 0), out_sh...  3.16 us
    pallas_call x1, Pallas kernels, head_plan(): kernel_call(functools.partial(index_kernel, (n, rows, live_cap, negs, per...  2.47 us
  transfers between devices with their start and end apart: 14, of which 9 were waited for; matrix products, arithmetic and copies ran while one was open for 4% of the time, Pallas kernels for 3%

profile of v1, /device:TPU:0, one launch (start us, length us, event | category | flops | bytes accessed | tf_op | source)
XLA Modules:
  0.0 84.8 jit_solution(14283517937517524955)
XLA Ops:
  0.6 1.5 %copy.13 = bf16[16,8,32,128]{3,2,1,0:T(8,128)(2,1)S(1)} copy(bf16[16,8,32,128]{3,1,2,0:T(8,128)(2,1)} %bitcast.21) | data formatting | bytes 2097152
  2.7 1.2 %reshape.37 = bf16[8,128,512]{2,1,0:T(8,128)(2,1)} reshape(bf16[8,128,4,128]{3,2,1,0:T(4,128)(2,1)S(1)} %bitcast.19) | data formatting | bytes 2097152 | tf_op jit(solution)/shard_map/reshape | solution.py:393
  3.9 6.5 %all-to-all-start.1 = ((bf16[8,128,512]{2,1,0:T(8,128)(2,1)}), bf16[8,128,512]{2,1,0:T(8,128)(2,1)S(1)}, u32[]{:S(2)}, u32[]{:S(2)}) async-start(bf16[8,128,512]{2,1,0:T(8,128)(2,1)} %reshape.37), calls=%async_computation.1 | async-start | bytes 2097152 | tf_op jit(solution)/shard_map/all_to_all | solution.py:394
  12.6 1.9 %collective-permute-start.1 = (bf16[2,80,128]{2,1,0:T(8,128)(2,1)S(1)}, bf16[2,80,128]{2,1,0:T(8,128)(2,1)S(1)}, u32[]{:S(2)}, u32[]{:S(2)}) collective-permute-start(bf16[2,80,128]{2,1,0:T(8,128)(2,1)S(1)} %pad_maximum_fusion.2), channel_id=1, source_target_pairs={{0,2},{1,3},{2,0},{3,1},{4,6},{5,7},{6,4},{7,5},{8,10},{9,11},{10,... | collective-permute-start | bytes 122888 | tf_op jit(solution)/shard_map/ppermute | solution.py:377
  14.5 14.7 %collective-permute-done.1 = bf16[2,80,128]{2,1,0:T(8,128)(2,1)S(1)} collective-permute-done((bf16[2,80,128]{2,1,0:T(8,128)(2,1)S(1)}, bf16[2,80,128]{2,1,0:T(8,128)(2,1)S(1)}, u32[]{:S(2)}, u32[]{:S(2)}) %collective-permute-start.1) | collective-permute-done | bytes 40992 | tf_op jit(solution)/shard_map/ppermute | solution.py:377
  29.2 4.6 %collective-permute-start.2 = (bf16[4,80,128]{2,1,0:T(8,128)(2,1)S(1)}, bf16[4,80,128]{2,1,0:T(8,128)(2,1)S(1)}, u32[]{:S(2)}, u32[]{:S(2)}) collective-permute-start(bf16[4,80,128]{2,1,0:T(8,128)(2,1)S(1)} %pad_maximum_fusion.1), channel_id=1, source_target_pairs={{0,4},{1,5},{2,6},{3,7},{4,0},{5,1},{6,2},{7,3},{8,12},{9,13},{10,... | collective-permute-start | bytes 245768 | tf_op jit(solution)/shard_map/ppermute | solution.py:377
  33.8 1.0 %constant_dynamic-slice_fusion.w_rows = bf16[128,1024]{1,0:T(8,128)(2,1)S(1)} fusion(bf16[1024,1024]{1,0:T(8,128)(2,1)} %param.11, s32[]{:T(128)S(6)} %select_n.18), kind=kLoop, calls=%fused_computation.22 | loop fusion | bytes 524292 | tf_op jit(solution)/shard_map/dynamic_slice | solution.py:411
  34.8 5.7 %collective-permute-done.2 = bf16[4,80,128]{2,1,0:T(8,128)(2,1)S(1)} collective-permute-done((bf16[4,80,128]{2,1,0:T(8,128)(2,1)S(1)}, bf16[4,80,128]{2,1,0:T(8,128)(2,1)S(1)}, u32[]{:S(2)}, u32[]{:S(2)}) %collective-permute-start.2) | collective-permute-done | bytes 81952 | tf_op jit(solution)/shard_map/ppermute | solution.py:377
  40.5 2.5 %shard_map.103 = (f32[8,128]{1,0:T(8,128)S(1)}, f32[8,128]{1,0:T(8,128)S(1)}, f32[8,128]{1,0:T(8,128)S(1)}, bf16[32,384]{1,0:T(8,128)(2,1)S(1)}, f32[384,128]{1,0:T(8,128)S(1)}, /*index=5*/bf16[32,1024]{1,0:T(8,128)(2,1)S(1)}) custom-call(s32[1]{0:T(128)} %bitcast.me_ref, s32[8]{0:T(128)S(1)} %bitcast.16, bf16[8,80,128]{2,1,0:T(8,128)(2,1)S(1)} %pad_maximum_fusion.gathered, ...), custom_call_target="tpu_custom_call" | custom-call | tf_op jit(solution)/shard_map/pallas_call | solution.py:412
  43.0 1.8 %shard_map.104 = (bf16[384,512]{1,0:T(8,128)(2,1)S(1)}, bf16[384,384]{1,0:T(8,128)(2,1)S(1)}, f32[384,128]{1,0:T(8,128)S(1)}, f32[8,384]{1,0:T(8,128)S(1)}) custom-call(s32[8]{0:T(128)S(1)} %bitcast.17, bf16[8,128,512]{2,1,0:T(8,128)(2,1)S(1)} %all-to-all-done.1.received, f32[8,128]{1,0:T(8,128)S(1)} %get-tuple-element.50.place, ...), custom_call_target="tpu_custom_call" | custom-call | tf_op jit(solution)/shard_map/pallas_call | solution.py:430
  44.8 1.2 %collective-permute-done.5 = f32[8,384]{1,0:T(8,128)S(1)} collective-permute-done((f32[8,384]{1,0:T(8,128)S(1)}, f32[8,384]{1,0:T(8,128)S(1)}, u32[]{:S(2)}, u32[]{:S(2)}) %collective-permute-start.5) | collective-permute-done | bytes 12320 | tf_op jit(solution)/shard_map/ppermute | solution.py:377
  46.1 1.8 %collective-permute-start.7 = (f32[8,384]{1,0:T(8,128)S(1)}, f32[8,384]{1,0:T(8,128)S(1)}, u32[]{:S(2)}, u32[]{:S(2)}) collective-permute-start(f32[8,384]{1,0:T(8,128)S(1)} %stack.5.st0), channel_id=1, source_target_pairs={{0,4},{1,5},{2,6},{3,7},{4,0},{5,1},{6,2},{7,3},{8,12},{9,13},{10,... | collective-permute-start | bytes 36872 | tf_op jit(solution)/shard_map/ppermute | solution.py:377
  47.9 2.6 %collective-permute-start.8 = (f32[8,384]{1,0:T(8,128)S(1)}, f32[8,384]{1,0:T(8,128)S(1)}, u32[]{:S(2)}, u32[]{:S(2)}) collective-permute-start(f32[8,384]{1,0:T(8,128)S(1)} %stack.5.st0), channel_id=1, source_target_pairs={{0,6},{1,7},{2,4},{3,5},{4,2},{5,3},{6,0},{7,1},{8,14},{9,15},{10,... | collective-permute-start | bytes 36872 | tf_op jit(solution)/shard_map/ppermute | solution.py:377
  50.8 2.6 %collective-permute-done.8.st3 = f32[8,384]{1,0:T(8,128)S(1)} collective-permute-done((f32[8,384]{1,0:T(8,128)S(1)}, f32[8,384]{1,0:T(8,128)S(1)}, u32[]{:S(2)}, u32[]{:S(2)}) %collective-permute-start.8) | collective-permute-done | bytes 12320 | tf_op jit(solution)/shard_map/ppermute | solution.py:377
  53.4 3.4 %shard_map.105 = (bf16[8,96,512]{2,1,0:T(8,128)(2,1)}, bf16[384,512]{1,0:T(8,128)(2,1)}, f32[32,128]{1,0:T(8,128)S(1)}) custom-call(s32[8]{0:T(128)S(1)} %bitcast.18, bf16[384,512]{1,0:T(8,128)(2,1)S(1)} %get-tuple-element.52.compact, bf16[384,384]{1,0:T(8,128)(2,1)S(1)} %get-tuple-element.53.weights, f32[384,128]{1,0:T(8,128)S(1)} %get-tuple-element.54.att, ...), custom_call_target="tpu_custom_call" | custom-call | tf_op jit(solution)/shard_map/pallas_call | solution.py:454
  56.8 3.8 %all-to-all-start.2 = ((bf16[8,96,512]{2,1,0:T(8,128)(2,1)}), bf16[8,96,512]{2,1,0:T(8,128)(2,1)S(1)}, u32[]{:S(2)}, u32[]{:S(2)}) async-start(bf16[8,96,512]{2,1,0:T(8,128)(2,1)} %get-tuple-element.57), calls=%async_computation.2 | async-start | bytes 1572864 | tf_op jit(solution)/shard_map/all_to_all | solution.py:463
  60.7 2.4 %collective-permute-start.11 = (f32[32,128]{1,0:T(8,128)S(1)}, f32[32,128]{1,0:T(8,128)S(1)}, u32[]{:S(2)}, u32[]{:S(2)}) collective-permute-start(f32[32,128]{1,0:T(8,128)S(1)} %get-tuple-element.61), channel_id=1, source_target_pairs={{0,24},{8,16},{16,8},{24,0},{1,25},{9,17},{17,9},{25,1},{2,26},{10... | collective-permute-start | bytes 49160 | tf_op jit(solution)/shard_map/ppermute | solution.py:377
  64.2 1.5 %collective-permute-start.3 = (f32[8,128]{1,0:T(8,128)S(1)}, f32[8,128]{1,0:T(8,128)S(1)}, u32[]{:S(2)}, u32[]{:S(2)}) collective-permute-start(f32[8,128]{1,0:T(8,128)S(1)} %get-tuple-element.48), channel_id=1, source_target_pairs={{0,8},{8,0},{16,24},{24,16},{1,9},{9,1},{17,25},{25,17},{2,10},{10... | collective-permute-start | bytes 12296 | tf_op jit(solution)/shard_map/ppermute | solution.py:377
  65.6 2.1 %collective-permute-done.3 = f32[8,128]{1,0:T(8,128)S(1)} collective-permute-done((f32[8,128]{1,0:T(8,128)S(1)}, f32[8,128]{1,0:T(8,128)S(1)}, u32[]{:S(2)}, u32[]{:S(2)}) %collective-permute-start.3) | collective-permute-done | bytes 4128 | tf_op jit(solution)/shard_map/ppermute | solution.py:377
  67.8 1.5 %collective-permute-start.4 = (f32[8,128]{1,0:T(8,128)S(1)}, f32[8,128]{1,0:T(8,128)S(1)}, u32[]{:S(2)}, u32[]{:S(2)}) collective-permute-start(f32[8,128]{1,0:T(8,128)S(1)} %max.6), channel_id=1, source_target_pairs={{0,16},{8,24},{16,0},{24,8},{1,17},{9,25},{17,1},{25,9},{2,18},{10... | collective-permute-start | bytes 12296 | tf_op jit(solution)/shard_map/ppermute | solution.py:377
  69.3 2.1 %collective-permute-done.4 = f32[8,128]{1,0:T(8,128)S(1)} collective-permute-done((f32[8,128]{1,0:T(8,128)S(1)}, f32[8,128]{1,0:T(8,128)S(1)}, u32[]{:S(2)}, u32[]{:S(2)}) %collective-permute-start.4) | collective-permute-done | bytes 4128 | tf_op jit(solution)/shard_map/ppermute | solution.py:377
  73.5 8.1 %all-to-all-done.2 = bf16[8,96,512]{2,1,0:T(8,128)(2,1)S(1)} async-done(((bf16[8,96,512]{2,1,0:T(8,128)(2,1)}), bf16[8,96,512]{2,1,0:T(8,128)(2,1)S(1)}, u32[]{:S(2)}, u32[]{:S(2)}) %all-to-all-start.2) | async-done | bytes 786464 | tf_op jit(solution)/shard_map/all_to_all | solution.py:463
  81.6 3.2 %conditional.1 = ((bf16[128,4096]{1,0:T(8,128)(2,1)}, bf16[128,1024]{1,0:T(8,128)(2,1)})) conditional(s32[]{:T(128)} %bitcast.7, (s32[1]{0:T(128)}, f32[8,128]{1,0:T(8,128)S(1)}, bf16[1024,1024]{1,0:T(8,128)(2,1)}, bf16[8,96,512]{2,1,0:T(8,128)(2,1)S(1)}) %tuple.14, (f32[8,128]{1,0:T(8,128)S(1)}, f32[8,128]{1,0:T(8,128)S(1)}, ...), branch_computations={%region_0.1_spmd, %region_1.2_spmd} | conditional | bytes 1048584 | solution.py:488
  81.6 3.2 %branch_0_fun.1 = (bf16[128,4096]{1,0:T(8,128)(2,1)}, bf16[128,1024]{1,0:T(8,128)(2,1)}) custom-call(s32[1]{0:T(128)} %get-tuple-element.20.me_ref, f32[8,128]{1,0:T(8,128)S(1)} %get-tuple-element.21.refs_0_, bf16[1024,1024]{1,0:T(8,128)(2,1)} %get-tuple-element.22.refs_1_, bf16[8,96,512]{2,1,0:T(8,128)(2,1)S(1)} %get-tuple-element.23.refs_2_), custom_call_target="tpu_custom_call" | custom-call | tf_op jit(solution)/shard_map/cond/branch_0_fun/pallas_call | solution.py:475
  (44 shorter events, 5.7 us)
Async XLA Ops:
  0.6 9.8 %copy-start = (bf16[512,1024]{1,0:T(8,128)(2,1)S(1)}, bf16[512,1024]{1,0:T(8,128)(2,1)}, u32[]{:S(2)}) copy-start(bf16[512,1024]{1,0:T(8,128)(2,1)} %param.13) | copy-start | bytes 3145732
  2.6 7.7 %copy-start.3 = (s32[1,128]{1,0:T(1,128)S(1)}, s32[1,128]{1,0:T(1,128)}, u32[]{:S(2)}) copy-start(s32[1,128]{1,0:T(1,128)} %param.16) | copy-start | bytes 1540
  2.6 7.7 %copy-start.4 = (s32[1,128]{1,0:T(1,128)S(1)}, s32[1,128]{1,0:T(1,128)}, u32[]{:S(2)}) copy-start(s32[1,128]{1,0:T(1,128)} %param.15) | copy-start | bytes 1540
  2.6 7.7 %copy-start.5 = (s32[4]{0:T(128)S(1)}, s32[4]{0:T(128)}, u32[]{:S(2)}) copy-start(s32[4]{0:T(128)} %param.14) | copy-start | bytes 52
  2.6 8.4 %copy-start.2 = (bf16[128,32]{0,1:T(8,128)(2,1)S(1)}, bf16[128,32]{0,1:T(8,128)(2,1)}, u32[]{:S(2)}) copy-start(bf16[128,32]{0,1:T(8,128)(2,1)} %param.12) | copy-start | bytes 24580
  3.9 36.6 %copy-start.1 = (s32[1,8]{1,0:T(1,128)S(1)}, s32[1,8]{1,0:T(1,128)}, u32[]{:S(2)}) copy-start(s32[1,8]{1,0:T(1,128)} %param.17) | copy-start | bytes 100
  3.9 39.1 %all-to-all-start.1 = ((bf16[8,128,512]{2,1,0:T(8,128)(2,1)}), bf16[8,128,512]{2,1,0:T(8,128)(2,1)S(1)}, u32[]{:S(2)}, u32[]{:S(2)}) async-start(bf16[8,128,512]{2,1,0:T(8,128)(2,1)} %reshape.37), calls=%async_computation.1 | async-start | bytes 2097152 | tf_op jit(solution)/shard_map/all_to_all | solution.py:394
  11.2 1.4 %collective-permute-start = (bf16[1,80,128]{2,1,0:T(8,128)(2,1)S(1)}, bf16[1,80,128]{2,1,0:T(8,128)(2,1)S(1)}, u32[]{:S(2)}, u32[]{:S(2)}) collective-permute-start(bf16[1,80,128]{2,1,0:T(8,128)(2,1)S(1)} %bitcast.22), channel_id=1, source_target_pairs={{0,1},{1,0},{2,3},{3,2},{4,5},{5,4},{6,7},{7,6},{8,9},{9,8},{10,11... | collective-permute-start | bytes 61448 | tf_op jit(solution)/shard_map/ppermute | solution.py:377
  12.6 16.6 %collective-permute-start.1 = (bf16[2,80,128]{2,1,0:T(8,128)(2,1)S(1)}, bf16[2,80,128]{2,1,0:T(8,128)(2,1)S(1)}, u32[]{:S(2)}, u32[]{:S(2)}) collective-permute-start(bf16[2,80,128]{2,1,0:T(8,128)(2,1)S(1)} %pad_maximum_fusion.2), channel_id=1, source_target_pairs={{0,2},{1,3},{2,0},{3,1},{4,6},{5,7},{6,4},{7,5},{8,10},{9,11},{10,... | collective-permute-start | bytes 122888 | tf_op jit(solution)/shard_map/ppermute | solution.py:377
  29.2 11.2 %collective-permute-start.2 = (bf16[4,80,128]{2,1,0:T(8,128)(2,1)S(1)}, bf16[4,80,128]{2,1,0:T(8,128)(2,1)S(1)}, u32[]{:S(2)}, u32[]{:S(2)}) collective-permute-start(bf16[4,80,128]{2,1,0:T(8,128)(2,1)S(1)} %pad_maximum_fusion.1), channel_id=1, source_target_pairs={{0,4},{1,5},{2,6},{3,7},{4,0},{5,1},{6,2},{7,3},{8,12},{9,13},{10,... | collective-permute-start | bytes 245768 | tf_op jit(solution)/shard_map/ppermute | solution.py:377
  44.8 1.2 %collective-permute-start.5 = (f32[8,384]{1,0:T(8,128)S(1)}, f32[8,384]{1,0:T(8,128)S(1)}, u32[]{:S(2)}, u32[]{:S(2)}) collective-permute-start(f32[8,384]{1,0:T(8,128)S(1)} %get-tuple-element.55), channel_id=1, source_target_pairs={{0,1},{1,0},{2,3},{3,2},{4,5},{5,4},{6,7},{7,6},{8,9},{9,8},{10,11... | collective-permute-start | bytes 36872 | tf_op jit(solution)/shard_map/ppermute | solution.py:377
  46.1 4.5 %collective-permute-start.6 = (f32[8,384]{1,0:T(8,128)S(1)}, f32[8,384]{1,0:T(8,128)S(1)}, u32[]{:S(2)}, u32[]{:S(2)}) collective-permute-start(f32[8,384]{1,0:T(8,128)S(1)} %stack.5.st0), channel_id=1, source_target_pairs={{0,2},{1,3},{2,0},{3,1},{4,6},{5,7},{6,4},{7,5},{8,10},{9,11},{10,... | collective-permute-start | bytes 36872 | tf_op jit(solution)/shard_map/ppermute | solution.py:377
  46.1 4.7 %collective-permute-start.7 = (f32[8,384]{1,0:T(8,128)S(1)}, f32[8,384]{1,0:T(8,128)S(1)}, u32[]{:S(2)}, u32[]{:S(2)}) collective-permute-start(f32[8,384]{1,0:T(8,128)S(1)} %stack.5.st0), channel_id=1, source_target_pairs={{0,4},{1,5},{2,6},{3,7},{4,0},{5,1},{6,2},{7,3},{8,12},{9,13},{10,... | collective-permute-start | bytes 36872 | tf_op jit(solution)/shard_map/ppermute | solution.py:377
  47.9 5.5 %collective-permute-start.8 = (f32[8,384]{1,0:T(8,128)S(1)}, f32[8,384]{1,0:T(8,128)S(1)}, u32[]{:S(2)}, u32[]{:S(2)}) collective-permute-start(f32[8,384]{1,0:T(8,128)S(1)} %stack.5.st0), channel_id=1, source_target_pairs={{0,6},{1,7},{2,4},{3,5},{4,2},{5,3},{6,0},{7,1},{8,14},{9,15},{10,... | collective-permute-start | bytes 36872 | tf_op jit(solution)/shard_map/ppermute | solution.py:377
  56.8 24.8 %all-to-all-start.2 = ((bf16[8,96,512]{2,1,0:T(8,128)(2,1)}), bf16[8,96,512]{2,1,0:T(8,128)(2,1)S(1)}, u32[]{:S(2)}, u32[]{:S(2)}) async-start(bf16[8,96,512]{2,1,0:T(8,128)(2,1)} %get-tuple-element.57), calls=%async_computation.2 | async-start | bytes 1572864 | tf_op jit(solution)/shard_map/all_to_all | solution.py:463
  60.7 11.9 %collective-permute-start.11 = (f32[32,128]{1,0:T(8,128)S(1)}, f32[32,128]{1,0:T(8,128)S(1)}, u32[]{:S(2)}, u32[]{:S(2)}) collective-permute-start(f32[32,128]{1,0:T(8,128)S(1)} %get-tuple-element.61), channel_id=1, source_target_pairs={{0,24},{8,16},{16,8},{24,0},{1,25},{9,17},{17,9},{25,1},{2,26},{10... | collective-permute-start | bytes 49160 | tf_op jit(solution)/shard_map/ppermute | solution.py:377
  63.1 9.5 %collective-permute-start.10 = (f32[32,128]{1,0:T(8,128)S(1)}, f32[32,128]{1,0:T(8,128)S(1)}, u32[]{:S(2)}, u32[]{:S(2)}) collective-permute-start(f32[32,128]{1,0:T(8,128)S(1)} %get-tuple-element.61), channel_id=1, source_target_pairs={{0,16},{8,24},{16,0},{24,8},{1,17},{9,25},{17,1},{25,9},{2,18},{10... | collective-permute-start | bytes 49160 | tf_op jit(solution)/shard_map/ppermute | solution.py:377
  63.6 9.0 %collective-permute-start.9 = (f32[32,128]{1,0:T(8,128)S(1)}, f32[32,128]{1,0:T(8,128)S(1)}, u32[]{:S(2)}, u32[]{:S(2)}) collective-permute-start(f32[32,128]{1,0:T(8,128)S(1)} %get-tuple-element.61), channel_id=1, source_target_pairs={{0,8},{8,0},{16,24},{24,16},{1,9},{9,1},{17,25},{25,17},{2,10},{10... | collective-permute-start | bytes 49160 | tf_op jit(solution)/shard_map/ppermute | solution.py:377
  64.2 3.6 %collective-permute-start.3 = (f32[8,128]{1,0:T(8,128)S(1)}, f32[8,128]{1,0:T(8,128)S(1)}, u32[]{:S(2)}, u32[]{:S(2)}) collective-permute-start(f32[8,128]{1,0:T(8,128)S(1)} %get-tuple-element.48), channel_id=1, source_target_pairs={{0,8},{8,0},{16,24},{24,16},{1,9},{9,1},{17,25},{25,17},{2,10},{10... | collective-permute-start | bytes 12296 | tf_op jit(solution)/shard_map/ppermute | solution.py:377
  67.8 3.6 %collective-permute-start.4 = (f32[8,128]{1,0:T(8,128)S(1)}, f32[8,128]{1,0:T(8,128)S(1)}, u32[]{:S(2)}, u32[]{:S(2)}) collective-permute-start(f32[8,128]{1,0:T(8,128)S(1)} %max.6), channel_id=1, source_target_pairs={{0,16},{8,24},{16,0},{24,8},{1,17},{9,25},{17,1},{25,9},{2,18},{10... | collective-permute-start | bytes 12296 | tf_op jit(solution)/shard_map/ppermute | solution.py:377

commit v2 on v0

--- a/solution.py
+++ b/solution.py
@@ -1,15 +1,28 @@
+import functools
 import math
 
 import jax
 import jax.numpy as jnp
 from jax import lax
+from jax.experimental import pallas as pl
+from jax.experimental.pallas import tpu as pltpu
 from jax.sharding import PartitionSpec as P
 
 HEADS = 8
 SPAN = 3
+PARTS = 4
+SLOTS = 64
+IDX_ROWS = 16
+LIMIT = 60 * 1024 * 1024
 
 
 eps = 1e-05
+
+VMEM = pl.BlockSpec(memory_space=pltpu.VMEM)
+SMEM = pl.BlockSpec(memory_space=pltpu.SMEM)
+ANY = pl.BlockSpec(memory_space=pl.ANY)
+F32 = jnp.float32
+BF16 = jnp.bfloat16
 
 
 def shifted(block, axis, distance):
@@ -39,7 +52,7 @@
     return heads_first.transpose(1, 0, 2).reshape(count, width)
 
 
-def on_device(qkvu, w_out, head_coef, item_table, neg_ids, send_order, recv_order, tile_len):
+def tile_plan(qkvu, w_out, head_coef, item_table, neg_ids, send_order, recv_order, tile_len):
     row_count = qkvu.shape[0]
     model_width = w_out.shape[0]
     head_dim = model_width // HEADS
@@ -152,6 +165,455 @@
     return (layer_out, d_home, d_w_out)
 
 
+def dot(a, b, dims=((1,), (0,))):
+    return lax.dot_general(a, b, (dims, ((), ())), preferred_element_type=F32)
+
+
+def iota(shape, dim):
+    return lax.broadcasted_iota(jnp.int32, shape, dim)
+
+
+def starts_of(len_ref, count):
+    starts = [jnp.int32(0)]
+    for t in range(count):
+        starts.append(starts[-1] + len_ref[0, t])
+    return starts
+
+
+def tile_of(position, starts):
+    tile = jnp.zeros(position.shape, jnp.int32)
+    for start in starts[1:-1]:
+        tile = tile + jnp.where(position >= start, 1, 0)
+    return tile
+
+
+def one_hot(condition):
+    return jnp.where(condition, 1.0, 0.0).astype(BF16)
+
+
+def prep_kernel(neg_ids, recv, coef_t, lens, table, small, meta, ids, recv_row, coef_rows, held, neg_rows, lines, sems):
+    per, chunk, width = held.shape
+    rows = small.shape[1]
+    negs = coef_t.shape[0]
+    first = [
+        pltpu.make_async_copy(neg_ids, ids, sems.at[0]),
+        pltpu.make_async_copy(recv, recv_row, sems.at[1]),
+        pltpu.make_async_copy(coef_t, coef_rows, sems.at[2]),
+        pltpu.make_async_copy(lens, meta, sems.at[3]),
+    ]
+    for copy in first:
+        copy.start()
+    first[0].wait()
+    copies = []
+    for j in range(per):
+        start = pl.multiple_of((ids[j] // chunk) * chunk, chunk)
+        copies.append(pltpu.make_async_copy(table.at[pl.ds(start, chunk)], held.at[j], sems.at[4 + j]))
+        copies[-1].start()
+    for copy in first[1:]:
+        copy.wait()
+    head = jnp.where(iota((IDX_ROWS, rows), 0) == 0, recv_row[...].astype(F32), 0.0)
+    small[0:IDX_ROWS] = head.astype(BF16)
+    small[IDX_ROWS : IDX_ROWS + negs] = coef_rows[...]
+    for j in range(per):
+        copies[j].wait()
+        own = iota((chunk, width), 0) == ids[j] % chunk
+        neg_rows[j : j + 1] = jnp.sum(jnp.where(own, held[j].astype(F32), 0.0), axis=0, keepdims=True)
+    for b in range(width // rows):
+        lines[per * b : per * (b + 1)] = neg_rows[0:per, b * rows : (b + 1) * rows]
+    small[IDX_ROWS + negs :] = lines[...].astype(BF16)
+
+
+def slot_table(me, len_ref, blocks, order_ref):
+    n, _, rows = order_ref.shape
+    cell = rows // n
+    for b in range(n):
+        order_ref[me ^ b] = blocks[b // 2][b % 2, 0:IDX_ROWS].astype(F32)[0:8]
+    starts = starts_of(len_ref, n)
+    pos = iota((cell, rows), 1)
+    filled = [jnp.broadcast_to(order_ref[t, 0:1], (cell, rows)) for t in range(n)]
+    value = [jnp.where(pos < len_ref[0, t], pos + starts[t] + 1, 0).astype(F32) for t in range(n)]
+    return jnp.concatenate(filled, axis=0), jnp.concatenate(value, axis=0)
+
+
+def slot_places(filled, value, source, cell):
+    slot = (iota(filled.shape, 0) % cell + source * cell).astype(F32)
+    return jnp.sum(jnp.where(filled == slot, value, 0.0), axis=1, keepdims=True)
+
+
+def slot_ranks(places):
+    rows = places.shape[0]
+    live = places > 0.5
+    before = dot(one_hot(iota((rows, rows), 1) < iota((rows, rows), 0)), one_hot(live))
+    return jnp.where(live, before, -1.0)
+
+
+def put_rows(me, head_dim, picked, outs):
+    width = picked.shape[1] // PARTS
+    for x in range(2 * len(outs)):
+        first = pl.multiple_of((me ^ x) * head_dim, head_dim)
+        outs[x // 2][x % 2] = jnp.concatenate([picked[:, pl.ds(i * width + first, head_dim)] for i in range(PARTS)], axis=1)
+
+
+def pack_kernel(sizes, me_ref, len_ref, b0, b1, b2, b3, send, qkvu, *refs):
+    n, rows, slots = sizes
+    pairs = n // 2
+    outs = refs[:pairs]
+    pick, order_ref, send_row, held, picked, sems = refs[pairs:]
+    cell = rows // n
+    me = me_ref[0]
+    copies = [pltpu.make_async_copy(send, send_row, sems.at[0]), pltpu.make_async_copy(qkvu, held, sems.at[1])]
+    for copy in copies:
+        copy.start()
+    filled, value = slot_table(me, len_ref, (b0, b1, b2, b3), order_ref)
+    places = jnp.broadcast_to(slot_places(filled, value, me, cell), (rows, rows))
+    lane = iota((rows, rows), 1)
+    sub = iota((rows, rows), 0)
+    by_rank = one_hot(slot_ranks(places) == lane.astype(F32))
+    copies[0].wait()
+    home = jnp.sum(jnp.where(lane == sub, send_row[...].astype(F32), 0.0), axis=1, keepdims=True)
+    chosen = dot(by_rank, one_hot(home == lane.astype(F32)), ((0,), (0,))).astype(BF16)
+    pick[...] = chosen
+    copies[1].wait()
+    picked[...] = dot(chosen[0:slots], held[...]).astype(BF16)
+    put_rows(me, held.shape[1] // (PARTS * n), picked, outs)
+
+
+def index_kernel(sizes, me_ref, len_ref, b0, b1, b2, b3, w_out, place, most, coef_c, d_mixed, negatives, order_ref, small_ref, neg_rows, w_rows, sem):
+    n, rows, live_cap, negs, per = sizes
+    cell = rows // n
+    me = me_ref[0]
+    blocks = (b0, b1, b2, b3)
+    span = w_rows.shape[0]
+    copy = pltpu.make_async_copy(w_out.at[pl.ds(pl.multiple_of(me * span, span), span)], w_rows, sem)
+    copy.start()
+    filled, value = slot_table(me, len_ref, blocks, order_ref)
+    lane = iota((rows, rows), 1)
+    places = jnp.zeros((rows, rows), F32)
+    columns = [slot_places(filled, value, s, cell) for s in range(n)]
+    for s in range(n):
+        places = jnp.where(lane == s, columns[s], places)
+    ranks = slot_ranks(places)
+    count = jnp.sum(jnp.where(places > 0.5, 1.0, 0.0), axis=0, keepdims=True)
+    most[...] = jnp.broadcast_to(jnp.max(count), most.shape)
+    for s in range(n):
+        hit = jnp.where(ranks[:, s : s + 1] == lane.astype(F32), columns[s], 0.0)
+        place[pl.ds(me ^ s, 1), :] = jnp.sum(hit, axis=0, keepdims=True) - 1.0
+    for b in range(n):
+        small_ref[me ^ b] = blocks[b // 2][b % 2, IDX_ROWS:].astype(F32)
+    starts = starts_of(len_ref, n)
+    total = jnp.zeros((negs, live_cap), F32)
+    wide = iota((live_cap, rows), 0)
+    pos = iota((live_cap, rows), 1)
+    for t in range(n):
+        pick = one_hot((wide == pos + starts[t]) & (pos < len_ref[0, t]))
+        total = total + dot(small_ref[t, 0:negs].astype(BF16), pick, ((1,), (1,)))
+    coef_t = total.astype(BF16)
+    coef_c[...] = coef_t
+    width = neg_rows.shape[1]
+    for s in range(n):
+        for b in range(width // rows):
+            neg_rows[per * s : per * (s + 1), b * rows : (b + 1) * rows] = small_ref[s, negs + per * b : negs + per * (b + 1)]
+    neg = neg_rows[...].astype(BF16)
+    negatives[...] = neg
+    head_grad = dot(coef_t, neg, ((0,), (0,))).astype(BF16)
+    copy.wait()
+    d_mixed[...] = dot(head_grad, w_rows[...], ((1,), (1,)))
+
+
+def pair_live(live_cap, starts):
+    row = iota((live_cap, 1), 0)
+    col = iota((1, live_cap), 1)
+    return (col <= row) & (tile_of(col, starts) > tile_of(row, starts) - SPAN) & (row < starts[-1])
+
+
+def slot_pick(live_cap, place, slots):
+    if slots < place.shape[1]:
+        pairs = [
+            jnp.concatenate([place[x : x + 1, :slots], place[x + 1 : x + 2, :slots]], axis=1)
+            for x in range(0, place.shape[0], 2)
+        ]
+    else:
+        pairs = [place[x : x + 1] for x in range(place.shape[0])]
+    row = iota((live_cap, pairs[0].shape[1]), 0).astype(F32)
+    return jnp.concatenate([one_hot(row == pair) for pair in pairs], axis=1)
+
+
+def by_distance(blocks):
+    return [block[i % 2] for i, block in enumerate(blocks)]
+
+
+def forward_kernel(sizes, len_ref, place, d_mixed, *refs):
+    n, rows, live_cap, slots = sizes
+    compact, weights, att, stats = refs[n:]
+    head_dim = att.shape[1]
+    starts = starts_of(len_ref, n)
+    both = dot(slot_pick(live_cap, place[...], slots), jnp.concatenate(by_distance(refs[:n]), axis=0)).astype(BF16)
+    compact[...] = both
+    u, v, q, k = (both[:, i * head_dim : (i + 1) * head_dim] for i in range(PARTS))
+    scores = dot(q, k, ((1,), (1,))) * (1.0 / math.sqrt(head_dim))
+    sig = jax.nn.sigmoid(scores)
+    w = jnp.where(pair_live(live_cap, starts), scores * sig * (1.0 / rows), 0.0).astype(BF16)
+    weights[...] = w
+    a = dot(w, v)
+    att[...] = a
+    dn = d_mixed[...] * u.astype(F32)
+    mean = jnp.sum(a, axis=1, keepdims=True) * (1.0 / head_dim)
+    cen = a - mean
+    lane = iota((live_cap, 128), 1)
+    cols = jnp.where(lane == 0, mean, 0.0)
+    cols = jnp.where(lane == 1, jnp.sum(cen * cen, axis=1, keepdims=True), cols)
+    cols = jnp.where(lane == 2, jnp.sum(dn, axis=1, keepdims=True), cols)
+    cols = jnp.where(lane == 3, jnp.sum(dn * cen, axis=1, keepdims=True), cols)
+    stats[...] = jnp.transpose(cols)[0:8]
+
+
+def merge_stats(a, b, count):
+    gap = b[0] - a[0]
+    return (
+        (a[0] + b[0]) * 0.5,
+        a[1] + b[1] + gap * gap * (0.5 * count),
+        a[2] + b[2],
+        a[3] + b[3] + (b[2] - a[2]) * gap * 0.5,
+    )
+
+
+def start_of(len_ref, n, tile):
+    start = jnp.int32(0)
+    for t in range(n):
+        start = start + jnp.where(t < tile, len_ref[0, t], 0)
+    return start
+
+
+def backward_kernel(sizes, me_ref, len_ref, compact, weights, att, d_mixed, st0, st1, st2, st3, place, *refs):
+    n, rows, live_cap, slots = sizes
+    outs = refs[: n // 2]
+    mixed_ref = refs[n // 2]
+    head_dim = att.shape[1]
+    width = head_dim * n
+    me = me_ref[0]
+    starts = starts_of(len_ref, n)
+    quad = [[st[i : i + 1] for i in range(4)] for st in (st0, st1, st2, st3)]
+    ab = merge_stats(quad[0], quad[1], 2 * head_dim)
+    cd = merge_stats(quad[2], quad[3], 2 * head_dim)
+    mean, m2, s_dn, s_dna = merge_stats(ab, cd, 4 * head_dim)
+    inv = lax.rsqrt(m2 * (1.0 / width) + eps)
+    table = jnp.concatenate([mean, inv, s_dn * (1.0 / width), s_dna * inv * (1.0 / width), jnp.zeros((124, live_cap), F32)], axis=0)
+    table = jnp.transpose(table)
+    mean, inv, mean_dn, mean_dnn = (table[:, i : i + 1] for i in range(4))
+    both = compact[...]
+    u, v, q, k = (both[:, i * head_dim : (i + 1) * head_dim] for i in range(PARTS))
+    u = u.astype(F32)
+    dm = d_mixed[...]
+    normed = (att[...] - mean) * inv
+    mixed = (normed * u).astype(BF16)
+    dn = dm * u
+    d_att = ((dn - mean_dn - normed * mean_dnn) * inv).astype(BF16)
+    scale = 1.0 / math.sqrt(head_dim)
+    scores = dot(q, k, ((1,), (1,))) * scale
+    sig = jax.nn.sigmoid(scores)
+    slope = sig * (1.0 + scores * (1.0 - sig)) * (scale / rows)
+    ds = jnp.where(pair_live(live_cap, starts), dot(d_att, v, ((1,), (1,))) * slope, 0.0).astype(BF16)
+    grad = jnp.concatenate(
+        [dm * normed, dot(weights[...], d_att, ((0,), (0,))), dot(ds, k), dot(ds, q, ((0,), (0,)))], axis=1
+    ).astype(BF16)
+    mixed_ref[...] = mixed
+    sent = dot(slot_pick(live_cap, place[...], slots), grad, ((0,), (0,))).astype(BF16)
+    quarter = rows // PARTS
+    col = iota((rows, live_cap), 1)
+    row = iota((rows, live_cap), 0)
+    for x in range(n):
+        outs[x // 2][x % 2, 0:slots] = sent[x * slots : (x + 1) * slots]
+        t = me ^ x
+        tile = dot(one_hot((col == row + start_of(len_ref, n, t)) & (row < len_ref[0, t])), mixed).astype(BF16)
+        outs[x // 2][x % 2, slots : slots + quarter] = jnp.concatenate(
+            [tile[b * quarter : (b + 1) * quarter] for b in range(PARTS)], axis=1
+        )
+
+
+def sums_kernel(coef_c, mixed, most, later, sums):
+    negs = coef_c.shape[0]
+    sums[0:negs] = dot(coef_c[...], mixed[...])
+    sums[negs:] = most[...]
+
+
+def finish_kernel(sizes, me_ref, pick_ref, w_out, negatives, *refs):
+    n, rows, slots, groups = sizes
+    sums = refs[:groups]
+    blocks = refs[groups : groups + n]
+    d_home, layer_out, d_w_out, mixed = refs[groups + n :]
+    me = me_ref[0]
+    wide = blocks[0].shape[2]
+    head_dim = wide // PARTS
+    width = head_dim * n
+    quarter = rows // PARTS
+    pick = pick_ref[0:slots]
+    for x, block in enumerate(by_distance(blocks)):
+        first = pl.multiple_of((me ^ x) * head_dim, head_dim)
+        full = dot(pick, block[0:slots], ((0,), (0,))).astype(BF16)
+        for i in range(PARTS):
+            d_home[:, pl.ds(i * width + first, head_dim)] = full[:, i * head_dim : (i + 1) * head_dim]
+        mixed[:, pl.ds(first, head_dim)] = jnp.concatenate(
+            [block[slots : slots + quarter, b * head_dim : (b + 1) * head_dim] for b in range(PARTS)], axis=0
+        )
+    layer_out[...] = dot(mixed[...], w_out[...]).astype(BF16)
+    negs = negatives.shape[0]
+    rest = functools.reduce(jnp.add, [part[0:negs] for part in sums])
+    columns = width // groups
+    neg = negatives[:, pl.ds(pl.multiple_of(me_ref[1] * columns, columns), columns)]
+    grad = jnp.zeros((head_dim, columns), F32)
+    for _ in range(3):
+        piece = rest.astype(BF16)
+        grad = grad + dot(piece, neg, ((0,), (0,)))
+        rest = rest - piece.astype(F32)
+    d_w_out[...] = grad
+
+
+def kernel_call(body, shapes, specs, scratch=(), limit=40):
+    return pl.pallas_call(
+        body,
+        out_shape=shapes,
+        in_specs=specs,
+        out_specs=jax.tree.map(lambda _: VMEM, shapes),
+        scratch_shapes=scratch,
+        compiler_params=pltpu.CompilerParams(vmem_limit_bytes=limit * 1024 * 1024),
+    )
+
+
+def swap(block, axis, distance):
+    return lax.ppermute(block, axis, [(i, i ^ distance) for i in range(lax.axis_size(axis))])
+
+
+def exchange(message, between):
+    far = [swap(own, "seq", 2 * d) for d, own in enumerate(message) if d > 0]
+    near = swap(message[0], "seq", 1)
+    made = between(near)
+    blocks = [message[0], near]
+    for own in far:
+        own, made = lax.optimization_barrier((own, made))
+        blocks += [own, swap(own, "seq", 1)]
+    return blocks, made
+
+
+def gather_small(block):
+    pair = jnp.stack([block, swap(block, "seq", 1)])
+    return [pair] + [swap(pair, "seq", d) for d in range(2, lax.axis_size("seq"), 2)]
+
+
+def head_plan(qkvu, w_out, head_coef, item_table, neg_ids, send_order, recv_order, tile_len):
+    n = lax.axis_size("seq")
+    groups = lax.axis_size("dp")
+    rows = qkvu.shape[0]
+    width = w_out.shape[0]
+    head_dim = width // HEADS
+    negs = head_coef.shape[1]
+    per = neg_ids.shape[0]
+    wide = PARTS * head_dim
+    live_cap = -(-(n * rows // 3) // 128) * 128
+    lines = per * width // rows
+    sds = jax.ShapeDtypeStruct
+    me = lax.axis_index("seq")
+    me_arr = jnp.stack([me, lax.axis_index("dp")]).astype(jnp.int32)
+    head_coef_t = head_coef.T
+
+    small, lens = pl.pallas_call(
+        prep_kernel,
+        out_shape=(sds((IDX_ROWS + negs + lines, rows), BF16), sds(tile_len.shape, jnp.int32)),
+        in_specs=[ANY] * 5,
+        out_specs=(VMEM, SMEM),
+        scratch_shapes=[
+            pltpu.SMEM((per,), jnp.int32),
+            pltpu.VMEM((1, rows), jnp.int32),
+            pltpu.VMEM((negs, rows), BF16),
+            pltpu.VMEM((per, 16, width), BF16),
+            pltpu.VMEM((8, width), F32),
+            pltpu.VMEM((lines, rows), F32),
+            pltpu.SemaphoreType.DMA((4 + per,)),
+        ],
+        compiler_params=pltpu.CompilerParams(vmem_limit_bytes=LIMIT),
+    )(neg_ids, recv_order, head_coef_t, tile_len, item_table)
+    blocks = gather_small(small)
+    def passes(slots):
+        *message, pick = kernel_call(
+            functools.partial(pack_kernel, (n, rows, slots)),
+            (sds((2, slots, wide), BF16),) * (n // 2) + (sds((rows, rows), BF16),),
+            [SMEM, SMEM] + [VMEM] * 4 + [ANY] * 2,
+            [
+                pltpu.VMEM((n, 8, rows), F32),
+                pltpu.VMEM((1, rows), jnp.int32),
+                pltpu.VMEM(qkvu.shape, BF16),
+                pltpu.VMEM((slots, PARTS * width), BF16),
+                pltpu.SemaphoreType.DMA((2,)),
+            ],
+        )(me_arr, lens, *blocks, send_order, qkvu)
+
+        def index(_):
+            return kernel_call(
+                functools.partial(index_kernel, (n, rows, live_cap, negs, per)),
+                (
+                    sds((n, rows), F32),
+                    sds((8, 128), F32),
+                    sds((negs, live_cap), BF16),
+                    sds((live_cap, head_dim), F32),
+                    sds((negs, width), BF16),
+                ),
+                [SMEM, SMEM] + [VMEM] * 4 + [ANY],
+                [
+                    pltpu.VMEM((n, 8, rows), F32),
+                    pltpu.VMEM((n, negs + lines, rows), F32),
+                    pltpu.VMEM((negs, width), F32),
+                    pltpu.VMEM((head_dim, width), BF16),
+                    pltpu.SemaphoreType.DMA,
+                ],
+            )(me_arr, lens, *blocks, w_out)
+
+        received, (place, most, coef_c, d_mixed, negatives) = exchange(message, index)
+        compact, weights, att, stats = kernel_call(
+            functools.partial(forward_kernel, (n, rows, live_cap, slots)),
+            (
+                sds((live_cap, wide), BF16),
+                sds((live_cap, live_cap), BF16),
+                sds((live_cap, head_dim), F32),
+                sds((8, live_cap), F32),
+            ),
+            [SMEM] + [VMEM] * (2 + n),
+        )(lens, place, d_mixed, *received)
+        other = swap(stats, "seq", 1)
+        paired = jnp.stack(
+            list(merge_stats([stats[i] for i in range(4)], [other[i] for i in range(4)], head_dim))
+            + [jnp.zeros_like(stats[0])] * 4
+        )
+        far = [swap(paired, "seq", d) for d in range(2, n, 2)]
+        *back, mixed = kernel_call(
+            functools.partial(backward_kernel, (n, rows, live_cap, slots)),
+            (sds((2, slots + rows // PARTS, wide), BF16),) * (n // 2) + (sds((live_cap, head_dim), BF16),),
+            [SMEM] * 2 + [VMEM] * 9,
+        )(me_arr, lens, compact, weights, att, d_mixed, paired, *far, place)
+
+        def group_sums(later):
+            sums = kernel_call(sums_kernel, sds((negs + 8, head_dim), F32), [VMEM] * 3 + [ANY])(
+                coef_c, mixed, most, later
+            )
+            sums = [sums] + [swap(sums, "dp", d) for d in range(1, groups)]
+            return sums, functools.reduce(jnp.maximum, sums)[negs, 0] > slots
+
+        returned, (sums, overflow) = exchange(back, group_sums)
+        return overflow, (pick, negatives, *sums, *returned)
+
+    def finish(slots, *parts):
+        return kernel_call(
+            functools.partial(finish_kernel, (n, rows, slots, groups)),
+            (sds((rows, PARTS * width), BF16), sds((rows, width), BF16), sds((head_dim, width // groups), F32)),
+            [SMEM] + [VMEM] * (3 + groups + n),
+            [pltpu.VMEM((rows, width), BF16)],
+        )(me_arr, parts[0], w_out, *parts[1:])
+
+    overflow, parts = passes(SLOTS)
+    d_home, layer_out, d_w_out = lax.cond(
+        overflow, lambda *_: finish(rows, *passes(rows)[1]), lambda *parts: finish(SLOTS, *parts), *parts
+    )
+    return (layer_out, d_home, d_w_out)
+
+
 def solution(mesh):
     placed = (
         P(("dp", "seq"), None),
@@ -164,7 +626,7 @@
         P("dp", None),
     )
     return jax.shard_map(
-        on_device,
+        head_plan if mesh.shape["seq"] == HEADS else tile_plan,
         mesh=mesh,
         in_specs=placed,
         out_specs=(P(("dp", "seq"), None), P(("dp", "seq"), None), P("seq", "dp")),

time: 204 us -> 69.6 us (0.34)
  the two profiles are of different devices: /device:TPU:0 before, /device:TPU:13 now
where the time goes in v2:
time: 69.6 us; the launch traced here: 69.3 us
  waiting for transfers between devices  24.7 us (35%)
  starting transfers between devices  23.7 us (34%)
  Pallas kernels  14 us (20%)
  between operations  3.37 us (5%)
  local copies, waits for them, and re-layouts  2.76 us (4%)
  other arithmetic  0.82 us (1%)
    ppermute x25, waiting for transfers between devices, swap(): lax.ppermute(block, axis, [(i, i ^ distance) for i in range(lax.axis_size...  24.7 us
    ppermute x25, starting transfers between devices, swap(): lax.ppermute(block, axis, [(i, i ^ distance) for i in range(lax.axis_size...  23.7 us
    pallas_call x1, Pallas kernels, finish(): kernel_call(functools.partial(finish_kernel, (n, rows, slots, groups)), (...  3 us
    slice x4, local copies, waits for them, and re-layouts, group_sums(): return (sums, functools.reduce(jnp.maximum, sums)[negs, 0] > slots)  2.72 us
    pallas_call x1, Pallas kernels, head_plan(): pl.pallas_call(prep_kernel, out_shape=(sds((IDX_ROWS + negs + lines, rows...  2.38 us
    pallas_call x1, Pallas kernels, index(): kernel_call(functools.partial(index_kernel, (n, rows, live_cap, negs, per...  2.31 us
    pallas_call x1, Pallas kernels, passes(): kernel_call(functools.partial(pack_kernel, (n, rows, slots)), (sds((2, sl...  2.25 us
    pallas_call x1, Pallas kernels, passes(): kernel_call(functools.partial(backward_kernel, (n, rows, live_cap, slots)...  2.23 us
  transfers between devices with their start and end apart: 25, of which 14 were waited for; matrix products, arithmetic and copies ran while one was open for 4% of the time, Pallas kernels for 4%

profile of v2, /device:TPU:13, one launch (start us, length us, event | category | flops | bytes accessed | tf_op | source)
XLA Modules:
  0.0 69.3 jit_solution(13820607139572337308)
XLA Ops:
  0.6 2.4 %shard_map.103 = (bf16[80,128]{1,0:T(8,128)(2,1)}, s32[1,8]{1,0:T(1,128)S(1)}) custom-call(s32[4]{0:T(128)} %neg_ids.1, s32[1,128]{1,0:T(1,128)} %recv.1, bf16[32,128]{1,0:T(8,128)(2,1)} %bitcast.8, s32[1,8]{1,0:T(1,128)} %lens.1, bf16[512,1024]{1,0:T(8,128)(2,1)} %table.1), custom_call_target="tpu_custom_call" | custom-call | tf_op jit(solution)/shard_map/pallas_call | solution.py:518
  5.5 1.3 %collective-permute-start.24 = (bf16[2,80,128]{2,1,0:T(8,128)(2,1)S(1)}, bf16[2,80,128]{2,1,0:T(8,128)(2,1)S(1)}, u32[]{:S(2)}, u32[]{:S(2)}) collective-permute-start(bf16[2,80,128]{2,1,0:T(8,128)(2,1)S(1)} %pad_maximum_fusion.b0), channel_id=1, source_target_pairs={{0,6},{1,7},{2,4},{3,5},{4,2},{5,3},{6,0},{7,1},{8,14},{9,15},{10,... | collective-permute-start | bytes 122888 | tf_op jit(solution)/shard_map/ppermute | solution.py:483
  7.8 1.2 %collective-permute-start.22 = (bf16[2,80,128]{2,1,0:T(8,128)(2,1)S(1)}, bf16[2,80,128]{2,1,0:T(8,128)(2,1)S(1)}, u32[]{:S(2)}, u32[]{:S(2)}) collective-permute-start(bf16[2,80,128]{2,1,0:T(8,128)(2,1)S(1)} %pad_maximum_fusion.b0), channel_id=1, source_target_pairs={{0,2},{1,3},{2,0},{3,1},{4,6},{5,7},{6,4},{7,5},{8,10},{9,11},{10,... | collective-permute-start | bytes 122888 | tf_op jit(solution)/shard_map/ppermute | solution.py:483
  9.1 1.5 %collective-permute-done.23.b2 = bf16[2,80,128]{2,1,0:T(8,128)(2,1)S(1)} collective-permute-done((bf16[2,80,128]{2,1,0:T(8,128)(2,1)S(1)}, bf16[2,80,128]{2,1,0:T(8,128)(2,1)S(1)}, u32[]{:S(2)}, u32[]{:S(2)}) %collective-permute-start.23) | collective-permute-done | bytes 40992 | tf_op jit(solution)/shard_map/ppermute | solution.py:483
  10.6 1.4 %collective-permute-done.22.b1 = bf16[2,80,128]{2,1,0:T(8,128)(2,1)S(1)} collective-permute-done((bf16[2,80,128]{2,1,0:T(8,128)(2,1)S(1)}, bf16[2,80,128]{2,1,0:T(8,128)(2,1)S(1)}, u32[]{:S(2)}, u32[]{:S(2)}) %collective-permute-start.22) | collective-permute-done | bytes 40992 | tf_op jit(solution)/shard_map/ppermute | solution.py:483
  12.0 2.3 %shard_map.104 = (bf16[2,64,512]{2,1,0:T(8,128)(2,1)S(1)}, bf16[2,64,512]{2,1,0:T(8,128)(2,1)S(1)}, bf16[2,64,512]{2,1,0:T(8,128)(2,1)S(1)}, bf16[2,64,512]{2,1,0:T(8,128)(2,1)S(1)}, bf16[128,128]{1,0:T(8,128)(2,1)S(1)}) custom-call(s32[2]{0:T(128)S(1)} %pad_add_fusion.me_ref, s32[1,8]{1,0:T(1,128)S(1)} %get-tuple-element.190.len_ref, ...), custom_call_target="tpu_custom_call" | custom-call | tf_op jit(solution)/shard_map/pallas_call | solution.py:536
  14.2 1.3 %collective-permute-start.27 = (bf16[2,64,512]{2,1,0:T(8,128)(2,1)S(1)}, bf16[2,64,512]{2,1,0:T(8,128)(2,1)S(1)}, u32[]{:S(2)}, u32[]{:S(2)}) collective-permute-start(bf16[2,64,512]{2,1,0:T(8,128)(2,1)S(1)} %get-tuple-element.194), channel_id=1, source_target_pairs={{0,2},{1,3},{2,0},{3,1},{4,6},{5,7},{6,4},{7,5},{8,10},{9,11},{10,... | collective-permute-start | bytes 393224 | tf_op jit(solution)/shard_map/ppermute | solution.py:483
  15.6 1.3 %collective-permute-start.26 = (bf16[2,64,512]{2,1,0:T(8,128)(2,1)S(1)}, bf16[2,64,512]{2,1,0:T(8,128)(2,1)S(1)}, u32[]{:S(2)}, u32[]{:S(2)}) collective-permute-start(bf16[2,64,512]{2,1,0:T(8,128)(2,1)S(1)} %get-tuple-element.193), channel_id=1, source_target_pairs={{0,4},{1,5},{2,6},{3,7},{4,0},{5,1},{6,2},{7,3},{8,12},{9,13},{10,... | collective-permute-start | bytes 393224 | tf_op jit(solution)/shard_map/ppermute | solution.py:483
  16.9 2.2 %collective-permute-start.28 = (bf16[2,64,512]{2,1,0:T(8,128)(2,1)S(1)}, bf16[2,64,512]{2,1,0:T(8,128)(2,1)S(1)}, u32[]{:S(2)}, u32[]{:S(2)}) collective-permute-start(bf16[2,64,512]{2,1,0:T(8,128)(2,1)S(1)} %get-tuple-element.212.refs_0_), channel_id=1, source_target_pairs={{0,1},{1,0},{2,3},{3,2},{4,5},{5,4},{6,7},{7,6},{8,9},{9,8},{10,11... | collective-permute-start | bytes 393224 | tf_op jit(solution)/shard_map/ppermute | solution.py:483
  19.2 2.3 %shard_map.105 = (f32[8,128]{1,0:T(8,128)S(1)}, f32[8,128]{1,0:T(8,128)S(1)}, bf16[32,384]{1,0:T(8,128)(2,1)S(1)}, f32[384,128]{1,0:T(8,128)S(1)}, bf16[32,1024]{1,0:T(8,128)(2,1)}) custom-call(s32[2]{0:T(128)S(1)} %pad_add_fusion.me_ref, s32[1,8]{1,0:T(1,128)S(1)} %get-tuple-element.190.len_ref, bf16[2,80,128]{2,1,0:T(8,128)(2,1)S(1)} %pad_maximum_fusion.b0, ...), custom_call_target="tpu_custom_call" | custom-call | tf_op jit(solution)/shard_map/pallas_call | solution.py:550
  21.5 6.2 %collective-permute-done.25.refs_6_ = bf16[2,64,512]{2,1,0:T(8,128)(2,1)S(1)} collective-permute-done((bf16[2,64,512]{2,1,0:T(8,128)(2,1)S(1)}, bf16[2,64,512]{2,1,0:T(8,128)(2,1)S(1)}, u32[]{:S(2)}, u32[]{:S(2)}) %collective-permute-start.25) | collective-permute-done | bytes 131104 | tf_op jit(solution)/shard_map/ppermute | solution.py:483
  27.7 2.1 %collective-permute-start.31 = (bf16[2,64,512]{2,1,0:T(8,128)(2,1)S(1)}, bf16[2,64,512]{2,1,0:T(8,128)(2,1)S(1)}, u32[]{:S(2)}, u32[]{:S(2)}) collective-permute-start(bf16[2,64,512]{2,1,0:T(8,128)(2,1)S(1)} %collective-permute-done.25.refs_6_), channel_id=1, source_target_pairs={{0,1},{1,0},{2,3},{3,2},{4,5},{5,4},{6,7},{7,6},{8,9},{9,8},{10,11... | collective-permute-start | bytes 393224 | tf_op jit(solution)/shard_map/ppermute | solution.py:483
  31.4 1.7 %shard_map.106 = (bf16[384,512]{1,0:T(8,128)(2,1)S(1)}, bf16[384,384]{1,0:T(8,128)(2,1)S(1)}, f32[384,128]{1,0:T(8,128)S(1)}, f32[8,384]{1,0:T(8,128)S(1)}) custom-call(s32[1,8]{1,0:T(1,128)S(1)} %get-tuple-element.190.len_ref, f32[8,128]{1,0:T(8,128)S(1)} %get-tuple-element.210.place, f32[384,128]{1,0:T(8,128)S(1)} %get-tuple-element.211.d_mixed, ...), custom_call_target="tpu_custom_call" | custom-call | tf_op jit(solution)/shard_map/pallas_call | solution.py:570
  34.3 1.4 %collective-permute-start.35 = (f32[8,384]{1,0:T(8,128)S(1)}, f32[8,384]{1,0:T(8,128)S(1)}, u32[]{:S(2)}, u32[]{:S(2)}) collective-permute-start(f32[8,384]{1,0:T(8,128)S(1)} %stack.38.st0), channel_id=1, source_target_pairs={{0,6},{1,7},{2,4},{3,5},{4,2},{5,3},{6,0},{7,1},{8,14},{9,15},{10,... | collective-permute-start | bytes 36872 | tf_op jit(solution)/shard_map/ppermute | solution.py:483
  37.0 2.1 %collective-permute-done.34.st2 = f32[8,384]{1,0:T(8,128)S(1)} collective-permute-done((f32[8,384]{1,0:T(8,128)S(1)}, f32[8,384]{1,0:T(8,128)S(1)}, u32[]{:S(2)}, u32[]{:S(2)}) %collective-permute-start.34) | collective-permute-done | bytes 12320 | tf_op jit(solution)/shard_map/ppermute | solution.py:483
  39.2 2.2 %shard_map.107 = (bf16[2,96,512]{2,1,0:T(8,128)(2,1)S(1)}, bf16[2,96,512]{2,1,0:T(8,128)(2,1)S(1)}, bf16[2,96,512]{2,1,0:T(8,128)(2,1)S(1)}, bf16[2,96,512]{2,1,0:T(8,128)(2,1)S(1)}, bf16[384,128]{1,0:T(8,128)(2,1)S(1)}) custom-call(s32[2]{0:T(128)S(1)} %pad_add_fusion.me_ref, s32[1,8]{1,0:T(1,128)S(1)} %get-tuple-element.190.len_ref, ...), custom_call_target="tpu_custom_call" | custom-call | tf_op jit(solution)/shard_map/pallas_call | solution.py:586
  41.4 1.8 %collective-permute-start.39 = (bf16[2,96,512]{2,1,0:T(8,128)(2,1)S(1)}, bf16[2,96,512]{2,1,0:T(8,128)(2,1)S(1)}, u32[]{:S(2)}, u32[]{:S(2)}) collective-permute-start(bf16[2,96,512]{2,1,0:T(8,128)(2,1)S(1)} %get-tuple-element.226), channel_id=1, source_target_pairs={{0,1},{1,0},{2,3},{3,2},{4,5},{5,4},{6,7},{7,6},{8,9},{9,8},{10,11... | collective-permute-start | bytes 589832 | tf_op jit(solution)/shard_map/ppermute | solution.py:483
  43.9 1.5 %collective-permute-start.37 = (bf16[2,96,512]{2,1,0:T(8,128)(2,1)S(1)}, bf16[2,96,512]{2,1,0:T(8,128)(2,1)S(1)}, u32[]{:S(2)}, u32[]{:S(2)}) collective-permute-start(bf16[2,96,512]{2,1,0:T(8,128)(2,1)S(1)} %get-tuple-element.221), channel_id=1, source_target_pairs={{0,4},{1,5},{2,6},{3,7},{4,0},{5,1},{6,2},{7,3},{8,12},{9,13},{10,... | collective-permute-start | bytes 589832 | tf_op jit(solution)/shard_map/ppermute | solution.py:483
  46.1 1.2 %collective-permute-start.40 = (f32[40,128]{1,0:T(8,128)S(1)}, f32[40,128]{1,0:T(8,128)S(1)}, u32[]{:S(2)}, u32[]{:S(2)}) collective-permute-start(f32[40,128]{1,0:T(8,128)S(1)} %shard_map.108), channel_id=1, source_target_pairs={{0,8},{8,0},{16,24},{24,16},{1,9},{9,1},{17,25},{25,17},{2,10},{10... | collective-permute-start | bytes 61448 | tf_op jit(solution)/shard_map/ppermute | solution.py:483
  47.5 1.5 %collective-permute-done.40 = f32[40,128]{1,0:T(8,128)S(1)} collective-permute-done((f32[40,128]{1,0:T(8,128)S(1)}, f32[40,128]{1,0:T(8,128)S(1)}, u32[]{:S(2)}, u32[]{:S(2)}) %collective-permute-start.40) | collective-permute-done | bytes 20512 | tf_op jit(solution)/shard_map/ppermute | solution.py:483
  53.7 1.2 %slice.72 = f32[1,1]{1,0:T(1,128)} slice(f32[40,128]{1,0:T(8,128)} %collective-permute-done.42), slice={[32:33], [0:1]} | slice | bytes 8 | tf_op jit(solution)/shard_map/slice | solution.py:597
  55.5 7.8 %collective-permute-done.36 = bf16[2,96,512]{2,1,0:T(8,128)(2,1)S(1)} collective-permute-done((bf16[2,96,512]{2,1,0:T(8,128)(2,1)S(1)}, bf16[2,96,512]{2,1,0:T(8,128)(2,1)S(1)}, u32[]{:S(2)}, u32[]{:S(2)}) %collective-permute-start.36) | collective-permute-done | bytes 196640 | tf_op jit(solution)/shard_map/ppermute | solution.py:483
  66.3 3.0 %conditional.1 = ((bf16[128,4096]{1,0:T(8,128)(2,1)}, bf16[128,1024]{1,0:T(8,128)(2,1)}, f32[128,256]{1,0:T(8,128)})) conditional(s32[]{:T(128)} %convert_element_type.3, (s32[2]{0:T(128)S(1)}, bf16[128,128]{1,0:T(8,128)(2,1)S(1)}, bf16[1024,1024]{1,0:T(8,128)(2,1)S(1)}, bf16[32,1024]{1,0:T(8,128)(2,1)}, f32[40,128]{1,0:T(8,128)S(1)}, ...), branch_computations={%region_0.0_spmd, %region_1.0_spmd} | conditional | flops 4992 | bytes 17007444 | solution.py:611
  66.3 3.0 %branch_0_fun.1 = (bf16[128,4096]{1,0:T(8,128)(2,1)}, bf16[128,1024]{1,0:T(8,128)(2,1)}, f32[128,256]{1,0:T(8,128)}) custom-call(s32[2]{0:T(128)S(1)} %get-tuple-element.50.me_ref, bf16[128,128]{1,0:T(8,128)(2,1)S(1)} %get-tuple-element.51.pick_ref, bf16[1024,1024]{1,0:T(8,128)(2,1)S(1)} %get-tuple-element.52.w_out, ...), custom_call_target="tpu_custom_call" | custom-call | tf_op jit(solution)/shard_map/cond/branch_0_fun/pallas_call | solution.py:603
  (49 shorter events, 15.0 us)
Async XLA Ops:
  3.0 1.8 %collective-permute-start.21 = (bf16[80,128]{1,0:T(8,128)(2,1)}, bf16[80,128]{1,0:T(8,128)(2,1)S(1)}, u32[]{:S(2)}, u32[]{:S(2)}) collective-permute-start(bf16[80,128]{1,0:T(8,128)(2,1)} %get-tuple-element.191), channel_id=1, source_target_pairs={{0,1},{1,0},{2,3},{3,2},{4,5},{5,4},{6,7},{7,6},{8,9},{9,8},{10,11... | collective-permute-start | bytes 61448 | tf_op jit(solution)/shard_map/ppermute | solution.py:483
  5.5 3.6 %collective-permute-start.24 = (bf16[2,80,128]{2,1,0:T(8,128)(2,1)S(1)}, bf16[2,80,128]{2,1,0:T(8,128)(2,1)S(1)}, u32[]{:S(2)}, u32[]{:S(2)}) collective-permute-start(bf16[2,80,128]{2,1,0:T(8,128)(2,1)S(1)} %pad_maximum_fusion.b0), channel_id=1, source_target_pairs={{0,6},{1,7},{2,4},{3,5},{4,2},{5,3},{6,0},{7,1},{8,14},{9,15},{10,... | collective-permute-start | bytes 122888 | tf_op jit(solution)/shard_map/ppermute | solution.py:483
  6.8 3.8 %collective-permute-start.23 = (bf16[2,80,128]{2,1,0:T(8,128)(2,1)S(1)}, bf16[2,80,128]{2,1,0:T(8,128)(2,1)S(1)}, u32[]{:S(2)}, u32[]{:S(2)}) collective-permute-start(bf16[2,80,128]{2,1,0:T(8,128)(2,1)S(1)} %pad_maximum_fusion.b0), channel_id=1, source_target_pairs={{0,4},{1,5},{2,6},{3,7},{4,0},{5,1},{6,2},{7,3},{8,12},{9,13},{10,... | collective-permute-start | bytes 122888 | tf_op jit(solution)/shard_map/ppermute | solution.py:483
  7.8 4.1 %collective-permute-start.22 = (bf16[2,80,128]{2,1,0:T(8,128)(2,1)S(1)}, bf16[2,80,128]{2,1,0:T(8,128)(2,1)S(1)}, u32[]{:S(2)}, u32[]{:S(2)}) collective-permute-start(bf16[2,80,128]{2,1,0:T(8,128)(2,1)S(1)} %pad_maximum_fusion.b0), channel_id=1, source_target_pairs={{0,2},{1,3},{2,0},{3,1},{4,6},{5,7},{6,4},{7,5},{8,10},{9,11},{10,... | collective-permute-start | bytes 122888 | tf_op jit(solution)/shard_map/ppermute | solution.py:483
  14.2 7.3 %collective-permute-start.27 = (bf16[2,64,512]{2,1,0:T(8,128)(2,1)S(1)}, bf16[2,64,512]{2,1,0:T(8,128)(2,1)S(1)}, u32[]{:S(2)}, u32[]{:S(2)}) collective-permute-start(bf16[2,64,512]{2,1,0:T(8,128)(2,1)S(1)} %get-tuple-element.194), channel_id=1, source_target_pairs={{0,2},{1,3},{2,0},{3,1},{4,6},{5,7},{6,4},{7,5},{8,10},{9,11},{10,... | collective-permute-start | bytes 393224 | tf_op jit(solution)/shard_map/ppermute | solution.py:483
  15.6 6.0 %collective-permute-start.26 = (bf16[2,64,512]{2,1,0:T(8,128)(2,1)S(1)}, bf16[2,64,512]{2,1,0:T(8,128)(2,1)S(1)}, u32[]{:S(2)}, u32[]{:S(2)}) collective-permute-start(bf16[2,64,512]{2,1,0:T(8,128)(2,1)S(1)} %get-tuple-element.193), channel_id=1, source_target_pairs={{0,4},{1,5},{2,6},{3,7},{4,0},{5,1},{6,2},{7,3},{8,12},{9,13},{10,... | collective-permute-start | bytes 393224 | tf_op jit(solution)/shard_map/ppermute | solution.py:483
  16.9 10.8 %collective-permute-start.25 = (bf16[2,64,512]{2,1,0:T(8,128)(2,1)S(1)}, bf16[2,64,512]{2,1,0:T(8,128)(2,1)S(1)}, u32[]{:S(2)}, u32[]{:S(2)}) collective-permute-start(bf16[2,64,512]{2,1,0:T(8,128)(2,1)S(1)} %get-tuple-element.192), channel_id=1, source_target_pairs={{0,6},{1,7},{2,4},{3,5},{4,2},{5,3},{6,0},{7,1},{8,14},{9,15},{10,... | collective-permute-start | bytes 393224 | tf_op jit(solution)/shard_map/ppermute | solution.py:483
  16.9 13.4 %collective-permute-start.28 = (bf16[2,64,512]{2,1,0:T(8,128)(2,1)S(1)}, bf16[2,64,512]{2,1,0:T(8,128)(2,1)S(1)}, u32[]{:S(2)}, u32[]{:S(2)}) collective-permute-start(bf16[2,64,512]{2,1,0:T(8,128)(2,1)S(1)} %get-tuple-element.212.refs_0_), channel_id=1, source_target_pairs={{0,1},{1,0},{2,3},{3,2},{4,5},{5,4},{6,7},{7,6},{8,9},{9,8},{10,11... | collective-permute-start | bytes 393224 | tf_op jit(solution)/shard_map/ppermute | solution.py:483
  27.7 3.1 %collective-permute-start.31 = (bf16[2,64,512]{2,1,0:T(8,128)(2,1)S(1)}, bf16[2,64,512]{2,1,0:T(8,128)(2,1)S(1)}, u32[]{:S(2)}, u32[]{:S(2)}) collective-permute-start(bf16[2,64,512]{2,1,0:T(8,128)(2,1)S(1)} %collective-permute-done.25.refs_6_), channel_id=1, source_target_pairs={{0,1},{1,0},{2,3},{3,2},{4,5},{5,4},{6,7},{7,6},{8,9},{9,8},{10,11... | collective-permute-start | bytes 393224 | tf_op jit(solution)/shard_map/ppermute | solution.py:483
  29.8 1.3 %collective-permute-start.30 = (bf16[2,64,512]{2,1,0:T(8,128)(2,1)S(1)}, bf16[2,64,512]{2,1,0:T(8,128)(2,1)S(1)}, u32[]{:S(2)}, u32[]{:S(2)}) collective-permute-start(bf16[2,64,512]{2,1,0:T(8,128)(2,1)S(1)} %collective-permute-done.26.refs_4_), channel_id=1, source_target_pairs={{0,1},{1,0},{2,3},{3,2},{4,5},{5,4},{6,7},{7,6},{8,9},{9,8},{10,11... | collective-permute-start | bytes 393224 | tf_op jit(solution)/shard_map/ppermute | solution.py:483
  29.9 1.5 %collective-permute-start.29 = (bf16[2,64,512]{2,1,0:T(8,128)(2,1)S(1)}, bf16[2,64,512]{2,1,0:T(8,128)(2,1)S(1)}, u32[]{:S(2)}, u32[]{:S(2)}) collective-permute-start(bf16[2,64,512]{2,1,0:T(8,128)(2,1)S(1)} %collective-permute-done.27.refs_2_), channel_id=1, source_target_pairs={{0,1},{1,0},{2,3},{3,2},{4,5},{5,4},{6,7},{7,6},{8,9},{9,8},{10,11... | collective-permute-start | bytes 393224 | tf_op jit(solution)/shard_map/ppermute | solution.py:483
  34.3 2.7 %collective-permute-start.35 = (f32[8,384]{1,0:T(8,128)S(1)}, f32[8,384]{1,0:T(8,128)S(1)}, u32[]{:S(2)}, u32[]{:S(2)}) collective-permute-start(f32[8,384]{1,0:T(8,128)S(1)} %stack.38.st0), channel_id=1, source_target_pairs={{0,6},{1,7},{2,4},{3,5},{4,2},{5,3},{6,0},{7,1},{8,14},{9,15},{10,... | collective-permute-start | bytes 36872 | tf_op jit(solution)/shard_map/ppermute | solution.py:483
  35.7 3.4 %collective-permute-start.34 = (f32[8,384]{1,0:T(8,128)S(1)}, f32[8,384]{1,0:T(8,128)S(1)}, u32[]{:S(2)}, u32[]{:S(2)}) collective-permute-start(f32[8,384]{1,0:T(8,128)S(1)} %stack.38.st0), channel_id=1, source_target_pairs={{0,4},{1,5},{2,6},{3,7},{4,0},{5,1},{6,2},{7,3},{8,12},{9,13},{10,... | collective-permute-start | bytes 36872 | tf_op jit(solution)/shard_map/ppermute | solution.py:483
  36.3 2.9 %collective-permute-start.33 = (f32[8,384]{1,0:T(8,128)S(1)}, f32[8,384]{1,0:T(8,128)S(1)}, u32[]{:S(2)}, u32[]{:S(2)}) collective-permute-start(f32[8,384]{1,0:T(8,128)S(1)} %stack.38.st0), channel_id=1, source_target_pairs={{0,2},{1,3},{2,0},{3,1},{4,6},{5,7},{6,4},{7,5},{8,10},{9,11},{10,... | collective-permute-start | bytes 36872 | tf_op jit(solution)/shard_map/ppermute | solution.py:483
  41.4 4.5 %collective-permute-start.39 = (bf16[2,96,512]{2,1,0:T(8,128)(2,1)S(1)}, bf16[2,96,512]{2,1,0:T(8,128)(2,1)S(1)}, u32[]{:S(2)}, u32[]{:S(2)}) collective-permute-start(bf16[2,96,512]{2,1,0:T(8,128)(2,1)S(1)} %get-tuple-element.226), channel_id=1, source_target_pairs={{0,1},{1,0},{2,3},{3,2},{4,5},{5,4},{6,7},{7,6},{8,9},{9,8},{10,11... | collective-permute-start | bytes 589832 | tf_op jit(solution)/shard_map/ppermute | solution.py:483
  43.3 12.2 %collective-permute-start.38 = (bf16[2,96,512]{2,1,0:T(8,128)(2,1)S(1)}, bf16[2,96,512]{2,1,0:T(8,128)(2,1)S(1)}, u32[]{:S(2)}, u32[]{:S(2)}) collective-permute-start(bf16[2,96,512]{2,1,0:T(8,128)(2,1)S(1)} %get-tuple-element.222), channel_id=1, source_target_pairs={{0,2},{1,3},{2,0},{3,1},{4,6},{5,7},{6,4},{7,5},{8,10},{9,11},{10,... | collective-permute-start | bytes 589832 | tf_op jit(solution)/shard_map/ppermute | solution.py:483
  43.9 11.6 %collective-permute-start.37 = (bf16[2,96,512]{2,1,0:T(8,128)(2,1)S(1)}, bf16[2,96,512]{2,1,0:T(8,128)(2,1)S(1)}, u32[]{:S(2)}, u32[]{:S(2)}) collective-permute-start(bf16[2,96,512]{2,1,0:T(8,128)(2,1)S(1)} %get-tuple-element.221), channel_id=1, source_target_pairs={{0,4},{1,5},{2,6},{3,7},{4,0},{5,1},{6,2},{7,3},{8,12},{9,13},{10,... | collective-permute-start | bytes 589832 | tf_op jit(solution)/shard_map/ppermute | solution.py:483
  45.5 17.8 %collective-permute-start.36 = (bf16[2,96,512]{2,1,0:T(8,128)(2,1)S(1)}, bf16[2,96,512]{2,1,0:T(8,128)(2,1)S(1)}, u32[]{:S(2)}, u32[]{:S(2)}) collective-permute-start(bf16[2,96,512]{2,1,0:T(8,128)(2,1)S(1)} %get-tuple-element.220), channel_id=1, source_target_pairs={{0,6},{1,7},{2,4},{3,5},{4,2},{5,3},{6,0},{7,1},{8,14},{9,15},{10,... | collective-permute-start | bytes 589832 | tf_op jit(solution)/shard_map/ppermute | solution.py:483
  46.1 2.9 %collective-permute-start.40 = (f32[40,128]{1,0:T(8,128)S(1)}, f32[40,128]{1,0:T(8,128)S(1)}, u32[]{:S(2)}, u32[]{:S(2)}) collective-permute-start(f32[40,128]{1,0:T(8,128)S(1)} %shard_map.108), channel_id=1, source_target_pairs={{0,8},{8,0},{16,24},{24,16},{1,9},{9,1},{17,25},{25,17},{2,10},{10... | collective-permute-start | bytes 61448 | tf_op jit(solution)/shard_map/ppermute | solution.py:483
  47.3 5.2 %collective-permute-start.41 = (f32[40,128]{1,0:T(8,128)S(1)}, f32[40,128]{1,0:T(8,128)S(1)}, u32[]{:S(2)}, u32[]{:S(2)}) collective-permute-start(f32[40,128]{1,0:T(8,128)S(1)} %shard_map.108), channel_id=1, source_target_pairs={{0,16},{8,24},{16,0},{24,8},{1,17},{9,25},{17,1},{25,9},{2,18},{10... | collective-permute-start | bytes 61448 | tf_op jit(solution)/shard_map/ppermute | solution.py:483
  49.0 4.7 %collective-permute-start.42 = (f32[40,128]{1,0:T(8,128)S(1)}, f32[40,128]{1,0:T(8,128)}, u32[]{:S(2)}, u32[]{:S(2)}) collective-permute-start(f32[40,128]{1,0:T(8,128)S(1)} %shard_map.108), channel_id=1, source_target_pairs={{0,24},{8,16},{16,8},{24,0},{1,25},{9,17},{17,9},{25,1},{2,26},{10... | collective-permute-start | bytes 61448 | tf_op jit(solution)/shard_map/ppermute | solution.py:483
  63.3 2.2 %collective-permute-start.45 = (bf16[2,96,512]{2,1,0:T(8,128)(2,1)S(1)}, bf16[2,96,512]{2,1,0:T(8,128)(2,1)S(1)}, u32[]{:S(2)}, u32[]{:S(2)}) collective-permute-start(bf16[2,96,512]{2,1,0:T(8,128)(2,1)S(1)} %collective-permute-done.36), channel_id=1, source_target_pairs={{0,1},{1,0},{2,3},{3,2},{4,5},{5,4},{6,7},{7,6},{8,9},{9,8},{10,11... | collective-permute-start | bytes 589832 | tf_op jit(solution)/shard_map/ppermute | solution.py:483
  64.5 1.7 %collective-permute-start.44 = (bf16[2,96,512]{2,1,0:T(8,128)(2,1)S(1)}, bf16[2,96,512]{2,1,0:T(8,128)(2,1)S(1)}, u32[]{:S(2)}, u32[]{:S(2)}) collective-permute-start(bf16[2,96,512]{2,1,0:T(8,128)(2,1)S(1)} %collective-permute-done.37), channel_id=1, source_target_pairs={{0,1},{1,0},{2,3},{3,2},{4,5},{5,4},{6,7},{7,6},{8,9},{9,8},{10,11... | collective-permute-start | bytes 589832 | tf_op jit(solution)/shard_map/ppermute | solution.py:483
  64.5 1.9 %collective-permute-start.43 = (bf16[2,96,512]{2,1,0:T(8,128)(2,1)S(1)}, bf16[2,96,512]{2,1,0:T(8,128)(2,1)}, u32[]{:S(2)}, u32[]{:S(2)}) collective-permute-start(bf16[2,96,512]{2,1,0:T(8,128)(2,1)S(1)} %collective-permute-done.38), channel_id=1, source_target_pairs={{0,1},{1,0},{2,3},{3,2},{4,5},{5,4},{6,7},{7,6},{8,9},{9,8},{10,11... | collective-permute-start | bytes 589832 | tf_op jit(solution)/shard_map/ppermute | solution.py:483
  (4 other events, 91.0 us)

commit v3 on v2

--- a/solution.py
+++ b/solution.py
@@ -12,8 +12,8 @@
 SPAN = 3
 PARTS = 4
 SLOTS = 64
-IDX_ROWS = 16
-LIMIT = 60 * 1024 * 1024
+EXTRA = 8
+LENS = 2
 
 
 eps = 1e-05
@@ -173,10 +173,10 @@
     return lax.broadcasted_iota(jnp.int32, shape, dim)
 
 
-def starts_of(len_ref, count):
+def starts_of(meta, count):
     starts = [jnp.int32(0)]
     for t in range(count):
-        starts.append(starts[-1] + len_ref[0, t])
+        starts.append(starts[-1] + meta[LENS + t])
     return starts
 
 
@@ -191,47 +191,15 @@
     return jnp.where(condition, 1.0, 0.0).astype(BF16)
 
 
-def prep_kernel(neg_ids, recv, coef_t, lens, table, small, meta, ids, recv_row, coef_rows, held, neg_rows, lines, sems):
-    per, chunk, width = held.shape
-    rows = small.shape[1]
-    negs = coef_t.shape[0]
-    first = [
-        pltpu.make_async_copy(neg_ids, ids, sems.at[0]),
-        pltpu.make_async_copy(recv, recv_row, sems.at[1]),
-        pltpu.make_async_copy(coef_t, coef_rows, sems.at[2]),
-        pltpu.make_async_copy(lens, meta, sems.at[3]),
-    ]
-    for copy in first:
-        copy.start()
-    first[0].wait()
-    copies = []
-    for j in range(per):
-        start = pl.multiple_of((ids[j] // chunk) * chunk, chunk)
-        copies.append(pltpu.make_async_copy(table.at[pl.ds(start, chunk)], held.at[j], sems.at[4 + j]))
-        copies[-1].start()
-    for copy in first[1:]:
-        copy.wait()
-    head = jnp.where(iota((IDX_ROWS, rows), 0) == 0, recv_row[...].astype(F32), 0.0)
-    small[0:IDX_ROWS] = head.astype(BF16)
-    small[IDX_ROWS : IDX_ROWS + negs] = coef_rows[...]
-    for j in range(per):
-        copies[j].wait()
-        own = iota((chunk, width), 0) == ids[j] % chunk
-        neg_rows[j : j + 1] = jnp.sum(jnp.where(own, held[j].astype(F32), 0.0), axis=0, keepdims=True)
-    for b in range(width // rows):
-        lines[per * b : per * (b + 1)] = neg_rows[0:per, b * rows : (b + 1) * rows]
-    small[IDX_ROWS + negs :] = lines[...].astype(BF16)
-
-
-def slot_table(me, len_ref, blocks, order_ref):
+def slot_table(meta, blocks, order_ref):
     n, _, rows = order_ref.shape
     cell = rows // n
     for b in range(n):
-        order_ref[me ^ b] = blocks[b // 2][b % 2, 0:IDX_ROWS].astype(F32)[0:8]
-    starts = starts_of(len_ref, n)
+        order_ref[meta[0] ^ b] = blocks[b // 2][b % 2].astype(F32)
+    starts = starts_of(meta, n)
     pos = iota((cell, rows), 1)
-    filled = [jnp.broadcast_to(order_ref[t, 0:1], (cell, rows)) for t in range(n)]
-    value = [jnp.where(pos < len_ref[0, t], pos + starts[t] + 1, 0).astype(F32) for t in range(n)]
+    filled = [jnp.broadcast_to(order_ref[t], (cell, rows)) for t in range(n)]
+    value = [jnp.where(pos < meta[LENS + t], pos + starts[t] + 1, 0).astype(F32) for t in range(n)]
     return jnp.concatenate(filled, axis=0), jnp.concatenate(value, axis=0)
 
 
@@ -254,39 +222,59 @@
         outs[x // 2][x % 2] = jnp.concatenate([picked[:, pl.ds(i * width + first, head_dim)] for i in range(PARTS)], axis=1)
 
 
-def pack_kernel(sizes, me_ref, len_ref, b0, b1, b2, b3, send, qkvu, *refs):
+def pack_kernel(sizes, meta, b0, b1, b2, b3, send, neg_ids, coef_t, table, qkvu, *refs):
     n, rows, slots = sizes
     pairs = n // 2
     outs = refs[:pairs]
-    pick, order_ref, send_row, held, picked, sems = refs[pairs:]
+    pick, order_ref, send_row, ids, coef_rows, items, neg_rows, held, picked, sems = refs[pairs:]
+    per, chunk, width = items.shape
+    wide = outs[0].shape[2]
     cell = rows // n
-    me = me_ref[0]
-    copies = [pltpu.make_async_copy(send, send_row, sems.at[0]), pltpu.make_async_copy(qkvu, held, sems.at[1])]
+    me = meta[0]
+    copies = [
+        pltpu.make_async_copy(source, target, sems.at[i])
+        for i, (source, target) in enumerate(((neg_ids, ids), (send, send_row), (coef_t, coef_rows), (qkvu, held)))
+    ]
     for copy in copies:
         copy.start()
-    filled, value = slot_table(me, len_ref, (b0, b1, b2, b3), order_ref)
+    copies[0].wait()
+    item_copies = []
+    for j in range(per):
+        start = pl.multiple_of((ids[j] // chunk) * chunk, chunk)
+        item_copies.append(pltpu.make_async_copy(table.at[pl.ds(start, chunk)], items.at[j], sems.at[4 + j]))
+        item_copies[-1].start()
+    filled, value = slot_table(meta, (b0, b1, b2, b3), order_ref)
     places = jnp.broadcast_to(slot_places(filled, value, me, cell), (rows, rows))
     lane = iota((rows, rows), 1)
     sub = iota((rows, rows), 0)
     by_rank = one_hot(slot_ranks(places) == lane.astype(F32))
-    copies[0].wait()
+    copies[1].wait()
     home = jnp.sum(jnp.where(lane == sub, send_row[...].astype(F32), 0.0), axis=1, keepdims=True)
     chosen = dot(by_rank, one_hot(home == lane.astype(F32)), ((0,), (0,))).astype(BF16)
     pick[...] = chosen
-    copies[1].wait()
+    copies[2].wait()
+    copies[3].wait()
     picked[...] = dot(chosen[0:slots], held[...]).astype(BF16)
-    put_rows(me, held.shape[1] // (PARTS * n), picked, outs)
-
-
-def index_kernel(sizes, me_ref, len_ref, b0, b1, b2, b3, w_out, place, most, coef_c, d_mixed, negatives, order_ref, small_ref, neg_rows, w_rows, sem):
-    n, rows, live_cap, negs, per = sizes
+    for j in range(per):
+        item_copies[j].wait()
+        own = iota((chunk, width), 0) == ids[j] % chunk
+        neg_rows[j : j + 1] = jnp.sum(jnp.where(own, items[j].astype(F32), 0.0), axis=0, keepdims=True)
+    step = coef_rows.shape[0] * rows // wide
+    coefs = jnp.concatenate([coef_rows[b * step : (b + 1) * step].astype(F32) for b in range(wide // rows)], axis=1)
+    negs = jnp.concatenate([neg_rows[0:per, b * wide : (b + 1) * wide] for b in range(width // wide)], axis=0)
+    head_dim = wide // PARTS
+    for x in range(n):
+        first = pl.multiple_of((me ^ x) * head_dim, head_dim)
+        out = outs[x // 2]
+        out[x % 2, 0:slots] = jnp.concatenate([picked[:, pl.ds(i * width + first, head_dim)] for i in range(PARTS)], axis=1)
+        out[x % 2, slots:] = (coefs, negs)[x % 2].astype(BF16)
+
+
+def index_kernel(sizes, meta, b0, b1, b2, b3, place, most, order_ref):
+    n, rows = sizes
     cell = rows // n
-    me = me_ref[0]
-    blocks = (b0, b1, b2, b3)
-    span = w_rows.shape[0]
-    copy = pltpu.make_async_copy(w_out.at[pl.ds(pl.multiple_of(me * span, span), span)], w_rows, sem)
-    copy.start()
-    filled, value = slot_table(me, len_ref, blocks, order_ref)
+    me = meta[0]
+    filled, value = slot_table(meta, (b0, b1, b2, b3), order_ref)
     lane = iota((rows, rows), 1)
     places = jnp.zeros((rows, rows), F32)
     columns = [slot_places(filled, value, s, cell) for s in range(n)]
@@ -298,26 +286,6 @@
     for s in range(n):
         hit = jnp.where(ranks[:, s : s + 1] == lane.astype(F32), columns[s], 0.0)
         place[pl.ds(me ^ s, 1), :] = jnp.sum(hit, axis=0, keepdims=True) - 1.0
-    for b in range(n):
-        small_ref[me ^ b] = blocks[b // 2][b % 2, IDX_ROWS:].astype(F32)
-    starts = starts_of(len_ref, n)
-    total = jnp.zeros((negs, live_cap), F32)
-    wide = iota((live_cap, rows), 0)
-    pos = iota((live_cap, rows), 1)
-    for t in range(n):
-        pick = one_hot((wide == pos + starts[t]) & (pos < len_ref[0, t]))
-        total = total + dot(small_ref[t, 0:negs].astype(BF16), pick, ((1,), (1,)))
-    coef_t = total.astype(BF16)
-    coef_c[...] = coef_t
-    width = neg_rows.shape[1]
-    for s in range(n):
-        for b in range(width // rows):
-            neg_rows[per * s : per * (s + 1), b * rows : (b + 1) * rows] = small_ref[s, negs + per * b : negs + per * (b + 1)]
-    neg = neg_rows[...].astype(BF16)
-    negatives[...] = neg
-    head_grad = dot(coef_t, neg, ((0,), (0,))).astype(BF16)
-    copy.wait()
-    d_mixed[...] = dot(head_grad, w_rows[...], ((1,), (1,)))
 
 
 def pair_live(live_cap, starts):
@@ -326,29 +294,51 @@
     return (col <= row) & (tile_of(col, starts) > tile_of(row, starts) - SPAN) & (row < starts[-1])
 
 
-def slot_pick(live_cap, place, slots):
-    if slots < place.shape[1]:
-        pairs = [
-            jnp.concatenate([place[x : x + 1, :slots], place[x + 1 : x + 2, :slots]], axis=1)
-            for x in range(0, place.shape[0], 2)
-        ]
-    else:
-        pairs = [place[x : x + 1] for x in range(place.shape[0])]
-    row = iota((live_cap, pairs[0].shape[1]), 0).astype(F32)
-    return jnp.concatenate([one_hot(row == pair) for pair in pairs], axis=1)
+def slot_pick(live_cap, place, slots, after):
+    n, rows = place.shape
+    padded = jnp.concatenate([place, jnp.full((n, rows), -1.0, F32)], axis=1)
+    padded = jnp.where(iota(padded.shape, 1) < slots, padded, -1.0)
+    line = jnp.concatenate([padded[x : x + 1, : slots + after] for x in range(n)], axis=1)
+    return one_hot(iota((live_cap, line.shape[1]), 0).astype(F32) == line)
 
 
 def by_distance(blocks):
     return [block[i % 2] for i, block in enumerate(blocks)]
 
 
-def forward_kernel(sizes, len_ref, place, d_mixed, *refs):
-    n, rows, live_cap, slots = sizes
-    compact, weights, att, stats = refs[n:]
+def forward_kernel(sizes, meta, place, w_out, *refs):
+    n, rows, live_cap, slots, per = sizes
+    blocks = refs[:n]
+    compact, weights, att, stats, coef_c, d_mixed, negatives, neg_rows, w_rows, sem = refs[n:]
     head_dim = att.shape[1]
-    starts = starts_of(len_ref, n)
-    both = dot(slot_pick(live_cap, place[...], slots), jnp.concatenate(by_distance(refs[:n]), axis=0)).astype(BF16)
+    negs = coef_c.shape[0]
+    wide = blocks[0].shape[2]
+    me = meta[0]
+    copy = pltpu.make_async_copy(w_out.at[pl.ds(pl.multiple_of(me * head_dim, head_dim), head_dim)], w_rows, sem)
+    copy.start()
+    starts = starts_of(meta, n)
+    both = dot(slot_pick(live_cap, place[...], slots, EXTRA), jnp.concatenate(by_distance(blocks), axis=0)).astype(BF16)
     compact[...] = both
+    total = jnp.zeros((negs, live_cap), F32)
+    tall = iota((live_cap, rows), 0)
+    pos = iota((live_cap, rows), 1)
+    for x in range(n):
+        t = me ^ x
+        hit = one_hot((tall == pos + start_of(meta, n, t)) & (pos < meta[LENS + t]))
+        coefs = blocks[x][0, slots:].astype(F32)
+        coefs = jnp.concatenate([coefs[:, b * rows : (b + 1) * rows] for b in range(wide // rows)], axis=0).astype(BF16)
+        total = total + dot(coefs, hit, ((1,), (1,)))
+        items = blocks[x][1, slots:].astype(F32)
+        for b in range(n * head_dim // wide):
+            neg_rows[t, 0:per, b * wide : (b + 1) * wide] = items[b * per : (b + 1) * per]
+    coef_t = total.astype(BF16)
+    coef_c[...] = coef_t
+    neg = jnp.concatenate([neg_rows[s, 0:per] for s in range(n)], axis=0).astype(BF16)
+    negatives[...] = neg
+    head_grad = dot(coef_t, neg, ((0,), (0,))).astype(BF16)
+    copy.wait()
+    dm = dot(head_grad, w_rows[...], ((1,), (1,)))
+    d_mixed[...] = dm
     u, v, q, k = (both[:, i * head_dim : (i + 1) * head_dim] for i in range(PARTS))
     scores = dot(q, k, ((1,), (1,))) * (1.0 / math.sqrt(head_dim))
     sig = jax.nn.sigmoid(scores)
@@ -356,7 +346,7 @@
     weights[...] = w
     a = dot(w, v)
     att[...] = a
-    dn = d_mixed[...] * u.astype(F32)
+    dn = dm * u.astype(F32)
     mean = jnp.sum(a, axis=1, keepdims=True) * (1.0 / head_dim)
     cen = a - mean
     lane = iota((live_cap, 128), 1)
@@ -377,21 +367,21 @@
     )
 
 
-def start_of(len_ref, n, tile):
+def start_of(meta, n, tile):
     start = jnp.int32(0)
     for t in range(n):
-        start = start + jnp.where(t < tile, len_ref[0, t], 0)
+        start = start + jnp.where(t < tile, meta[LENS + t], 0)
     return start
 
 
-def backward_kernel(sizes, me_ref, len_ref, compact, weights, att, d_mixed, st0, st1, st2, st3, place, *refs):
+def backward_kernel(sizes, meta, compact, weights, att, d_mixed, st0, st1, st2, st3, place, *refs):
     n, rows, live_cap, slots = sizes
     outs = refs[: n // 2]
     mixed_ref = refs[n // 2]
     head_dim = att.shape[1]
     width = head_dim * n
-    me = me_ref[0]
-    starts = starts_of(len_ref, n)
+    me = meta[0]
+    starts = starts_of(meta, n)
     quad = [[st[i : i + 1] for i in range(4)] for st in (st0, st1, st2, st3)]
     ab = merge_stats(quad[0], quad[1], 2 * head_dim)
     cd = merge_stats(quad[2], quad[3], 2 * head_dim)
@@ -417,31 +407,37 @@
         [dm * normed, dot(weights[...], d_att, ((0,), (0,))), dot(ds, k), dot(ds, q, ((0,), (0,)))], axis=1
     ).astype(BF16)
     mixed_ref[...] = mixed
-    sent = dot(slot_pick(live_cap, place[...], slots), grad, ((0,), (0,))).astype(BF16)
+    sent = dot(slot_pick(live_cap, place[...], slots, 0), grad, ((0,), (0,))).astype(BF16)
     quarter = rows // PARTS
     col = iota((rows, live_cap), 1)
     row = iota((rows, live_cap), 0)
     for x in range(n):
-        outs[x // 2][x % 2, 0:slots] = sent[x * slots : (x + 1) * slots]
+        outs[x // 2][x % 2, quarter:] = sent[x * slots : (x + 1) * slots]
         t = me ^ x
-        tile = dot(one_hot((col == row + start_of(len_ref, n, t)) & (row < len_ref[0, t])), mixed).astype(BF16)
-        outs[x // 2][x % 2, slots : slots + quarter] = jnp.concatenate(
+        tile = dot(one_hot((col == row + start_of(meta, n, t)) & (row < meta[LENS + t])), mixed).astype(BF16)
+        outs[x // 2][x % 2, 0:quarter] = jnp.concatenate(
             [tile[b * quarter : (b + 1) * quarter] for b in range(PARTS)], axis=1
         )
 
 
-def sums_kernel(coef_c, mixed, most, later, sums):
+def sums_kernel(coef_c, mixed, most, sums):
     negs = coef_c.shape[0]
     sums[0:negs] = dot(coef_c[...], mixed[...])
     sums[negs:] = most[...]
 
 
-def finish_kernel(sizes, me_ref, pick_ref, w_out, negatives, *refs):
+def total_kernel(*refs):
+    sums, (total, most) = refs[:-2], refs[-2:]
+    negs = total.shape[0]
+    total[...] = functools.reduce(jnp.add, [part[0:negs] for part in sums])
+    most[...] = functools.reduce(jnp.maximum, [part[negs:] for part in sums])
+
+
+def finish_kernel(sizes, meta, pick_ref, w_out, negatives, total, *refs):
     n, rows, slots, groups = sizes
-    sums = refs[:groups]
-    blocks = refs[groups : groups + n]
-    d_home, layer_out, d_w_out, mixed = refs[groups + n :]
-    me = me_ref[0]
+    blocks = refs[:n]
+    d_home, layer_out, d_w_out, mixed = refs[n:]
+    me = meta[0]
     wide = blocks[0].shape[2]
     head_dim = wide // PARTS
     width = head_dim * n
@@ -449,17 +445,16 @@
     pick = pick_ref[0:slots]
     for x, block in enumerate(by_distance(blocks)):
         first = pl.multiple_of((me ^ x) * head_dim, head_dim)
-        full = dot(pick, block[0:slots], ((0,), (0,))).astype(BF16)
+        full = dot(pick, block[quarter:], ((0,), (0,))).astype(BF16)
         for i in range(PARTS):
             d_home[:, pl.ds(i * width + first, head_dim)] = full[:, i * head_dim : (i + 1) * head_dim]
         mixed[:, pl.ds(first, head_dim)] = jnp.concatenate(
-            [block[slots : slots + quarter, b * head_dim : (b + 1) * head_dim] for b in range(PARTS)], axis=0
+            [block[0:quarter, b * head_dim : (b + 1) * head_dim] for b in range(PARTS)], axis=0
         )
     layer_out[...] = dot(mixed[...], w_out[...]).astype(BF16)
-    negs = negatives.shape[0]
-    rest = functools.reduce(jnp.add, [part[0:negs] for part in sums])
     columns = width // groups
-    neg = negatives[:, pl.ds(pl.multiple_of(me_ref[1] * columns, columns), columns)]
+    neg = negatives[:, pl.ds(pl.multiple_of(meta[1] * columns, columns), columns)]
+    rest = total[...]
     grad = jnp.zeros((head_dim, columns), F32)
     for _ in range(3):
         piece = rest.astype(BF16)
@@ -485,9 +480,8 @@
 
 def exchange(message, between):
     far = [swap(own, "seq", 2 * d) for d, own in enumerate(message) if d > 0]
-    near = swap(message[0], "seq", 1)
-    made = between(near)
-    blocks = [message[0], near]
+    made = between()
+    blocks = [message[0], swap(message[0], "seq", 1)]
     for own in far:
         own, made = lax.optimization_barrier((own, made))
         blocks += [own, swap(own, "seq", 1)]
@@ -509,74 +503,53 @@
     per = neg_ids.shape[0]
     wide = PARTS * head_dim
     live_cap = -(-(n * rows // 3) // 128) * 128
-    lines = per * width // rows
     sds = jax.ShapeDtypeStruct
     me = lax.axis_index("seq")
-    me_arr = jnp.stack([me, lax.axis_index("dp")]).astype(jnp.int32)
+    meta = jnp.concatenate([jnp.stack([me, lax.axis_index("dp")]).astype(jnp.int32), tile_len[0]])
     head_coef_t = head_coef.T
 
-    small, lens = pl.pallas_call(
-        prep_kernel,
-        out_shape=(sds((IDX_ROWS + negs + lines, rows), BF16), sds(tile_len.shape, jnp.int32)),
-        in_specs=[ANY] * 5,
-        out_specs=(VMEM, SMEM),
-        scratch_shapes=[
-            pltpu.SMEM((per,), jnp.int32),
-            pltpu.VMEM((1, rows), jnp.int32),
-            pltpu.VMEM((negs, rows), BF16),
-            pltpu.VMEM((per, 16, width), BF16),
-            pltpu.VMEM((8, width), F32),
-            pltpu.VMEM((lines, rows), F32),
-            pltpu.SemaphoreType.DMA((4 + per,)),
-        ],
-        compiler_params=pltpu.CompilerParams(vmem_limit_bytes=LIMIT),
-    )(neg_ids, recv_order, head_coef_t, tile_len, item_table)
-    blocks = gather_small(small)
     def passes(slots):
+        orders = gather_small(recv_order)
         *message, pick = kernel_call(
             functools.partial(pack_kernel, (n, rows, slots)),
-            (sds((2, slots, wide), BF16),) * (n // 2) + (sds((rows, rows), BF16),),
-            [SMEM, SMEM] + [VMEM] * 4 + [ANY] * 2,
+            (sds((2, slots + EXTRA, wide), BF16),) * (n // 2) + (sds((rows, rows), BF16),),
+            [SMEM] + [VMEM] * 4 + [ANY] * 5,
             [
-                pltpu.VMEM((n, 8, rows), F32),
+                pltpu.VMEM((n, 1, rows), F32),
                 pltpu.VMEM((1, rows), jnp.int32),
+                pltpu.SMEM((per,), jnp.int32),
+                pltpu.VMEM((negs, rows), BF16),
+                pltpu.VMEM((per, 16, width), BF16),
+                pltpu.VMEM((8, width), F32),
                 pltpu.VMEM(qkvu.shape, BF16),
                 pltpu.VMEM((slots, PARTS * width), BF16),
-                pltpu.SemaphoreType.DMA((2,)),
+                pltpu.SemaphoreType.DMA((4 + per,)),
             ],
-        )(me_arr, lens, *blocks, send_order, qkvu)
-
-        def index(_):
+        )(meta, *orders, send_order, neg_ids, head_coef_t, item_table, qkvu)
+
+        def index():
             return kernel_call(
-                functools.partial(index_kernel, (n, rows, live_cap, negs, per)),
-                (
-                    sds((n, rows), F32),
-                    sds((8, 128), F32),
-                    sds((negs, live_cap), BF16),
-                    sds((live_cap, head_dim), F32),
-                    sds((negs, width), BF16),
-                ),
-                [SMEM, SMEM] + [VMEM] * 4 + [ANY],
-                [
-                    pltpu.VMEM((n, 8, rows), F32),
-                    pltpu.VMEM((n, negs + lines, rows), F32),
-                    pltpu.VMEM((negs, width), F32),
-                    pltpu.VMEM((head_dim, width), BF16),
-                    pltpu.SemaphoreType.DMA,
-                ],
-            )(me_arr, lens, *blocks, w_out)
-
-        received, (place, most, coef_c, d_mixed, negatives) = exchange(message, index)
-        compact, weights, att, stats = kernel_call(
-            functools.partial(forward_kernel, (n, rows, live_cap, slots)),
+                functools.partial(index_kernel, (n, rows)),
+                (sds((n, rows), F32), sds((8, 128), F32)),
+                [SMEM] + [VMEM] * 4,
+                [pltpu.VMEM((n, 1, rows), F32)],
+            )(meta, *orders)
+
+        received, (place, most) = exchange(message, index)
+        compact, weights, att, stats, coef_c, d_mixed, negatives = kernel_call(
+            functools.partial(forward_kernel, (n, rows, live_cap, slots, per)),
             (
                 sds((live_cap, wide), BF16),
                 sds((live_cap, live_cap), BF16),
                 sds((live_cap, head_dim), F32),
                 sds((8, live_cap), F32),
+                sds((negs, live_cap), BF16),
+                sds((live_cap, head_dim), F32),
+                sds((negs, width), BF16),
             ),
-            [SMEM] + [VMEM] * (2 + n),
-        )(lens, place, d_mixed, *received)
+            [SMEM, VMEM, ANY] + [VMEM] * n,
+            [pltpu.VMEM((n, 8, width), F32), pltpu.VMEM((head_dim, width), BF16), pltpu.SemaphoreType.DMA],
+        )(meta, place, w_out, *received)
         other = swap(stats, "seq", 1)
         paired = jnp.stack(
             list(merge_stats([stats[i] for i in range(4)], [other[i] for i in range(4)], head_dim))
@@ -586,26 +559,27 @@
         *back, mixed = kernel_call(
             functools.partial(backward_kernel, (n, rows, live_cap, slots)),
             (sds((2, slots + rows // PARTS, wide), BF16),) * (n // 2) + (sds((live_cap, head_dim), BF16),),
-            [SMEM] * 2 + [VMEM] * 9,
-        )(me_arr, lens, compact, weights, att, d_mixed, paired, *far, place)
-
-        def group_sums(later):
-            sums = kernel_call(sums_kernel, sds((negs + 8, head_dim), F32), [VMEM] * 3 + [ANY])(
-                coef_c, mixed, most, later
-            )
+            [SMEM] + [VMEM] * 9,
+        )(meta, compact, weights, att, d_mixed, paired, *far, place)
+
+        def group_sums():
+            sums = kernel_call(sums_kernel, sds((negs + 8, head_dim), F32), [VMEM] * 3)(coef_c, mixed, most)
             sums = [sums] + [swap(sums, "dp", d) for d in range(1, groups)]
-            return sums, functools.reduce(jnp.maximum, sums)[negs, 0] > slots
-
-        returned, (sums, overflow) = exchange(back, group_sums)
-        return overflow, (pick, negatives, *sums, *returned)
+            total, most_of_all = kernel_call(
+                total_kernel, (sds((negs, head_dim), F32), sds((8, 128), F32)), [VMEM] * groups
+            )(*sums)
+            return total, most_of_all[0, 0] > slots
+
+        returned, (total, overflow) = exchange(back, group_sums)
+        return overflow, (pick, negatives, total, *returned)
 
     def finish(slots, *parts):
         return kernel_call(
             functools.partial(finish_kernel, (n, rows, slots, groups)),
             (sds((rows, PARTS * width), BF16), sds((rows, width), BF16), sds((head_dim, width // groups), F32)),
-            [SMEM] + [VMEM] * (3 + groups + n),
+            [SMEM] + [VMEM] * (4 + n),
             [pltpu.VMEM((rows, width), BF16)],
-        )(me_arr, parts[0], w_out, *parts[1:])
+        )(meta, parts[0], w_out, *parts[1:])
 
     overflow, parts = passes(SLOTS)
     d_home, layer_out, d_w_out = lax.cond(

time: 69.6 us -> 67.5 us (0.970)
  the two profiles are of different devices: /device:TPU:13 before, /device:TPU:0 now
where the time goes in v3:
time: 67.5 us; the launch traced here: 67.1 us
  waiting for transfers between devices  26.7 us (40%)
  starting transfers between devices  25.1 us (37%)
  Pallas kernels  12 us (18%)
  other arithmetic  1.4 us (2%)
  between operations  1.38 us (2%)
    ppermute x25, waiting for transfers between devices, swap(): lax.ppermute(block, axis, [(i, i ^ distance) for i in range(lax.axis_size...  26.7 us
    ppermute x25, starting transfers between devices, swap(): lax.ppermute(block, axis, [(i, i ^ distance) for i in range(lax.axis_size...  25.1 us
    pallas_call x1, Pallas kernels, passes(): kernel_call(functools.partial(forward_kernel, (n, rows, live_cap, slots,...  3.18 us
    pallas_call x1, Pallas kernels, finish(): kernel_call(functools.partial(finish_kernel, (n, rows, slots, groups)), (...  2.91 us
    pallas_call x1, Pallas kernels, passes(): kernel_call(functools.partial(pack_kernel, (n, rows, slots)), (sds((2, sl...  2.38 us
    pallas_call x1, Pallas kernels, passes(): kernel_call(functools.partial(backward_kernel, (n, rows, live_cap, slots)...  2.22 us
  transfers between devices with their start and end apart: 25, of which 19 were waited for; matrix products, arithmetic and copies ran while one was open for 2% of the time, Pallas kernels for 2%

profile of v3, /device:TPU:0, one launch (start us, length us, event | category | flops | bytes accessed | tf_op | source)
XLA Modules:
  0.0 67.1 jit_solution(2024298718412556672)
XLA Ops:
  2.8 4.9 %collective-permute-start.28 = (s32[2,1,128]{2,1,0:T(1,128)S(1)}, s32[2,1,128]{2,1,0:T(1,128)S(1)}, u32[]{:S(2)}, u32[]{:S(2)}) collective-permute-start(s32[2,1,128]{2,1,0:T(1,128)S(1)} %pad_add_fusion.1.b0), channel_id=1, source_target_pairs={{0,6},{1,7},{2,4},{3,5},{4,2},{5,3},{6,0},{7,1},{8,14},{9,15},{10,... | collective-permute-start | bytes 3080 | tf_op jit(solution)/shard_map/ppermute | solution.py:478
  9.2 2.9 %collective-permute-done.27.b2 = s32[2,1,128]{2,1,0:T(1,128)S(1)} collective-permute-done((s32[2,1,128]{2,1,0:T(1,128)S(1)}, s32[2,1,128]{2,1,0:T(1,128)S(1)}, u32[]{:S(2)}, u32[]{:S(2)}) %collective-permute-start.27) | collective-permute-done | bytes 1056 | tf_op jit(solution)/shard_map/ppermute | solution.py:478
  12.1 2.4 %shard_map.103 = (bf16[2,72,512]{2,1,0:T(8,128)(2,1)S(1)}, bf16[2,72,512]{2,1,0:T(8,128)(2,1)S(1)}, bf16[2,72,512]{2,1,0:T(8,128)(2,1)S(1)}, bf16[2,72,512]{2,1,0:T(8,128)(2,1)S(1)}, bf16[128,128]{1,0:T(8,128)(2,1)S(1)}) custom-call(s32[10]{0:T(128)S(1)} %pad_add_fusion.2.meta, s32[2,1,128]{2,1,0:T(1,128)S(1)} %pad_add_fusion.1.b0, ...), custom_call_target="tpu_custom_call" | custom-call | tf_op jit(solution)/shard_map/pallas_call | solution.py:513
  14.6 2.1 %collective-permute-start.30 = (bf16[2,72,512]{2,1,0:T(8,128)(2,1)S(1)}, bf16[2,72,512]{2,1,0:T(8,128)(2,1)S(1)}, u32[]{:S(2)}, u32[]{:S(2)}) collective-permute-start(bf16[2,72,512]{2,1,0:T(8,128)(2,1)S(1)} %get-tuple-element.144), channel_id=1, source_target_pairs={{0,4},{1,5},{2,6},{3,7},{4,0},{5,1},{6,2},{7,3},{8,12},{9,13},{10,... | collective-permute-start | bytes 442376 | tf_op jit(solution)/shard_map/ppermute | solution.py:478
  16.7 2.3 %collective-permute-start.29 = (bf16[2,72,512]{2,1,0:T(8,128)(2,1)S(1)}, bf16[2,72,512]{2,1,0:T(8,128)(2,1)S(1)}, u32[]{:S(2)}, u32[]{:S(2)}) collective-permute-start(bf16[2,72,512]{2,1,0:T(8,128)(2,1)S(1)} %get-tuple-element.143), channel_id=1, source_target_pairs={{0,6},{1,7},{2,4},{3,5},{4,2},{5,3},{6,0},{7,1},{8,14},{9,15},{10,... | collective-permute-start | bytes 442376 | tf_op jit(solution)/shard_map/ppermute | solution.py:478
  19.0 1.1 %shard_map.104 = (f32[8,128]{1,0:T(8,128)S(1)}, f32[8,128]{1,0:T(8,128)S(1)}) custom-call(s32[10]{0:T(128)S(1)} %pad_add_fusion.2.meta, s32[2,1,128]{2,1,0:T(1,128)S(1)} %pad_add_fusion.1.b0, s32[2,1,128]{2,1,0:T(1,128)S(1)} %collective-permute-done.26.b1, s32[2,1,128]{2,1,0:T(1,128)S(1)} %collective-permute-done.27.b2, ...), custom_call_target="tpu_custom_call" | custom-call | tf_op jit(solution)/shard_map/pallas_call | solution.py:531
  21.0 7.1 %collective-permute-done.30.refs_4_ = bf16[2,72,512]{2,1,0:T(8,128)(2,1)S(1)} collective-permute-done((bf16[2,72,512]{2,1,0:T(8,128)(2,1)S(1)}, bf16[2,72,512]{2,1,0:T(8,128)(2,1)S(1)}, u32[]{:S(2)}, u32[]{:S(2)}) %collective-permute-start.30) | collective-permute-done | bytes 147488 | tf_op jit(solution)/shard_map/ppermute | solution.py:478
  30.0 3.2 %shard_map.105 = (bf16[384,512]{1,0:T(8,128)(2,1)S(1)}, bf16[384,384]{1,0:T(8,128)(2,1)S(1)}, f32[384,128]{1,0:T(8,128)S(1)}, f32[8,384]{1,0:T(8,128)S(1)}, bf16...) custom-call(s32[10]{0:T(128)S(1)} %pad_add_fusion.2.meta, ...), custom_call_target="tpu_custom_call" | custom-call | tf_op jit(solution)/shard_map/pallas_call | solution.py:539
  33.4 1.0 %collective-permute-done.36 = f32[8,384]{1,0:T(8,128)S(1)} collective-permute-done((f32[8,384]{1,0:T(8,128)S(1)}, f32[8,384]{1,0:T(8,128)S(1)}, u32[]{:S(2)}, u32[]{:S(2)}) %collective-permute-start.36) | collective-permute-done | bytes 12320 | tf_op jit(solution)/shard_map/ppermute | solution.py:478
  34.5 2.6 %collective-permute-start.39 = (f32[8,384]{1,0:T(8,128)S(1)}, f32[8,384]{1,0:T(8,128)S(1)}, u32[]{:S(2)}, u32[]{:S(2)}) collective-permute-start(f32[8,384]{1,0:T(8,128)S(1)} %stack.43.st0), channel_id=1, source_target_pairs={{0,6},{1,7},{2,4},{3,5},{4,2},{5,3},{6,0},{7,1},{8,14},{9,15},{10,... | collective-permute-start | bytes 36872 | tf_op jit(solution)/shard_map/ppermute | solution.py:478
  37.1 1.0 %collective-permute-start.38 = (f32[8,384]{1,0:T(8,128)S(1)}, f32[8,384]{1,0:T(8,128)S(1)}, u32[]{:S(2)}, u32[]{:S(2)}) collective-permute-start(f32[8,384]{1,0:T(8,128)S(1)} %stack.43.st0), channel_id=1, source_target_pairs={{0,4},{1,5},{2,6},{3,7},{4,0},{5,1},{6,2},{7,3},{8,12},{9,13},{10,... | collective-permute-start | bytes 36872 | tf_op jit(solution)/shard_map/ppermute | solution.py:478
  38.9 1.1 %collective-permute-done.39.st3 = f32[8,384]{1,0:T(8,128)S(1)} collective-permute-done((f32[8,384]{1,0:T(8,128)S(1)}, f32[8,384]{1,0:T(8,128)S(1)}, u32[]{:S(2)}, u32[]{:S(2)}) %collective-permute-start.39) | collective-permute-done | bytes 12320 | tf_op jit(solution)/shard_map/ppermute | solution.py:478
  40.0 1.6 %collective-permute-done.38.st2 = f32[8,384]{1,0:T(8,128)S(1)} collective-permute-done((f32[8,384]{1,0:T(8,128)S(1)}, f32[8,384]{1,0:T(8,128)S(1)}, u32[]{:S(2)}, u32[]{:S(2)}) %collective-permute-start.38) | collective-permute-done | bytes 12320 | tf_op jit(solution)/shard_map/ppermute | solution.py:478
  41.8 2.2 %shard_map.106 = (bf16[2,96,512]{2,1,0:T(8,128)(2,1)S(1)}, bf16[2,96,512]{2,1,0:T(8,128)(2,1)S(1)}, bf16[2,96,512]{2,1,0:T(8,128)(2,1)S(1)}, bf16[2,96,512]{2,1,0:T(8,128)(2,1)S(1)}, bf16[384,128]{1,0:T(8,128)(2,1)S(1)}) custom-call(s32[10]{0:T(128)S(1)} %pad_add_fusion.2.meta, bf16[384,512]{1,0:T(8,128)(2,1)S(1)} %get-tuple-element.157.compact, ...), custom_call_target="tpu_custom_call" | custom-call | tf_op jit(solution)/shard_map/pallas_call | solution.py:559
  44.1 1.4 %collective-permute-start.42 = (bf16[2,96,512]{2,1,0:T(8,128)(2,1)S(1)}, bf16[2,96,512]{2,1,0:T(8,128)(2,1)S(1)}, u32[]{:S(2)}, u32[]{:S(2)}) collective-permute-start(bf16[2,96,512]{2,1,0:T(8,128)(2,1)S(1)} %get-tuple-element.164), channel_id=1, source_target_pairs={{0,2},{1,3},{2,0},{3,1},{4,6},{5,7},{6,4},{7,5},{8,10},{9,11},{10,... | collective-permute-start | bytes 589832 | tf_op jit(solution)/shard_map/ppermute | solution.py:478
  45.4 2.0 %collective-permute-start.41 = (bf16[2,96,512]{2,1,0:T(8,128)(2,1)S(1)}, bf16[2,96,512]{2,1,0:T(8,128)(2,1)S(1)}, u32[]{:S(2)}, u32[]{:S(2)}) collective-permute-start(bf16[2,96,512]{2,1,0:T(8,128)(2,1)S(1)} %get-tuple-element.163), channel_id=1, source_target_pairs={{0,4},{1,5},{2,6},{3,7},{4,0},{5,1},{6,2},{7,3},{8,12},{9,13},{10,... | collective-permute-start | bytes 589832 | tf_op jit(solution)/shard_map/ppermute | solution.py:478
  47.5 1.1 %collective-permute-start.40 = (bf16[2,96,512]{2,1,0:T(8,128)(2,1)S(1)}, bf16[2,96,512]{2,1,0:T(8,128)(2,1)S(1)}, u32[]{:S(2)}, u32[]{:S(2)}) collective-permute-start(bf16[2,96,512]{2,1,0:T(8,128)(2,1)S(1)} %get-tuple-element.162), channel_id=1, source_target_pairs={{0,6},{1,7},{2,4},{3,5},{4,2},{5,3},{6,0},{7,1},{8,14},{9,15},{10,... | collective-permute-start | bytes 589832 | tf_op jit(solution)/shard_map/ppermute | solution.py:478
  48.6 2.4 %collective-permute-start.45 = (f32[40,128]{1,0:T(8,128)S(1)}, f32[40,128]{1,0:T(8,128)S(1)}, u32[]{:S(2)}, u32[]{:S(2)}) collective-permute-start(f32[40,128]{1,0:T(8,128)S(1)} %shard_map.107.refs_0_), channel_id=1, source_target_pairs={{0,24},{8,16},{16,8},{24,0},{1,25},{9,17},{17,9},{25,1},{2,26},{10... | collective-permute-start | bytes 61448 | tf_op jit(solution)/shard_map/ppermute | solution.py:478
  51.6 1.7 %collective-permute-done.45.refs_3_ = f32[40,128]{1,0:T(8,128)S(1)} collective-permute-done((f32[40,128]{1,0:T(8,128)S(1)}, f32[40,128]{1,0:T(8,128)S(1)}, u32[]{:S(2)}, u32[]{:S(2)}) %collective-permute-start.45) | collective-permute-done | bytes 20512 | tf_op jit(solution)/shard_map/ppermute | solution.py:478
  53.3 1.5 %collective-permute-start.43 = (f32[40,128]{1,0:T(8,128)S(1)}, f32[40,128]{1,0:T(8,128)S(1)}, u32[]{:S(2)}, u32[]{:S(2)}) collective-permute-start(f32[40,128]{1,0:T(8,128)S(1)} %shard_map.107.refs_0_), channel_id=1, source_target_pairs={{0,8},{8,0},{16,24},{24,16},{1,9},{9,1},{17,25},{25,17},{2,10},{10... | collective-permute-start | bytes 61448 | tf_op jit(solution)/shard_map/ppermute | solution.py:478
  54.9 2.2 %collective-permute-done.43.refs_1_ = f32[40,128]{1,0:T(8,128)S(1)} collective-permute-done((f32[40,128]{1,0:T(8,128)S(1)}, f32[40,128]{1,0:T(8,128)S(1)}, u32[]{:S(2)}, u32[]{:S(2)}) %collective-permute-start.43) | collective-permute-done | bytes 20512 | tf_op jit(solution)/shard_map/ppermute | solution.py:478
  58.3 3.7 %collective-permute-done.41 = bf16[2,96,512]{2,1,0:T(8,128)(2,1)S(1)} collective-permute-done((bf16[2,96,512]{2,1,0:T(8,128)(2,1)S(1)}, bf16[2,96,512]{2,1,0:T(8,128)(2,1)S(1)}, u32[]{:S(2)}, u32[]{:S(2)}) %collective-permute-start.41) | collective-permute-done | bytes 196640 | tf_op jit(solution)/shard_map/ppermute | solution.py:478
  64.2 2.9 %conditional.1 = ((bf16[128,4096]{1,0:T(8,128)(2,1)}, bf16[128,1024]{1,0:T(8,128)(2,1)}, f32[128,256]{1,0:T(8,128)})) conditional(s32[]{:T(128)} %convert_element_type.3, (s32[10]{0:T(128)S(1)}, bf16[128,128]{1,0:T(8,128)(2,1)S(1)}, bf16[1024,1024]{1,0:T(8,128)(2,1)S(1)}, bf16[32,1024]{1,0:T(8,128)(2,1)}, f32[32,128]{1,0:T(8,128)S(1)}, ...), branch_computations={%region_0.0_spmd, %region_1.0_spmd} | conditional | flops 5248 | bytes 17482740 | solution.py:585
  64.2 2.9 %branch_0_fun.1 = (bf16[128,4096]{1,0:T(8,128)(2,1)}, bf16[128,1024]{1,0:T(8,128)(2,1)}, f32[128,256]{1,0:T(8,128)}) custom-call(s32[10]{0:T(128)S(1)} %get-tuple-element.42.meta, bf16[128,128]{1,0:T(8,128)(2,1)S(1)} %get-tuple-element.43.pick_ref, bf16[1024,1024]{1,0:T(8,128)(2,1)S(1)} %get-tuple-element.44.w_out, ...), custom_call_target="tpu_custom_call" | custom-call | tf_op jit(solution)/shard_map/cond/branch_0_fun/pallas_call | solution.py:577
  (46 shorter events, 11.1 us)
Async XLA Ops:
  0.6 1.5 %collective-permute-start.25 = (s32[1,128]{1,0:T(1,128)}, s32[1,128]{1,0:T(1,128)S(1)}, u32[]{:S(2)}, u32[]{:S(2)}) collective-permute-start(s32[1,128]{1,0:T(1,128)} %param.16), channel_id=1, source_target_pairs={{0,1},{1,0},{2,3},{3,2},{4,5},{5,4},{6,7},{7,6},{8,9},{9,8},{10,11... | collective-permute-start | bytes 1544 | tf_op jit(solution)/shard_map/ppermute | solution.py:478
  2.8 6.4 %collective-permute-start.28 = (s32[2,1,128]{2,1,0:T(1,128)S(1)}, s32[2,1,128]{2,1,0:T(1,128)S(1)}, u32[]{:S(2)}, u32[]{:S(2)}) collective-permute-start(s32[2,1,128]{2,1,0:T(1,128)S(1)} %pad_add_fusion.1.b0), channel_id=1, source_target_pairs={{0,6},{1,7},{2,4},{3,5},{4,2},{5,3},{6,0},{7,1},{8,14},{9,15},{10,... | collective-permute-start | bytes 3080 | tf_op jit(solution)/shard_map/ppermute | solution.py:478
  7.7 4.5 %collective-permute-start.27 = (s32[2,1,128]{2,1,0:T(1,128)S(1)}, s32[2,1,128]{2,1,0:T(1,128)S(1)}, u32[]{:S(2)}, u32[]{:S(2)}) collective-permute-start(s32[2,1,128]{2,1,0:T(1,128)S(1)} %pad_add_fusion.1.b0), channel_id=1, source_target_pairs={{0,4},{1,5},{2,6},{3,7},{4,0},{5,1},{6,2},{7,3},{8,12},{9,13},{10,... | collective-permute-start | bytes 3080 | tf_op jit(solution)/shard_map/ppermute | solution.py:478
  7.7 4.5 %collective-permute-start.26 = (s32[2,1,128]{2,1,0:T(1,128)S(1)}, s32[2,1,128]{2,1,0:T(1,128)S(1)}, u32[]{:S(2)}, u32[]{:S(2)}) collective-permute-start(s32[2,1,128]{2,1,0:T(1,128)S(1)} %pad_add_fusion.1.b0), channel_id=1, source_target_pairs={{0,2},{1,3},{2,0},{3,1},{4,6},{5,7},{6,4},{7,5},{8,10},{9,11},{10,... | collective-permute-start | bytes 3080 | tf_op jit(solution)/shard_map/ppermute | solution.py:478
  14.5 6.5 %collective-permute-start.31 = (bf16[2,72,512]{2,1,0:T(8,128)(2,1)S(1)}, bf16[2,72,512]{2,1,0:T(8,128)(2,1)S(1)}, u32[]{:S(2)}, u32[]{:S(2)}) collective-permute-start(bf16[2,72,512]{2,1,0:T(8,128)(2,1)S(1)} %get-tuple-element.145), channel_id=1, source_target_pairs={{0,2},{1,3},{2,0},{3,1},{4,6},{5,7},{6,4},{7,5},{8,10},{9,11},{10,... | collective-permute-start | bytes 442376 | tf_op jit(solution)/shard_map/ppermute | solution.py:478
  14.6 13.5 %collective-permute-start.30 = (bf16[2,72,512]{2,1,0:T(8,128)(2,1)S(1)}, bf16[2,72,512]{2,1,0:T(8,128)(2,1)S(1)}, u32[]{:S(2)}, u32[]{:S(2)}) collective-permute-start(bf16[2,72,512]{2,1,0:T(8,128)(2,1)S(1)} %get-tuple-element.144), channel_id=1, source_target_pairs={{0,4},{1,5},{2,6},{3,7},{4,0},{5,1},{6,2},{7,3},{8,12},{9,13},{10,... | collective-permute-start | bytes 442376 | tf_op jit(solution)/shard_map/ppermute | solution.py:478
  16.7 11.4 %collective-permute-start.29 = (bf16[2,72,512]{2,1,0:T(8,128)(2,1)S(1)}, bf16[2,72,512]{2,1,0:T(8,128)(2,1)S(1)}, u32[]{:S(2)}, u32[]{:S(2)}) collective-permute-start(bf16[2,72,512]{2,1,0:T(8,128)(2,1)S(1)} %get-tuple-element.143), channel_id=1, source_target_pairs={{0,6},{1,7},{2,4},{3,5},{4,2},{5,3},{6,0},{7,1},{8,14},{9,15},{10,... | collective-permute-start | bytes 442376 | tf_op jit(solution)/shard_map/ppermute | solution.py:478
  19.0 9.6 %collective-permute-start.32 = (bf16[2,72,512]{2,1,0:T(8,128)(2,1)S(1)}, bf16[2,72,512]{2,1,0:T(8,128)(2,1)S(1)}, u32[]{:S(2)}, u32[]{:S(2)}) collective-permute-start(bf16[2,72,512]{2,1,0:T(8,128)(2,1)S(1)} %get-tuple-element.153.refs_0_), channel_id=1, source_target_pairs={{0,1},{1,0},{2,3},{3,2},{4,5},{5,4},{6,7},{7,6},{8,9},{9,8},{10,11... | collective-permute-start | bytes 442376 | tf_op jit(solution)/shard_map/ppermute | solution.py:478
  28.1 1.4 %collective-permute-start.35 = (bf16[2,72,512]{2,1,0:T(8,128)(2,1)S(1)}, bf16[2,72,512]{2,1,0:T(8,128)(2,1)S(1)}, u32[]{:S(2)}, u32[]{:S(2)}) collective-permute-start(bf16[2,72,512]{2,1,0:T(8,128)(2,1)S(1)} %collective-permute-done.29.refs_6_), channel_id=1, source_target_pairs={{0,1},{1,0},{2,3},{3,2},{4,5},{5,4},{6,7},{7,6},{8,9},{9,8},{10,11... | collective-permute-start | bytes 442376 | tf_op jit(solution)/shard_map/ppermute | solution.py:478
  28.1 1.6 %collective-permute-start.34 = (bf16[2,72,512]{2,1,0:T(8,128)(2,1)S(1)}, bf16[2,72,512]{2,1,0:T(8,128)(2,1)S(1)}, u32[]{:S(2)}, u32[]{:S(2)}) collective-permute-start(bf16[2,72,512]{2,1,0:T(8,128)(2,1)S(1)} %collective-permute-done.30.refs_4_), channel_id=1, source_target_pairs={{0,1},{1,0},{2,3},{3,2},{4,5},{5,4},{6,7},{7,6},{8,9},{9,8},{10,11... | collective-permute-start | bytes 442376 | tf_op jit(solution)/shard_map/ppermute | solution.py:478
  28.6 1.4 %collective-permute-start.33 = (bf16[2,72,512]{2,1,0:T(8,128)(2,1)S(1)}, bf16[2,72,512]{2,1,0:T(8,128)(2,1)S(1)}, u32[]{:S(2)}, u32[]{:S(2)}) collective-permute-start(bf16[2,72,512]{2,1,0:T(8,128)(2,1)S(1)} %collective-permute-done.31.refs_2_), channel_id=1, source_target_pairs={{0,1},{1,0},{2,3},{3,2},{4,5},{5,4},{6,7},{7,6},{8,9},{9,8},{10,11... | collective-permute-start | bytes 442376 | tf_op jit(solution)/shard_map/ppermute | solution.py:478
  34.5 5.6 %collective-permute-start.39 = (f32[8,384]{1,0:T(8,128)S(1)}, f32[8,384]{1,0:T(8,128)S(1)}, u32[]{:S(2)}, u32[]{:S(2)}) collective-permute-start(f32[8,384]{1,0:T(8,128)S(1)} %stack.43.st0), channel_id=1, source_target_pairs={{0,6},{1,7},{2,4},{3,5},{4,2},{5,3},{6,0},{7,1},{8,14},{9,15},{10,... | collective-permute-start | bytes 36872 | tf_op jit(solution)/shard_map/ppermute | solution.py:478
  37.1 4.6 %collective-permute-start.38 = (f32[8,384]{1,0:T(8,128)S(1)}, f32[8,384]{1,0:T(8,128)S(1)}, u32[]{:S(2)}, u32[]{:S(2)}) collective-permute-start(f32[8,384]{1,0:T(8,128)S(1)} %stack.43.st0), channel_id=1, source_target_pairs={{0,4},{1,5},{2,6},{3,7},{4,0},{5,1},{6,2},{7,3},{8,12},{9,13},{10,... | collective-permute-start | bytes 36872 | tf_op jit(solution)/shard_map/ppermute | solution.py:478
  38.1 3.7 %collective-permute-start.37 = (f32[8,384]{1,0:T(8,128)S(1)}, f32[8,384]{1,0:T(8,128)S(1)}, u32[]{:S(2)}, u32[]{:S(2)}) collective-permute-start(f32[8,384]{1,0:T(8,128)S(1)} %stack.43.st0), channel_id=1, source_target_pairs={{0,2},{1,3},{2,0},{3,1},{4,6},{5,7},{6,4},{7,5},{8,10},{9,11},{10,... | collective-permute-start | bytes 36872 | tf_op jit(solution)/shard_map/ppermute | solution.py:478
  44.1 14.2 %collective-permute-start.42 = (bf16[2,96,512]{2,1,0:T(8,128)(2,1)S(1)}, bf16[2,96,512]{2,1,0:T(8,128)(2,1)S(1)}, u32[]{:S(2)}, u32[]{:S(2)}) collective-permute-start(bf16[2,96,512]{2,1,0:T(8,128)(2,1)S(1)} %get-tuple-element.164), channel_id=1, source_target_pairs={{0,2},{1,3},{2,0},{3,1},{4,6},{5,7},{6,4},{7,5},{8,10},{9,11},{10,... | collective-permute-start | bytes 589832 | tf_op jit(solution)/shard_map/ppermute | solution.py:478
  45.4 16.6 %collective-permute-start.41 = (bf16[2,96,512]{2,1,0:T(8,128)(2,1)S(1)}, bf16[2,96,512]{2,1,0:T(8,128)(2,1)S(1)}, u32[]{:S(2)}, u32[]{:S(2)}) collective-permute-start(bf16[2,96,512]{2,1,0:T(8,128)(2,1)S(1)} %get-tuple-element.163), channel_id=1, source_target_pairs={{0,4},{1,5},{2,6},{3,7},{4,0},{5,1},{6,2},{7,3},{8,12},{9,13},{10,... | collective-permute-start | bytes 589832 | tf_op jit(solution)/shard_map/ppermute | solution.py:478
  47.5 14.6 %collective-permute-start.40 = (bf16[2,96,512]{2,1,0:T(8,128)(2,1)S(1)}, bf16[2,96,512]{2,1,0:T(8,128)(2,1)S(1)}, u32[]{:S(2)}, u32[]{:S(2)}) collective-permute-start(bf16[2,96,512]{2,1,0:T(8,128)(2,1)S(1)} %get-tuple-element.162), channel_id=1, source_target_pairs={{0,6},{1,7},{2,4},{3,5},{4,2},{5,3},{6,0},{7,1},{8,14},{9,15},{10,... | collective-permute-start | bytes 589832 | tf_op jit(solution)/shard_map/ppermute | solution.py:478
  48.6 4.7 %collective-permute-start.45 = (f32[40,128]{1,0:T(8,128)S(1)}, f32[40,128]{1,0:T(8,128)S(1)}, u32[]{:S(2)}, u32[]{:S(2)}) collective-permute-start(f32[40,128]{1,0:T(8,128)S(1)} %shard_map.107.refs_0_), channel_id=1, source_target_pairs={{0,24},{8,16},{16,8},{24,0},{1,25},{9,17},{17,9},{25,1},{2,26},{10... | collective-permute-start | bytes 61448 | tf_op jit(solution)/shard_map/ppermute | solution.py:478
  51.1 3.8 %collective-permute-start.44 = (f32[40,128]{1,0:T(8,128)S(1)}, f32[40,128]{1,0:T(8,128)S(1)}, u32[]{:S(2)}, u32[]{:S(2)}) collective-permute-start(f32[40,128]{1,0:T(8,128)S(1)} %shard_map.107.refs_0_), channel_id=1, source_target_pairs={{0,16},{8,24},{16,0},{24,8},{1,17},{9,25},{17,1},{25,9},{2,18},{10... | collective-permute-start | bytes 61448 | tf_op jit(solution)/shard_map/ppermute | solution.py:478
  53.3 3.8 %collective-permute-start.43 = (f32[40,128]{1,0:T(8,128)S(1)}, f32[40,128]{1,0:T(8,128)S(1)}, u32[]{:S(2)}, u32[]{:S(2)}) collective-permute-start(f32[40,128]{1,0:T(8,128)S(1)} %shard_map.107.refs_0_), channel_id=1, source_target_pairs={{0,8},{8,0},{16,24},{24,16},{1,9},{9,1},{17,25},{25,17},{2,10},{10... | collective-permute-start | bytes 61448 | tf_op jit(solution)/shard_map/ppermute | solution.py:478
  54.9 7.7 %collective-permute-start.46 = (bf16[2,96,512]{2,1,0:T(8,128)(2,1)S(1)}, bf16[2,96,512]{2,1,0:T(8,128)(2,1)S(1)}, u32[]{:S(2)}, u32[]{:S(2)}) collective-permute-start(bf16[2,96,512]{2,1,0:T(8,128)(2,1)S(1)} %get-tuple-element.178), channel_id=1, source_target_pairs={{0,1},{1,0},{2,3},{3,2},{4,5},{5,4},{6,7},{7,6},{8,9},{9,8},{10,11... | collective-permute-start | bytes 589832 | tf_op jit(solution)/shard_map/ppermute | solution.py:478
  62.1 1.4 %collective-permute-start.49 = (bf16[2,96,512]{2,1,0:T(8,128)(2,1)S(1)}, bf16[2,96,512]{2,1,0:T(8,128)(2,1)S(1)}, u32[]{:S(2)}, u32[]{:S(2)}) collective-permute-start(bf16[2,96,512]{2,1,0:T(8,128)(2,1)S(1)} %collective-permute-done.40), channel_id=1, source_target_pairs={{0,1},{1,0},{2,3},{3,2},{4,5},{5,4},{6,7},{7,6},{8,9},{9,8},{10,11... | collective-permute-start | bytes 589832 | tf_op jit(solution)/shard_map/ppermute | solution.py:478
  62.1 1.8 %collective-permute-start.48 = (bf16[2,96,512]{2,1,0:T(8,128)(2,1)S(1)}, bf16[2,96,512]{2,1,0:T(8,128)(2,1)S(1)}, u32[]{:S(2)}, u32[]{:S(2)}) collective-permute-start(bf16[2,96,512]{2,1,0:T(8,128)(2,1)S(1)} %collective-permute-done.41), channel_id=1, source_target_pairs={{0,1},{1,0},{2,3},{3,2},{4,5},{5,4},{6,7},{7,6},{8,9},{9,8},{10,11... | collective-permute-start | bytes 589832 | tf_op jit(solution)/shard_map/ppermute | solution.py:478
  62.6 1.6 %collective-permute-start.47 = (bf16[2,96,512]{2,1,0:T(8,128)(2,1)S(1)}, bf16[2,96,512]{2,1,0:T(8,128)(2,1)}, u32[]{:S(2)}, u32[]{:S(2)}) collective-permute-start(bf16[2,96,512]{2,1,0:T(8,128)(2,1)S(1)} %collective-permute-done.42), channel_id=1, source_target_pairs={{0,1},{1,0},{2,3},{3,2},{4,5},{5,4},{6,7},{7,6},{8,9},{9,8},{10,11... | collective-permute-start | bytes 589832 | tf_op jit(solution)/shard_map/ppermute | solution.py:478
  (4 other events, 117.0 us)

commit v4 on v3

--- a/solution.py
+++ b/solution.py
@@ -11,8 +11,8 @@
 HEADS = 8
 SPAN = 3
 PARTS = 4
-SLOTS = 64
-EXTRA = 8
+SLOTS = 60
+POOL = 104
 LENS = 2
 
 
@@ -226,9 +226,10 @@
     n, rows, slots = sizes
     pairs = n // 2
     outs = refs[:pairs]
-    pick, order_ref, send_row, ids, coef_rows, items, neg_rows, held, picked, sems = refs[pairs:]
+    pick, order_ref, send_row, ids, coef_rows, items, neg_rows, held, sems = refs[pairs:]
     per, chunk, width = items.shape
-    wide = outs[0].shape[2]
+    wide = outs[0].shape[1]
+    head_dim = wide // PARTS
     cell = rows // n
     me = meta[0]
     copies = [
@@ -250,11 +251,14 @@
     by_rank = one_hot(slot_ranks(places) == lane.astype(F32))
     copies[1].wait()
     home = jnp.sum(jnp.where(lane == sub, send_row[...].astype(F32), 0.0), axis=1, keepdims=True)
-    chosen = dot(by_rank, one_hot(home == lane.astype(F32)), ((0,), (0,))).astype(BF16)
-    pick[...] = chosen
+    chosen = dot(by_rank, one_hot(home == lane.astype(F32)), ((0,), (0,)))
+    pick[...] = chosen.astype(BF16)
+    none = jnp.zeros((slots, rows), F32)
+    both = jnp.concatenate(
+        [jnp.concatenate([chosen[0:slots], none], axis=1), jnp.concatenate([none, chosen[0:slots]], axis=1)], axis=0
+    ).astype(BF16)
     copies[2].wait()
     copies[3].wait()
-    picked[...] = dot(chosen[0:slots], held[...]).astype(BF16)
     for j in range(per):
         item_copies[j].wait()
         own = iota((chunk, width), 0) == ids[j] % chunk
@@ -262,30 +266,56 @@
     step = coef_rows.shape[0] * rows // wide
     coefs = jnp.concatenate([coef_rows[b * step : (b + 1) * step].astype(F32) for b in range(wide // rows)], axis=1)
     negs = jnp.concatenate([neg_rows[0:per, b * wide : (b + 1) * wide] for b in range(width // wide)], axis=0)
-    head_dim = wide // PARTS
-    for x in range(n):
-        first = pl.multiple_of((me ^ x) * head_dim, head_dim)
-        out = outs[x // 2]
-        out[x % 2, 0:slots] = jnp.concatenate([picked[:, pl.ds(i * width + first, head_dim)] for i in range(PARTS)], axis=1)
-        out[x % 2, slots:] = (coefs, negs)[x % 2].astype(BF16)
-
-
-def index_kernel(sizes, meta, b0, b1, b2, b3, place, most, order_ref):
-    n, rows = sizes
+    below = jnp.concatenate([coefs, negs], axis=0).astype(BF16)
+    for d in range(pairs):
+        columns = []
+        for x in (2 * d, 2 * d + 1):
+            first = pl.multiple_of((me ^ x) * head_dim, head_dim)
+            columns.append(jnp.concatenate([held[:, pl.ds(i * width + first, head_dim)] for i in range(PARTS)], axis=1))
+        outs[d][0 : 2 * slots] = dot(both, jnp.concatenate(columns, axis=0)).astype(BF16)
+        outs[d][2 * slots :] = below
+
+
+def index_kernel(sizes, meta, b0, b1, b2, b3, pick, pick_in, pick_out, home_even, home_odd, live, most, order_ref):
+    n, rows, slots, pool = sizes
     cell = rows // n
+    live_cap = live.shape[0]
+    span = pick_in.shape[1] // n
     me = meta[0]
     filled, value = slot_table(meta, (b0, b1, b2, b3), order_ref)
     lane = iota((rows, rows), 1)
+    columns = [slot_places(filled, value, me ^ x, cell) for x in range(n)]
     places = jnp.zeros((rows, rows), F32)
-    columns = [slot_places(filled, value, s, cell) for s in range(n)]
-    for s in range(n):
-        places = jnp.where(lane == s, columns[s], places)
+    for x in range(n):
+        places = jnp.where(lane == x, columns[x], places)
     ranks = slot_ranks(places)
     count = jnp.sum(jnp.where(places > 0.5, 1.0, 0.0), axis=0, keepdims=True)
-    most[...] = jnp.broadcast_to(jnp.max(count), most.shape)
-    for s in range(n):
-        hit = jnp.where(ranks[:, s : s + 1] == lane.astype(F32), columns[s], 0.0)
-        place[pl.ds(me ^ s, 1), :] = jnp.sum(hit, axis=0, keepdims=True) - 1.0
+    counts = [count[:, x : x + 1] for x in range(n)]
+    excess = [c - slots for c in counts] + [counts[2 * d] + counts[2 * d + 1] - pool for d in range(n // 2)]
+    most[...] = jnp.broadcast_to(functools.reduce(jnp.maximum, excess), most.shape)
+
+    def placed(x, first, width):
+        at = ranks[:, x : x + 1] + first
+        hit = jnp.where(at == iota((rows, width), 1).astype(F32), columns[x], 0.0)
+        return jnp.sum(hit, axis=0, keepdims=True)
+
+    lines = []
+    for x in range(n):
+        first = span - slots if x % 2 else 0
+        line = placed(x, first, max(span, rows))[:, :span]
+        at = iota((1, span), 1)
+        lines.append(jnp.where((at >= first) & (at < first + slots), line, 0.0))
+    line = jnp.concatenate(lines, axis=1) - 1.0
+    pick_in[...] = one_hot(iota((live_cap, line.shape[1]), 0).astype(F32) == line)
+    reach = -(-pool // rows) * rows
+    for d in range(n // 2):
+        line = placed(2 * d, 0.0, reach) + placed(2 * d + 1, counts[2 * d], reach) - 1.0
+        hit = one_hot(iota((live_cap, reach), 0).astype(F32) == line)
+        pick_out[:, d * pool : (d + 1) * pool] = hit[:, :pool]
+    slot = iota((reach, rows), 0).astype(F32)
+    home_even[...] = dot(one_hot(slot == lane[0:1].astype(F32)), pick[...]).astype(BF16)[:pool]
+    home_odd[...] = dot(one_hot(slot == lane[0:1].astype(F32) + counts[1]), pick[...]).astype(BF16)[:pool]
+    live[...] = jnp.where(pair_live(live_cap, starts_of(meta, n)), 1.0 / rows, 0.0)
 
 
 def pair_live(live_cap, starts):
@@ -294,43 +324,32 @@
     return (col <= row) & (tile_of(col, starts) > tile_of(row, starts) - SPAN) & (row < starts[-1])
 
 
-def slot_pick(live_cap, place, slots, after):
-    n, rows = place.shape
-    padded = jnp.concatenate([place, jnp.full((n, rows), -1.0, F32)], axis=1)
-    padded = jnp.where(iota(padded.shape, 1) < slots, padded, -1.0)
-    line = jnp.concatenate([padded[x : x + 1, : slots + after] for x in range(n)], axis=1)
-    return one_hot(iota((live_cap, line.shape[1]), 0).astype(F32) == line)
-
-
-def by_distance(blocks):
-    return [block[i % 2] for i, block in enumerate(blocks)]
-
-
-def forward_kernel(sizes, meta, place, w_out, *refs):
-    n, rows, live_cap, slots, per = sizes
+def forward_kernel(sizes, meta, pick, live, w_out, *refs):
+    n, rows, slots, per = sizes
     blocks = refs[:n]
     compact, weights, att, stats, coef_c, d_mixed, negatives, neg_rows, w_rows, sem = refs[n:]
-    head_dim = att.shape[1]
+    live_cap, head_dim = att.shape
     negs = coef_c.shape[0]
-    wide = blocks[0].shape[2]
+    wide = blocks[0].shape[1]
+    span = pick.shape[1] // n
     me = meta[0]
     copy = pltpu.make_async_copy(w_out.at[pl.ds(pl.multiple_of(me * head_dim, head_dim), head_dim)], w_rows, sem)
     copy.start()
-    starts = starts_of(meta, n)
-    both = dot(slot_pick(live_cap, place[...], slots, EXTRA), jnp.concatenate(by_distance(blocks), axis=0)).astype(BF16)
+    received = [block[2 * slots - span : 2 * slots] if x % 2 else block[0:span] for x, block in enumerate(blocks)]
+    both = dot(pick[...], jnp.concatenate(received, axis=0)).astype(BF16)
     compact[...] = both
     total = jnp.zeros((negs, live_cap), F32)
-    tall = iota((live_cap, rows), 0)
-    pos = iota((live_cap, rows), 1)
+    lane = iota((negs, live_cap), 1)
+    step = negs * rows // wide
     for x in range(n):
         t = me ^ x
-        hit = one_hot((tall == pos + start_of(meta, n, t)) & (pos < meta[LENS + t]))
-        coefs = blocks[x][0, slots:].astype(F32)
-        coefs = jnp.concatenate([coefs[:, b * rows : (b + 1) * rows] for b in range(wide // rows)], axis=0).astype(BF16)
-        total = total + dot(coefs, hit, ((1,), (1,)))
-        items = blocks[x][1, slots:].astype(F32)
+        start = start_of(meta, n, t)
+        below = blocks[x][2 * slots :].astype(F32)
+        coefs = jnp.concatenate([below[0:step, b * rows : (b + 1) * rows] for b in range(wide // rows)], axis=0)
+        coefs = jnp.concatenate([coefs, jnp.zeros((negs, live_cap - rows), F32)], axis=1)
+        total = jnp.where((lane >= start) & (lane < start + meta[LENS + t]), pltpu.roll(coefs, start, 1), total)
         for b in range(n * head_dim // wide):
-            neg_rows[t, 0:per, b * wide : (b + 1) * wide] = items[b * per : (b + 1) * per]
+            neg_rows[t, 0:per, b * wide : (b + 1) * wide] = below[step + b * per : step + (b + 1) * per]
     coef_t = total.astype(BF16)
     coef_c[...] = coef_t
     neg = jnp.concatenate([neg_rows[s, 0:per] for s in range(n)], axis=0).astype(BF16)
@@ -342,7 +361,7 @@
     u, v, q, k = (both[:, i * head_dim : (i + 1) * head_dim] for i in range(PARTS))
     scores = dot(q, k, ((1,), (1,))) * (1.0 / math.sqrt(head_dim))
     sig = jax.nn.sigmoid(scores)
-    w = jnp.where(pair_live(live_cap, starts), scores * sig * (1.0 / rows), 0.0).astype(BF16)
+    w = (scores * sig * live[...]).astype(BF16)
     weights[...] = w
     a = dot(w, v)
     att[...] = a
@@ -374,14 +393,13 @@
     return start
 
 
-def backward_kernel(sizes, meta, compact, weights, att, d_mixed, st0, st1, st2, st3, place, *refs):
-    n, rows, live_cap, slots = sizes
+def backward_kernel(sizes, meta, compact, weights, att, d_mixed, st0, st1, st2, st3, pick, live, *refs):
+    n, rows, pool = sizes
     outs = refs[: n // 2]
-    mixed_ref = refs[n // 2]
-    head_dim = att.shape[1]
+    mixed_ref, mixed_rows = refs[n // 2 :]
+    live_cap, head_dim = att.shape
     width = head_dim * n
     me = meta[0]
-    starts = starts_of(meta, n)
     quad = [[st[i : i + 1] for i in range(4)] for st in (st0, st1, st2, st3)]
     ab = merge_stats(quad[0], quad[1], 2 * head_dim)
     cd = merge_stats(quad[2], quad[3], 2 * head_dim)
@@ -401,23 +419,27 @@
     scale = 1.0 / math.sqrt(head_dim)
     scores = dot(q, k, ((1,), (1,))) * scale
     sig = jax.nn.sigmoid(scores)
-    slope = sig * (1.0 + scores * (1.0 - sig)) * (scale / rows)
-    ds = jnp.where(pair_live(live_cap, starts), dot(d_att, v, ((1,), (1,))) * slope, 0.0).astype(BF16)
+    slope = sig * (1.0 + scores * (1.0 - sig)) * scale * live[...]
+    ds = (dot(d_att, v, ((1,), (1,))) * slope).astype(BF16)
     grad = jnp.concatenate(
         [dm * normed, dot(weights[...], d_att, ((0,), (0,))), dot(ds, k), dot(ds, q, ((0,), (0,)))], axis=1
     ).astype(BF16)
     mixed_ref[...] = mixed
-    sent = dot(slot_pick(live_cap, place[...], slots, 0), grad, ((0,), (0,))).astype(BF16)
+    sent = dot(pick[...], grad, ((0,), (0,))).astype(BF16)
+    mixed_rows[0:live_cap] = mixed.astype(F32)
+    mixed_rows[live_cap:] = jnp.zeros((rows, head_dim), F32)
     quarter = rows // PARTS
-    col = iota((rows, live_cap), 1)
-    row = iota((rows, live_cap), 0)
+    row = iota((rows, head_dim), 0)
     for x in range(n):
-        outs[x // 2][x % 2, quarter:] = sent[x * slots : (x + 1) * slots]
         t = me ^ x
-        tile = dot(one_hot((col == row + start_of(meta, n, t)) & (row < meta[LENS + t])), mixed).astype(BF16)
-        outs[x // 2][x % 2, 0:quarter] = jnp.concatenate(
+        tile = mixed_rows[pl.ds(start_of(meta, n, t), rows), :]
+        tile = jnp.where(row < meta[LENS + t], tile, 0.0)
+        first = quarter * (x % 2)
+        outs[x // 2][first : first + quarter] = jnp.concatenate(
             [tile[b * quarter : (b + 1) * quarter] for b in range(PARTS)], axis=1
-        )
+        ).astype(BF16)
+    for d in range(n // 2):
+        outs[d][2 * quarter :] = sent[d * pool : (d + 1) * pool]
 
 
 def sums_kernel(coef_c, mixed, most, sums):
@@ -433,25 +455,26 @@
     most[...] = functools.reduce(jnp.maximum, [part[negs:] for part in sums])
 
 
-def finish_kernel(sizes, meta, pick_ref, w_out, negatives, total, *refs):
-    n, rows, slots, groups = sizes
-    blocks = refs[:n]
-    d_home, layer_out, d_w_out, mixed = refs[n:]
-    me = meta[0]
-    wide = blocks[0].shape[2]
-    head_dim = wide // PARTS
-    width = head_dim * n
+def finish_kernel(sizes, meta, even, odd, w_out, negatives, total, *refs):
+    n, rows, groups = sizes
+    blocks, (d_home, layer_out, d_w_out) = refs[:n], refs[n:]
+    width = w_out.shape[0]
+    head_dim = width // n
     quarter = rows // PARTS
-    pick = pick_ref[0:slots]
-    for x, block in enumerate(by_distance(blocks)):
-        first = pl.multiple_of((me ^ x) * head_dim, head_dim)
-        full = dot(pick, block[quarter:], ((0,), (0,))).astype(BF16)
-        for i in range(PARTS):
-            d_home[:, pl.ds(i * width + first, head_dim)] = full[:, i * head_dim : (i + 1) * head_dim]
-        mixed[:, pl.ds(first, head_dim)] = jnp.concatenate(
-            [block[0:quarter, b * head_dim : (b + 1) * head_dim] for b in range(PARTS)], axis=0
-        )
-    layer_out[...] = dot(mixed[...], w_out[...]).astype(BF16)
+    layer = jnp.zeros((rows, width), F32)
+    for d in range(0, n, 2):
+        mixed, weights = [], []
+        for x in (d, d + 1):
+            head = pl.multiple_of((meta[0] ^ x) * head_dim, head_dim)
+            block = blocks[x]
+            part = dot((odd if x % 2 else even)[...], block[2 * quarter :], ((0,), (0,))).astype(BF16)
+            for i in range(PARTS):
+                d_home[:, pl.ds(i * width + head, head_dim)] = part[:, i * head_dim : (i + 1) * head_dim]
+            lines = block[quarter * (x % 2) : quarter * (x % 2 + 1)]
+            mixed.append(jnp.concatenate([lines[:, b * head_dim : (b + 1) * head_dim] for b in range(PARTS)], axis=0))
+            weights.append(w_out[pl.ds(head, head_dim), :])
+        layer = layer + dot(jnp.concatenate(mixed, axis=1), jnp.concatenate(weights, axis=0))
+    layer_out[...] = layer.astype(BF16)
     columns = width // groups
     neg = negatives[:, pl.ds(pl.multiple_of(meta[1] * columns, columns), columns)]
     rest = total[...]
@@ -508,11 +531,16 @@
     meta = jnp.concatenate([jnp.stack([me, lax.axis_index("dp")]).astype(jnp.int32), tile_len[0]])
     head_coef_t = head_coef.T
 
-    def passes(slots):
+    half = n // 2
+    quarter = rows // PARTS
+    below = (negs * rows + per * width) // wide
+
+    def passes(slots, pool):
+        span = -(-slots // 8) * 8
         orders = gather_small(recv_order)
         *message, pick = kernel_call(
             functools.partial(pack_kernel, (n, rows, slots)),
-            (sds((2, slots + EXTRA, wide), BF16),) * (n // 2) + (sds((rows, rows), BF16),),
+            (sds((2 * slots + below, wide), BF16),) * half + (sds((rows, rows), BF16),),
             [SMEM] + [VMEM] * 4 + [ANY] * 5,
             [
                 pltpu.VMEM((n, 1, rows), F32),
@@ -522,22 +550,28 @@
                 pltpu.VMEM((per, 16, width), BF16),
                 pltpu.VMEM((8, width), F32),
                 pltpu.VMEM(qkvu.shape, BF16),
-                pltpu.VMEM((slots, PARTS * width), BF16),
                 pltpu.SemaphoreType.DMA((4 + per,)),
             ],
         )(meta, *orders, send_order, neg_ids, head_coef_t, item_table, qkvu)
 
         def index():
             return kernel_call(
-                functools.partial(index_kernel, (n, rows)),
-                (sds((n, rows), F32), sds((8, 128), F32)),
-                [SMEM] + [VMEM] * 4,
+                functools.partial(index_kernel, (n, rows, slots, pool)),
+                (
+                    sds((live_cap, n * span), BF16),
+                    sds((live_cap, half * pool), BF16),
+                    sds((pool, rows), BF16),
+                    sds((pool, rows), BF16),
+                    sds((live_cap, live_cap), F32),
+                    sds((8, 128), F32),
+                ),
+                [SMEM] + [VMEM] * 5,
                 [pltpu.VMEM((n, 1, rows), F32)],
-            )(meta, *orders)
-
-        received, (place, most) = exchange(message, index)
+            )(meta, *orders, pick)
+
+        received, (pick_in, pick_out, even, odd, live, most) = exchange(message, index)
         compact, weights, att, stats, coef_c, d_mixed, negatives = kernel_call(
-            functools.partial(forward_kernel, (n, rows, live_cap, slots, per)),
+            functools.partial(forward_kernel, (n, rows, slots, per)),
             (
                 sds((live_cap, wide), BF16),
                 sds((live_cap, live_cap), BF16),
@@ -547,9 +581,9 @@
                 sds((live_cap, head_dim), F32),
                 sds((negs, width), BF16),
             ),
-            [SMEM, VMEM, ANY] + [VMEM] * n,
+            [SMEM, VMEM, VMEM, ANY] + [VMEM] * n,
             [pltpu.VMEM((n, 8, width), F32), pltpu.VMEM((head_dim, width), BF16), pltpu.SemaphoreType.DMA],
-        )(meta, place, w_out, *received)
+        )(meta, pick_in, live, w_out, *received)
         other = swap(stats, "seq", 1)
         paired = jnp.stack(
             list(merge_stats([stats[i] for i in range(4)], [other[i] for i in range(4)], head_dim))
@@ -557,10 +591,11 @@
         )
         far = [swap(paired, "seq", d) for d in range(2, n, 2)]
         *back, mixed = kernel_call(
-            functools.partial(backward_kernel, (n, rows, live_cap, slots)),
-            (sds((2, slots + rows // PARTS, wide), BF16),) * (n // 2) + (sds((live_cap, head_dim), BF16),),
-            [SMEM] + [VMEM] * 9,
-        )(meta, compact, weights, att, d_mixed, paired, *far, place)
+            functools.partial(backward_kernel, (n, rows, pool)),
+            (sds((2 * quarter + pool, wide), BF16),) * half + (sds((live_cap, head_dim), BF16),),
+            [SMEM] + [VMEM] * 10,
+            [pltpu.VMEM((live_cap + rows, head_dim), F32)],
+        )(meta, compact, weights, att, d_mixed, paired, *far, pick_out, live)
 
         def group_sums():
             sums = kernel_call(sums_kernel, sds((negs + 8, head_dim), F32), [VMEM] * 3)(coef_c, mixed, most)
@@ -568,23 +603,20 @@
             total, most_of_all = kernel_call(
                 total_kernel, (sds((negs, head_dim), F32), sds((8, 128), F32)), [VMEM] * groups
             )(*sums)
-            return total, most_of_all[0, 0] > slots
+            return total, most_of_all[0, 0] > 0.0
 
         returned, (total, overflow) = exchange(back, group_sums)
-        return overflow, (pick, negatives, total, *returned)
-
-    def finish(slots, *parts):
+        return overflow, (even, odd, w_out, negatives, total, *returned)
+
+    def finish(*parts):
         return kernel_call(
-            functools.partial(finish_kernel, (n, rows, slots, groups)),
+            functools.partial(finish_kernel, (n, rows, groups)),
             (sds((rows, PARTS * width), BF16), sds((rows, width), BF16), sds((head_dim, width // groups), F32)),
-            [SMEM] + [VMEM] * (4 + n),
-            [pltpu.VMEM((rows, width), BF16)],
-        )(meta, parts[0], w_out, *parts[1:])
-
-    overflow, parts = passes(SLOTS)
-    d_home, layer_out, d_w_out = lax.cond(
-        overflow, lambda *_: finish(rows, *passes(rows)[1]), lambda *parts: finish(SLOTS, *parts), *parts
-    )
+            [SMEM] + [VMEM] * (5 + n),
+        )(meta, *parts)
+
+    overflow, parts = passes(SLOTS, POOL)
+    d_home, layer_out, d_w_out = lax.cond(overflow, lambda *_: finish(*passes(rows, 2 * rows)[1]), finish, *parts)
     return (layer_out, d_home, d_w_out)
 
 

time: 67.5 us -> 64.8 us (0.960)
  waiting for transfers between devices: 26.7 us -> 22.2 us
  starting transfers between devices: 25.1 us -> 26.2 us
  Pallas kernels: 12 us -> 12.7 us
    ppermute x25, waiting for transfers between devices: 26.7 us -> 22.2 us  [swap(): lax.ppermute(block, axis, [(i, i ^ distance) for i in range(lax.axis_size...]
    ppermute x25, starting transfers between devices: 25.1 us -> 26.2 us  [swap(): lax.ppermute(block, axis, [(i, i ^ distance) for i in range(lax.axis_size...]
    pallas_call x5, Pallas kernels: 11.8 us -> 12.5 us  [the longest x1 3.54 us: finish(): kernel_call(functools.partial(finish_kernel, (n, rows, groups)), (sds((ro...]
  transfers between devices with their start and end apart: 25 -> 25, of which waited for: 19 -> 17; matrix products, arithmetic and copies ran while one was open for 2% -> 2% of each run, Pallas kernels for 2% -> 4%
where the time goes in v4:
time: 64.8 us; the launch traced here: 64.6 us
  starting transfers between devices  26.2 us (40%)
  waiting for transfers between devices  22.2 us (34%)
  Pallas kernels  12.7 us (20%)
  between operations  1.42 us (2%)
  other arithmetic  1.4 us (2%)
    ppermute x25, starting transfers between devices, swap(): lax.ppermute(block, axis, [(i, i ^ distance) for i in range(lax.axis_size...  26.2 us
    ppermute x25, waiting for transfers between devices, swap(): lax.ppermute(block, axis, [(i, i ^ distance) for i in range(lax.axis_size...  22.2 us
    pallas_call x1, Pallas kernels, finish(): kernel_call(functools.partial(finish_kernel, (n, rows, groups)), (sds((ro...  3.54 us
    pallas_call x1, Pallas kernels, passes(): kernel_call(functools.partial(pack_kernel, (n, rows, slots)), (sds((2 * s...  2.69 us
    pallas_call x1, Pallas kernels, index(): kernel_call(functools.partial(index_kernel, (n, rows, slots, pool)), (sds...  2.32 us
    pallas_call x1, Pallas kernels, passes(): kernel_call(functools.partial(forward_kernel, (n, rows, slots, per)), (sd...  2.01 us
    pallas_call x1, Pallas kernels, passes(): kernel_call(functools.partial(backward_kernel, (n, rows, pool)), (sds((2...  1.98 us
  transfers between devices with their start and end apart: 25, of which 17 were waited for; matrix products, arithmetic and copies ran while one was open for 2% of the time, Pallas kernels for 4%

profile of v4, /device:TPU:0, one launch (start us, length us, event | category | flops | bytes accessed | tf_op | source)
XLA Modules:
  0.0 64.6 jit_solution(9809280094001626935)
XLA Ops:
  1.1 1.0 %collective-permute-done.25 = s32[1,128]{1,0:T(1,128)S(1)} collective-permute-done((s32[1,128]{1,0:T(1,128)}, s32[1,128]{1,0:T(1,128)S(1)}, u32[]{:S(2)}, u32[]{:S(2)}) %collective-permute-start.25) | collective-permute-done | bytes 544 | tf_op jit(solution)/shard_map/ppermute | solution.py:501
  2.8 2.9 %collective-permute-start.26 = (s32[2,1,128]{2,1,0:T(1,128)S(1)}, s32[2,1,128]{2,1,0:T(1,128)S(1)}, u32[]{:S(2)}, u32[]{:S(2)}) collective-permute-start(s32[2,1,128]{2,1,0:T(1,128)S(1)} %pad_add_fusion.1.b0), channel_id=1, source_target_pairs={{0,2},{1,3},{2,0},{3,1},{4,6},{5,7},{6,4},{7,5},{8,10},{9,11},{10,... | collective-permute-start | bytes 3080 | tf_op jit(solution)/shard_map/ppermute | solution.py:501
  5.6 2.6 %collective-permute-start.27 = (s32[2,1,128]{2,1,0:T(1,128)S(1)}, s32[2,1,128]{2,1,0:T(1,128)S(1)}, u32[]{:S(2)}, u32[]{:S(2)}) collective-permute-start(s32[2,1,128]{2,1,0:T(1,128)S(1)} %pad_add_fusion.1.b0), channel_id=1, source_target_pairs={{0,4},{1,5},{2,6},{3,7},{4,0},{5,1},{6,2},{7,3},{8,12},{9,13},{10,... | collective-permute-start | bytes 3080 | tf_op jit(solution)/shard_map/ppermute | solution.py:501
  9.0 1.1 %collective-permute-done.27.b2 = s32[2,1,128]{2,1,0:T(1,128)S(1)} collective-permute-done((s32[2,1,128]{2,1,0:T(1,128)S(1)}, s32[2,1,128]{2,1,0:T(1,128)S(1)}, u32[]{:S(2)}, u32[]{:S(2)}) %collective-permute-start.27) | collective-permute-done | bytes 1056 | tf_op jit(solution)/shard_map/ppermute | solution.py:501
  10.1 3.5 %collective-permute-done.28.b3 = s32[2,1,128]{2,1,0:T(1,128)S(1)} collective-permute-done((s32[2,1,128]{2,1,0:T(1,128)S(1)}, s32[2,1,128]{2,1,0:T(1,128)S(1)}, u32[]{:S(2)}, u32[]{:S(2)}) %collective-permute-start.28) | collective-permute-done | bytes 1056 | tf_op jit(solution)/shard_map/ppermute | solution.py:501
  13.6 2.7 %shard_map.103 = (bf16[136,512]{1,0:T(8,128)(2,1)S(1)}, bf16[136,512]{1,0:T(8,128)(2,1)S(1)}, bf16[136,512]{1,0:T(8,128)(2,1)S(1)}, bf16[136,512]{1,0:T(8,128)(2,1)S(1)}, bf16[128,128]{1,0:T(8,128)(2,1)S(1)}) custom-call(s32[10]{0:T(128)S(1)} %pad_add_fusion.2.meta, s32[2,1,128]{2,1,0:T(1,128)S(1)} %pad_add_fusion.1.b0, ...), custom_call_target="tpu_custom_call" | custom-call | tf_op jit(solution)/shard_map/pallas_call | solution.py:541
  16.9 3.8 %collective-permute-start.29 = (bf16[136,512]{1,0:T(8,128)(2,1)S(1)}, bf16[136,512]{1,0:T(8,128)(2,1)S(1)}, u32[]{:S(2)}, u32[]{:S(2)}) collective-permute-start(bf16[136,512]{1,0:T(8,128)(2,1)S(1)} %get-tuple-element.178), channel_id=1, source_target_pairs={{0,6},{1,7},{2,4},{3,5},{4,2},{5,3},{6,0},{7,1},{8,14},{9,15},{10,... | collective-permute-start | bytes 417800 | tf_op jit(solution)/shard_map/ppermute | solution.py:501
  20.7 2.3 %shard_map.104 = (bf16[384,512]{1,0:T(8,128)(2,1)S(1)}, bf16[384,416]{1,0:T(8,128)(2,1)S(1)}, bf16[104,128]{1,0:T(8,128)(2,1)S(1)}, bf16[104,128]{1,0:T(8,128)(2...) custom-call(s32[10]{0:T(128)S(1)} %pad_add_fusion.2.meta, s32[2,1,128]{2,1,0:T(1,128)S(1)} %pad_add_fusion.1.b0, ...), custom_call_target="tpu_custom_call" | custom-call | tf_op jit(solution)/shard_map/pallas_call | solution.py:558
  23.2 5.8 %collective-permute-done.30.refs_4_ = bf16[136,512]{1,0:T(8,128)(2,1)S(1)} collective-permute-done((bf16[136,512]{1,0:T(8,128)(2,1)S(1)}, bf16[136,512]{1,0:T(8,128)(2,1)S(1)}, u32[]{:S(2)}, u32[]{:S(2)}) %collective-permute-start.30) | collective-permute-done | bytes 139296 | tf_op jit(solution)/shard_map/ppermute | solution.py:501
  30.8 2.0 %shard_map.105 = (bf16[384,512]{1,0:T(8,128)(2,1)S(1)}, bf16[384,384]{1,0:T(8,128)(2,1)S(1)}, f32[384,128]{1,0:T(8,128)S(1)}, f32[8,384]{1,0:T(8,128)S(1)}, bf16...) custom-call(s32[10]{0:T(128)S(1)} %pad_add_fusion.2.meta, ...), custom_call_target="tpu_custom_call" | custom-call | tf_op jit(solution)/shard_map/pallas_call | solution.py:573
  33.1 1.0 %collective-permute-done.36 = f32[8,384]{1,0:T(8,128)S(1)} collective-permute-done((f32[8,384]{1,0:T(8,128)S(1)}, f32[8,384]{1,0:T(8,128)S(1)}, u32[]{:S(2)}, u32[]{:S(2)}) %collective-permute-start.36) | collective-permute-done | bytes 12320 | tf_op jit(solution)/shard_map/ppermute | solution.py:501
  34.2 2.1 %collective-permute-start.37 = (f32[8,384]{1,0:T(8,128)S(1)}, f32[8,384]{1,0:T(8,128)S(1)}, u32[]{:S(2)}, u32[]{:S(2)}) collective-permute-start(f32[8,384]{1,0:T(8,128)S(1)} %stack.43.st0), channel_id=1, source_target_pairs={{0,2},{1,3},{2,0},{3,1},{4,6},{5,7},{6,4},{7,5},{8,10},{9,11},{10,... | collective-permute-start | bytes 36872 | tf_op jit(solution)/shard_map/ppermute | solution.py:501
  36.3 2.4 %collective-permute-start.39 = (f32[8,384]{1,0:T(8,128)S(1)}, f32[8,384]{1,0:T(8,128)S(1)}, u32[]{:S(2)}, u32[]{:S(2)}) collective-permute-start(f32[8,384]{1,0:T(8,128)S(1)} %stack.43.st0), channel_id=1, source_target_pairs={{0,6},{1,7},{2,4},{3,5},{4,2},{5,3},{6,0},{7,1},{8,14},{9,15},{10,... | collective-permute-start | bytes 36872 | tf_op jit(solution)/shard_map/ppermute | solution.py:501
  38.7 2.2 %collective-permute-done.38.st2 = f32[8,384]{1,0:T(8,128)S(1)} collective-permute-done((f32[8,384]{1,0:T(8,128)S(1)}, f32[8,384]{1,0:T(8,128)S(1)}, u32[]{:S(2)}, u32[]{:S(2)}) %collective-permute-start.38) | collective-permute-done | bytes 12320 | tf_op jit(solution)/shard_map/ppermute | solution.py:501
  41.8 2.0 %shard_map.106 = (bf16[168,512]{1,0:T(8,128)(2,1)S(1)}, bf16[168,512]{1,0:T(8,128)(2,1)S(1)}, bf16[168,512]{1,0:T(8,128)(2,1)S(1)}, bf16[168,512]{1,0:T(8,128)(2,1)S(1)}, bf16[384,128]{1,0:T(8,128)(2,1)S(1)}) custom-call(s32[10]{0:T(128)S(1)} %pad_add_fusion.2.meta, bf16[384,512]{1,0:T(8,128)(2,1)S(1)} %get-tuple-element.206.compact, ...), custom_call_target="tpu_custom_call" | custom-call | tf_op jit(solution)/shard_map/pallas_call | solution.py:593
  43.9 2.9 %collective-permute-start.41 = (bf16[168,512]{1,0:T(8,128)(2,1)S(1)}, bf16[168,512]{1,0:T(8,128)(2,1)S(1)}, u32[]{:S(2)}, u32[]{:S(2)}) collective-permute-start(bf16[168,512]{1,0:T(8,128)(2,1)S(1)} %get-tuple-element.213), channel_id=1, source_target_pairs={{0,4},{1,5},{2,6},{3,7},{4,0},{5,1},{6,2},{7,3},{8,12},{9,13},{10,... | collective-permute-start | bytes 516104 | tf_op jit(solution)/shard_map/ppermute | solution.py:501
  46.8 1.4 %collective-permute-start.40 = (bf16[168,512]{1,0:T(8,128)(2,1)S(1)}, bf16[168,512]{1,0:T(8,128)(2,1)S(1)}, u32[]{:S(2)}, u32[]{:S(2)}) collective-permute-start(bf16[168,512]{1,0:T(8,128)(2,1)S(1)} %get-tuple-element.212), channel_id=1, source_target_pairs={{0,6},{1,7},{2,4},{3,5},{4,2},{5,3},{6,0},{7,1},{8,14},{9,15},{10,... | collective-permute-start | bytes 516104 | tf_op jit(solution)/shard_map/ppermute | solution.py:501
  48.4 1.5 %collective-permute-start.43 = (f32[40,128]{1,0:T(8,128)S(1)}, f32[40,128]{1,0:T(8,128)S(1)}, u32[]{:S(2)}, u32[]{:S(2)}) collective-permute-start(f32[40,128]{1,0:T(8,128)S(1)} %shard_map.107.refs_0_), channel_id=1, source_target_pairs={{0,8},{8,0},{16,24},{24,16},{1,9},{9,1},{17,25},{25,17},{2,10},{10... | collective-permute-start | bytes 61448 | tf_op jit(solution)/shard_map/ppermute | solution.py:501
  49.9 1.5 %collective-permute-start.44 = (f32[40,128]{1,0:T(8,128)S(1)}, f32[40,128]{1,0:T(8,128)S(1)}, u32[]{:S(2)}, u32[]{:S(2)}) collective-permute-start(f32[40,128]{1,0:T(8,128)S(1)} %shard_map.107.refs_0_), channel_id=1, source_target_pairs={{0,16},{8,24},{16,0},{24,8},{1,17},{9,25},{17,1},{25,9},{2,18},{10... | collective-permute-start | bytes 61448 | tf_op jit(solution)/shard_map/ppermute | solution.py:501
  52.2 2.5 %collective-permute-start.45 = (f32[40,128]{1,0:T(8,128)S(1)}, f32[40,128]{1,0:T(8,128)S(1)}, u32[]{:S(2)}, u32[]{:S(2)}) collective-permute-start(f32[40,128]{1,0:T(8,128)S(1)} %shard_map.107.refs_0_), channel_id=1, source_target_pairs={{0,24},{8,16},{16,8},{24,0},{1,25},{9,17},{17,9},{25,1},{2,26},{10... | collective-permute-start | bytes 61448 | tf_op jit(solution)/shard_map/ppermute | solution.py:501
  54.7 2.2 %collective-permute-done.45.refs_3_ = f32[40,128]{1,0:T(8,128)S(1)} collective-permute-done((f32[40,128]{1,0:T(8,128)S(1)}, f32[40,128]{1,0:T(8,128)S(1)}, u32[]{:S(2)}, u32[]{:S(2)}) %collective-permute-start.45) | collective-permute-done | bytes 20512 | tf_op jit(solution)/shard_map/ppermute | solution.py:501
  58.0 1.0 %collective-permute-done.41 = bf16[168,512]{1,0:T(8,128)(2,1)S(1)} collective-permute-done((bf16[168,512]{1,0:T(8,128)(2,1)S(1)}, bf16[168,512]{1,0:T(8,128)(2,1)S(1)}, u32[]{:S(2)}, u32[]{:S(2)}) %collective-permute-start.41) | collective-permute-done | bytes 172064 | tf_op jit(solution)/shard_map/ppermute | solution.py:501
  61.0 3.6 %conditional.1 = ((bf16[128,4096]{1,0:T(8,128)(2,1)}, bf16[128,1024]{1,0:T(8,128)(2,1)}, f32[128,256]{1,0:T(8,128)})) conditional(s32[]{:T(128)} %convert_element_type.3, (s32[10]{0:T(128)S(1)}, bf16[104,128]{1,0:T(8,128)(2,1)S(1)}, bf16[104,128]{1,0:T(8,128)(2,1)}, bf16[1024,1024]{1,0:T(8,128)(2,1)}, bf16[32,1024]{1,0:T(8,128)(2,1)S(1)}, ...), branch_computations={%region_0.0_spmd, %region_1.0_spmd} | conditional | flops 5248 | bytes 34260012 | solution.py:619
  61.0 3.5 %branch_0_fun.1 = (bf16[128,4096]{1,0:T(8,128)(2,1)}, bf16[128,1024]{1,0:T(8,128)(2,1)}, f32[128,256]{1,0:T(8,128)}) custom-call(s32[10]{0:T(128)S(1)} %get-tuple-element.44.meta, bf16[104,128]{1,0:T(8,128)(2,1)S(1)} %get-tuple-element.45.even, bf16[104,128]{1,0:T(8,128)(2,1)} %get-tuple-element.46.odd, bf16[1024,1024]{1,0:T(8,128)(2,1)} %get-tuple-element.47.w_out, ...), custom_call_target="tpu_custom_call" | custom-call | tf_op jit(solution)/shard_map/cond/branch_0_fun/pallas_call | solution.py:612
  (52 shorter events, 9.3 us)
Async XLA Ops:
  0.6 1.5 %collective-permute-start.25 = (s32[1,128]{1,0:T(1,128)}, s32[1,128]{1,0:T(1,128)S(1)}, u32[]{:S(2)}, u32[]{:S(2)}) collective-permute-start(s32[1,128]{1,0:T(1,128)} %param.16), channel_id=1, source_target_pairs={{0,1},{1,0},{2,3},{3,2},{4,5},{5,4},{6,7},{7,6},{8,9},{9,8},{10,11... | collective-permute-start | bytes 1544 | tf_op jit(solution)/shard_map/ppermute | solution.py:501
  2.8 6.2 %collective-permute-start.26 = (s32[2,1,128]{2,1,0:T(1,128)S(1)}, s32[2,1,128]{2,1,0:T(1,128)S(1)}, u32[]{:S(2)}, u32[]{:S(2)}) collective-permute-start(s32[2,1,128]{2,1,0:T(1,128)S(1)} %pad_add_fusion.1.b0), channel_id=1, source_target_pairs={{0,2},{1,3},{2,0},{3,1},{4,6},{5,7},{6,4},{7,5},{8,10},{9,11},{10,... | collective-permute-start | bytes 3080 | tf_op jit(solution)/shard_map/ppermute | solution.py:501
  5.6 4.5 %collective-permute-start.27 = (s32[2,1,128]{2,1,0:T(1,128)S(1)}, s32[2,1,128]{2,1,0:T(1,128)S(1)}, u32[]{:S(2)}, u32[]{:S(2)}) collective-permute-start(s32[2,1,128]{2,1,0:T(1,128)S(1)} %pad_add_fusion.1.b0), channel_id=1, source_target_pairs={{0,4},{1,5},{2,6},{3,7},{4,0},{5,1},{6,2},{7,3},{8,12},{9,13},{10,... | collective-permute-start | bytes 3080 | tf_op jit(solution)/shard_map/ppermute | solution.py:501
  8.2 5.4 %collective-permute-start.28 = (s32[2,1,128]{2,1,0:T(1,128)S(1)}, s32[2,1,128]{2,1,0:T(1,128)S(1)}, u32[]{:S(2)}, u32[]{:S(2)}) collective-permute-start(s32[2,1,128]{2,1,0:T(1,128)S(1)} %pad_add_fusion.1.b0), channel_id=1, source_target_pairs={{0,6},{1,7},{2,4},{3,5},{4,2},{5,3},{6,0},{7,1},{8,14},{9,15},{10,... | collective-permute-start | bytes 3080 | tf_op jit(solution)/shard_map/ppermute | solution.py:501
  16.3 6.9 %collective-permute-start.31 = (bf16[136,512]{1,0:T(8,128)(2,1)S(1)}, bf16[136,512]{1,0:T(8,128)(2,1)S(1)}, u32[]{:S(2)}, u32[]{:S(2)}) collective-permute-start(bf16[136,512]{1,0:T(8,128)(2,1)S(1)} %get-tuple-element.180), channel_id=1, source_target_pairs={{0,2},{1,3},{2,0},{3,1},{4,6},{5,7},{6,4},{7,5},{8,10},{9,11},{10,... | collective-permute-start | bytes 417800 | tf_op jit(solution)/shard_map/ppermute | solution.py:501
  16.4 12.6 %collective-permute-start.30 = (bf16[136,512]{1,0:T(8,128)(2,1)S(1)}, bf16[136,512]{1,0:T(8,128)(2,1)S(1)}, u32[]{:S(2)}, u32[]{:S(2)}) collective-permute-start(bf16[136,512]{1,0:T(8,128)(2,1)S(1)} %get-tuple-element.179), channel_id=1, source_target_pairs={{0,4},{1,5},{2,6},{3,7},{4,0},{5,1},{6,2},{7,3},{8,12},{9,13},{10,... | collective-permute-start | bytes 417800 | tf_op jit(solution)/shard_map/ppermute | solution.py:501
  16.9 12.0 %collective-permute-start.29 = (bf16[136,512]{1,0:T(8,128)(2,1)S(1)}, bf16[136,512]{1,0:T(8,128)(2,1)S(1)}, u32[]{:S(2)}, u32[]{:S(2)}) collective-permute-start(bf16[136,512]{1,0:T(8,128)(2,1)S(1)} %get-tuple-element.178), channel_id=1, source_target_pairs={{0,6},{1,7},{2,4},{3,5},{4,2},{5,3},{6,0},{7,1},{8,14},{9,15},{10,... | collective-permute-start | bytes 417800 | tf_op jit(solution)/shard_map/ppermute | solution.py:501
  20.7 8.7 %collective-permute-start.32 = (bf16[136,512]{1,0:T(8,128)(2,1)S(1)}, bf16[136,512]{1,0:T(8,128)(2,1)S(1)}, u32[]{:S(2)}, u32[]{:S(2)}) collective-permute-start(bf16[136,512]{1,0:T(8,128)(2,1)S(1)} %get-tuple-element.202.refs_0_), channel_id=1, source_target_pairs={{0,1},{1,0},{2,3},{3,2},{4,5},{5,4},{6,7},{7,6},{8,9},{9,8},{10,11... | collective-permute-start | bytes 417800 | tf_op jit(solution)/shard_map/ppermute | solution.py:501
  28.9 1.4 %collective-permute-start.35 = (bf16[136,512]{1,0:T(8,128)(2,1)S(1)}, bf16[136,512]{1,0:T(8,128)(2,1)S(1)}, u32[]{:S(2)}, u32[]{:S(2)}) collective-permute-start(bf16[136,512]{1,0:T(8,128)(2,1)S(1)} %collective-permute-done.29.refs_6_), channel_id=1, source_target_pairs={{0,1},{1,0},{2,3},{3,2},{4,5},{5,4},{6,7},{7,6},{8,9},{9,8},{10,11... | collective-permute-start | bytes 417800 | tf_op jit(solution)/shard_map/ppermute | solution.py:501
  28.9 1.6 %collective-permute-start.34 = (bf16[136,512]{1,0:T(8,128)(2,1)S(1)}, bf16[136,512]{1,0:T(8,128)(2,1)S(1)}, u32[]{:S(2)}, u32[]{:S(2)}) collective-permute-start(bf16[136,512]{1,0:T(8,128)(2,1)S(1)} %collective-permute-done.30.refs_4_), channel_id=1, source_target_pairs={{0,1},{1,0},{2,3},{3,2},{4,5},{5,4},{6,7},{7,6},{8,9},{9,8},{10,11... | collective-permute-start | bytes 417800 | tf_op jit(solution)/shard_map/ppermute | solution.py:501
  29.4 1.4 %collective-permute-start.33 = (bf16[136,512]{1,0:T(8,128)(2,1)S(1)}, bf16[136,512]{1,0:T(8,128)(2,1)S(1)}, u32[]{:S(2)}, u32[]{:S(2)}) collective-permute-start(bf16[136,512]{1,0:T(8,128)(2,1)S(1)} %collective-permute-done.31.refs_2_), channel_id=1, source_target_pairs={{0,1},{1,0},{2,3},{3,2},{4,5},{5,4},{6,7},{7,6},{8,9},{9,8},{10,11... | collective-permute-start | bytes 417800 | tf_op jit(solution)/shard_map/ppermute | solution.py:501
  34.2 4.6 %collective-permute-start.37 = (f32[8,384]{1,0:T(8,128)S(1)}, f32[8,384]{1,0:T(8,128)S(1)}, u32[]{:S(2)}, u32[]{:S(2)}) collective-permute-start(f32[8,384]{1,0:T(8,128)S(1)} %stack.43.st0), channel_id=1, source_target_pairs={{0,2},{1,3},{2,0},{3,1},{4,6},{5,7},{6,4},{7,5},{8,10},{9,11},{10,... | collective-permute-start | bytes 36872 | tf_op jit(solution)/shard_map/ppermute | solution.py:501
  36.3 4.6 %collective-permute-start.38 = (f32[8,384]{1,0:T(8,128)S(1)}, f32[8,384]{1,0:T(8,128)S(1)}, u32[]{:S(2)}, u32[]{:S(2)}) collective-permute-start(f32[8,384]{1,0:T(8,128)S(1)} %stack.43.st0), channel_id=1, source_target_pairs={{0,4},{1,5},{2,6},{3,7},{4,0},{5,1},{6,2},{7,3},{8,12},{9,13},{10,... | collective-permute-start | bytes 36872 | tf_op jit(solution)/shard_map/ppermute | solution.py:501
  36.3 5.5 %collective-permute-start.39 = (f32[8,384]{1,0:T(8,128)S(1)}, f32[8,384]{1,0:T(8,128)S(1)}, u32[]{:S(2)}, u32[]{:S(2)}) collective-permute-start(f32[8,384]{1,0:T(8,128)S(1)} %stack.43.st0), channel_id=1, source_target_pairs={{0,6},{1,7},{2,4},{3,5},{4,2},{5,3},{6,0},{7,1},{8,14},{9,15},{10,... | collective-permute-start | bytes 36872 | tf_op jit(solution)/shard_map/ppermute | solution.py:501
  43.8 14.2 %collective-permute-start.42 = (bf16[168,512]{1,0:T(8,128)(2,1)S(1)}, bf16[168,512]{1,0:T(8,128)(2,1)S(1)}, u32[]{:S(2)}, u32[]{:S(2)}) collective-permute-start(bf16[168,512]{1,0:T(8,128)(2,1)S(1)} %get-tuple-element.214), channel_id=1, source_target_pairs={{0,2},{1,3},{2,0},{3,1},{4,6},{5,7},{6,4},{7,5},{8,10},{9,11},{10,... | collective-permute-start | bytes 516104 | tf_op jit(solution)/shard_map/ppermute | solution.py:501
  43.9 15.1 %collective-permute-start.41 = (bf16[168,512]{1,0:T(8,128)(2,1)S(1)}, bf16[168,512]{1,0:T(8,128)(2,1)S(1)}, u32[]{:S(2)}, u32[]{:S(2)}) collective-permute-start(bf16[168,512]{1,0:T(8,128)(2,1)S(1)} %get-tuple-element.213), channel_id=1, source_target_pairs={{0,4},{1,5},{2,6},{3,7},{4,0},{5,1},{6,2},{7,3},{8,12},{9,13},{10,... | collective-permute-start | bytes 516104 | tf_op jit(solution)/shard_map/ppermute | solution.py:501
  46.8 12.2 %collective-permute-start.40 = (bf16[168,512]{1,0:T(8,128)(2,1)S(1)}, bf16[168,512]{1,0:T(8,128)(2,1)S(1)}, u32[]{:S(2)}, u32[]{:S(2)}) collective-permute-start(bf16[168,512]{1,0:T(8,128)(2,1)S(1)} %get-tuple-element.212), channel_id=1, source_target_pairs={{0,6},{1,7},{2,4},{3,5},{4,2},{5,3},{6,0},{7,1},{8,14},{9,15},{10,... | collective-permute-start | bytes 516104 | tf_op jit(solution)/shard_map/ppermute | solution.py:501
  48.4 3.8 %collective-permute-start.43 = (f32[40,128]{1,0:T(8,128)S(1)}, f32[40,128]{1,0:T(8,128)S(1)}, u32[]{:S(2)}, u32[]{:S(2)}) collective-permute-start(f32[40,128]{1,0:T(8,128)S(1)} %shard_map.107.refs_0_), channel_id=1, source_target_pairs={{0,8},{8,0},{16,24},{24,16},{1,9},{9,1},{17,25},{25,17},{2,10},{10... | collective-permute-start | bytes 61448 | tf_op jit(solution)/shard_map/ppermute | solution.py:501
  49.9 4.8 %collective-permute-start.44 = (f32[40,128]{1,0:T(8,128)S(1)}, f32[40,128]{1,0:T(8,128)S(1)}, u32[]{:S(2)}, u32[]{:S(2)}) collective-permute-start(f32[40,128]{1,0:T(8,128)S(1)} %shard_map.107.refs_0_), channel_id=1, source_target_pairs={{0,16},{8,24},{16,0},{24,8},{1,17},{9,25},{17,1},{25,9},{2,18},{10... | collective-permute-start | bytes 61448 | tf_op jit(solution)/shard_map/ppermute | solution.py:501
  52.2 4.7 %collective-permute-start.45 = (f32[40,128]{1,0:T(8,128)S(1)}, f32[40,128]{1,0:T(8,128)S(1)}, u32[]{:S(2)}, u32[]{:S(2)}) collective-permute-start(f32[40,128]{1,0:T(8,128)S(1)} %shard_map.107.refs_0_), channel_id=1, source_target_pairs={{0,24},{8,16},{16,8},{24,0},{1,25},{9,17},{17,9},{25,1},{2,26},{10... | collective-permute-start | bytes 61448 | tf_op jit(solution)/shard_map/ppermute | solution.py:501
  54.6 4.9 %collective-permute-start.46 = (bf16[168,512]{1,0:T(8,128)(2,1)S(1)}, bf16[168,512]{1,0:T(8,128)(2,1)S(1)}, u32[]{:S(2)}, u32[]{:S(2)}) collective-permute-start(bf16[168,512]{1,0:T(8,128)(2,1)S(1)} %get-tuple-element.229), channel_id=1, source_target_pairs={{0,1},{1,0},{2,3},{3,2},{4,5},{5,4},{6,7},{7,6},{8,9},{9,8},{10,11... | collective-permute-start | bytes 516104 | tf_op jit(solution)/shard_map/ppermute | solution.py:501
  59.1 1.4 %collective-permute-start.49 = (bf16[168,512]{1,0:T(8,128)(2,1)S(1)}, bf16[168,512]{1,0:T(8,128)(2,1)S(1)}, u32[]{:S(2)}, u32[]{:S(2)}) collective-permute-start(bf16[168,512]{1,0:T(8,128)(2,1)S(1)} %collective-permute-done.40), channel_id=1, source_target_pairs={{0,1},{1,0},{2,3},{3,2},{4,5},{5,4},{6,7},{7,6},{8,9},{9,8},{10,11... | collective-permute-start | bytes 516104 | tf_op jit(solution)/shard_map/ppermute | solution.py:501
  59.1 1.7 %collective-permute-start.48 = (bf16[168,512]{1,0:T(8,128)(2,1)S(1)}, bf16[168,512]{1,0:T(8,128)(2,1)S(1)}, u32[]{:S(2)}, u32[]{:S(2)}) collective-permute-start(bf16[168,512]{1,0:T(8,128)(2,1)S(1)} %collective-permute-done.41), channel_id=1, source_target_pairs={{0,1},{1,0},{2,3},{3,2},{4,5},{5,4},{6,7},{7,6},{8,9},{9,8},{10,11... | collective-permute-start | bytes 516104 | tf_op jit(solution)/shard_map/ppermute | solution.py:501
  59.6 1.4 %collective-permute-start.47 = (bf16[168,512]{1,0:T(8,128)(2,1)S(1)}, bf16[168,512]{1,0:T(8,128)(2,1)S(1)}, u32[]{:S(2)}, u32[]{:S(2)}) collective-permute-start(bf16[168,512]{1,0:T(8,128)(2,1)S(1)} %collective-permute-done.42), channel_id=1, source_target_pairs={{0,1},{1,0},{2,3},{3,2},{4,5},{5,4},{6,7},{7,6},{8,9},{9,8},{10,11... | collective-permute-start | bytes 516104 | tf_op jit(solution)/shard_map/ppermute | solution.py:501
  (7 other events, 171.6 us)

commit v5 on v4

--- a/solution.py
+++ b/solution.py
@@ -195,7 +195,7 @@
     n, _, rows = order_ref.shape
     cell = rows // n
     for b in range(n):
-        order_ref[meta[0] ^ b] = blocks[b // 2][b % 2].astype(F32)
+        order_ref[meta[0] ^ b] = blocks[b // (n // 2)][b % (n // 2)].astype(F32)
     starts = starts_of(meta, n)
     pos = iota((cell, rows), 1)
     filled = [jnp.broadcast_to(order_ref[t], (cell, rows)) for t in range(n)]
@@ -222,67 +222,72 @@
         outs[x // 2][x % 2] = jnp.concatenate([picked[:, pl.ds(i * width + first, head_dim)] for i in range(PARTS)], axis=1)
 
 
-def pack_kernel(sizes, meta, b0, b1, b2, b3, send, neg_ids, coef_t, table, qkvu, *refs):
+def prep_kernel(ids, send, coef_t, table, qkvu, held, below, home, send_row, coef_rows, items, neg_rows, sems):
+    per, chunk, width = items.shape
+    rows = send_row.shape[1]
+    wide = below.shape[1]
+    copies = [
+        pltpu.make_async_copy(source, target, sems.at[i])
+        for i, (source, target) in enumerate(((send, send_row), (coef_t, coef_rows), (qkvu, held)))
+    ]
+    for j in range(per):
+        start = pl.multiple_of((ids[j] // chunk) * chunk, chunk)
+        copies.append(pltpu.make_async_copy(table.at[pl.ds(start, chunk)], items.at[j], sems.at[3 + j]))
+    for copy in copies:
+        copy.start()
+    lane = iota((rows, rows), 1)
+    copies[0].wait()
+    own = jnp.where(lane == iota((rows, rows), 0), send_row[...].astype(F32), 0.0)
+    home[...] = one_hot(jnp.sum(own, axis=1, keepdims=True) == lane.astype(F32))
+    copies[1].wait()
+    for j in range(per):
+        copies[3 + j].wait()
+        own = iota((chunk, width), 0) == ids[j] % chunk
+        neg_rows[j : j + 1] = jnp.sum(jnp.where(own, items[j].astype(F32), 0.0), axis=0, keepdims=True)
+    step = coef_rows.shape[0] * rows // wide
+    coefs = jnp.concatenate([coef_rows[b * step : (b + 1) * step].astype(F32) for b in range(wide // rows)], axis=1)
+    negs = jnp.concatenate([neg_rows[0:per, b * wide : (b + 1) * wide] for b in range(width // wide)], axis=0)
+    below[...] = jnp.concatenate([coefs, negs], axis=0).astype(BF16)
+    copies[2].wait()
+
+
+def pack_kernel(sizes, meta, b0, b1, held, below, home, *refs):
     n, rows, slots = sizes
     pairs = n // 2
     outs = refs[:pairs]
-    pick, order_ref, send_row, ids, coef_rows, items, neg_rows, held, sems = refs[pairs:]
-    per, chunk, width = items.shape
-    wide = outs[0].shape[1]
-    head_dim = wide // PARTS
+    pick, order_ref = refs[pairs:]
+    head_dim = outs[0].shape[1] // PARTS
+    width = head_dim * n
     cell = rows // n
     me = meta[0]
-    copies = [
-        pltpu.make_async_copy(source, target, sems.at[i])
-        for i, (source, target) in enumerate(((neg_ids, ids), (send, send_row), (coef_t, coef_rows), (qkvu, held)))
-    ]
-    for copy in copies:
-        copy.start()
-    copies[0].wait()
-    item_copies = []
-    for j in range(per):
-        start = pl.multiple_of((ids[j] // chunk) * chunk, chunk)
-        item_copies.append(pltpu.make_async_copy(table.at[pl.ds(start, chunk)], items.at[j], sems.at[4 + j]))
-        item_copies[-1].start()
-    filled, value = slot_table(meta, (b0, b1, b2, b3), order_ref)
+    filled, value = slot_table(meta, (b0, b1), order_ref)
     places = jnp.broadcast_to(slot_places(filled, value, me, cell), (rows, rows))
-    lane = iota((rows, rows), 1)
-    sub = iota((rows, rows), 0)
-    by_rank = one_hot(slot_ranks(places) == lane.astype(F32))
-    copies[1].wait()
-    home = jnp.sum(jnp.where(lane == sub, send_row[...].astype(F32), 0.0), axis=1, keepdims=True)
-    chosen = dot(by_rank, one_hot(home == lane.astype(F32)), ((0,), (0,)))
+    by_rank = one_hot(slot_ranks(places) == iota((rows, rows), 1).astype(F32))
+    chosen = dot(by_rank, home[...], ((0,), (0,)))
     pick[...] = chosen.astype(BF16)
     none = jnp.zeros((slots, rows), F32)
     both = jnp.concatenate(
         [jnp.concatenate([chosen[0:slots], none], axis=1), jnp.concatenate([none, chosen[0:slots]], axis=1)], axis=0
     ).astype(BF16)
-    copies[2].wait()
-    copies[3].wait()
-    for j in range(per):
-        item_copies[j].wait()
-        own = iota((chunk, width), 0) == ids[j] % chunk
-        neg_rows[j : j + 1] = jnp.sum(jnp.where(own, items[j].astype(F32), 0.0), axis=0, keepdims=True)
-    step = coef_rows.shape[0] * rows // wide
-    coefs = jnp.concatenate([coef_rows[b * step : (b + 1) * step].astype(F32) for b in range(wide // rows)], axis=1)
-    negs = jnp.concatenate([neg_rows[0:per, b * wide : (b + 1) * wide] for b in range(width // wide)], axis=0)
-    below = jnp.concatenate([coefs, negs], axis=0).astype(BF16)
     for d in range(pairs):
         columns = []
         for x in (2 * d, 2 * d + 1):
             first = pl.multiple_of((me ^ x) * head_dim, head_dim)
             columns.append(jnp.concatenate([held[:, pl.ds(i * width + first, head_dim)] for i in range(PARTS)], axis=1))
         outs[d][0 : 2 * slots] = dot(both, jnp.concatenate(columns, axis=0)).astype(BF16)
-        outs[d][2 * slots :] = below
-
-
-def index_kernel(sizes, meta, b0, b1, b2, b3, pick, pick_in, pick_out, home_even, home_odd, live, most, order_ref):
+        outs[d][2 * slots :] = below[...]
+
+
+def index_kernel(sizes, meta, b0, b1, pick, w_out, pick_in, pick_out, home_even, home_odd, live, most, w_cols, order_ref, w_rows, sem):
     n, rows, slots, pool = sizes
     cell = rows // n
     live_cap = live.shape[0]
+    head_dim = w_rows.shape[0]
+    copy = pltpu.make_async_copy(w_out.at[pl.ds(pl.multiple_of(meta[0] * head_dim, head_dim), head_dim)], w_rows, sem)
+    copy.start()
     span = pick_in.shape[1] // n
     me = meta[0]
-    filled, value = slot_table(meta, (b0, b1, b2, b3), order_ref)
+    filled, value = slot_table(meta, (b0, b1), order_ref)
     lane = iota((rows, rows), 1)
     columns = [slot_places(filled, value, me ^ x, cell) for x in range(n)]
     places = jnp.zeros((rows, rows), F32)
@@ -311,10 +316,13 @@
     for d in range(n // 2):
         line = placed(2 * d, 0.0, reach) + placed(2 * d + 1, counts[2 * d], reach) - 1.0
         hit = one_hot(iota((live_cap, reach), 0).astype(F32) == line)
-        pick_out[:, d * pool : (d + 1) * pool] = hit[:, :pool]
+        pick_out[d * pool : (d + 1) * pool] = jnp.transpose(hit.astype(F32))[:pool].astype(BF16)
     slot = iota((reach, rows), 0).astype(F32)
-    home_even[...] = dot(one_hot(slot == lane[0:1].astype(F32)), pick[...]).astype(BF16)[:pool]
-    home_odd[...] = dot(one_hot(slot == lane[0:1].astype(F32) + counts[1]), pick[...]).astype(BF16)[:pool]
+    for home, first in ((home_even, jnp.zeros((1, 1), F32)), (home_odd, counts[1])):
+        moved = dot(one_hot(slot == lane[0:1].astype(F32) + first), pick[...])
+        home[...] = moved[:pool].astype(BF16)
+    copy.wait()
+    w_cols[...] = jnp.transpose(w_rows[...].astype(F32)).astype(BF16)
     live[...] = jnp.where(pair_live(live_cap, starts_of(meta, n)), 1.0 / rows, 0.0)
 
 
@@ -324,17 +332,15 @@
     return (col <= row) & (tile_of(col, starts) > tile_of(row, starts) - SPAN) & (row < starts[-1])
 
 
-def forward_kernel(sizes, meta, pick, live, w_out, *refs):
+def forward_kernel(sizes, meta, pick, live, w_cols, *refs):
     n, rows, slots, per = sizes
     blocks = refs[:n]
-    compact, weights, att, stats, coef_c, d_mixed, negatives, neg_rows, w_rows, sem = refs[n:]
+    compact, weights, att, stats, coef_c, d_mixed, negatives, neg_rows = refs[n:]
     live_cap, head_dim = att.shape
     negs = coef_c.shape[0]
     wide = blocks[0].shape[1]
     span = pick.shape[1] // n
     me = meta[0]
-    copy = pltpu.make_async_copy(w_out.at[pl.ds(pl.multiple_of(me * head_dim, head_dim), head_dim)], w_rows, sem)
-    copy.start()
     received = [block[2 * slots - span : 2 * slots] if x % 2 else block[0:span] for x, block in enumerate(blocks)]
     both = dot(pick[...], jnp.concatenate(received, axis=0)).astype(BF16)
     compact[...] = both
@@ -355,8 +361,7 @@
     neg = jnp.concatenate([neg_rows[s, 0:per] for s in range(n)], axis=0).astype(BF16)
     negatives[...] = neg
     head_grad = dot(coef_t, neg, ((0,), (0,))).astype(BF16)
-    copy.wait()
-    dm = dot(head_grad, w_rows[...], ((1,), (1,)))
+    dm = dot(head_grad, w_cols[...])
     d_mixed[...] = dm
     u, v, q, k = (both[:, i * head_dim : (i + 1) * head_dim] for i in range(PARTS))
     scores = dot(q, k, ((1,), (1,))) * (1.0 / math.sqrt(head_dim))
@@ -425,7 +430,7 @@
         [dm * normed, dot(weights[...], d_att, ((0,), (0,))), dot(ds, k), dot(ds, q, ((0,), (0,)))], axis=1
     ).astype(BF16)
     mixed_ref[...] = mixed
-    sent = dot(pick[...], grad, ((0,), (0,))).astype(BF16)
+    sent = dot(pick[...], grad).astype(BF16)
     mixed_rows[0:live_cap] = mixed.astype(F32)
     mixed_rows[live_cap:] = jnp.zeros((rows, head_dim), F32)
     quarter = rows // PARTS
@@ -448,17 +453,32 @@
     sums[negs:] = most[...]
 
 
-def total_kernel(*refs):
-    sums, (total, most) = refs[:-2], refs[-2:]
-    negs = total.shape[0]
-    total[...] = functools.reduce(jnp.add, [part[0:negs] for part in sums])
+def total_kernel(meta, even, odd, negatives, w_out, *refs):
+    sums, (d_w_out, most, kit, sem) = refs[:-4], refs[-4:]
+    width = w_out.shape[0]
+    copy = pltpu.make_async_copy(w_out, kit.at[pl.ds(0, width)], sem)
+    copy.start()
+    pool, rows = even.shape
+    kit[width : width + pool, 0:rows] = even[...]
+    kit[width : width + pool, rows : 2 * rows] = odd[...]
+    negs, groups = negatives.shape[0], len(sums)
     most[...] = functools.reduce(jnp.maximum, [part[negs:] for part in sums])
-
-
-def finish_kernel(sizes, meta, even, odd, w_out, negatives, total, *refs):
-    n, rows, groups = sizes
-    blocks, (d_home, layer_out, d_w_out) = refs[:n], refs[n:]
-    width = w_out.shape[0]
+    rest = functools.reduce(jnp.add, [part[0:negs] for part in sums])
+    columns = width // groups
+    neg = negatives[:, pl.ds(pl.multiple_of(meta[1] * columns, columns), columns)]
+    grad = jnp.zeros((rest.shape[1], columns), F32)
+    for _ in range(3):
+        piece = rest.astype(BF16)
+        grad = grad + dot(piece, neg, ((0,), (0,)))
+        rest = rest - piece.astype(F32)
+    d_w_out[...] = grad
+    copy.wait()
+
+
+def finish_kernel(sizes, meta, kit, *refs):
+    n, rows = sizes
+    blocks, (d_home, layer_out) = refs[:n], refs[n:]
+    width = kit.shape[1]
     head_dim = width // n
     quarter = rows // PARTS
     layer = jnp.zeros((rows, width), F32)
@@ -467,23 +487,15 @@
         for x in (d, d + 1):
             head = pl.multiple_of((meta[0] ^ x) * head_dim, head_dim)
             block = blocks[x]
-            part = dot((odd if x % 2 else even)[...], block[2 * quarter :], ((0,), (0,))).astype(BF16)
+            pick = kit[width : width + block.shape[0] - 2 * quarter, rows * (x % 2) : rows * (x % 2 + 1)]
+            part = dot(pick, block[2 * quarter :], ((0,), (0,))).astype(BF16)
             for i in range(PARTS):
                 d_home[:, pl.ds(i * width + head, head_dim)] = part[:, i * head_dim : (i + 1) * head_dim]
             lines = block[quarter * (x % 2) : quarter * (x % 2 + 1)]
             mixed.append(jnp.concatenate([lines[:, b * head_dim : (b + 1) * head_dim] for b in range(PARTS)], axis=0))
-            weights.append(w_out[pl.ds(head, head_dim), :])
+            weights.append(kit[pl.ds(head, head_dim), :])
         layer = layer + dot(jnp.concatenate(mixed, axis=1), jnp.concatenate(weights, axis=0))
     layer_out[...] = layer.astype(BF16)
-    columns = width // groups
-    neg = negatives[:, pl.ds(pl.multiple_of(meta[1] * columns, columns), columns)]
-    rest = total[...]
-    grad = jnp.zeros((head_dim, columns), F32)
-    for _ in range(3):
-        piece = rest.astype(BF16)
-        grad = grad + dot(piece, neg, ((0,), (0,)))
-        rest = rest - piece.astype(F32)
-    d_w_out[...] = grad
 
 
 def kernel_call(body, shapes, specs, scratch=(), limit=40):
@@ -505,15 +517,21 @@
     far = [swap(own, "seq", 2 * d) for d, own in enumerate(message) if d > 0]
     made = between()
     blocks = [message[0], swap(message[0], "seq", 1)]
-    for own in far:
-        own, made = lax.optimization_barrier((own, made))
+    for d, own in enumerate(far):
+        if d == len(far) - 1:
+            own, made = lax.optimization_barrier((own, made))
         blocks += [own, swap(own, "seq", 1)]
     return blocks, made
 
 
-def gather_small(block):
-    pair = jnp.stack([block, swap(block, "seq", 1)])
-    return [pair] + [swap(pair, "seq", d) for d in range(2, lax.axis_size("seq"), 2)]
+def gather_small(block, between):
+    n = lax.axis_size("seq")
+    known, distance = block[None], 1
+    while distance < n // 2:
+        known = jnp.concatenate([known, swap(known, "seq", distance)], axis=0)
+        distance *= 2
+    known, made = lax.optimization_barrier((known, between()))
+    return [known, swap(known, "seq", distance)], made
 
 
 def head_plan(qkvu, w_out, head_coef, item_table, neg_ids, send_order, recv_order, tile_len):
@@ -537,39 +555,45 @@
 
     def passes(slots, pool):
         span = -(-slots // 8) * 8
-        orders = gather_small(recv_order)
+        def prep():
+            return kernel_call(
+                prep_kernel,
+                (sds(qkvu.shape, BF16), sds((below, wide), BF16), sds((rows, rows), BF16)),
+                [SMEM] + [ANY] * 4,
+                [
+                    pltpu.VMEM((1, rows), jnp.int32),
+                    pltpu.VMEM((negs, rows), BF16),
+                    pltpu.VMEM((per, 16, width), BF16),
+                    pltpu.VMEM((8, width), F32),
+                    pltpu.SemaphoreType.DMA((3 + per,)),
+                ],
+            )(neg_ids, send_order, head_coef_t, item_table, qkvu)
+
+        orders, prepared = gather_small(recv_order, prep)
         *message, pick = kernel_call(
             functools.partial(pack_kernel, (n, rows, slots)),
             (sds((2 * slots + below, wide), BF16),) * half + (sds((rows, rows), BF16),),
-            [SMEM] + [VMEM] * 4 + [ANY] * 5,
-            [
-                pltpu.VMEM((n, 1, rows), F32),
-                pltpu.VMEM((1, rows), jnp.int32),
-                pltpu.SMEM((per,), jnp.int32),
-                pltpu.VMEM((negs, rows), BF16),
-                pltpu.VMEM((per, 16, width), BF16),
-                pltpu.VMEM((8, width), F32),
-                pltpu.VMEM(qkvu.shape, BF16),
-                pltpu.SemaphoreType.DMA((4 + per,)),
-            ],
-        )(meta, *orders, send_order, neg_ids, head_coef_t, item_table, qkvu)
+            [SMEM] + [VMEM] * 5,
+            [pltpu.VMEM((n, 1, rows), F32)],
+        )(meta, *orders, *prepared)
 
         def index():
             return kernel_call(
                 functools.partial(index_kernel, (n, rows, slots, pool)),
                 (
                     sds((live_cap, n * span), BF16),
-                    sds((live_cap, half * pool), BF16),
+                    sds((half * pool, live_cap), BF16),
                     sds((pool, rows), BF16),
                     sds((pool, rows), BF16),
                     sds((live_cap, live_cap), F32),
                     sds((8, 128), F32),
+                    sds((width, head_dim), BF16),
                 ),
-                [SMEM] + [VMEM] * 5,
-                [pltpu.VMEM((n, 1, rows), F32)],
-            )(meta, *orders, pick)
-
-        received, (pick_in, pick_out, even, odd, live, most) = exchange(message, index)
+                [SMEM] + [VMEM] * 3 + [ANY],
+                [pltpu.VMEM((n, 1, rows), F32), pltpu.VMEM((head_dim, width), BF16), pltpu.SemaphoreType.DMA],
+            )(meta, *orders, pick, w_out)
+
+        received, (pick_in, pick_out, even, odd, live, most, w_cols) = exchange(message, index)
         compact, weights, att, stats, coef_c, d_mixed, negatives = kernel_call(
             functools.partial(forward_kernel, (n, rows, slots, per)),
             (
@@ -581,14 +605,11 @@
                 sds((live_cap, head_dim), F32),
                 sds((negs, width), BF16),
             ),
-            [SMEM, VMEM, VMEM, ANY] + [VMEM] * n,
-            [pltpu.VMEM((n, 8, width), F32), pltpu.VMEM((head_dim, width), BF16), pltpu.SemaphoreType.DMA],
-        )(meta, pick_in, live, w_out, *received)
-        other = swap(stats, "seq", 1)
-        paired = jnp.stack(
-            list(merge_stats([stats[i] for i in range(4)], [other[i] for i in range(4)], head_dim))
-            + [jnp.zeros_like(stats[0])] * 4
-        )
+            [SMEM] + [VMEM] * (3 + n),
+            [pltpu.VMEM((n, 8, width), F32)],
+        )(meta, pick_in, live, w_cols, *received)
+        paired = merge_stats(stats, swap(stats, "seq", 1), head_dim)
+        paired = jnp.stack(list(paired) + [jnp.zeros_like(stats[0])] * 4)
         far = [swap(paired, "seq", d) for d in range(2, n, 2)]
         *back, mixed = kernel_call(
             functools.partial(backward_kernel, (n, rows, pool)),
@@ -600,23 +621,29 @@
         def group_sums():
             sums = kernel_call(sums_kernel, sds((negs + 8, head_dim), F32), [VMEM] * 3)(coef_c, mixed, most)
             sums = [sums] + [swap(sums, "dp", d) for d in range(1, groups)]
-            total, most_of_all = kernel_call(
-                total_kernel, (sds((negs, head_dim), F32), sds((8, 128), F32)), [VMEM] * groups
-            )(*sums)
-            return total, most_of_all[0, 0] > 0.0
-
-        returned, (total, overflow) = exchange(back, group_sums)
-        return overflow, (even, odd, w_out, negatives, total, *returned)
-
-    def finish(*parts):
-        return kernel_call(
-            functools.partial(finish_kernel, (n, rows, groups)),
-            (sds((rows, PARTS * width), BF16), sds((rows, width), BF16), sds((head_dim, width // groups), F32)),
-            [SMEM] + [VMEM] * (5 + n),
+            d_w, most_of_all, kit = kernel_call(
+                total_kernel,
+                (sds((head_dim, width // groups), F32), sds((8, 128), F32), sds((width + -(-pool // 16) * 16, width), BF16)),
+                [SMEM] + [VMEM] * 3 + [ANY] + [VMEM] * groups,
+                [pltpu.SemaphoreType.DMA],
+            )(meta, even, odd, negatives, w_out, *sums)
+            return d_w, kit, most_of_all
+
+        returned, (d_w, kit, most_of_all) = exchange(back, group_sums)
+        return most_of_all[0, 0] > 0.0, (d_w, kit, *returned)
+
+    def finish(d_w, *parts):
+        outs = kernel_call(
+            functools.partial(finish_kernel, (n, rows)),
+            (sds((rows, PARTS * width), BF16), sds((rows, width), BF16)),
+            [SMEM] + [VMEM] * (1 + n),
         )(meta, *parts)
+        return (*outs, d_w)
 
     overflow, parts = passes(SLOTS, POOL)
-    d_home, layer_out, d_w_out = lax.cond(overflow, lambda *_: finish(*passes(rows, 2 * rows)[1]), finish, *parts)
+    d_home, layer_out, d_w_out = lax.cond(
+        overflow, lambda *_: finish(*passes(rows, 2 * rows)[1]), lambda *outs: outs, *finish(*parts)
+    )
     return (layer_out, d_home, d_w_out)
 
 

time: 64.8 us -> 63.4 us (0.978)
  waiting for transfers between devices: 22.2 us -> 20.1 us
  starting transfers between devices: 26.2 us -> 25.2 us
  Pallas kernels: 12.7 us -> 13.4 us
  other arithmetic: 1.4 us -> 2.06 us
    pallas_call x2 -> x3, Pallas kernels: 3.55 us -> 6.16 us  [the longest x1 2.43 us: finish(): kernel_call(functools.partial(finish_kernel, (n, rows)), (sds((rows, PART...]
    ppermute x25 -> x24, waiting for transfers between devices: 22.2 us -> 20.1 us  [swap(): lax.ppermute(block, axis, [(i, i ^ distance) for i in range(lax.axis_size...]
    pallas_call x1, Pallas kernels: 2.69 us -> 1.32 us  [passes(): kernel_call(functools.partial(pack_kernel, (n, rows, slots)), (sds((2 * s...]
    concatenate x0 -> x2, other arithmetic: none -> 1.32 us  [gather_small(): known = jnp.concatenate([known, swap(known, 'seq', distance)], axis=0)]
    ppermute x25 -> x24, starting transfers between devices: 26.2 us -> 25.2 us  [swap(): lax.ppermute(block, axis, [(i, i ^ distance) for i in range(lax.axis_size...]
    another operation x1 -> x0, other arithmetic: 0.66 us -> none  [gather_small(): pair = jnp.stack([block, swap(block, 'seq', 1)])]
  transfers between devices with their start and end apart: 25 -> 24, of which waited for: 17 -> 14; matrix products, arithmetic and copies ran while one was open for 2% -> 2% of each run, Pallas kernels for 4% -> 9%
where the time goes in v5:
time: 63.4 us; the launch traced here: 63.2 us
  starting transfers between devices  25.2 us (40%)
  waiting for transfers between devices  20.1 us (32%)
  Pallas kernels  13.4 us (21%)
  other arithmetic  2.06 us (3%)
  between operations  1.66 us (3%)
    ppermute x24, starting transfers between devices, swap(): lax.ppermute(block, axis, [(i, i ^ distance) for i in range(lax.axis_size...  25.2 us
    ppermute x24, waiting for transfers between devices, swap(): lax.ppermute(block, axis, [(i, i ^ distance) for i in range(lax.axis_size...  20.1 us
    pallas_call x1, Pallas kernels, finish(): kernel_call(functools.partial(finish_kernel, (n, rows)), (sds((rows, PART...  2.43 us
    pallas_call x1, Pallas kernels, prep(): kernel_call(prep_kernel, (sds(qkvu.shape, BF16), sds((below, wide), BF16)...  2.15 us
    pallas_call x1, Pallas kernels, index(): kernel_call(functools.partial(index_kernel, (n, rows, slots, pool)), (sds...  2.07 us
    pallas_call x1, Pallas kernels, passes(): kernel_call(functools.partial(backward_kernel, (n, rows, pool)), (sds((2...  1.95 us
    pallas_call x1, Pallas kernels, passes(): kernel_call(functools.partial(forward_kernel, (n, rows, slots, per)), (sd...  1.78 us
    pallas_call x1, Pallas kernels, group_sums(): kernel_call(total_kernel, (sds((head_dim, width // groups), F32), sds((8,...  1.59 us
  transfers between devices with their start and end apart: 24, of which 14 were waited for; matrix products, arithmetic and copies ran while one was open for 2% of the time, Pallas kernels for 9%

profile of v5, /device:TPU:0, one launch (start us, length us, event | category | flops | bytes accessed | tf_op | source)
XLA Modules:
  0.0 63.2 jit_solution(14447532736310847922)
XLA Ops:
  2.8 2.9 %collective-permute-start.25 = (s32[2,1,128]{2,1,0:T(1,128)S(1)}, s32[2,1,128]{2,1,0:T(1,128)S(1)}, u32[]{:S(2)}, u32[]{:S(2)}) collective-permute-start(s32[2,1,128]{2,1,0:T(1,128)S(1)} %pad_add_fusion.3), channel_id=1, source_target_pairs={{0,2},{1,3},{2,0},{3,1},{4,6},{5,7},{6,4},{7,5},{8,10},{9,11},{10,... | collective-permute-start | bytes 3080 | tf_op jit(solution)/shard_map/ppermute | solution.py:513
  5.6 2.1 %shard_map.103 = (bf16[128,4096]{1,0:T(8,128)(2,1)S(1)}, bf16[16,512]{1,0:T(8,128)(2,1)S(1)}, bf16[128,128]{1,0:T(8,128)(2,1)S(1)}) custom-call(s32[4]{0:T(128)} %ids.1, s32[1,128]{1,0:T(1,128)} %send.1, bf16[32,128]{1,0:T(8,128)(2,1)} %bitcast.7, bf16[512,1024]{1,0:T(8,128)(2,1)} %table.1, bf16[128,4096]{1,0:T(8,128)(2,1)} %qkvu.1), custom_call_target="tpu_custom_call" | custom-call | tf_op jit(solution)/shard_map/pallas_call | solution.py:559
  8.5 2.6 %collective-permute-start.26 = (s32[4,1,128]{2,1,0:T(1,128)S(1)}, s32[4,1,128]{2,1,0:T(1,128)S(1)}, u32[]{:S(2)}, u32[]{:S(2)}) collective-permute-start(s32[4,1,128]{2,1,0:T(1,128)S(1)} %pad_add_fusion.2.b0), channel_id=1, source_target_pairs={{0,4},{1,5},{2,6},{3,7},{4,0},{5,1},{6,2},{7,3},{8,12},{9,13},{10,... | collective-permute-start | bytes 6152 | tf_op jit(solution)/shard_map/ppermute | solution.py:513
  11.8 1.2 %collective-permute-done.26.b1 = s32[4,1,128]{2,1,0:T(1,128)S(1)} collective-permute-done((s32[4,1,128]{2,1,0:T(1,128)S(1)}, s32[4,1,128]{2,1,0:T(1,128)S(1)}, u32[]{:S(2)}, u32[]{:S(2)}) %collective-permute-start.26) | collective-permute-done | bytes 2080 | tf_op jit(solution)/shard_map/ppermute | solution.py:513
  12.9 1.3 %shard_map.104 = (bf16[136,512]{1,0:T(8,128)(2,1)S(1)}, bf16[136,512]{1,0:T(8,128)(2,1)S(1)}, bf16[136,512]{1,0:T(8,128)(2,1)S(1)}, bf16[136,512]{1,0:T(8,128)(2,1)S(1)}, bf16[128,128]{1,0:T(8,128)(2,1)S(1)}) custom-call(s32[10]{0:T(128)S(1)} %pad_add_fusion.4.meta, s32[4,1,128]{2,1,0:T(1,128)S(1)} %pad_add_fusion.2.b0, ...), custom_call_target="tpu_custom_call" | custom-call | tf_op jit(solution)/shard_map/pallas_call | solution.py:573
  14.3 3.5 %collective-permute-start.27 = (bf16[136,512]{1,0:T(8,128)(2,1)S(1)}, bf16[136,512]{1,0:T(8,128)(2,1)S(1)}, u32[]{:S(2)}, u32[]{:S(2)}) collective-permute-start(bf16[136,512]{1,0:T(8,128)(2,1)S(1)} %get-tuple-element.137), channel_id=1, source_target_pairs={{0,6},{1,7},{2,4},{3,5},{4,2},{5,3},{6,0},{7,1},{8,14},{9,15},{10,... | collective-permute-start | bytes 417800 | tf_op jit(solution)/shard_map/ppermute | solution.py:513
  18.7 2.1 %shard_map.105 = (bf16[384,512]{1,0:T(8,128)(2,1)S(1)}, bf16[416,384]{1,0:T(8,128)(2,1)S(1)}, bf16[104,128]{1,0:T(8,128)(2,1)S(1)}, bf16[104,128]{1,0:T(8,128)(2...) custom-call(s32[10]{0:T(128)S(1)} %pad_add_fusion.4.meta, ...), custom_call_target="tpu_custom_call" | custom-call | tf_op jit(solution)/shard_map/pallas_call | solution.py:581
  20.8 2.0 %collective-permute-done.27.refs_6_ = bf16[136,512]{1,0:T(8,128)(2,1)S(1)} collective-permute-done((bf16[136,512]{1,0:T(8,128)(2,1)S(1)}, bf16[136,512]{1,0:T(8,128)(2,1)S(1)}, u32[]{:S(2)}, u32[]{:S(2)}) %collective-permute-start.27) | collective-permute-done | bytes 139296 | tf_op jit(solution)/shard_map/ppermute | solution.py:513
  22.8 1.4 %collective-permute-done.29.refs_2_ = bf16[136,512]{1,0:T(8,128)(2,1)S(1)} collective-permute-done((bf16[136,512]{1,0:T(8,128)(2,1)S(1)}, bf16[136,512]{1,0:T(8,128)(2,1)S(1)}, u32[]{:S(2)}, u32[]{:S(2)}) %collective-permute-start.29) | collective-permute-done | bytes 139296 | tf_op jit(solution)/shard_map/ppermute | solution.py:513
  24.2 4.3 %collective-permute-done.31.refs_4_ = bf16[136,512]{1,0:T(8,128)(2,1)S(1)} collective-permute-done((bf16[136,512]{1,0:T(8,128)(2,1)S(1)}, bf16[136,512]{1,0:T(8,128)(2,1)S(1)}, u32[]{:S(2)}, u32[]{:S(2)}) %collective-permute-start.31) | collective-permute-done | bytes 139296 | tf_op jit(solution)/shard_map/ppermute | solution.py:513
  30.1 1.8 %shard_map.106 = (bf16[384,512]{1,0:T(8,128)(2,1)S(1)}, bf16[384,384]{1,0:T(8,128)(2,1)S(1)}, f32[384,128]{1,0:T(8,128)S(1)}, f32[8,384]{1,0:T(8,128)S(1)}, bf16...) custom-call(s32[10]{0:T(128)S(1)} %pad_add_fusion.4.meta, ...), custom_call_target="tpu_custom_call" | custom-call | tf_op jit(solution)/shard_map/pallas_call | solution.py:597
  33.1 2.7 %collective-permute-start.37 = (f32[8,384]{1,0:T(8,128)S(1)}, f32[8,384]{1,0:T(8,128)S(1)}, u32[]{:S(2)}, u32[]{:S(2)}) collective-permute-start(f32[8,384]{1,0:T(8,128)S(1)} %stack.10.st0), channel_id=1, source_target_pairs={{0,6},{1,7},{2,4},{3,5},{4,2},{5,3},{6,0},{7,1},{8,14},{9,15},{10,... | collective-permute-start | bytes 36872 | tf_op jit(solution)/shard_map/ppermute | solution.py:513
  35.9 1.7 %collective-permute-start.35 = (f32[8,384]{1,0:T(8,128)S(1)}, f32[8,384]{1,0:T(8,128)S(1)}, u32[]{:S(2)}, u32[]{:S(2)}) collective-permute-start(f32[8,384]{1,0:T(8,128)S(1)} %stack.10.st0), channel_id=1, source_target_pairs={{0,2},{1,3},{2,0},{3,1},{4,6},{5,7},{6,4},{7,5},{8,10},{9,11},{10,... | collective-permute-start | bytes 36872 | tf_op jit(solution)/shard_map/ppermute | solution.py:513
  38.7 1.7 %collective-permute-done.36.st2 = f32[8,384]{1,0:T(8,128)S(1)} collective-permute-done((f32[8,384]{1,0:T(8,128)S(1)}, f32[8,384]{1,0:T(8,128)S(1)}, u32[]{:S(2)}, u32[]{:S(2)}) %collective-permute-start.36) | collective-permute-done | bytes 12320 | tf_op jit(solution)/shard_map/ppermute | solution.py:513
  40.5 1.9 %shard_map.107 = (bf16[168,512]{1,0:T(8,128)(2,1)S(1)}, bf16[168,512]{1,0:T(8,128)(2,1)S(1)}, bf16[168,512]{1,0:T(8,128)(2,1)S(1)}, bf16[168,512]{1,0:T(8,128)(2,1)S(1)}, bf16[384,128]{1,0:T(8,128)(2,1)S(1)}) custom-call(s32[10]{0:T(128)S(1)} %pad_add_fusion.4.meta, bf16[384,512]{1,0:T(8,128)(2,1)S(1)} %get-tuple-element.153.compact, ...), custom_call_target="tpu_custom_call" | custom-call | tf_op jit(solution)/shard_map/pallas_call | solution.py:614
  42.4 1.5 %collective-permute-start.38 = (bf16[168,512]{1,0:T(8,128)(2,1)S(1)}, bf16[168,512]{1,0:T(8,128)(2,1)S(1)}, u32[]{:S(2)}, u32[]{:S(2)}) collective-permute-start(bf16[168,512]{1,0:T(8,128)(2,1)S(1)} %get-tuple-element.159), channel_id=1, source_target_pairs={{0,6},{1,7},{2,4},{3,5},{4,2},{5,3},{6,0},{7,1},{8,14},{9,15},{10,... | collective-permute-start | bytes 516104 | tf_op jit(solution)/shard_map/ppermute | solution.py:513
  45.1 1.8 %collective-permute-start.45 = (bf16[168,512]{1,0:T(8,128)(2,1)S(1)}, bf16[168,512]{1,0:T(8,128)(2,1)S(1)}, u32[]{:S(2)}, u32[]{:S(2)}) collective-permute-start(bf16[168,512]{1,0:T(8,128)(2,1)S(1)} %get-tuple-element.173), channel_id=1, source_target_pairs={{0,4},{1,5},{2,6},{3,7},{4,0},{5,1},{6,2},{7,3},{8,12},{9,13},{10,... | collective-permute-start | bytes 516104 | tf_op jit(solution)/shard_map/ppermute | solution.py:513
  47.0 2.4 %collective-permute-start.41 = (f32[40,128]{1,0:T(8,128)S(1)}, f32[40,128]{1,0:T(8,128)S(1)}, u32[]{:S(2)}, u32[]{:S(2)}) collective-permute-start(f32[40,128]{1,0:T(8,128)S(1)} %shard_map.108.refs_0_), channel_id=1, source_target_pairs={{0,24},{8,16},{16,8},{24,0},{1,25},{9,17},{17,9},{25,1},{2,26},{10... | collective-permute-start | bytes 61448 | tf_op jit(solution)/shard_map/ppermute | solution.py:513
  49.9 1.7 %collective-permute-done.41.refs_3_ = f32[40,128]{1,0:T(8,128)S(1)} collective-permute-done((f32[40,128]{1,0:T(8,128)S(1)}, f32[40,128]{1,0:T(8,128)S(1)}, u32[]{:S(2)}, u32[]{:S(2)}) %collective-permute-start.41) | collective-permute-done | bytes 20512 | tf_op jit(solution)/shard_map/ppermute | solution.py:513
  51.7 1.5 %collective-permute-start.39 = (f32[40,128]{1,0:T(8,128)S(1)}, f32[40,128]{1,0:T(8,128)S(1)}, u32[]{:S(2)}, u32[]{:S(2)}) collective-permute-start(f32[40,128]{1,0:T(8,128)S(1)} %shard_map.108.refs_0_), channel_id=1, source_target_pairs={{0,8},{8,0},{16,24},{24,16},{1,9},{9,1},{17,25},{25,17},{2,10},{10... | collective-permute-start | bytes 61448 | tf_op jit(solution)/shard_map/ppermute | solution.py:513
  53.2 2.2 %collective-permute-done.39.refs_1_ = f32[40,128]{1,0:T(8,128)S(1)} collective-permute-done((f32[40,128]{1,0:T(8,128)S(1)}, f32[40,128]{1,0:T(8,128)S(1)}, u32[]{:S(2)}, u32[]{:S(2)}) %collective-permute-start.39) | collective-permute-done | bytes 20512 | tf_op jit(solution)/shard_map/ppermute | solution.py:513
  55.5 1.6 %shard_map.109 = (f32[128,256]{1,0:T(8,128)}, f32[8,128]{1,0:T(8,128)S(1)}, bf16[1136,1024]{1,0:T(8,128)(2,1)S(1)}) custom-call(s32[10]{0:T(128)S(1)} %pad_add_fusion.4.meta, bf16[104,128]{1,0:T(8,128)(2,1)S(1)} %get-tuple-element.160.even, bf16[104,128]{1,0:T(8,128)(2,1)S(1)} %get-tuple-element.161.odd, bf16[32,1024]{1,0:T(8,128)(2,1)S(1)} %get-tuple-element.162.negatives, ...), custom_call_target="tpu_custom_call" | custom-call | tf_op jit(solution)/shard_map/pallas_call | solution.py:624
  57.2 1.5 %collective-permute-done.45.refs_4_ = bf16[168,512]{1,0:T(8,128)(2,1)S(1)} collective-permute-done((bf16[168,512]{1,0:T(8,128)(2,1)S(1)}, bf16[168,512]{1,0:T(8,128)(2,1)S(1)}, u32[]{:S(2)}, u32[]{:S(2)}) %collective-permute-start.45) | collective-permute-done | bytes 172064 | tf_op jit(solution)/shard_map/ppermute | solution.py:513
  60.4 2.4 %shard_map.110 = (bf16[128,4096]{1,0:T(8,128)(2,1)}, bf16[128,1024]{1,0:T(8,128)(2,1)}) custom-call(s32[10]{0:T(128)S(1)} %pad_add_fusion.4.meta, bf16[1136,1024]{1,0:T(8,128)(2,1)S(1)} %get-tuple-element.170.kit, bf16[168,512]{1,0:T(8,128)(2,1)S(1)} %get-tuple-element.171.refs_0_, bf16[168,512]{1,0:T(8,128)(2,1)S(1)} %collective-permute-done.42.refs_1_, ...), custom_call_target="tpu_custom_call" | custom-call | tf_op jit(solution)/shard_map/pallas_call | solution.py:636
  (56 shorter events, 11.6 us)
Async XLA Ops:
  0.6 1.5 %collective-permute-start.24 = (s32[1,1,128]{2,1,0:T(1,128)}, s32[1,1,128]{2,1,0:T(1,128)S(1)}, u32[]{:S(2)}, u32[]{:S(2)}) collective-permute-start(s32[1,1,128]{2,1,0:T(1,128)} %bitcast.9), channel_id=1, source_target_pairs={{0,1},{1,0},{2,3},{3,2},{4,5},{5,4},{6,7},{7,6},{8,9},{9,8},{10,11... | collective-permute-start | bytes 1544 | tf_op jit(solution)/shard_map/ppermute | solution.py:513
  2.8 5.0 %collective-permute-start.25 = (s32[2,1,128]{2,1,0:T(1,128)S(1)}, s32[2,1,128]{2,1,0:T(1,128)S(1)}, u32[]{:S(2)}, u32[]{:S(2)}) collective-permute-start(s32[2,1,128]{2,1,0:T(1,128)S(1)} %pad_add_fusion.3), channel_id=1, source_target_pairs={{0,2},{1,3},{2,0},{3,1},{4,6},{5,7},{6,4},{7,5},{8,10},{9,11},{10,... | collective-permute-start | bytes 3080 | tf_op jit(solution)/shard_map/ppermute | solution.py:513
  8.5 4.5 %collective-permute-start.26 = (s32[4,1,128]{2,1,0:T(1,128)S(1)}, s32[4,1,128]{2,1,0:T(1,128)S(1)}, u32[]{:S(2)}, u32[]{:S(2)}) collective-permute-start(s32[4,1,128]{2,1,0:T(1,128)S(1)} %pad_add_fusion.2.b0), channel_id=1, source_target_pairs={{0,4},{1,5},{2,6},{3,7},{4,0},{5,1},{6,2},{7,3},{8,12},{9,13},{10,... | collective-permute-start | bytes 6152 | tf_op jit(solution)/shard_map/ppermute | solution.py:513
  14.3 8.6 %collective-permute-start.27 = (bf16[136,512]{1,0:T(8,128)(2,1)S(1)}, bf16[136,512]{1,0:T(8,128)(2,1)S(1)}, u32[]{:S(2)}, u32[]{:S(2)}) collective-permute-start(bf16[136,512]{1,0:T(8,128)(2,1)S(1)} %get-tuple-element.137), channel_id=1, source_target_pairs={{0,6},{1,7},{2,4},{3,5},{4,2},{5,3},{6,0},{7,1},{8,14},{9,15},{10,... | collective-permute-start | bytes 417800 | tf_op jit(solution)/shard_map/ppermute | solution.py:513
  17.8 6.5 %collective-permute-start.29 = (bf16[136,512]{1,0:T(8,128)(2,1)S(1)}, bf16[136,512]{1,0:T(8,128)(2,1)S(1)}, u32[]{:S(2)}, u32[]{:S(2)}) collective-permute-start(bf16[136,512]{1,0:T(8,128)(2,1)S(1)} %get-tuple-element.150), channel_id=1, source_target_pairs={{0,2},{1,3},{2,0},{3,1},{4,6},{5,7},{6,4},{7,5},{8,10},{9,11},{10,... | collective-permute-start | bytes 417800 | tf_op jit(solution)/shard_map/ppermute | solution.py:513
  17.8 10.7 %collective-permute-start.31 = (bf16[136,512]{1,0:T(8,128)(2,1)S(1)}, bf16[136,512]{1,0:T(8,128)(2,1)S(1)}, u32[]{:S(2)}, u32[]{:S(2)}) collective-permute-start(bf16[136,512]{1,0:T(8,128)(2,1)S(1)} %get-tuple-element.151), channel_id=1, source_target_pairs={{0,4},{1,5},{2,6},{3,7},{4,0},{5,1},{6,2},{7,3},{8,12},{9,13},{10,... | collective-permute-start | bytes 417800 | tf_op jit(solution)/shard_map/ppermute | solution.py:513
  18.7 10.3 %collective-permute-start.28 = (bf16[136,512]{1,0:T(8,128)(2,1)S(1)}, bf16[136,512]{1,0:T(8,128)(2,1)S(1)}, u32[]{:S(2)}, u32[]{:S(2)}) collective-permute-start(bf16[136,512]{1,0:T(8,128)(2,1)S(1)} %get-tuple-element.149.refs_0_), channel_id=1, source_target_pairs={{0,1},{1,0},{2,3},{3,2},{4,5},{5,4},{6,7},{7,6},{8,9},{9,8},{10,11... | collective-permute-start | bytes 417800 | tf_op jit(solution)/shard_map/ppermute | solution.py:513
  24.2 4.8 %collective-permute-start.30 = (bf16[136,512]{1,0:T(8,128)(2,1)S(1)}, bf16[136,512]{1,0:T(8,128)(2,1)S(1)}, u32[]{:S(2)}, u32[]{:S(2)}) collective-permute-start(bf16[136,512]{1,0:T(8,128)(2,1)S(1)} %collective-permute-done.29.refs_2_), channel_id=1, source_target_pairs={{0,1},{1,0},{2,3},{3,2},{4,5},{5,4},{6,7},{7,6},{8,9},{9,8},{10,11... | collective-permute-start | bytes 417800 | tf_op jit(solution)/shard_map/ppermute | solution.py:513
  28.5 1.4 %collective-permute-start.32 = (bf16[136,512]{1,0:T(8,128)(2,1)S(1)}, bf16[136,512]{1,0:T(8,128)(2,1)S(1)}, u32[]{:S(2)}, u32[]{:S(2)}) collective-permute-start(bf16[136,512]{1,0:T(8,128)(2,1)S(1)} %collective-permute-done.31.refs_4_), channel_id=1, source_target_pairs={{0,1},{1,0},{2,3},{3,2},{4,5},{5,4},{6,7},{7,6},{8,9},{9,8},{10,11... | collective-permute-start | bytes 417800 | tf_op jit(solution)/shard_map/ppermute | solution.py:513
  28.5 1.6 %collective-permute-start.33 = (bf16[136,512]{1,0:T(8,128)(2,1)S(1)}, bf16[136,512]{1,0:T(8,128)(2,1)S(1)}, u32[]{:S(2)}, u32[]{:S(2)}) collective-permute-start(bf16[136,512]{1,0:T(8,128)(2,1)S(1)} %collective-permute-done.27.refs_6_), channel_id=1, source_target_pairs={{0,1},{1,0},{2,3},{3,2},{4,5},{5,4},{6,7},{7,6},{8,9},{9,8},{10,11... | collective-permute-start | bytes 417800 | tf_op jit(solution)/shard_map/ppermute | solution.py:513
  31.9 1.2 %collective-permute-start.34 = (f32[8,384]{1,0:T(8,128)S(1)}, f32[8,384]{1,0:T(8,128)S(1)}, u32[]{:S(2)}, u32[]{:S(2)}) collective-permute-start(f32[8,384]{1,0:T(8,128)S(1)} %get-tuple-element.157), channel_id=1, source_target_pairs={{0,1},{1,0},{2,3},{3,2},{4,5},{5,4},{6,7},{7,6},{8,9},{9,8},{10,11... | collective-permute-start | bytes 36872 | tf_op jit(solution)/shard_map/ppermute | solution.py:513
  33.1 5.6 %collective-permute-start.37 = (f32[8,384]{1,0:T(8,128)S(1)}, f32[8,384]{1,0:T(8,128)S(1)}, u32[]{:S(2)}, u32[]{:S(2)}) collective-permute-start(f32[8,384]{1,0:T(8,128)S(1)} %stack.10.st0), channel_id=1, source_target_pairs={{0,6},{1,7},{2,4},{3,5},{4,2},{5,3},{6,0},{7,1},{8,14},{9,15},{10,... | collective-permute-start | bytes 36872 | tf_op jit(solution)/shard_map/ppermute | solution.py:513
  35.9 4.6 %collective-permute-start.36 = (f32[8,384]{1,0:T(8,128)S(1)}, f32[8,384]{1,0:T(8,128)S(1)}, u32[]{:S(2)}, u32[]{:S(2)}) collective-permute-start(f32[8,384]{1,0:T(8,128)S(1)} %stack.10.st0), channel_id=1, source_target_pairs={{0,4},{1,5},{2,6},{3,7},{4,0},{5,1},{6,2},{7,3},{8,12},{9,13},{10,... | collective-permute-start | bytes 36872 | tf_op jit(solution)/shard_map/ppermute | solution.py:513
  35.9 4.6 %collective-permute-start.35 = (f32[8,384]{1,0:T(8,128)S(1)}, f32[8,384]{1,0:T(8,128)S(1)}, u32[]{:S(2)}, u32[]{:S(2)}) collective-permute-start(f32[8,384]{1,0:T(8,128)S(1)} %stack.10.st0), channel_id=1, source_target_pairs={{0,2},{1,3},{2,0},{3,1},{4,6},{5,7},{6,4},{7,5},{8,10},{9,11},{10,... | collective-permute-start | bytes 36872 | tf_op jit(solution)/shard_map/ppermute | solution.py:513
  42.4 14.7 %collective-permute-start.38 = (bf16[168,512]{1,0:T(8,128)(2,1)S(1)}, bf16[168,512]{1,0:T(8,128)(2,1)S(1)}, u32[]{:S(2)}, u32[]{:S(2)}) collective-permute-start(bf16[168,512]{1,0:T(8,128)(2,1)S(1)} %get-tuple-element.159), channel_id=1, source_target_pairs={{0,6},{1,7},{2,4},{3,5},{4,2},{5,3},{6,0},{7,1},{8,14},{9,15},{10,... | collective-permute-start | bytes 516104 | tf_op jit(solution)/shard_map/ppermute | solution.py:513
  43.9 13.2 %collective-permute-start.43 = (bf16[168,512]{1,0:T(8,128)(2,1)S(1)}, bf16[168,512]{1,0:T(8,128)(2,1)S(1)}, u32[]{:S(2)}, u32[]{:S(2)}) collective-permute-start(bf16[168,512]{1,0:T(8,128)(2,1)S(1)} %get-tuple-element.172), channel_id=1, source_target_pairs={{0,2},{1,3},{2,0},{3,1},{4,6},{5,7},{6,4},{7,5},{8,10},{9,11},{10,... | collective-permute-start | bytes 516104 | tf_op jit(solution)/shard_map/ppermute | solution.py:513
  45.1 13.6 %collective-permute-start.45 = (bf16[168,512]{1,0:T(8,128)(2,1)S(1)}, bf16[168,512]{1,0:T(8,128)(2,1)S(1)}, u32[]{:S(2)}, u32[]{:S(2)}) collective-permute-start(bf16[168,512]{1,0:T(8,128)(2,1)S(1)} %get-tuple-element.173), channel_id=1, source_target_pairs={{0,4},{1,5},{2,6},{3,7},{4,0},{5,1},{6,2},{7,3},{8,12},{9,13},{10,... | collective-permute-start | bytes 516104 | tf_op jit(solution)/shard_map/ppermute | solution.py:513
  47.0 4.7 %collective-permute-start.41 = (f32[40,128]{1,0:T(8,128)S(1)}, f32[40,128]{1,0:T(8,128)S(1)}, u32[]{:S(2)}, u32[]{:S(2)}) collective-permute-start(f32[40,128]{1,0:T(8,128)S(1)} %shard_map.108.refs_0_), channel_id=1, source_target_pairs={{0,24},{8,16},{16,8},{24,0},{1,25},{9,17},{17,9},{25,1},{2,26},{10... | collective-permute-start | bytes 61448 | tf_op jit(solution)/shard_map/ppermute | solution.py:513
  49.4 3.8 %collective-permute-start.40 = (f32[40,128]{1,0:T(8,128)S(1)}, f32[40,128]{1,0:T(8,128)S(1)}, u32[]{:S(2)}, u32[]{:S(2)}) collective-permute-start(f32[40,128]{1,0:T(8,128)S(1)} %shard_map.108.refs_0_), channel_id=1, source_target_pairs={{0,16},{8,24},{16,0},{24,8},{1,17},{9,25},{17,1},{25,9},{2,18},{10... | collective-permute-start | bytes 61448 | tf_op jit(solution)/shard_map/ppermute | solution.py:513
  51.7 3.8 %collective-permute-start.39 = (f32[40,128]{1,0:T(8,128)S(1)}, f32[40,128]{1,0:T(8,128)S(1)}, u32[]{:S(2)}, u32[]{:S(2)}) collective-permute-start(f32[40,128]{1,0:T(8,128)S(1)} %shard_map.108.refs_0_), channel_id=1, source_target_pairs={{0,8},{8,0},{16,24},{24,16},{1,9},{9,1},{17,25},{25,17},{2,10},{10... | collective-permute-start | bytes 61448 | tf_op jit(solution)/shard_map/ppermute | solution.py:513
  53.2 7.1 %collective-permute-start.42 = (bf16[168,512]{1,0:T(8,128)(2,1)S(1)}, bf16[168,512]{1,0:T(8,128)(2,1)S(1)}, u32[]{:S(2)}, u32[]{:S(2)}) collective-permute-start(bf16[168,512]{1,0:T(8,128)(2,1)S(1)} %get-tuple-element.171.refs_0_), channel_id=1, source_target_pairs={{0,1},{1,0},{2,3},{3,2},{4,5},{5,4},{6,7},{7,6},{8,9},{9,8},{10,11... | collective-permute-start | bytes 516104 | tf_op jit(solution)/shard_map/ppermute | solution.py:513
  57.2 3.2 %collective-permute-start.44 = (bf16[168,512]{1,0:T(8,128)(2,1)S(1)}, bf16[168,512]{1,0:T(8,128)(2,1)S(1)}, u32[]{:S(2)}, u32[]{:S(2)}) collective-permute-start(bf16[168,512]{1,0:T(8,128)(2,1)S(1)} %collective-permute-done.43.refs_2_), channel_id=1, source_target_pairs={{0,1},{1,0},{2,3},{3,2},{4,5},{5,4},{6,7},{7,6},{8,9},{9,8},{10,11... | collective-permute-start | bytes 516104 | tf_op jit(solution)/shard_map/ppermute | solution.py:513
  58.7 1.7 %collective-permute-start.46 = (bf16[168,512]{1,0:T(8,128)(2,1)S(1)}, bf16[168,512]{1,0:T(8,128)(2,1)S(1)}, u32[]{:S(2)}, u32[]{:S(2)}) collective-permute-start(bf16[168,512]{1,0:T(8,128)(2,1)S(1)} %collective-permute-done.45.refs_4_), channel_id=1, source_target_pairs={{0,1},{1,0},{2,3},{3,2},{4,5},{5,4},{6,7},{7,6},{8,9},{9,8},{10,11... | collective-permute-start | bytes 516104 | tf_op jit(solution)/shard_map/ppermute | solution.py:513
  58.7 1.7 %collective-permute-start.47 = (bf16[168,512]{1,0:T(8,128)(2,1)S(1)}, bf16[168,512]{1,0:T(8,128)(2,1)S(1)}, u32[]{:S(2)}, u32[]{:S(2)}) collective-permute-start(bf16[168,512]{1,0:T(8,128)(2,1)S(1)} %collective-permute-done.38.refs_6_), channel_id=1, source_target_pairs={{0,1},{1,0},{2,3},{3,2},{4,5},{5,4},{6,7},{7,6},{8,9},{9,8},{10,11... | collective-permute-start | bytes 516104 | tf_op jit(solution)/shard_map/ppermute | solution.py:513
  (8 other events, 70.0 us)

commit v6 on v5

--- a/solution.py
+++ b/solution.py
@@ -195,7 +195,7 @@
     n, _, rows = order_ref.shape
     cell = rows // n
     for b in range(n):
-        order_ref[meta[0] ^ b] = blocks[b // (n // 2)][b % (n // 2)].astype(F32)
+        order_ref[meta[0] ^ b] = blocks[b // (n // 2)][b % (n // 2) : b % (n // 2) + 1].astype(F32)
     starts = starts_of(meta, n)
     pos = iota((cell, rows), 1)
     filled = [jnp.broadcast_to(order_ref[t], (cell, rows)) for t in range(n)]
@@ -524,11 +524,21 @@
     return blocks, made
 
 
+def load_kernel(block, out):
+    out[...] = block[...]
+
+
+def join_kernel(first, second, out):
+    out[0 : first.shape[0]] = first[...]
+    out[first.shape[0] :] = second[...]
+
+
 def gather_small(block, between):
     n = lax.axis_size("seq")
-    known, distance = block[None], 1
+    known, distance = kernel_call(load_kernel, jax.ShapeDtypeStruct(block.shape, block.dtype), [VMEM])(block), 1
     while distance < n // 2:
-        known = jnp.concatenate([known, swap(known, "seq", distance)], axis=0)
+        shape = jax.ShapeDtypeStruct((2 * known.shape[0], known.shape[1]), known.dtype)
+        known = kernel_call(join_kernel, shape, [VMEM] * 2)(known, swap(block if distance == 1 else known, "seq", distance))
         distance *= 2
     known, made = lax.optimization_barrier((known, between()))
     return [known, swap(known, "seq", distance)], made

time: 63.4 us -> 62.2 us (0.981)
  other arithmetic: 2.06 us -> 0.74 us
  waiting for transfers between devices: 20.1 us -> 19.4 us
  Pallas kernels: 13.4 us -> 14.1 us
    concatenate x2 -> x0, other arithmetic: 1.32 us -> none  [gather_small(): known = jnp.concatenate([known, swap(known, 'seq', distance)], axis=0)]
    ppermute x24, waiting for transfers between devices: 20.1 us -> 19.4 us  [swap(): lax.ppermute(block, axis, [(i, i ^ distance) for i in range(lax.axis_size...]
    pallas_call x0 -> x3, Pallas kernels: none -> 0.66 us  [the longest x1 0.66 us: gather_small(): kernel_call(load_kernel, jax.ShapeDtypeStruct(block.shape, block.dtype),...]
  transfers between devices with their start and end apart: 24 -> 24, of which waited for: 14 -> 14; matrix products, arithmetic and copies ran while one was open for 2% -> 2% of each run, Pallas kernels for 9% -> 11%
where the time goes in v6:
time: 62.2 us; the launch traced here: 62 us
  starting transfers between devices  25.3 us (41%)
  waiting for transfers between devices  19.4 us (31%)
  Pallas kernels  14.1 us (23%)
  between operations  1.67 us (3%)
  other arithmetic  0.74 us (1%)
    ppermute x24, starting transfers between devices, swap(): lax.ppermute(block, axis, [(i, i ^ distance) for i in range(lax.axis_size...  25.3 us
    ppermute x24, waiting for transfers between devices, swap(): lax.ppermute(block, axis, [(i, i ^ distance) for i in range(lax.axis_size...  19.4 us
    pallas_call x1, Pallas kernels, finish(): kernel_call(functools.partial(finish_kernel, (n, rows)), (sds((rows, PART...  2.44 us
    pallas_call x1, Pallas kernels, prep(): kernel_call(prep_kernel, (sds(qkvu.shape, BF16), sds((below, wide), BF16)...  2.17 us
    pallas_call x1, Pallas kernels, index(): kernel_call(functools.partial(index_kernel, (n, rows, slots, pool)), (sds...  2.07 us
    pallas_call x1, Pallas kernels, passes(): kernel_call(functools.partial(backward_kernel, (n, rows, pool)), (sds((2...  1.95 us
    pallas_call x1, Pallas kernels, passes(): kernel_call(functools.partial(forward_kernel, (n, rows, slots, per)), (sd...  1.78 us
    pallas_call x1, Pallas kernels, group_sums(): kernel_call(total_kernel, (sds((head_dim, width // groups), F32), sds((8,...  1.59 us
  transfers between devices with their start and end apart: 24, of which 14 were waited for; matrix products, arithmetic and copies ran while one was open for 2% of the time, Pallas kernels for 11%

profile of v6, /device:TPU:0, one launch (start us, length us, event | category | flops | bytes accessed | tf_op | source)
XLA Modules:
  0.0 62.0 jit_solution(3733878317499653103)
XLA Ops:
  2.1 2.9 %collective-permute-start.25 = (s32[2,128]{1,0:T(2,128)S(1)}, s32[2,128]{1,0:T(2,128)S(1)}, u32[]{:S(2)}, u32[]{:S(2)}) collective-permute-start(s32[2,128]{1,0:T(2,128)S(1)} %shard_map.104.first), channel_id=1, source_target_pairs={{0,2},{1,3},{2,0},{3,1},{4,6},{5,7},{6,4},{7,5},{8,10},{9,11},{10,... | collective-permute-start | bytes 3080 | tf_op jit(solution)/shard_map/ppermute | solution.py:513
  5.0 2.2 %shard_map.106 = (bf16[128,4096]{1,0:T(8,128)(2,1)S(1)}, bf16[16,512]{1,0:T(8,128)(2,1)S(1)}, bf16[128,128]{1,0:T(8,128)(2,1)S(1)}) custom-call(s32[4]{0:T(128)} %ids.1, s32[1,128]{1,0:T(1,128)} %send.1, bf16[32,128]{1,0:T(8,128)(2,1)} %bitcast.5, bf16[512,1024]{1,0:T(8,128)(2,1)} %table.1, bf16[128,4096]{1,0:T(8,128)(2,1)} %qkvu.1), custom_call_target="tpu_custom_call" | custom-call | tf_op jit(solution)/shard_map/pallas_call | solution.py:569
  7.2 2.7 %collective-permute-start.26 = (s32[4,128]{1,0:T(4,128)S(1)}, s32[4,128]{1,0:T(4,128)S(1)}, u32[]{:S(2)}, u32[]{:S(2)}) collective-permute-start(s32[4,128]{1,0:T(4,128)S(1)} %shard_map.105.b0), channel_id=1, source_target_pairs={{0,4},{1,5},{2,6},{3,7},{4,0},{5,1},{6,2},{7,3},{8,12},{9,13},{10,... | collective-permute-start | bytes 6152 | tf_op jit(solution)/shard_map/ppermute | solution.py:513
  10.6 1.2 %collective-permute-done.26.b1 = s32[4,128]{1,0:T(4,128)S(1)} collective-permute-done((s32[4,128]{1,0:T(4,128)S(1)}, s32[4,128]{1,0:T(4,128)S(1)}, u32[]{:S(2)}, u32[]{:S(2)}) %collective-permute-start.26) | collective-permute-done | bytes 2080 | tf_op jit(solution)/shard_map/ppermute | solution.py:513
  11.7 1.3 %shard_map.107 = (bf16[136,512]{1,0:T(8,128)(2,1)S(1)}, bf16[136,512]{1,0:T(8,128)(2,1)S(1)}, bf16[136,512]{1,0:T(8,128)(2,1)S(1)}, bf16[136,512]{1,0:T(8,128)(2,1)S(1)}, bf16[128,128]{1,0:T(8,128)(2,1)S(1)}) custom-call(s32[10]{0:T(128)S(1)} %pad_add_fusion.meta, s32[4,128]{1,0:T(4,128)S(1)} %shard_map.105.b0, s32[4,128]{1,0:T(4,128)S(1)} %collective-permute-done.26.b1, ...), custom_call_target="tpu_custom_call" | custom-call | tf_op jit(solution)/shard_map/pallas_call | solution.py:583
  13.1 3.4 %collective-permute-start.27 = (bf16[136,512]{1,0:T(8,128)(2,1)S(1)}, bf16[136,512]{1,0:T(8,128)(2,1)S(1)}, u32[]{:S(2)}, u32[]{:S(2)}) collective-permute-start(bf16[136,512]{1,0:T(8,128)(2,1)S(1)} %get-tuple-element.137), channel_id=1, source_target_pairs={{0,6},{1,7},{2,4},{3,5},{4,2},{5,3},{6,0},{7,1},{8,14},{9,15},{10,... | collective-permute-start | bytes 417800 | tf_op jit(solution)/shard_map/ppermute | solution.py:513
  17.5 2.1 %shard_map.108 = (bf16[384,512]{1,0:T(8,128)(2,1)S(1)}, bf16[416,384]{1,0:T(8,128)(2,1)S(1)}, bf16[104,128]{1,0:T(8,128)(2,1)S(1)}, bf16[104,128]{1,0:T(8,128)(2...) custom-call(s32[10]{0:T(128)S(1)} %pad_add_fusion.meta, ...), custom_call_target="tpu_custom_call" | custom-call | tf_op jit(solution)/shard_map/pallas_call | solution.py:591
  19.6 2.0 %collective-permute-done.27.refs_6_ = bf16[136,512]{1,0:T(8,128)(2,1)S(1)} collective-permute-done((bf16[136,512]{1,0:T(8,128)(2,1)S(1)}, bf16[136,512]{1,0:T(8,128)(2,1)S(1)}, u32[]{:S(2)}, u32[]{:S(2)}) %collective-permute-start.27) | collective-permute-done | bytes 139296 | tf_op jit(solution)/shard_map/ppermute | solution.py:513
  21.6 1.3 %collective-permute-done.29.refs_2_ = bf16[136,512]{1,0:T(8,128)(2,1)S(1)} collective-permute-done((bf16[136,512]{1,0:T(8,128)(2,1)S(1)}, bf16[136,512]{1,0:T(8,128)(2,1)S(1)}, u32[]{:S(2)}, u32[]{:S(2)}) %collective-permute-start.29) | collective-permute-done | bytes 139296 | tf_op jit(solution)/shard_map/ppermute | solution.py:513
  23.0 4.3 %collective-permute-done.31.refs_4_ = bf16[136,512]{1,0:T(8,128)(2,1)S(1)} collective-permute-done((bf16[136,512]{1,0:T(8,128)(2,1)S(1)}, bf16[136,512]{1,0:T(8,128)(2,1)S(1)}, u32[]{:S(2)}, u32[]{:S(2)}) %collective-permute-start.31) | collective-permute-done | bytes 139296 | tf_op jit(solution)/shard_map/ppermute | solution.py:513
  28.8 1.8 %shard_map.109 = (bf16[384,512]{1,0:T(8,128)(2,1)S(1)}, bf16[384,384]{1,0:T(8,128)(2,1)S(1)}, f32[384,128]{1,0:T(8,128)S(1)}, f32[8,384]{1,0:T(8,128)S(1)}, bf16...) custom-call(s32[10]{0:T(128)S(1)} %pad_add_fusion.meta, ...), custom_call_target="tpu_custom_call" | custom-call | tf_op jit(solution)/shard_map/pallas_call | solution.py:607
  31.9 2.7 %collective-permute-start.37 = (f32[8,384]{1,0:T(8,128)S(1)}, f32[8,384]{1,0:T(8,128)S(1)}, u32[]{:S(2)}, u32[]{:S(2)}) collective-permute-start(f32[8,384]{1,0:T(8,128)S(1)} %stack.10.st0), channel_id=1, source_target_pairs={{0,6},{1,7},{2,4},{3,5},{4,2},{5,3},{6,0},{7,1},{8,14},{9,15},{10,... | collective-permute-start | bytes 36872 | tf_op jit(solution)/shard_map/ppermute | solution.py:513
  34.6 1.7 %collective-permute-start.35 = (f32[8,384]{1,0:T(8,128)S(1)}, f32[8,384]{1,0:T(8,128)S(1)}, u32[]{:S(2)}, u32[]{:S(2)}) collective-permute-start(f32[8,384]{1,0:T(8,128)S(1)} %stack.10.st0), channel_id=1, source_target_pairs={{0,2},{1,3},{2,0},{3,1},{4,6},{5,7},{6,4},{7,5},{8,10},{9,11},{10,... | collective-permute-start | bytes 36872 | tf_op jit(solution)/shard_map/ppermute | solution.py:513
  37.5 1.7 %collective-permute-done.36.st2 = f32[8,384]{1,0:T(8,128)S(1)} collective-permute-done((f32[8,384]{1,0:T(8,128)S(1)}, f32[8,384]{1,0:T(8,128)S(1)}, u32[]{:S(2)}, u32[]{:S(2)}) %collective-permute-start.36) | collective-permute-done | bytes 12320 | tf_op jit(solution)/shard_map/ppermute | solution.py:513
  39.2 1.9 %shard_map.110 = (bf16[168,512]{1,0:T(8,128)(2,1)S(1)}, bf16[168,512]{1,0:T(8,128)(2,1)S(1)}, bf16[168,512]{1,0:T(8,128)(2,1)S(1)}, bf16[168,512]{1,0:T(8,128)(2,1)S(1)}, bf16[384,128]{1,0:T(8,128)(2,1)S(1)}) custom-call(s32[10]{0:T(128)S(1)} %pad_add_fusion.meta, bf16[384,512]{1,0:T(8,128)(2,1)S(1)} %get-tuple-element.153.compact, ...), custom_call_target="tpu_custom_call" | custom-call | tf_op jit(solution)/shard_map/pallas_call | solution.py:624
  41.1 1.5 %collective-permute-start.38 = (bf16[168,512]{1,0:T(8,128)(2,1)S(1)}, bf16[168,512]{1,0:T(8,128)(2,1)S(1)}, u32[]{:S(2)}, u32[]{:S(2)}) collective-permute-start(bf16[168,512]{1,0:T(8,128)(2,1)S(1)} %get-tuple-element.159), channel_id=1, source_target_pairs={{0,6},{1,7},{2,4},{3,5},{4,2},{5,3},{6,0},{7,1},{8,14},{9,15},{10,... | collective-permute-start | bytes 516104 | tf_op jit(solution)/shard_map/ppermute | solution.py:513
  43.8 1.8 %collective-permute-start.45 = (bf16[168,512]{1,0:T(8,128)(2,1)S(1)}, bf16[168,512]{1,0:T(8,128)(2,1)S(1)}, u32[]{:S(2)}, u32[]{:S(2)}) collective-permute-start(bf16[168,512]{1,0:T(8,128)(2,1)S(1)} %get-tuple-element.173), channel_id=1, source_target_pairs={{0,4},{1,5},{2,6},{3,7},{4,0},{5,1},{6,2},{7,3},{8,12},{9,13},{10,... | collective-permute-start | bytes 516104 | tf_op jit(solution)/shard_map/ppermute | solution.py:513
  45.7 2.4 %collective-permute-start.41 = (f32[40,128]{1,0:T(8,128)S(1)}, f32[40,128]{1,0:T(8,128)S(1)}, u32[]{:S(2)}, u32[]{:S(2)}) collective-permute-start(f32[40,128]{1,0:T(8,128)S(1)} %shard_map.111.refs_0_), channel_id=1, source_target_pairs={{0,24},{8,16},{16,8},{24,0},{1,25},{9,17},{17,9},{25,1},{2,26},{10... | collective-permute-start | bytes 61448 | tf_op jit(solution)/shard_map/ppermute | solution.py:513
  48.7 1.7 %collective-permute-done.41.refs_3_ = f32[40,128]{1,0:T(8,128)S(1)} collective-permute-done((f32[40,128]{1,0:T(8,128)S(1)}, f32[40,128]{1,0:T(8,128)S(1)}, u32[]{:S(2)}, u32[]{:S(2)}) %collective-permute-start.41) | collective-permute-done | bytes 20512 | tf_op jit(solution)/shard_map/ppermute | solution.py:513
  50.4 1.5 %collective-permute-start.39 = (f32[40,128]{1,0:T(8,128)S(1)}, f32[40,128]{1,0:T(8,128)S(1)}, u32[]{:S(2)}, u32[]{:S(2)}) collective-permute-start(f32[40,128]{1,0:T(8,128)S(1)} %shard_map.111.refs_0_), channel_id=1, source_target_pairs={{0,8},{8,0},{16,24},{24,16},{1,9},{9,1},{17,25},{25,17},{2,10},{10... | collective-permute-start | bytes 61448 | tf_op jit(solution)/shard_map/ppermute | solution.py:513
  52.0 2.2 %collective-permute-done.39.refs_1_ = f32[40,128]{1,0:T(8,128)S(1)} collective-permute-done((f32[40,128]{1,0:T(8,128)S(1)}, f32[40,128]{1,0:T(8,128)S(1)}, u32[]{:S(2)}, u32[]{:S(2)}) %collective-permute-start.39) | collective-permute-done | bytes 20512 | tf_op jit(solution)/shard_map/ppermute | solution.py:513
  54.2 1.6 %shard_map.112 = (f32[128,256]{1,0:T(8,128)}, f32[8,128]{1,0:T(8,128)S(1)}, bf16[1136,1024]{1,0:T(8,128)(2,1)S(1)}) custom-call(s32[10]{0:T(128)S(1)} %pad_add_fusion.meta, bf16[104,128]{1,0:T(8,128)(2,1)S(1)} %get-tuple-element.160.even, bf16[104,128]{1,0:T(8,128)(2,1)S(1)} %get-tuple-element.161.odd, bf16[32,1024]{1,0:T(8,128)(2,1)S(1)} %get-tuple-element.162.negatives, ...), custom_call_target="tpu_custom_call" | custom-call | tf_op jit(solution)/shard_map/pallas_call | solution.py:634
  56.0 1.5 %collective-permute-done.45.refs_4_ = bf16[168,512]{1,0:T(8,128)(2,1)S(1)} collective-permute-done((bf16[168,512]{1,0:T(8,128)(2,1)S(1)}, bf16[168,512]{1,0:T(8,128)(2,1)S(1)}, u32[]{:S(2)}, u32[]{:S(2)}) %collective-permute-start.45) | collective-permute-done | bytes 172064 | tf_op jit(solution)/shard_map/ppermute | solution.py:513
  59.2 2.4 %shard_map.113 = (bf16[128,4096]{1,0:T(8,128)(2,1)}, bf16[128,1024]{1,0:T(8,128)(2,1)}) custom-call(s32[10]{0:T(128)S(1)} %pad_add_fusion.meta, bf16[1136,1024]{1,0:T(8,128)(2,1)S(1)} %get-tuple-element.170.kit, bf16[168,512]{1,0:T(8,128)(2,1)S(1)} %get-tuple-element.171.refs_0_, bf16[168,512]{1,0:T(8,128)(2,1)S(1)} %collective-permute-done.42.refs_1_, ...), custom_call_target="tpu_custom_call" | custom-call | tf_op jit(solution)/shard_map/pallas_call | solution.py:646
  (57 shorter events, 10.4 us)
Async XLA Ops:
  0.6 1.5 %collective-permute-start.24 = (s32[1,128]{1,0:T(1,128)}, s32[1,128]{1,0:T(1,128)S(1)}, u32[]{:S(2)}, u32[]{:S(2)}) collective-permute-start(s32[1,128]{1,0:T(1,128)} %block.1), channel_id=1, source_target_pairs={{0,1},{1,0},{2,3},{3,2},{4,5},{5,4},{6,7},{7,6},{8,9},{9,8},{10,11... | collective-permute-start | bytes 1544 | tf_op jit(solution)/shard_map/ppermute | solution.py:513
  2.1 5.1 %collective-permute-start.25 = (s32[2,128]{1,0:T(2,128)S(1)}, s32[2,128]{1,0:T(2,128)S(1)}, u32[]{:S(2)}, u32[]{:S(2)}) collective-permute-start(s32[2,128]{1,0:T(2,128)S(1)} %shard_map.104.first), channel_id=1, source_target_pairs={{0,2},{1,3},{2,0},{3,1},{4,6},{5,7},{6,4},{7,5},{8,10},{9,11},{10,... | collective-permute-start | bytes 3080 | tf_op jit(solution)/shard_map/ppermute | solution.py:513
  7.2 4.5 %collective-permute-start.26 = (s32[4,128]{1,0:T(4,128)S(1)}, s32[4,128]{1,0:T(4,128)S(1)}, u32[]{:S(2)}, u32[]{:S(2)}) collective-permute-start(s32[4,128]{1,0:T(4,128)S(1)} %shard_map.105.b0), channel_id=1, source_target_pairs={{0,4},{1,5},{2,6},{3,7},{4,0},{5,1},{6,2},{7,3},{8,12},{9,13},{10,... | collective-permute-start | bytes 6152 | tf_op jit(solution)/shard_map/ppermute | solution.py:513
  13.1 8.6 %collective-permute-start.27 = (bf16[136,512]{1,0:T(8,128)(2,1)S(1)}, bf16[136,512]{1,0:T(8,128)(2,1)S(1)}, u32[]{:S(2)}, u32[]{:S(2)}) collective-permute-start(bf16[136,512]{1,0:T(8,128)(2,1)S(1)} %get-tuple-element.137), channel_id=1, source_target_pairs={{0,6},{1,7},{2,4},{3,5},{4,2},{5,3},{6,0},{7,1},{8,14},{9,15},{10,... | collective-permute-start | bytes 417800 | tf_op jit(solution)/shard_map/ppermute | solution.py:513
  16.5 6.5 %collective-permute-start.29 = (bf16[136,512]{1,0:T(8,128)(2,1)S(1)}, bf16[136,512]{1,0:T(8,128)(2,1)S(1)}, u32[]{:S(2)}, u32[]{:S(2)}) collective-permute-start(bf16[136,512]{1,0:T(8,128)(2,1)S(1)} %get-tuple-element.150), channel_id=1, source_target_pairs={{0,2},{1,3},{2,0},{3,1},{4,6},{5,7},{6,4},{7,5},{8,10},{9,11},{10,... | collective-permute-start | bytes 417800 | tf_op jit(solution)/shard_map/ppermute | solution.py:513
  16.5 10.8 %collective-permute-start.31 = (bf16[136,512]{1,0:T(8,128)(2,1)S(1)}, bf16[136,512]{1,0:T(8,128)(2,1)S(1)}, u32[]{:S(2)}, u32[]{:S(2)}) collective-permute-start(bf16[136,512]{1,0:T(8,128)(2,1)S(1)} %get-tuple-element.151), channel_id=1, source_target_pairs={{0,4},{1,5},{2,6},{3,7},{4,0},{5,1},{6,2},{7,3},{8,12},{9,13},{10,... | collective-permute-start | bytes 417800 | tf_op jit(solution)/shard_map/ppermute | solution.py:513
  17.5 10.3 %collective-permute-start.28 = (bf16[136,512]{1,0:T(8,128)(2,1)S(1)}, bf16[136,512]{1,0:T(8,128)(2,1)S(1)}, u32[]{:S(2)}, u32[]{:S(2)}) collective-permute-start(bf16[136,512]{1,0:T(8,128)(2,1)S(1)} %get-tuple-element.149.refs_0_), channel_id=1, source_target_pairs={{0,1},{1,0},{2,3},{3,2},{4,5},{5,4},{6,7},{7,6},{8,9},{9,8},{10,11... | collective-permute-start | bytes 417800 | tf_op jit(solution)/shard_map/ppermute | solution.py:513
  23.0 4.8 %collective-permute-start.30 = (bf16[136,512]{1,0:T(8,128)(2,1)S(1)}, bf16[136,512]{1,0:T(8,128)(2,1)S(1)}, u32[]{:S(2)}, u32[]{:S(2)}) collective-permute-start(bf16[136,512]{1,0:T(8,128)(2,1)S(1)} %collective-permute-done.29.refs_2_), channel_id=1, source_target_pairs={{0,1},{1,0},{2,3},{3,2},{4,5},{5,4},{6,7},{7,6},{8,9},{9,8},{10,11... | collective-permute-start | bytes 417800 | tf_op jit(solution)/shard_map/ppermute | solution.py:513
  27.3 1.4 %collective-permute-start.32 = (bf16[136,512]{1,0:T(8,128)(2,1)S(1)}, bf16[136,512]{1,0:T(8,128)(2,1)S(1)}, u32[]{:S(2)}, u32[]{:S(2)}) collective-permute-start(bf16[136,512]{1,0:T(8,128)(2,1)S(1)} %collective-permute-done.31.refs_4_), channel_id=1, source_target_pairs={{0,1},{1,0},{2,3},{3,2},{4,5},{5,4},{6,7},{7,6},{8,9},{9,8},{10,11... | collective-permute-start | bytes 417800 | tf_op jit(solution)/shard_map/ppermute | solution.py:513
  27.3 1.6 %collective-permute-start.33 = (bf16[136,512]{1,0:T(8,128)(2,1)S(1)}, bf16[136,512]{1,0:T(8,128)(2,1)S(1)}, u32[]{:S(2)}, u32[]{:S(2)}) collective-permute-start(bf16[136,512]{1,0:T(8,128)(2,1)S(1)} %collective-permute-done.27.refs_6_), channel_id=1, source_target_pairs={{0,1},{1,0},{2,3},{3,2},{4,5},{5,4},{6,7},{7,6},{8,9},{9,8},{10,11... | collective-permute-start | bytes 417800 | tf_op jit(solution)/shard_map/ppermute | solution.py:513
  30.6 1.2 %collective-permute-start.34 = (f32[8,384]{1,0:T(8,128)S(1)}, f32[8,384]{1,0:T(8,128)S(1)}, u32[]{:S(2)}, u32[]{:S(2)}) collective-permute-start(f32[8,384]{1,0:T(8,128)S(1)} %get-tuple-element.157), channel_id=1, source_target_pairs={{0,1},{1,0},{2,3},{3,2},{4,5},{5,4},{6,7},{7,6},{8,9},{9,8},{10,11... | collective-permute-start | bytes 36872 | tf_op jit(solution)/shard_map/ppermute | solution.py:513
  31.9 5.6 %collective-permute-start.37 = (f32[8,384]{1,0:T(8,128)S(1)}, f32[8,384]{1,0:T(8,128)S(1)}, u32[]{:S(2)}, u32[]{:S(2)}) collective-permute-start(f32[8,384]{1,0:T(8,128)S(1)} %stack.10.st0), channel_id=1, source_target_pairs={{0,6},{1,7},{2,4},{3,5},{4,2},{5,3},{6,0},{7,1},{8,14},{9,15},{10,... | collective-permute-start | bytes 36872 | tf_op jit(solution)/shard_map/ppermute | solution.py:513
  34.6 4.6 %collective-permute-start.36 = (f32[8,384]{1,0:T(8,128)S(1)}, f32[8,384]{1,0:T(8,128)S(1)}, u32[]{:S(2)}, u32[]{:S(2)}) collective-permute-start(f32[8,384]{1,0:T(8,128)S(1)} %stack.10.st0), channel_id=1, source_target_pairs={{0,4},{1,5},{2,6},{3,7},{4,0},{5,1},{6,2},{7,3},{8,12},{9,13},{10,... | collective-permute-start | bytes 36872 | tf_op jit(solution)/shard_map/ppermute | solution.py:513
  34.6 4.6 %collective-permute-start.35 = (f32[8,384]{1,0:T(8,128)S(1)}, f32[8,384]{1,0:T(8,128)S(1)}, u32[]{:S(2)}, u32[]{:S(2)}) collective-permute-start(f32[8,384]{1,0:T(8,128)S(1)} %stack.10.st0), channel_id=1, source_target_pairs={{0,2},{1,3},{2,0},{3,1},{4,6},{5,7},{6,4},{7,5},{8,10},{9,11},{10,... | collective-permute-start | bytes 36872 | tf_op jit(solution)/shard_map/ppermute | solution.py:513
  41.1 14.7 %collective-permute-start.38 = (bf16[168,512]{1,0:T(8,128)(2,1)S(1)}, bf16[168,512]{1,0:T(8,128)(2,1)S(1)}, u32[]{:S(2)}, u32[]{:S(2)}) collective-permute-start(bf16[168,512]{1,0:T(8,128)(2,1)S(1)} %get-tuple-element.159), channel_id=1, source_target_pairs={{0,6},{1,7},{2,4},{3,5},{4,2},{5,3},{6,0},{7,1},{8,14},{9,15},{10,... | collective-permute-start | bytes 516104 | tf_op jit(solution)/shard_map/ppermute | solution.py:513
  42.7 13.2 %collective-permute-start.43 = (bf16[168,512]{1,0:T(8,128)(2,1)S(1)}, bf16[168,512]{1,0:T(8,128)(2,1)S(1)}, u32[]{:S(2)}, u32[]{:S(2)}) collective-permute-start(bf16[168,512]{1,0:T(8,128)(2,1)S(1)} %get-tuple-element.172), channel_id=1, source_target_pairs={{0,2},{1,3},{2,0},{3,1},{4,6},{5,7},{6,4},{7,5},{8,10},{9,11},{10,... | collective-permute-start | bytes 516104 | tf_op jit(solution)/shard_map/ppermute | solution.py:513
  43.8 13.6 %collective-permute-start.45 = (bf16[168,512]{1,0:T(8,128)(2,1)S(1)}, bf16[168,512]{1,0:T(8,128)(2,1)S(1)}, u32[]{:S(2)}, u32[]{:S(2)}) collective-permute-start(bf16[168,512]{1,0:T(8,128)(2,1)S(1)} %get-tuple-element.173), channel_id=1, source_target_pairs={{0,4},{1,5},{2,6},{3,7},{4,0},{5,1},{6,2},{7,3},{8,12},{9,13},{10,... | collective-permute-start | bytes 516104 | tf_op jit(solution)/shard_map/ppermute | solution.py:513
  45.7 4.7 %collective-permute-start.41 = (f32[40,128]{1,0:T(8,128)S(1)}, f32[40,128]{1,0:T(8,128)S(1)}, u32[]{:S(2)}, u32[]{:S(2)}) collective-permute-start(f32[40,128]{1,0:T(8,128)S(1)} %shard_map.111.refs_0_), channel_id=1, source_target_pairs={{0,24},{8,16},{16,8},{24,0},{1,25},{9,17},{17,9},{25,1},{2,26},{10... | collective-permute-start | bytes 61448 | tf_op jit(solution)/shard_map/ppermute | solution.py:513
  48.2 3.8 %collective-permute-start.40 = (f32[40,128]{1,0:T(8,128)S(1)}, f32[40,128]{1,0:T(8,128)S(1)}, u32[]{:S(2)}, u32[]{:S(2)}) collective-permute-start(f32[40,128]{1,0:T(8,128)S(1)} %shard_map.111.refs_0_), channel_id=1, source_target_pairs={{0,16},{8,24},{16,0},{24,8},{1,17},{9,25},{17,1},{25,9},{2,18},{10... | collective-permute-start | bytes 61448 | tf_op jit(solution)/shard_map/ppermute | solution.py:513
  50.4 3.8 %collective-permute-start.39 = (f32[40,128]{1,0:T(8,128)S(1)}, f32[40,128]{1,0:T(8,128)S(1)}, u32[]{:S(2)}, u32[]{:S(2)}) collective-permute-start(f32[40,128]{1,0:T(8,128)S(1)} %shard_map.111.refs_0_), channel_id=1, source_target_pairs={{0,8},{8,0},{16,24},{24,16},{1,9},{9,1},{17,25},{25,17},{2,10},{10... | collective-permute-start | bytes 61448 | tf_op jit(solution)/shard_map/ppermute | solution.py:513
  52.0 7.2 %collective-permute-start.42 = (bf16[168,512]{1,0:T(8,128)(2,1)S(1)}, bf16[168,512]{1,0:T(8,128)(2,1)S(1)}, u32[]{:S(2)}, u32[]{:S(2)}) collective-permute-start(bf16[168,512]{1,0:T(8,128)(2,1)S(1)} %get-tuple-element.171.refs_0_), channel_id=1, source_target_pairs={{0,1},{1,0},{2,3},{3,2},{4,5},{5,4},{6,7},{7,6},{8,9},{9,8},{10,11... | collective-permute-start | bytes 516104 | tf_op jit(solution)/shard_map/ppermute | solution.py:513
  55.9 3.2 %collective-permute-start.44 = (bf16[168,512]{1,0:T(8,128)(2,1)S(1)}, bf16[168,512]{1,0:T(8,128)(2,1)S(1)}, u32[]{:S(2)}, u32[]{:S(2)}) collective-permute-start(bf16[168,512]{1,0:T(8,128)(2,1)S(1)} %collective-permute-done.43.refs_2_), channel_id=1, source_target_pairs={{0,1},{1,0},{2,3},{3,2},{4,5},{5,4},{6,7},{7,6},{8,9},{9,8},{10,11... | collective-permute-start | bytes 516104 | tf_op jit(solution)/shard_map/ppermute | solution.py:513
  57.4 1.7 %collective-permute-start.46 = (bf16[168,512]{1,0:T(8,128)(2,1)S(1)}, bf16[168,512]{1,0:T(8,128)(2,1)S(1)}, u32[]{:S(2)}, u32[]{:S(2)}) collective-permute-start(bf16[168,512]{1,0:T(8,128)(2,1)S(1)} %collective-permute-done.45.refs_4_), channel_id=1, source_target_pairs={{0,1},{1,0},{2,3},{3,2},{4,5},{5,4},{6,7},{7,6},{8,9},{9,8},{10,11... | collective-permute-start | bytes 516104 | tf_op jit(solution)/shard_map/ppermute | solution.py:513
  57.4 1.7 %collective-permute-start.47 = (bf16[168,512]{1,0:T(8,128)(2,1)S(1)}, bf16[168,512]{1,0:T(8,128)(2,1)S(1)}, u32[]{:S(2)}, u32[]{:S(2)}) collective-permute-start(bf16[168,512]{1,0:T(8,128)(2,1)S(1)} %collective-permute-done.38.refs_6_), channel_id=1, source_target_pairs={{0,1},{1,0},{2,3},{3,2},{4,5},{5,4},{6,7},{7,6},{8,9},{9,8},{10,11... | collective-permute-start | bytes 516104 | tf_op jit(solution)/shard_map/ppermute | solution.py:513
  (8 other events, 69.5 us)

commit v7 on v6

--- a/solution.py
+++ b/solution.py
@@ -12,7 +12,7 @@
 SPAN = 3
 PARTS = 4
 SLOTS = 60
-POOL = 104
+POOL = 152
 LENS = 2
 
 
@@ -278,7 +278,7 @@
         outs[d][2 * slots :] = below[...]
 
 
-def index_kernel(sizes, meta, b0, b1, pick, w_out, pick_in, pick_out, home_even, home_odd, live, most, w_cols, order_ref, w_rows, sem):
+def index_kernel(sizes, meta, b0, b1, pick, w_out, pick_in, pick_out, home_even, home_odd, tile, live, most, w_cols, order_ref, w_rows, sem):
     n, rows, slots, pool = sizes
     cell = rows // n
     live_cap = live.shape[0]
@@ -296,7 +296,8 @@
     ranks = slot_ranks(places)
     count = jnp.sum(jnp.where(places > 0.5, 1.0, 0.0), axis=0, keepdims=True)
     counts = [count[:, x : x + 1] for x in range(n)]
-    excess = [c - slots for c in counts] + [counts[2 * d] + counts[2 * d + 1] - pool for d in range(n // 2)]
+    lines_of = [pair_lines(meta, (me >> 1) ^ d) for d in range(n // 2)]
+    excess = [c - slots for c in counts] + [counts[2 * d] + counts[2 * d + 1] + (lines_of[d] - pool).astype(F32) for d in range(n // 2)]
     most[...] = jnp.broadcast_to(functools.reduce(jnp.maximum, excess), most.shape)
 
     def placed(x, first, width):
@@ -314,13 +315,22 @@
     pick_in[...] = one_hot(iota((live_cap, line.shape[1]), 0).astype(F32) == line)
     reach = -(-pool // rows) * rows
     for d in range(n // 2):
-        line = placed(2 * d, 0.0, reach) + placed(2 * d + 1, counts[2 * d], reach) - 1.0
+        first = lines_of[d].astype(F32)
+        line = placed(2 * d, first, reach) + placed(2 * d + 1, counts[2 * d] + first, reach) - 1.0
         hit = one_hot(iota((live_cap, reach), 0).astype(F32) == line)
         pick_out[d * pool : (d + 1) * pool] = jnp.transpose(hit.astype(F32))[:pool].astype(BF16)
     slot = iota((reach, rows), 0).astype(F32)
     for home, first in ((home_even, jnp.zeros((1, 1), F32)), (home_odd, counts[1])):
+        first = first + lines_of[0].astype(F32)
         moved = dot(one_hot(slot == lane[0:1].astype(F32) + first), pick[...])
-        home[...] = moved[:pool].astype(BF16)
+        home[...] = jnp.transpose(moved).astype(BF16)
+    quarter = tile.shape[1] // PARTS
+    line = iota((rows, quarter), 1)
+    row = iota((rows, quarter), 0)
+    before = jnp.where(me % 2 == 1, meta[LENS + (me ^ 1)], 0)
+    for b in range(PARTS):
+        hit = (line + b * lines_of[0] == row + before) & (line < lines_of[0]) & (row < meta[LENS + me])
+        tile[:, b * quarter : (b + 1) * quarter] = one_hot(hit)
     copy.wait()
     w_cols[...] = jnp.transpose(w_rows[...].astype(F32)).astype(BF16)
     live[...] = jnp.where(pair_live(live_cap, starts_of(meta, n)), 1.0 / rows, 0.0)
@@ -391,6 +401,10 @@
     )
 
 
+def pair_lines(meta, chip):
+    return (meta[LENS + 2 * chip] + meta[LENS + 2 * chip + 1] + PARTS - 1) // PARTS
+
+
 def start_of(meta, n, tile):
     start = jnp.int32(0)
     for t in range(n):
@@ -430,21 +444,22 @@
         [dm * normed, dot(weights[...], d_att, ((0,), (0,))), dot(ds, k), dot(ds, q, ((0,), (0,)))], axis=1
     ).astype(BF16)
     mixed_ref[...] = mixed
-    sent = dot(pick[...], grad).astype(BF16)
+    sent = dot(pick[...], grad)
     mixed_rows[0:live_cap] = mixed.astype(F32)
-    mixed_rows[live_cap:] = jnp.zeros((rows, head_dim), F32)
-    quarter = rows // PARTS
-    row = iota((rows, head_dim), 0)
-    for x in range(n):
-        t = me ^ x
-        tile = mixed_rows[pl.ds(start_of(meta, n, t), rows), :]
-        tile = jnp.where(row < meta[LENS + t], tile, 0.0)
-        first = quarter * (x % 2)
-        outs[x // 2][first : first + quarter] = jnp.concatenate(
-            [tile[b * quarter : (b + 1) * quarter] for b in range(PARTS)], axis=1
-        ).astype(BF16)
+    mixed_rows[live_cap:] = jnp.zeros((2 * rows, head_dim), F32)
+    half = 2 * rows // PARTS
+    row = iota((half, head_dim), 0)
     for d in range(n // 2):
-        outs[d][2 * quarter :] = sent[d * pool : (d + 1) * pool]
+        chip = (me >> 1) ^ d
+        lines = pair_lines(meta, chip)
+        count = meta[LENS + 2 * chip] + meta[LENS + 2 * chip + 1]
+        parts = []
+        for b in range(PARTS):
+            part = mixed_rows[pl.ds(start_of(meta, n, 2 * chip) + b * lines, half), :]
+            parts.append(jnp.where((row < lines) & (row + b * lines < count), part, 0.0))
+        rows_out = sent[d * pool : (d + 1) * pool]
+        outs[d][0:half] = (rows_out[0:half] + jnp.concatenate(parts, axis=1)).astype(BF16)
+        outs[d][half:] = rows_out[half:].astype(BF16)
 
 
 def sums_kernel(coef_c, mixed, most, sums):
@@ -453,14 +468,15 @@
     sums[negs:] = most[...]
 
 
-def total_kernel(meta, even, odd, negatives, w_out, *refs):
+def total_kernel(meta, even, odd, tile, negatives, w_out, *refs):
     sums, (d_w_out, most, kit, sem) = refs[:-4], refs[-4:]
     width = w_out.shape[0]
     copy = pltpu.make_async_copy(w_out, kit.at[pl.ds(0, width)], sem)
     copy.start()
-    pool, rows = even.shape
-    kit[width : width + pool, 0:rows] = even[...]
-    kit[width : width + pool, rows : 2 * rows] = odd[...]
+    rows, reach = even.shape
+    kit[width:, 0:reach] = even[...]
+    kit[width:, reach : 2 * reach] = odd[...]
+    kit[width:, 2 * reach : 2 * reach + 2 * rows] = tile[...]
     negs, groups = negatives.shape[0], len(sums)
     most[...] = functools.reduce(jnp.maximum, [part[negs:] for part in sums])
     rest = functools.reduce(jnp.add, [part[0:negs] for part in sums])
@@ -481,20 +497,17 @@
     width = kit.shape[1]
     head_dim = width // n
     quarter = rows // PARTS
-    layer = jnp.zeros((rows, width), F32)
-    for d in range(0, n, 2):
-        mixed, weights = [], []
-        for x in (d, d + 1):
-            head = pl.multiple_of((meta[0] ^ x) * head_dim, head_dim)
-            block = blocks[x]
-            pick = kit[width : width + block.shape[0] - 2 * quarter, rows * (x % 2) : rows * (x % 2 + 1)]
-            part = dot(pick, block[2 * quarter :], ((0,), (0,))).astype(BF16)
-            for i in range(PARTS):
-                d_home[:, pl.ds(i * width + head, head_dim)] = part[:, i * head_dim : (i + 1) * head_dim]
-            lines = block[quarter * (x % 2) : quarter * (x % 2 + 1)]
-            mixed.append(jnp.concatenate([lines[:, b * head_dim : (b + 1) * head_dim] for b in range(PARTS)], axis=0))
-            weights.append(kit[pl.ds(head, head_dim), :])
-        layer = layer + dot(jnp.concatenate(mixed, axis=1), jnp.concatenate(weights, axis=0))
+    reach = -(-blocks[0].shape[0] // rows) * rows
+    for x in range(n):
+        head = pl.multiple_of((meta[0] ^ x) * head_dim, head_dim)
+        block = blocks[x][...]
+        pick = kit[width:, reach * (x % 2) : reach * (x % 2) + block.shape[0]]
+        part = dot(pick, block).astype(BF16)
+        for i in range(PARTS):
+            d_home[:, pl.ds(i * width + head, head_dim)] = part[:, i * head_dim : (i + 1) * head_dim]
+        lines = jnp.concatenate([block[0 : 2 * quarter, b * head_dim : (b + 1) * head_dim] for b in range(PARTS)], axis=0)
+        layer_out[:, pl.ds(head, head_dim)] = dot(kit[width:, 2 * reach : 2 * reach + 2 * rows], lines).astype(BF16)
+    layer = dot(layer_out[...], kit[0:width])
     layer_out[...] = layer.astype(BF16)
 
 
@@ -565,6 +578,7 @@
 
     def passes(slots, pool):
         span = -(-slots // 8) * 8
+        reach = -(-pool // rows) * rows
         def prep():
             return kernel_call(
                 prep_kernel,
@@ -593,8 +607,9 @@
                 (
                     sds((live_cap, n * span), BF16),
                     sds((half * pool, live_cap), BF16),
-                    sds((pool, rows), BF16),
-                    sds((pool, rows), BF16),
+                    sds((rows, reach), BF16),
+                    sds((rows, reach), BF16),
+                    sds((rows, 2 * rows), BF16),
                     sds((live_cap, live_cap), F32),
                     sds((8, 128), F32),
                     sds((width, head_dim), BF16),
@@ -603,7 +618,7 @@
                 [pltpu.VMEM((n, 1, rows), F32), pltpu.VMEM((head_dim, width), BF16), pltpu.SemaphoreType.DMA],
             )(meta, *orders, pick, w_out)
 
-        received, (pick_in, pick_out, even, odd, live, most, w_cols) = exchange(message, index)
+        received, (pick_in, pick_out, even, odd, tile, live, most, w_cols) = exchange(message, index)
         compact, weights, att, stats, coef_c, d_mixed, negatives = kernel_call(
             functools.partial(forward_kernel, (n, rows, slots, per)),
             (
@@ -620,12 +635,12 @@
         )(meta, pick_in, live, w_cols, *received)
         paired = merge_stats(stats, swap(stats, "seq", 1), head_dim)
         paired = jnp.stack(list(paired) + [jnp.zeros_like(stats[0])] * 4)
-        far = [swap(paired, "seq", d) for d in range(2, n, 2)]
+        far = [swap(paired, "seq", d) for d in range(n - 2, 0, -2)]
         *back, mixed = kernel_call(
             functools.partial(backward_kernel, (n, rows, pool)),
-            (sds((2 * quarter + pool, wide), BF16),) * half + (sds((live_cap, head_dim), BF16),),
+            (sds((pool, wide), BF16),) * half + (sds((live_cap, head_dim), BF16),),
             [SMEM] + [VMEM] * 10,
-            [pltpu.VMEM((live_cap + rows, head_dim), F32)],
+            [pltpu.VMEM((live_cap + 2 * rows, head_dim), F32)],
         )(meta, compact, weights, att, d_mixed, paired, *far, pick_out, live)
 
         def group_sums():
@@ -633,10 +648,10 @@
             sums = [sums] + [swap(sums, "dp", d) for d in range(1, groups)]
             d_w, most_of_all, kit = kernel_call(
                 total_kernel,
-                (sds((head_dim, width // groups), F32), sds((8, 128), F32), sds((width + -(-pool // 16) * 16, width), BF16)),
-                [SMEM] + [VMEM] * 3 + [ANY] + [VMEM] * groups,
+                (sds((head_dim, width // groups), F32), sds((8, 128), F32), sds((width + rows, width), BF16)),
+                [SMEM] + [VMEM] * 4 + [ANY] + [VMEM] * groups,
                 [pltpu.SemaphoreType.DMA],
-            )(meta, even, odd, negatives, w_out, *sums)
+            )(meta, even, odd, tile, negatives, w_out, *sums)
             return d_w, kit, most_of_all
 
         returned, (d_w, kit, most_of_all) = exchange(back, group_sums)
@@ -652,7 +667,7 @@
 
     overflow, parts = passes(SLOTS, POOL)
     d_home, layer_out, d_w_out = lax.cond(
-        overflow, lambda *_: finish(*passes(rows, 2 * rows)[1]), lambda *outs: outs, *finish(*parts)
+        overflow, lambda *_: finish(*passes(rows, 2 * rows + 2 * quarter)[1]), lambda *outs: outs, *finish(*parts)
     )
     return (layer_out, d_home, d_w_out)
 

time: 62.2 us -> 60.8 us (0.977)
  waiting for transfers between devices: 19.4 us -> 16.9 us
    ppermute x24, waiting for transfers between devices: 19.4 us -> 16.9 us  [swap(): lax.ppermute(block, axis, [(i, i ^ distance) for i in range(lax.axis_size...]
  transfers between devices with their start and end apart: 24 -> 24, of which waited for: 14 -> 12; matrix products, arithmetic and copies ran while one was open for 2% -> 2% of each run, Pallas kernels for 11% -> 12%
where the time goes in v7:
time: 60.8 us; the launch traced here: 60.6 us
  starting transfers between devices  25.8 us (42%)
  waiting for transfers between devices  16.9 us (28%)
  Pallas kernels  14.7 us (24%)
  between operations  1.67 us (3%)
  other arithmetic  0.74 us (1%)
    ppermute x24, starting transfers between devices, swap(): lax.ppermute(block, axis, [(i, i ^ distance) for i in range(lax.axis_size...  25.8 us
    ppermute x24, waiting for transfers between devices, swap(): lax.ppermute(block, axis, [(i, i ^ distance) for i in range(lax.axis_size...  16.9 us
    pallas_call x1, Pallas kernels, index(): kernel_call(functools.partial(index_kernel, (n, rows, slots, pool)), (sds...  2.55 us
    pallas_call x1, Pallas kernels, finish(): kernel_call(functools.partial(finish_kernel, (n, rows)), (sds((rows, PART...  2.53 us
    pallas_call x1, Pallas kernels, prep(): kernel_call(prep_kernel, (sds(qkvu.shape, BF16), sds((below, wide), BF16)...  2.11 us
    pallas_call x1, Pallas kernels, passes(): kernel_call(functools.partial(backward_kernel, (n, rows, pool)), (sds((po...  1.98 us
    pallas_call x1, Pallas kernels, passes(): kernel_call(functools.partial(forward_kernel, (n, rows, slots, per)), (sd...  1.79 us
    pallas_call x1, Pallas kernels, group_sums(): kernel_call(total_kernel, (sds((head_dim, width // groups), F32), sds((8,...  1.6 us
  transfers between devices with their start and end apart: 24, of which 12 were waited for; matrix products, arithmetic and copies ran while one was open for 2% of the time, Pallas kernels for 12%

profile of v7, /device:TPU:0, one launch (start us, length us, event | category | flops | bytes accessed | tf_op | source)
XLA Modules:
  0.0 60.6 jit_solution(16765363405181998095)
XLA Ops:
  2.1 2.9 %collective-permute-start.25 = (s32[2,128]{1,0:T(2,128)S(1)}, s32[2,128]{1,0:T(2,128)S(1)}, u32[]{:S(2)}, u32[]{:S(2)}) collective-permute-start(s32[2,128]{1,0:T(2,128)S(1)} %shard_map.104.first), channel_id=1, source_target_pairs={{0,2},{1,3},{2,0},{3,1},{4,6},{5,7},{6,4},{7,5},{8,10},{9,11},{10,... | collective-permute-start | bytes 3080 | tf_op jit(solution)/shard_map/ppermute | solution.py:526
  5.0 2.1 %shard_map.106 = (bf16[128,4096]{1,0:T(8,128)(2,1)S(1)}, bf16[16,512]{1,0:T(8,128)(2,1)S(1)}, bf16[128,128]{1,0:T(8,128)(2,1)S(1)}) custom-call(s32[4]{0:T(128)} %ids.1, s32[1,128]{1,0:T(1,128)} %send.1, bf16[32,128]{1,0:T(8,128)(2,1)} %bitcast.5, bf16[512,1024]{1,0:T(8,128)(2,1)} %table.1, bf16[128,4096]{1,0:T(8,128)(2,1)} %qkvu.1), custom_call_target="tpu_custom_call" | custom-call | tf_op jit(solution)/shard_map/pallas_call | solution.py:583
  7.1 2.7 %collective-permute-start.26 = (s32[4,128]{1,0:T(4,128)S(1)}, s32[4,128]{1,0:T(4,128)S(1)}, u32[]{:S(2)}, u32[]{:S(2)}) collective-permute-start(s32[4,128]{1,0:T(4,128)S(1)} %shard_map.105.b0), channel_id=1, source_target_pairs={{0,4},{1,5},{2,6},{3,7},{4,0},{5,1},{6,2},{7,3},{8,12},{9,13},{10,... | collective-permute-start | bytes 6152 | tf_op jit(solution)/shard_map/ppermute | solution.py:526
  11.7 1.3 %shard_map.107 = (bf16[136,512]{1,0:T(8,128)(2,1)S(1)}, bf16[136,512]{1,0:T(8,128)(2,1)S(1)}, bf16[136,512]{1,0:T(8,128)(2,1)S(1)}, bf16[136,512]{1,0:T(8,128)(2,1)S(1)}, bf16[128,128]{1,0:T(8,128)(2,1)S(1)}) custom-call(s32[10]{0:T(128)S(1)} %pad_add_fusion.meta, s32[4,128]{1,0:T(4,128)S(1)} %shard_map.105.b0, s32[4,128]{1,0:T(4,128)S(1)} %collective-permute-done.26.b1, ...), custom_call_target="tpu_custom_call" | custom-call | tf_op jit(solution)/shard_map/pallas_call | solution.py:597
  13.0 3.5 %collective-permute-start.27 = (bf16[136,512]{1,0:T(8,128)(2,1)S(1)}, bf16[136,512]{1,0:T(8,128)(2,1)S(1)}, u32[]{:S(2)}, u32[]{:S(2)}) collective-permute-start(bf16[136,512]{1,0:T(8,128)(2,1)S(1)} %get-tuple-element.141), channel_id=1, source_target_pairs={{0,6},{1,7},{2,4},{3,5},{4,2},{5,3},{6,0},{7,1},{8,14},{9,15},{10,... | collective-permute-start | bytes 417800 | tf_op jit(solution)/shard_map/ppermute | solution.py:526
  17.5 2.6 %shard_map.108 = (bf16[384,512]{1,0:T(8,128)(2,1)S(1)}, bf16[608,384]{1,0:T(8,128)(2,1)S(1)}, bf16[128,256]{1,0:T(8,128)(2,1)S(1)}, bf16[128,256]{1,0:T(8,128)(2...) custom-call(s32[10]{0:T(128)S(1)} %pad_add_fusion.meta, ...), custom_call_target="tpu_custom_call" | custom-call | tf_op jit(solution)/shard_map/pallas_call | solution.py:605
  20.0 1.5 %collective-permute-done.27.refs_6_ = bf16[136,512]{1,0:T(8,128)(2,1)S(1)} collective-permute-done((bf16[136,512]{1,0:T(8,128)(2,1)S(1)}, bf16[136,512]{1,0:T(8,128)(2,1)S(1)}, u32[]{:S(2)}, u32[]{:S(2)}) %collective-permute-start.27) | collective-permute-done | bytes 139296 | tf_op jit(solution)/shard_map/ppermute | solution.py:526
  21.6 1.5 %collective-permute-done.29.refs_2_ = bf16[136,512]{1,0:T(8,128)(2,1)S(1)} collective-permute-done((bf16[136,512]{1,0:T(8,128)(2,1)S(1)}, bf16[136,512]{1,0:T(8,128)(2,1)S(1)}, u32[]{:S(2)}, u32[]{:S(2)}) %collective-permute-start.29) | collective-permute-done | bytes 139296 | tf_op jit(solution)/shard_map/ppermute | solution.py:526
  23.1 4.1 %collective-permute-done.31.refs_4_ = bf16[136,512]{1,0:T(8,128)(2,1)S(1)} collective-permute-done((bf16[136,512]{1,0:T(8,128)(2,1)S(1)}, bf16[136,512]{1,0:T(8,128)(2,1)S(1)}, u32[]{:S(2)}, u32[]{:S(2)}) %collective-permute-start.31) | collective-permute-done | bytes 139296 | tf_op jit(solution)/shard_map/ppermute | solution.py:526
  27.2 1.3 %collective-permute-done.32.refs_5_ = bf16[136,512]{1,0:T(8,128)(2,1)S(1)} collective-permute-done((bf16[136,512]{1,0:T(8,128)(2,1)S(1)}, bf16[136,512]{1,0:T(8,128)(2,1)S(1)}, u32[]{:S(2)}, u32[]{:S(2)}) %collective-permute-start.32) | collective-permute-done | bytes 139296 | tf_op jit(solution)/shard_map/ppermute | solution.py:526
  28.6 1.8 %shard_map.109 = (bf16[384,512]{1,0:T(8,128)(2,1)S(1)}, bf16[384,384]{1,0:T(8,128)(2,1)S(1)}, f32[384,128]{1,0:T(8,128)S(1)}, f32[8,384]{1,0:T(8,128)S(1)}, bf16...) custom-call(s32[10]{0:T(128)S(1)} %pad_add_fusion.meta, ...), custom_call_target="tpu_custom_call" | custom-call | tf_op jit(solution)/shard_map/pallas_call | solution.py:622
  31.7 2.7 %collective-permute-start.35 = (f32[8,384]{1,0:T(8,128)S(1)}, f32[8,384]{1,0:T(8,128)S(1)}, u32[]{:S(2)}, u32[]{:S(2)}) collective-permute-start(f32[8,384]{1,0:T(8,128)S(1)} %stack.10.st0), channel_id=1, source_target_pairs={{0,6},{1,7},{2,4},{3,5},{4,2},{5,3},{6,0},{7,1},{8,14},{9,15},{10,... | collective-permute-start | bytes 36872 | tf_op jit(solution)/shard_map/ppermute | solution.py:526
  34.4 1.7 %collective-permute-start.37 = (f32[8,384]{1,0:T(8,128)S(1)}, f32[8,384]{1,0:T(8,128)S(1)}, u32[]{:S(2)}, u32[]{:S(2)}) collective-permute-start(f32[8,384]{1,0:T(8,128)S(1)} %stack.10.st0), channel_id=1, source_target_pairs={{0,2},{1,3},{2,0},{3,1},{4,6},{5,7},{6,4},{7,5},{8,10},{9,11},{10,... | collective-permute-start | bytes 36872 | tf_op jit(solution)/shard_map/ppermute | solution.py:526
  37.2 1.7 %collective-permute-done.36.st2 = f32[8,384]{1,0:T(8,128)S(1)} collective-permute-done((f32[8,384]{1,0:T(8,128)S(1)}, f32[8,384]{1,0:T(8,128)S(1)}, u32[]{:S(2)}, u32[]{:S(2)}) %collective-permute-start.36) | collective-permute-done | bytes 12320 | tf_op jit(solution)/shard_map/ppermute | solution.py:526
  39.0 2.0 %shard_map.110 = (bf16[152,512]{1,0:T(8,128)(2,1)S(1)}, bf16[152,512]{1,0:T(8,128)(2,1)S(1)}, bf16[152,512]{1,0:T(8,128)(2,1)S(1)}, bf16[152,512]{1,0:T(8,128)(2,1)S(1)}, bf16[384,128]{1,0:T(8,128)(2,1)S(1)}) custom-call(s32[10]{0:T(128)S(1)} %pad_add_fusion.meta, bf16[384,512]{1,0:T(8,128)(2,1)S(1)} %get-tuple-element.158.compact, ...), custom_call_target="tpu_custom_call" | custom-call | tf_op jit(solution)/shard_map/pallas_call | solution.py:639
  41.0 1.5 %collective-permute-start.38 = (bf16[152,512]{1,0:T(8,128)(2,1)S(1)}, bf16[152,512]{1,0:T(8,128)(2,1)S(1)}, u32[]{:S(2)}, u32[]{:S(2)}) collective-permute-start(bf16[152,512]{1,0:T(8,128)(2,1)S(1)} %get-tuple-element.164), channel_id=1, source_target_pairs={{0,6},{1,7},{2,4},{3,5},{4,2},{5,3},{6,0},{7,1},{8,14},{9,15},{10,... | collective-permute-start | bytes 466952 | tf_op jit(solution)/shard_map/ppermute | solution.py:526
  42.5 1.1 %collective-permute-start.43 = (bf16[152,512]{1,0:T(8,128)(2,1)S(1)}, bf16[152,512]{1,0:T(8,128)(2,1)S(1)}, u32[]{:S(2)}, u32[]{:S(2)}) collective-permute-start(bf16[152,512]{1,0:T(8,128)(2,1)S(1)} %get-tuple-element.178), channel_id=1, source_target_pairs={{0,2},{1,3},{2,0},{3,1},{4,6},{5,7},{6,4},{7,5},{8,10},{9,11},{10,... | collective-permute-start | bytes 466952 | tf_op jit(solution)/shard_map/ppermute | solution.py:526
  43.6 1.8 %collective-permute-start.45 = (bf16[152,512]{1,0:T(8,128)(2,1)S(1)}, bf16[152,512]{1,0:T(8,128)(2,1)S(1)}, u32[]{:S(2)}, u32[]{:S(2)}) collective-permute-start(bf16[152,512]{1,0:T(8,128)(2,1)S(1)} %get-tuple-element.179), channel_id=1, source_target_pairs={{0,4},{1,5},{2,6},{3,7},{4,0},{5,1},{6,2},{7,3},{8,12},{9,13},{10,... | collective-permute-start | bytes 466952 | tf_op jit(solution)/shard_map/ppermute | solution.py:526
  45.5 1.5 %collective-permute-start.39 = (f32[40,128]{1,0:T(8,128)S(1)}, f32[40,128]{1,0:T(8,128)S(1)}, u32[]{:S(2)}, u32[]{:S(2)}) collective-permute-start(f32[40,128]{1,0:T(8,128)S(1)} %shard_map.111.refs_0_), channel_id=1, source_target_pairs={{0,8},{8,0},{16,24},{24,16},{1,9},{9,1},{17,25},{25,17},{2,10},{10... | collective-permute-start | bytes 61448 | tf_op jit(solution)/shard_map/ppermute | solution.py:526
  47.0 1.5 %collective-permute-start.40 = (f32[40,128]{1,0:T(8,128)S(1)}, f32[40,128]{1,0:T(8,128)S(1)}, u32[]{:S(2)}, u32[]{:S(2)}) collective-permute-start(f32[40,128]{1,0:T(8,128)S(1)} %shard_map.111.refs_0_), channel_id=1, source_target_pairs={{0,16},{8,24},{16,0},{24,8},{1,17},{9,25},{17,1},{25,9},{2,18},{10... | collective-permute-start | bytes 61448 | tf_op jit(solution)/shard_map/ppermute | solution.py:526
  49.3 2.5 %collective-permute-start.41 = (f32[40,128]{1,0:T(8,128)S(1)}, f32[40,128]{1,0:T(8,128)S(1)}, u32[]{:S(2)}, u32[]{:S(2)}) collective-permute-start(f32[40,128]{1,0:T(8,128)S(1)} %shard_map.111.refs_0_), channel_id=1, source_target_pairs={{0,24},{8,16},{16,8},{24,0},{1,25},{9,17},{17,9},{25,1},{2,26},{10... | collective-permute-start | bytes 61448 | tf_op jit(solution)/shard_map/ppermute | solution.py:526
  51.8 2.2 %collective-permute-done.41.refs_3_ = f32[40,128]{1,0:T(8,128)S(1)} collective-permute-done((f32[40,128]{1,0:T(8,128)S(1)}, f32[40,128]{1,0:T(8,128)S(1)}, u32[]{:S(2)}, u32[]{:S(2)}) %collective-permute-start.41) | collective-permute-done | bytes 20512 | tf_op jit(solution)/shard_map/ppermute | solution.py:526
  54.0 1.6 %shard_map.112 = (f32[128,256]{1,0:T(8,128)}, f32[8,128]{1,0:T(8,128)S(1)}, bf16[1152,1024]{1,0:T(8,128)(2,1)S(1)}) custom-call(s32[10]{0:T(128)S(1)} %pad_add_fusion.meta, bf16[128,256]{1,0:T(8,128)(2,1)S(1)} %get-tuple-element.165.even, bf16[128,256]{1,0:T(8,128)(2,1)S(1)} %get-tuple-element.166.odd, bf16[128,256]{1,0:T(8,128)(2,1)S(1)} %get-tuple-element.167.tile, ...), custom_call_target="tpu_custom_call" | custom-call | tf_op jit(solution)/shard_map/pallas_call | solution.py:649
  57.7 2.5 %shard_map.113 = (bf16[128,4096]{1,0:T(8,128)(2,1)}, bf16[128,1024]{1,0:T(8,128)(2,1)}) custom-call(s32[10]{0:T(128)S(1)} %pad_add_fusion.meta, bf16[1152,1024]{1,0:T(8,128)(2,1)S(1)} %get-tuple-element.176.kit, bf16[152,512]{1,0:T(8,128)(2,1)S(1)} %get-tuple-element.177.refs_0_, bf16[152,512]{1,0:T(8,128)(2,1)S(1)} %collective-permute-done.42.refs_1_, ...), custom_call_target="tpu_custom_call" | custom-call | tf_op jit(solution)/shard_map/pallas_call | solution.py:661
  (57 shorter events, 9.1 us)
Async XLA Ops:
  0.6 1.5 %collective-permute-start.24 = (s32[1,128]{1,0:T(1,128)}, s32[1,128]{1,0:T(1,128)S(1)}, u32[]{:S(2)}, u32[]{:S(2)}) collective-permute-start(s32[1,128]{1,0:T(1,128)} %block.1), channel_id=1, source_target_pairs={{0,1},{1,0},{2,3},{3,2},{4,5},{5,4},{6,7},{7,6},{8,9},{9,8},{10,11... | collective-permute-start | bytes 1544 | tf_op jit(solution)/shard_map/ppermute | solution.py:526
  2.1 5.0 %collective-permute-start.25 = (s32[2,128]{1,0:T(2,128)S(1)}, s32[2,128]{1,0:T(2,128)S(1)}, u32[]{:S(2)}, u32[]{:S(2)}) collective-permute-start(s32[2,128]{1,0:T(2,128)S(1)} %shard_map.104.first), channel_id=1, source_target_pairs={{0,2},{1,3},{2,0},{3,1},{4,6},{5,7},{6,4},{7,5},{8,10},{9,11},{10,... | collective-permute-start | bytes 3080 | tf_op jit(solution)/shard_map/ppermute | solution.py:526
  7.1 4.5 %collective-permute-start.26 = (s32[4,128]{1,0:T(4,128)S(1)}, s32[4,128]{1,0:T(4,128)S(1)}, u32[]{:S(2)}, u32[]{:S(2)}) collective-permute-start(s32[4,128]{1,0:T(4,128)S(1)} %shard_map.105.b0), channel_id=1, source_target_pairs={{0,4},{1,5},{2,6},{3,7},{4,0},{5,1},{6,2},{7,3},{8,12},{9,13},{10,... | collective-permute-start | bytes 6152 | tf_op jit(solution)/shard_map/ppermute | solution.py:526
  13.0 8.6 %collective-permute-start.27 = (bf16[136,512]{1,0:T(8,128)(2,1)S(1)}, bf16[136,512]{1,0:T(8,128)(2,1)S(1)}, u32[]{:S(2)}, u32[]{:S(2)}) collective-permute-start(bf16[136,512]{1,0:T(8,128)(2,1)S(1)} %get-tuple-element.141), channel_id=1, source_target_pairs={{0,6},{1,7},{2,4},{3,5},{4,2},{5,3},{6,0},{7,1},{8,14},{9,15},{10,... | collective-permute-start | bytes 417800 | tf_op jit(solution)/shard_map/ppermute | solution.py:526
  16.5 6.7 %collective-permute-start.29 = (bf16[136,512]{1,0:T(8,128)(2,1)S(1)}, bf16[136,512]{1,0:T(8,128)(2,1)S(1)}, u32[]{:S(2)}, u32[]{:S(2)}) collective-permute-start(bf16[136,512]{1,0:T(8,128)(2,1)S(1)} %get-tuple-element.155), channel_id=1, source_target_pairs={{0,2},{1,3},{2,0},{3,1},{4,6},{5,7},{6,4},{7,5},{8,10},{9,11},{10,... | collective-permute-start | bytes 417800 | tf_op jit(solution)/shard_map/ppermute | solution.py:526
  16.5 10.8 %collective-permute-start.31 = (bf16[136,512]{1,0:T(8,128)(2,1)S(1)}, bf16[136,512]{1,0:T(8,128)(2,1)S(1)}, u32[]{:S(2)}, u32[]{:S(2)}) collective-permute-start(bf16[136,512]{1,0:T(8,128)(2,1)S(1)} %get-tuple-element.156), channel_id=1, source_target_pairs={{0,4},{1,5},{2,6},{3,7},{4,0},{5,1},{6,2},{7,3},{8,12},{9,13},{10,... | collective-permute-start | bytes 417800 | tf_op jit(solution)/shard_map/ppermute | solution.py:526
  17.5 9.8 %collective-permute-start.28 = (bf16[136,512]{1,0:T(8,128)(2,1)S(1)}, bf16[136,512]{1,0:T(8,128)(2,1)S(1)}, u32[]{:S(2)}, u32[]{:S(2)}) collective-permute-start(bf16[136,512]{1,0:T(8,128)(2,1)S(1)} %get-tuple-element.154.refs_0_), channel_id=1, source_target_pairs={{0,1},{1,0},{2,3},{3,2},{4,5},{5,4},{6,7},{7,6},{8,9},{9,8},{10,11... | collective-permute-start | bytes 417800 | tf_op jit(solution)/shard_map/ppermute | solution.py:526
  21.6 5.7 %collective-permute-start.33 = (bf16[136,512]{1,0:T(8,128)(2,1)S(1)}, bf16[136,512]{1,0:T(8,128)(2,1)S(1)}, u32[]{:S(2)}, u32[]{:S(2)}) collective-permute-start(bf16[136,512]{1,0:T(8,128)(2,1)S(1)} %collective-permute-done.27.refs_6_), channel_id=1, source_target_pairs={{0,1},{1,0},{2,3},{3,2},{4,5},{5,4},{6,7},{7,6},{8,9},{9,8},{10,11... | collective-permute-start | bytes 417800 | tf_op jit(solution)/shard_map/ppermute | solution.py:526
  23.1 4.1 %collective-permute-start.30 = (bf16[136,512]{1,0:T(8,128)(2,1)S(1)}, bf16[136,512]{1,0:T(8,128)(2,1)S(1)}, u32[]{:S(2)}, u32[]{:S(2)}) collective-permute-start(bf16[136,512]{1,0:T(8,128)(2,1)S(1)} %collective-permute-done.29.refs_2_), channel_id=1, source_target_pairs={{0,1},{1,0},{2,3},{3,2},{4,5},{5,4},{6,7},{7,6},{8,9},{9,8},{10,11... | collective-permute-start | bytes 417800 | tf_op jit(solution)/shard_map/ppermute | solution.py:526
  27.2 1.4 %collective-permute-start.32 = (bf16[136,512]{1,0:T(8,128)(2,1)S(1)}, bf16[136,512]{1,0:T(8,128)(2,1)S(1)}, u32[]{:S(2)}, u32[]{:S(2)}) collective-permute-start(bf16[136,512]{1,0:T(8,128)(2,1)S(1)} %collective-permute-done.31.refs_4_), channel_id=1, source_target_pairs={{0,1},{1,0},{2,3},{3,2},{4,5},{5,4},{6,7},{7,6},{8,9},{9,8},{10,11... | collective-permute-start | bytes 417800 | tf_op jit(solution)/shard_map/ppermute | solution.py:526
  30.4 1.2 %collective-permute-start.34 = (f32[8,384]{1,0:T(8,128)S(1)}, f32[8,384]{1,0:T(8,128)S(1)}, u32[]{:S(2)}, u32[]{:S(2)}) collective-permute-start(f32[8,384]{1,0:T(8,128)S(1)} %get-tuple-element.162), channel_id=1, source_target_pairs={{0,1},{1,0},{2,3},{3,2},{4,5},{5,4},{6,7},{7,6},{8,9},{9,8},{10,11... | collective-permute-start | bytes 36872 | tf_op jit(solution)/shard_map/ppermute | solution.py:526
  31.7 5.6 %collective-permute-start.35 = (f32[8,384]{1,0:T(8,128)S(1)}, f32[8,384]{1,0:T(8,128)S(1)}, u32[]{:S(2)}, u32[]{:S(2)}) collective-permute-start(f32[8,384]{1,0:T(8,128)S(1)} %stack.10.st0), channel_id=1, source_target_pairs={{0,6},{1,7},{2,4},{3,5},{4,2},{5,3},{6,0},{7,1},{8,14},{9,15},{10,... | collective-permute-start | bytes 36872 | tf_op jit(solution)/shard_map/ppermute | solution.py:526
  34.4 4.6 %collective-permute-start.36 = (f32[8,384]{1,0:T(8,128)S(1)}, f32[8,384]{1,0:T(8,128)S(1)}, u32[]{:S(2)}, u32[]{:S(2)}) collective-permute-start(f32[8,384]{1,0:T(8,128)S(1)} %stack.10.st0), channel_id=1, source_target_pairs={{0,4},{1,5},{2,6},{3,7},{4,0},{5,1},{6,2},{7,3},{8,12},{9,13},{10,... | collective-permute-start | bytes 36872 | tf_op jit(solution)/shard_map/ppermute | solution.py:526
  34.4 4.6 %collective-permute-start.37 = (f32[8,384]{1,0:T(8,128)S(1)}, f32[8,384]{1,0:T(8,128)S(1)}, u32[]{:S(2)}, u32[]{:S(2)}) collective-permute-start(f32[8,384]{1,0:T(8,128)S(1)} %stack.10.st0), channel_id=1, source_target_pairs={{0,2},{1,3},{2,0},{3,1},{4,6},{5,7},{6,4},{7,5},{8,10},{9,11},{10,... | collective-permute-start | bytes 36872 | tf_op jit(solution)/shard_map/ppermute | solution.py:526
  41.0 14.7 %collective-permute-start.38 = (bf16[152,512]{1,0:T(8,128)(2,1)S(1)}, bf16[152,512]{1,0:T(8,128)(2,1)S(1)}, u32[]{:S(2)}, u32[]{:S(2)}) collective-permute-start(bf16[152,512]{1,0:T(8,128)(2,1)S(1)} %get-tuple-element.164), channel_id=1, source_target_pairs={{0,6},{1,7},{2,4},{3,5},{4,2},{5,3},{6,0},{7,1},{8,14},{9,15},{10,... | collective-permute-start | bytes 466952 | tf_op jit(solution)/shard_map/ppermute | solution.py:526
  42.5 13.3 %collective-permute-start.43 = (bf16[152,512]{1,0:T(8,128)(2,1)S(1)}, bf16[152,512]{1,0:T(8,128)(2,1)S(1)}, u32[]{:S(2)}, u32[]{:S(2)}) collective-permute-start(bf16[152,512]{1,0:T(8,128)(2,1)S(1)} %get-tuple-element.178), channel_id=1, source_target_pairs={{0,2},{1,3},{2,0},{3,1},{4,6},{5,7},{6,4},{7,5},{8,10},{9,11},{10,... | collective-permute-start | bytes 466952 | tf_op jit(solution)/shard_map/ppermute | solution.py:526
  43.6 12.7 %collective-permute-start.45 = (bf16[152,512]{1,0:T(8,128)(2,1)S(1)}, bf16[152,512]{1,0:T(8,128)(2,1)S(1)}, u32[]{:S(2)}, u32[]{:S(2)}) collective-permute-start(bf16[152,512]{1,0:T(8,128)(2,1)S(1)} %get-tuple-element.179), channel_id=1, source_target_pairs={{0,4},{1,5},{2,6},{3,7},{4,0},{5,1},{6,2},{7,3},{8,12},{9,13},{10,... | collective-permute-start | bytes 466952 | tf_op jit(solution)/shard_map/ppermute | solution.py:526
  45.5 3.8 %collective-permute-start.39 = (f32[40,128]{1,0:T(8,128)S(1)}, f32[40,128]{1,0:T(8,128)S(1)}, u32[]{:S(2)}, u32[]{:S(2)}) collective-permute-start(f32[40,128]{1,0:T(8,128)S(1)} %shard_map.111.refs_0_), channel_id=1, source_target_pairs={{0,8},{8,0},{16,24},{24,16},{1,9},{9,1},{17,25},{25,17},{2,10},{10... | collective-permute-start | bytes 61448 | tf_op jit(solution)/shard_map/ppermute | solution.py:526
  47.0 4.8 %collective-permute-start.40 = (f32[40,128]{1,0:T(8,128)S(1)}, f32[40,128]{1,0:T(8,128)S(1)}, u32[]{:S(2)}, u32[]{:S(2)}) collective-permute-start(f32[40,128]{1,0:T(8,128)S(1)} %shard_map.111.refs_0_), channel_id=1, source_target_pairs={{0,16},{8,24},{16,0},{24,8},{1,17},{9,25},{17,1},{25,9},{2,18},{10... | collective-permute-start | bytes 61448 | tf_op jit(solution)/shard_map/ppermute | solution.py:526
  49.3 4.7 %collective-permute-start.41 = (f32[40,128]{1,0:T(8,128)S(1)}, f32[40,128]{1,0:T(8,128)S(1)}, u32[]{:S(2)}, u32[]{:S(2)}) collective-permute-start(f32[40,128]{1,0:T(8,128)S(1)} %shard_map.111.refs_0_), channel_id=1, source_target_pairs={{0,24},{8,16},{16,8},{24,0},{1,25},{9,17},{17,9},{25,1},{2,26},{10... | collective-permute-start | bytes 61448 | tf_op jit(solution)/shard_map/ppermute | solution.py:526
  51.8 5.7 %collective-permute-start.42 = (bf16[152,512]{1,0:T(8,128)(2,1)S(1)}, bf16[152,512]{1,0:T(8,128)(2,1)S(1)}, u32[]{:S(2)}, u32[]{:S(2)}) collective-permute-start(bf16[152,512]{1,0:T(8,128)(2,1)S(1)} %get-tuple-element.177.refs_0_), channel_id=1, source_target_pairs={{0,1},{1,0},{2,3},{3,2},{4,5},{5,4},{6,7},{7,6},{8,9},{9,8},{10,11... | collective-permute-start | bytes 466952 | tf_op jit(solution)/shard_map/ppermute | solution.py:526
  55.7 1.8 %collective-permute-start.47 = (bf16[152,512]{1,0:T(8,128)(2,1)S(1)}, bf16[152,512]{1,0:T(8,128)(2,1)S(1)}, u32[]{:S(2)}, u32[]{:S(2)}) collective-permute-start(bf16[152,512]{1,0:T(8,128)(2,1)S(1)} %collective-permute-done.38.refs_6_), channel_id=1, source_target_pairs={{0,1},{1,0},{2,3},{3,2},{4,5},{5,4},{6,7},{7,6},{8,9},{9,8},{10,11... | collective-permute-start | bytes 466952 | tf_op jit(solution)/shard_map/ppermute | solution.py:526
  55.8 1.8 %collective-permute-start.44 = (bf16[152,512]{1,0:T(8,128)(2,1)S(1)}, bf16[152,512]{1,0:T(8,128)(2,1)S(1)}, u32[]{:S(2)}, u32[]{:S(2)}) collective-permute-start(bf16[152,512]{1,0:T(8,128)(2,1)S(1)} %collective-permute-done.43.refs_2_), channel_id=1, source_target_pairs={{0,1},{1,0},{2,3},{3,2},{4,5},{5,4},{6,7},{7,6},{8,9},{9,8},{10,11... | collective-permute-start | bytes 466952 | tf_op jit(solution)/shard_map/ppermute | solution.py:526
  56.3 1.4 %collective-permute-start.46 = (bf16[152,512]{1,0:T(8,128)(2,1)S(1)}, bf16[152,512]{1,0:T(8,128)(2,1)S(1)}, u32[]{:S(2)}, u32[]{:S(2)}) collective-permute-start(bf16[152,512]{1,0:T(8,128)(2,1)S(1)} %collective-permute-done.45.refs_4_), channel_id=1, source_target_pairs={{0,1},{1,0},{2,3},{3,2},{4,5},{5,4},{6,7},{7,6},{8,9},{9,8},{10,11... | collective-permute-start | bytes 466952 | tf_op jit(solution)/shard_map/ppermute | solution.py:526
  (8 other events, 62.2 us)

commit v8 on v7

--- a/solution.py
+++ b/solution.py
@@ -527,13 +527,13 @@
 
 
 def exchange(message, between):
-    far = [swap(own, "seq", 2 * d) for d, own in enumerate(message) if d > 0]
+    order = (1, 3, 2)
+    far = {d: swap(message[d], "seq", 2 * d) for d in order}
     made = between()
-    blocks = [message[0], swap(message[0], "seq", 1)]
-    for d, own in enumerate(far):
-        if d == len(far) - 1:
-            own, made = lax.optimization_barrier((own, made))
-        blocks += [own, swap(own, "seq", 1)]
+    far[0] = message[0]
+    far[order[-1]], made = lax.optimization_barrier((far[order[-1]], made))
+    near = {d: swap(far[d], "seq", 1) for d in (0, *order)}
+    blocks = [block for d in range(len(message)) for block in (far[d], near[d])]
     return blocks, made
 
 

time: 60.8 us -> 59.8 us (0.984)
  waiting for transfers between devices: 16.9 us -> 15.3 us
    ppermute x24, waiting for transfers between devices: 16.9 us -> 15.3 us  [swap(): lax.ppermute(block, axis, [(i, i ^ distance) for i in range(lax.axis_size...]
    ppermute x24, starting transfers between devices: 25.8 us -> 26.4 us  [swap(): lax.ppermute(block, axis, [(i, i ^ distance) for i in range(lax.axis_size...]
  transfers between devices with their start and end apart: 24 -> 24, of which waited for: 12 -> 13; matrix products, arithmetic and copies ran while one was open for 2% -> 2% of each run, Pallas kernels for 12% -> 12%
where the time goes in v8:
time: 59.8 us; the launch traced here: 59.6 us
  starting transfers between devices  26.4 us (44%)
  waiting for transfers between devices  15.3 us (26%)
  Pallas kernels  14.7 us (25%)
  between operations  1.66 us (3%)
  other arithmetic  0.74 us (1%)
    ppermute x24, starting transfers between devices, swap(): lax.ppermute(block, axis, [(i, i ^ distance) for i in range(lax.axis_size...  26.4 us
    ppermute x24, waiting for transfers between devices, swap(): lax.ppermute(block, axis, [(i, i ^ distance) for i in range(lax.axis_size...  15.3 us
    pallas_call x1, Pallas kernels, index(): kernel_call(functools.partial(index_kernel, (n, rows, slots, pool)), (sds...  2.55 us
    pallas_call x1, Pallas kernels, finish(): kernel_call(functools.partial(finish_kernel, (n, rows)), (sds((rows, PART...  2.53 us
    pallas_call x1, Pallas kernels, prep(): kernel_call(prep_kernel, (sds(qkvu.shape, BF16), sds((below, wide), BF16)...  2.17 us
    pallas_call x1, Pallas kernels, passes(): kernel_call(functools.partial(backward_kernel, (n, rows, pool)), (sds((po...  1.98 us
    pallas_call x1, Pallas kernels, passes(): kernel_call(functools.partial(forward_kernel, (n, rows, slots, per)), (sd...  1.79 us
    pallas_call x1, Pallas kernels, group_sums(): kernel_call(total_kernel, (sds((head_dim, width // groups), F32), sds((8,...  1.59 us
  transfers between devices with their start and end apart: 24, of which 13 were waited for; matrix products, arithmetic and copies ran while one was open for 2% of the time, Pallas kernels for 12%

profile of v8, /device:TPU:0, one launch (start us, length us, event | category | flops | bytes accessed | tf_op | source)
XLA Modules:
  0.0 59.6 jit_solution(9894234465723840336)
XLA Ops:
  2.1 2.9 %collective-permute-start.25 = (s32[2,128]{1,0:T(2,128)S(1)}, s32[2,128]{1,0:T(2,128)S(1)}, u32[]{:S(2)}, u32[]{:S(2)}) collective-permute-start(s32[2,128]{1,0:T(2,128)S(1)} %shard_map.104.first), channel_id=1, source_target_pairs={{0,2},{1,3},{2,0},{3,1},{4,6},{5,7},{6,4},{7,5},{8,10},{9,11},{10,... | collective-permute-start | bytes 3080 | tf_op jit(solution)/shard_map/ppermute | solution.py:526
  5.0 2.2 %shard_map.106 = (bf16[128,4096]{1,0:T(8,128)(2,1)S(1)}, bf16[16,512]{1,0:T(8,128)(2,1)S(1)}, bf16[128,128]{1,0:T(8,128)(2,1)S(1)}) custom-call(s32[4]{0:T(128)} %ids.1, s32[1,128]{1,0:T(1,128)} %send.1, bf16[32,128]{1,0:T(8,128)(2,1)} %bitcast.5, bf16[512,1024]{1,0:T(8,128)(2,1)} %table.1, bf16[128,4096]{1,0:T(8,128)(2,1)} %qkvu.1), custom_call_target="tpu_custom_call" | custom-call | tf_op jit(solution)/shard_map/pallas_call | solution.py:583
  7.2 2.6 %collective-permute-start.26 = (s32[4,128]{1,0:T(4,128)S(1)}, s32[4,128]{1,0:T(4,128)S(1)}, u32[]{:S(2)}, u32[]{:S(2)}) collective-permute-start(s32[4,128]{1,0:T(4,128)S(1)} %shard_map.105.b0), channel_id=1, source_target_pairs={{0,4},{1,5},{2,6},{3,7},{4,0},{5,1},{6,2},{7,3},{8,12},{9,13},{10,... | collective-permute-start | bytes 6152 | tf_op jit(solution)/shard_map/ppermute | solution.py:526
  10.6 1.2 %collective-permute-done.26.b1 = s32[4,128]{1,0:T(4,128)S(1)} collective-permute-done((s32[4,128]{1,0:T(4,128)S(1)}, s32[4,128]{1,0:T(4,128)S(1)}, u32[]{:S(2)}, u32[]{:S(2)}) %collective-permute-start.26) | collective-permute-done | bytes 2080 | tf_op jit(solution)/shard_map/ppermute | solution.py:526
  11.7 1.3 %shard_map.107 = (bf16[136,512]{1,0:T(8,128)(2,1)S(1)}, bf16[136,512]{1,0:T(8,128)(2,1)S(1)}, bf16[136,512]{1,0:T(8,128)(2,1)S(1)}, bf16[136,512]{1,0:T(8,128)(2,1)S(1)}, bf16[128,128]{1,0:T(8,128)(2,1)S(1)}) custom-call(s32[10]{0:T(128)S(1)} %pad_add_fusion.meta, s32[4,128]{1,0:T(4,128)S(1)} %shard_map.105.b0, s32[4,128]{1,0:T(4,128)S(1)} %collective-permute-done.26.b1, ...), custom_call_target="tpu_custom_call" | custom-call | tf_op jit(solution)/shard_map/pallas_call | solution.py:597
  13.1 2.6 %collective-permute-start.27 = (bf16[136,512]{1,0:T(8,128)(2,1)S(1)}, bf16[136,512]{1,0:T(8,128)(2,1)S(1)}, u32[]{:S(2)}, u32[]{:S(2)}) collective-permute-start(bf16[136,512]{1,0:T(8,128)(2,1)S(1)} %get-tuple-element.141), channel_id=1, source_target_pairs={{0,4},{1,5},{2,6},{3,7},{4,0},{5,1},{6,2},{7,3},{8,12},{9,13},{10,... | collective-permute-start | bytes 417800 | tf_op jit(solution)/shard_map/ppermute | solution.py:526
  15.7 1.3 %collective-permute-start.29 = (bf16[136,512]{1,0:T(8,128)(2,1)S(1)}, bf16[136,512]{1,0:T(8,128)(2,1)S(1)}, u32[]{:S(2)}, u32[]{:S(2)}) collective-permute-start(bf16[136,512]{1,0:T(8,128)(2,1)S(1)} %get-tuple-element.155), channel_id=1, source_target_pairs={{0,2},{1,3},{2,0},{3,1},{4,6},{5,7},{6,4},{7,5},{8,10},{9,11},{10,... | collective-permute-start | bytes 417800 | tf_op jit(solution)/shard_map/ppermute | solution.py:526
  17.5 2.6 %shard_map.108 = (bf16[384,512]{1,0:T(8,128)(2,1)S(1)}, bf16[608,384]{1,0:T(8,128)(2,1)S(1)}, bf16[128,256]{1,0:T(8,128)(2,1)S(1)}, bf16[128,256]{1,0:T(8,128)(2...) custom-call(s32[10]{0:T(128)S(1)} %pad_add_fusion.meta, ...), custom_call_target="tpu_custom_call" | custom-call | tf_op jit(solution)/shard_map/pallas_call | solution.py:605
  20.1 5.1 %collective-permute-done.27.refs_4_ = bf16[136,512]{1,0:T(8,128)(2,1)S(1)} collective-permute-done((bf16[136,512]{1,0:T(8,128)(2,1)S(1)}, bf16[136,512]{1,0:T(8,128)(2,1)S(1)}, u32[]{:S(2)}, u32[]{:S(2)}) %collective-permute-start.27) | collective-permute-done | bytes 139296 | tf_op jit(solution)/shard_map/ppermute | solution.py:526
  27.2 1.8 %shard_map.109 = (bf16[384,512]{1,0:T(8,128)(2,1)S(1)}, bf16[384,384]{1,0:T(8,128)(2,1)S(1)}, f32[384,128]{1,0:T(8,128)S(1)}, f32[8,384]{1,0:T(8,128)S(1)}, bf16...) custom-call(s32[10]{0:T(128)S(1)} %pad_add_fusion.meta, ...), custom_call_target="tpu_custom_call" | custom-call | tf_op jit(solution)/shard_map/pallas_call | solution.py:622
  29.4 0.9 %collective-permute-done.34 = f32[8,384]{1,0:T(8,128)S(1)} collective-permute-done((f32[8,384]{1,0:T(8,128)S(1)}, f32[8,384]{1,0:T(8,128)S(1)}, u32[]{:S(2)}, u32[]{:S(2)}) %collective-permute-start.34) | collective-permute-done | bytes 12320 | tf_op jit(solution)/shard_map/ppermute | solution.py:526
  30.3 3.1 %collective-permute-start.35 = (f32[8,384]{1,0:T(8,128)S(1)}, f32[8,384]{1,0:T(8,128)S(1)}, u32[]{:S(2)}, u32[]{:S(2)}) collective-permute-start(f32[8,384]{1,0:T(8,128)S(1)} %stack.10.st0), channel_id=1, source_target_pairs={{0,6},{1,7},{2,4},{3,5},{4,2},{5,3},{6,0},{7,1},{8,14},{9,15},{10,... | collective-permute-start | bytes 36872 | tf_op jit(solution)/shard_map/ppermute | solution.py:526
  33.8 1.0 %collective-permute-start.37 = (f32[8,384]{1,0:T(8,128)S(1)}, f32[8,384]{1,0:T(8,128)S(1)}, u32[]{:S(2)}, u32[]{:S(2)}) collective-permute-start(f32[8,384]{1,0:T(8,128)S(1)} %stack.10.st0), channel_id=1, source_target_pairs={{0,2},{1,3},{2,0},{3,1},{4,6},{5,7},{6,4},{7,5},{8,10},{9,11},{10,... | collective-permute-start | bytes 36872 | tf_op jit(solution)/shard_map/ppermute | solution.py:526
  34.8 1.1 %collective-permute-done.35.st1 = f32[8,384]{1,0:T(8,128)S(1)} collective-permute-done((f32[8,384]{1,0:T(8,128)S(1)}, f32[8,384]{1,0:T(8,128)S(1)}, u32[]{:S(2)}, u32[]{:S(2)}) %collective-permute-start.35) | collective-permute-done | bytes 12320 | tf_op jit(solution)/shard_map/ppermute | solution.py:526
  35.9 2.1 %collective-permute-done.36.st2 = f32[8,384]{1,0:T(8,128)S(1)} collective-permute-done((f32[8,384]{1,0:T(8,128)S(1)}, f32[8,384]{1,0:T(8,128)S(1)}, u32[]{:S(2)}, u32[]{:S(2)}) %collective-permute-start.36) | collective-permute-done | bytes 12320 | tf_op jit(solution)/shard_map/ppermute | solution.py:526
  38.0 2.0 %shard_map.110 = (bf16[152,512]{1,0:T(8,128)(2,1)S(1)}, bf16[152,512]{1,0:T(8,128)(2,1)S(1)}, bf16[152,512]{1,0:T(8,128)(2,1)S(1)}, bf16[152,512]{1,0:T(8,128)(2,1)S(1)}, bf16[384,128]{1,0:T(8,128)(2,1)S(1)}) custom-call(s32[10]{0:T(128)S(1)} %pad_add_fusion.meta, bf16[384,512]{1,0:T(8,128)(2,1)S(1)} %get-tuple-element.158.compact, ...), custom_call_target="tpu_custom_call" | custom-call | tf_op jit(solution)/shard_map/pallas_call | solution.py:639
  40.0 2.1 %collective-permute-start.38 = (bf16[152,512]{1,0:T(8,128)(2,1)S(1)}, bf16[152,512]{1,0:T(8,128)(2,1)S(1)}, u32[]{:S(2)}, u32[]{:S(2)}) collective-permute-start(bf16[152,512]{1,0:T(8,128)(2,1)S(1)} %get-tuple-element.164), channel_id=1, source_target_pairs={{0,4},{1,5},{2,6},{3,7},{4,0},{5,1},{6,2},{7,3},{8,12},{9,13},{10,... | collective-permute-start | bytes 466952 | tf_op jit(solution)/shard_map/ppermute | solution.py:526
  42.7 1.7 %collective-permute-start.46 = (bf16[152,512]{1,0:T(8,128)(2,1)S(1)}, bf16[152,512]{1,0:T(8,128)(2,1)S(1)}, u32[]{:S(2)}, u32[]{:S(2)}) collective-permute-start(bf16[152,512]{1,0:T(8,128)(2,1)S(1)} %get-tuple-element.180), channel_id=1, source_target_pairs={{0,6},{1,7},{2,4},{3,5},{4,2},{5,3},{6,0},{7,1},{8,14},{9,15},{10,... | collective-permute-start | bytes 466952 | tf_op jit(solution)/shard_map/ppermute | solution.py:526
  44.6 1.5 %collective-permute-start.39 = (f32[40,128]{1,0:T(8,128)S(1)}, f32[40,128]{1,0:T(8,128)S(1)}, u32[]{:S(2)}, u32[]{:S(2)}) collective-permute-start(f32[40,128]{1,0:T(8,128)S(1)} %shard_map.111.refs_0_), channel_id=1, source_target_pairs={{0,8},{8,0},{16,24},{24,16},{1,9},{9,1},{17,25},{25,17},{2,10},{10... | collective-permute-start | bytes 61448 | tf_op jit(solution)/shard_map/ppermute | solution.py:526
  46.1 1.5 %collective-permute-start.40 = (f32[40,128]{1,0:T(8,128)S(1)}, f32[40,128]{1,0:T(8,128)S(1)}, u32[]{:S(2)}, u32[]{:S(2)}) collective-permute-start(f32[40,128]{1,0:T(8,128)S(1)} %shard_map.111.refs_0_), channel_id=1, source_target_pairs={{0,16},{8,24},{16,0},{24,8},{1,17},{9,25},{17,1},{25,9},{2,18},{10... | collective-permute-start | bytes 61448 | tf_op jit(solution)/shard_map/ppermute | solution.py:526
  48.4 2.5 %collective-permute-start.41 = (f32[40,128]{1,0:T(8,128)S(1)}, f32[40,128]{1,0:T(8,128)S(1)}, u32[]{:S(2)}, u32[]{:S(2)}) collective-permute-start(f32[40,128]{1,0:T(8,128)S(1)} %shard_map.111.refs_0_), channel_id=1, source_target_pairs={{0,24},{8,16},{16,8},{24,0},{1,25},{9,17},{17,9},{25,1},{2,26},{10... | collective-permute-start | bytes 61448 | tf_op jit(solution)/shard_map/ppermute | solution.py:526
  50.9 2.2 %collective-permute-done.41.refs_3_ = f32[40,128]{1,0:T(8,128)S(1)} collective-permute-done((f32[40,128]{1,0:T(8,128)S(1)}, f32[40,128]{1,0:T(8,128)S(1)}, u32[]{:S(2)}, u32[]{:S(2)}) %collective-permute-start.41) | collective-permute-done | bytes 20512 | tf_op jit(solution)/shard_map/ppermute | solution.py:526
  53.1 1.6 %shard_map.112 = (f32[128,256]{1,0:T(8,128)}, f32[8,128]{1,0:T(8,128)S(1)}, bf16[1152,1024]{1,0:T(8,128)(2,1)S(1)}) custom-call(s32[10]{0:T(128)S(1)} %pad_add_fusion.meta, bf16[128,256]{1,0:T(8,128)(2,1)S(1)} %get-tuple-element.165.even, bf16[128,256]{1,0:T(8,128)(2,1)S(1)} %get-tuple-element.166.odd, bf16[128,256]{1,0:T(8,128)(2,1)S(1)} %get-tuple-element.167.tile, ...), custom_call_target="tpu_custom_call" | custom-call | tf_op jit(solution)/shard_map/pallas_call | solution.py:649
  56.7 2.5 %shard_map.113 = (bf16[128,4096]{1,0:T(8,128)(2,1)}, bf16[128,1024]{1,0:T(8,128)(2,1)}) custom-call(s32[10]{0:T(128)S(1)} %pad_add_fusion.meta, bf16[1152,1024]{1,0:T(8,128)(2,1)S(1)} %get-tuple-element.176.kit, bf16[152,512]{1,0:T(8,128)(2,1)S(1)} %get-tuple-element.177.refs_0_, bf16[152,512]{1,0:T(8,128)(2,1)S(1)} %collective-permute-done.42.refs_1_, ...), custom_call_target="tpu_custom_call" | custom-call | tf_op jit(solution)/shard_map/pallas_call | solution.py:661
  (57 shorter events, 8.6 us)
Async XLA Ops:
  0.6 1.5 %collective-permute-start.24 = (s32[1,128]{1,0:T(1,128)}, s32[1,128]{1,0:T(1,128)S(1)}, u32[]{:S(2)}, u32[]{:S(2)}) collective-permute-start(s32[1,128]{1,0:T(1,128)} %block.1), channel_id=1, source_target_pairs={{0,1},{1,0},{2,3},{3,2},{4,5},{5,4},{6,7},{7,6},{8,9},{9,8},{10,11... | collective-permute-start | bytes 1544 | tf_op jit(solution)/shard_map/ppermute | solution.py:526
  2.1 5.1 %collective-permute-start.25 = (s32[2,128]{1,0:T(2,128)S(1)}, s32[2,128]{1,0:T(2,128)S(1)}, u32[]{:S(2)}, u32[]{:S(2)}) collective-permute-start(s32[2,128]{1,0:T(2,128)S(1)} %shard_map.104.first), channel_id=1, source_target_pairs={{0,2},{1,3},{2,0},{3,1},{4,6},{5,7},{6,4},{7,5},{8,10},{9,11},{10,... | collective-permute-start | bytes 3080 | tf_op jit(solution)/shard_map/ppermute | solution.py:526
  7.2 4.5 %collective-permute-start.26 = (s32[4,128]{1,0:T(4,128)S(1)}, s32[4,128]{1,0:T(4,128)S(1)}, u32[]{:S(2)}, u32[]{:S(2)}) collective-permute-start(s32[4,128]{1,0:T(4,128)S(1)} %shard_map.105.b0), channel_id=1, source_target_pairs={{0,4},{1,5},{2,6},{3,7},{4,0},{5,1},{6,2},{7,3},{8,12},{9,13},{10,... | collective-permute-start | bytes 6152 | tf_op jit(solution)/shard_map/ppermute | solution.py:526
  13.1 12.1 %collective-permute-start.27 = (bf16[136,512]{1,0:T(8,128)(2,1)S(1)}, bf16[136,512]{1,0:T(8,128)(2,1)S(1)}, u32[]{:S(2)}, u32[]{:S(2)}) collective-permute-start(bf16[136,512]{1,0:T(8,128)(2,1)S(1)} %get-tuple-element.141), channel_id=1, source_target_pairs={{0,4},{1,5},{2,6},{3,7},{4,0},{5,1},{6,2},{7,3},{8,12},{9,13},{10,... | collective-permute-start | bytes 417800 | tf_op jit(solution)/shard_map/ppermute | solution.py:526
  15.7 10.0 %collective-permute-start.29 = (bf16[136,512]{1,0:T(8,128)(2,1)S(1)}, bf16[136,512]{1,0:T(8,128)(2,1)S(1)}, u32[]{:S(2)}, u32[]{:S(2)}) collective-permute-start(bf16[136,512]{1,0:T(8,128)(2,1)S(1)} %get-tuple-element.155), channel_id=1, source_target_pairs={{0,2},{1,3},{2,0},{3,1},{4,6},{5,7},{6,4},{7,5},{8,10},{9,11},{10,... | collective-permute-start | bytes 417800 | tf_op jit(solution)/shard_map/ppermute | solution.py:526
  17.0 8.7 %collective-permute-start.32 = (bf16[136,512]{1,0:T(8,128)(2,1)S(1)}, bf16[136,512]{1,0:T(8,128)(2,1)S(1)}, u32[]{:S(2)}, u32[]{:S(2)}) collective-permute-start(bf16[136,512]{1,0:T(8,128)(2,1)S(1)} %get-tuple-element.157), channel_id=1, source_target_pairs={{0,6},{1,7},{2,4},{3,5},{4,2},{5,3},{6,0},{7,1},{8,14},{9,15},{10,... | collective-permute-start | bytes 417800 | tf_op jit(solution)/shard_map/ppermute | solution.py:526
  17.5 8.7 %collective-permute-start.28 = (bf16[136,512]{1,0:T(8,128)(2,1)S(1)}, bf16[136,512]{1,0:T(8,128)(2,1)S(1)}, u32[]{:S(2)}, u32[]{:S(2)}) collective-permute-start(bf16[136,512]{1,0:T(8,128)(2,1)S(1)} %get-tuple-element.154.refs_0_), channel_id=1, source_target_pairs={{0,1},{1,0},{2,3},{3,2},{4,5},{5,4},{6,7},{7,6},{8,9},{9,8},{10,11... | collective-permute-start | bytes 417800 | tf_op jit(solution)/shard_map/ppermute | solution.py:526
  25.2 1.4 %collective-permute-start.31 = (bf16[136,512]{1,0:T(8,128)(2,1)S(1)}, bf16[136,512]{1,0:T(8,128)(2,1)S(1)}, u32[]{:S(2)}, u32[]{:S(2)}) collective-permute-start(bf16[136,512]{1,0:T(8,128)(2,1)S(1)} %collective-permute-done.27.refs_4_), channel_id=1, source_target_pairs={{0,1},{1,0},{2,3},{3,2},{4,5},{5,4},{6,7},{7,6},{8,9},{9,8},{10,11... | collective-permute-start | bytes 417800 | tf_op jit(solution)/shard_map/ppermute | solution.py:526
  25.7 1.4 %collective-permute-start.30 = (bf16[136,512]{1,0:T(8,128)(2,1)S(1)}, bf16[136,512]{1,0:T(8,128)(2,1)S(1)}, u32[]{:S(2)}, u32[]{:S(2)}) collective-permute-start(bf16[136,512]{1,0:T(8,128)(2,1)S(1)} %collective-permute-done.29.refs_2_), channel_id=1, source_target_pairs={{0,1},{1,0},{2,3},{3,2},{4,5},{5,4},{6,7},{7,6},{8,9},{9,8},{10,11... | collective-permute-start | bytes 417800 | tf_op jit(solution)/shard_map/ppermute | solution.py:526
  25.7 1.6 %collective-permute-start.33 = (bf16[136,512]{1,0:T(8,128)(2,1)S(1)}, bf16[136,512]{1,0:T(8,128)(2,1)S(1)}, u32[]{:S(2)}, u32[]{:S(2)}) collective-permute-start(bf16[136,512]{1,0:T(8,128)(2,1)S(1)} %collective-permute-done.32.refs_6_), channel_id=1, source_target_pairs={{0,1},{1,0},{2,3},{3,2},{4,5},{5,4},{6,7},{7,6},{8,9},{9,8},{10,11... | collective-permute-start | bytes 417800 | tf_op jit(solution)/shard_map/ppermute | solution.py:526
  29.0 1.2 %collective-permute-start.34 = (f32[8,384]{1,0:T(8,128)S(1)}, f32[8,384]{1,0:T(8,128)S(1)}, u32[]{:S(2)}, u32[]{:S(2)}) collective-permute-start(f32[8,384]{1,0:T(8,128)S(1)} %get-tuple-element.162), channel_id=1, source_target_pairs={{0,1},{1,0},{2,3},{3,2},{4,5},{5,4},{6,7},{7,6},{8,9},{9,8},{10,11... | collective-permute-start | bytes 36872 | tf_op jit(solution)/shard_map/ppermute | solution.py:526
  30.3 5.6 %collective-permute-start.35 = (f32[8,384]{1,0:T(8,128)S(1)}, f32[8,384]{1,0:T(8,128)S(1)}, u32[]{:S(2)}, u32[]{:S(2)}) collective-permute-start(f32[8,384]{1,0:T(8,128)S(1)} %stack.10.st0), channel_id=1, source_target_pairs={{0,6},{1,7},{2,4},{3,5},{4,2},{5,3},{6,0},{7,1},{8,14},{9,15},{10,... | collective-permute-start | bytes 36872 | tf_op jit(solution)/shard_map/ppermute | solution.py:526
  33.4 4.6 %collective-permute-start.36 = (f32[8,384]{1,0:T(8,128)S(1)}, f32[8,384]{1,0:T(8,128)S(1)}, u32[]{:S(2)}, u32[]{:S(2)}) collective-permute-start(f32[8,384]{1,0:T(8,128)S(1)} %stack.10.st0), channel_id=1, source_target_pairs={{0,4},{1,5},{2,6},{3,7},{4,0},{5,1},{6,2},{7,3},{8,12},{9,13},{10,... | collective-permute-start | bytes 36872 | tf_op jit(solution)/shard_map/ppermute | solution.py:526
  33.8 4.2 %collective-permute-start.37 = (f32[8,384]{1,0:T(8,128)S(1)}, f32[8,384]{1,0:T(8,128)S(1)}, u32[]{:S(2)}, u32[]{:S(2)}) collective-permute-start(f32[8,384]{1,0:T(8,128)S(1)} %stack.10.st0), channel_id=1, source_target_pairs={{0,2},{1,3},{2,0},{3,1},{4,6},{5,7},{6,4},{7,5},{8,10},{9,11},{10,... | collective-permute-start | bytes 36872 | tf_op jit(solution)/shard_map/ppermute | solution.py:526
  40.0 14.7 %collective-permute-start.38 = (bf16[152,512]{1,0:T(8,128)(2,1)S(1)}, bf16[152,512]{1,0:T(8,128)(2,1)S(1)}, u32[]{:S(2)}, u32[]{:S(2)}) collective-permute-start(bf16[152,512]{1,0:T(8,128)(2,1)S(1)} %get-tuple-element.164), channel_id=1, source_target_pairs={{0,4},{1,5},{2,6},{3,7},{4,0},{5,1},{6,2},{7,3},{8,12},{9,13},{10,... | collective-permute-start | bytes 466952 | tf_op jit(solution)/shard_map/ppermute | solution.py:526
  42.1 12.8 %collective-permute-start.43 = (bf16[152,512]{1,0:T(8,128)(2,1)S(1)}, bf16[152,512]{1,0:T(8,128)(2,1)S(1)}, u32[]{:S(2)}, u32[]{:S(2)}) collective-permute-start(bf16[152,512]{1,0:T(8,128)(2,1)S(1)} %get-tuple-element.178), channel_id=1, source_target_pairs={{0,2},{1,3},{2,0},{3,1},{4,6},{5,7},{6,4},{7,5},{8,10},{9,11},{10,... | collective-permute-start | bytes 466952 | tf_op jit(solution)/shard_map/ppermute | solution.py:526
  42.7 12.6 %collective-permute-start.46 = (bf16[152,512]{1,0:T(8,128)(2,1)S(1)}, bf16[152,512]{1,0:T(8,128)(2,1)S(1)}, u32[]{:S(2)}, u32[]{:S(2)}) collective-permute-start(bf16[152,512]{1,0:T(8,128)(2,1)S(1)} %get-tuple-element.180), channel_id=1, source_target_pairs={{0,6},{1,7},{2,4},{3,5},{4,2},{5,3},{6,0},{7,1},{8,14},{9,15},{10,... | collective-permute-start | bytes 466952 | tf_op jit(solution)/shard_map/ppermute | solution.py:526
  44.6 3.8 %collective-permute-start.39 = (f32[40,128]{1,0:T(8,128)S(1)}, f32[40,128]{1,0:T(8,128)S(1)}, u32[]{:S(2)}, u32[]{:S(2)}) collective-permute-start(f32[40,128]{1,0:T(8,128)S(1)} %shard_map.111.refs_0_), channel_id=1, source_target_pairs={{0,8},{8,0},{16,24},{24,16},{1,9},{9,1},{17,25},{25,17},{2,10},{10... | collective-permute-start | bytes 61448 | tf_op jit(solution)/shard_map/ppermute | solution.py:526
  46.1 4.8 %collective-permute-start.40 = (f32[40,128]{1,0:T(8,128)S(1)}, f32[40,128]{1,0:T(8,128)S(1)}, u32[]{:S(2)}, u32[]{:S(2)}) collective-permute-start(f32[40,128]{1,0:T(8,128)S(1)} %shard_map.111.refs_0_), channel_id=1, source_target_pairs={{0,16},{8,24},{16,0},{24,8},{1,17},{9,25},{17,1},{25,9},{2,18},{10... | collective-permute-start | bytes 61448 | tf_op jit(solution)/shard_map/ppermute | solution.py:526
  48.4 4.7 %collective-permute-start.41 = (f32[40,128]{1,0:T(8,128)S(1)}, f32[40,128]{1,0:T(8,128)S(1)}, u32[]{:S(2)}, u32[]{:S(2)}) collective-permute-start(f32[40,128]{1,0:T(8,128)S(1)} %shard_map.111.refs_0_), channel_id=1, source_target_pairs={{0,24},{8,16},{16,8},{24,0},{1,25},{9,17},{17,9},{25,1},{2,26},{10... | collective-permute-start | bytes 61448 | tf_op jit(solution)/shard_map/ppermute | solution.py:526
  50.9 5.7 %collective-permute-start.42 = (bf16[152,512]{1,0:T(8,128)(2,1)S(1)}, bf16[152,512]{1,0:T(8,128)(2,1)S(1)}, u32[]{:S(2)}, u32[]{:S(2)}) collective-permute-start(bf16[152,512]{1,0:T(8,128)(2,1)S(1)} %get-tuple-element.177.refs_0_), channel_id=1, source_target_pairs={{0,1},{1,0},{2,3},{3,2},{4,5},{5,4},{6,7},{7,6},{8,9},{9,8},{10,11... | collective-permute-start | bytes 466952 | tf_op jit(solution)/shard_map/ppermute | solution.py:526
  54.7 1.8 %collective-permute-start.45 = (bf16[152,512]{1,0:T(8,128)(2,1)S(1)}, bf16[152,512]{1,0:T(8,128)(2,1)S(1)}, u32[]{:S(2)}, u32[]{:S(2)}) collective-permute-start(bf16[152,512]{1,0:T(8,128)(2,1)S(1)} %collective-permute-done.38.refs_4_), channel_id=1, source_target_pairs={{0,1},{1,0},{2,3},{3,2},{4,5},{5,4},{6,7},{7,6},{8,9},{9,8},{10,11... | collective-permute-start | bytes 466952 | tf_op jit(solution)/shard_map/ppermute | solution.py:526
  54.8 1.8 %collective-permute-start.44 = (bf16[152,512]{1,0:T(8,128)(2,1)S(1)}, bf16[152,512]{1,0:T(8,128)(2,1)S(1)}, u32[]{:S(2)}, u32[]{:S(2)}) collective-permute-start(bf16[152,512]{1,0:T(8,128)(2,1)S(1)} %collective-permute-done.43.refs_2_), channel_id=1, source_target_pairs={{0,1},{1,0},{2,3},{3,2},{4,5},{5,4},{6,7},{7,6},{8,9},{9,8},{10,11... | collective-permute-start | bytes 466952 | tf_op jit(solution)/shard_map/ppermute | solution.py:526
  55.3 1.4 %collective-permute-start.47 = (bf16[152,512]{1,0:T(8,128)(2,1)S(1)}, bf16[152,512]{1,0:T(8,128)(2,1)S(1)}, u32[]{:S(2)}, u32[]{:S(2)}) collective-permute-start(bf16[152,512]{1,0:T(8,128)(2,1)S(1)} %collective-permute-done.46.refs_6_), channel_id=1, source_target_pairs={{0,1},{1,0},{2,3},{3,2},{4,5},{5,4},{6,7},{7,6},{8,9},{9,8},{10,11... | collective-permute-start | bytes 466952 | tf_op jit(solution)/shard_map/ppermute | solution.py:526
  (8 other events, 62.7 us)

commit v9 on v8

--- a/solution.py
+++ b/solution.py
@@ -645,7 +645,7 @@
 
         def group_sums():
             sums = kernel_call(sums_kernel, sds((negs + 8, head_dim), F32), [VMEM] * 3)(coef_c, mixed, most)
-            sums = [sums] + [swap(sums, "dp", d) for d in range(1, groups)]
+            sums = [sums] + [swap(sums, "dp", d) for d in (2, 3, 1)]
             d_w, most_of_all, kit = kernel_call(
                 total_kernel,
                 (sds((head_dim, width // groups), F32), sds((8, 128), F32), sds((width + rows, width), BF16)),

time: 59.8 us -> 58.9 us (0.985)
  starting transfers between devices: 26.4 us -> 25.4 us
    ppermute x24, starting transfers between devices: 26.4 us -> 25.4 us  [swap(): lax.ppermute(block, axis, [(i, i ^ distance) for i in range(lax.axis_size...]
  transfers between devices with their start and end apart: 24 -> 24, of which waited for: 13 -> 14; matrix products, arithmetic and copies ran while one was open for 2% -> 2% of each run, Pallas kernels for 12% -> 12%
where the time goes in v9:
time: 58.9 us; the launch traced here: 58.7 us
  starting transfers between devices  25.4 us (43%)
  waiting for transfers between devices  15.4 us (26%)
  Pallas kernels  14.7 us (25%)
  between operations  1.66 us (3%)
  other arithmetic  0.74 us (1%)
  local copies, waits for them, and re-layouts  0.59 us (1%)
    ppermute x24, starting transfers between devices, swap(): lax.ppermute(block, axis, [(i, i ^ distance) for i in range(lax.axis_size...  25.4 us
    ppermute x24, waiting for transfers between devices, swap(): lax.ppermute(block, axis, [(i, i ^ distance) for i in range(lax.axis_size...  15.4 us
    pallas_call x1, Pallas kernels, index(): kernel_call(functools.partial(index_kernel, (n, rows, slots, pool)), (sds...  2.56 us
    pallas_call x1, Pallas kernels, finish(): kernel_call(functools.partial(finish_kernel, (n, rows)), (sds((rows, PART...  2.53 us
    pallas_call x1, Pallas kernels, prep(): kernel_call(prep_kernel, (sds(qkvu.shape, BF16), sds((below, wide), BF16)...  2.13 us
    pallas_call x1, Pallas kernels, passes(): kernel_call(functools.partial(backward_kernel, (n, rows, pool)), (sds((po...  1.98 us
    pallas_call x1, Pallas kernels, passes(): kernel_call(functools.partial(forward_kernel, (n, rows, slots, per)), (sd...  1.79 us
    pallas_call x1, Pallas kernels, group_sums(): kernel_call(total_kernel, (sds((head_dim, width // groups), F32), sds((8,...  1.59 us
  transfers between devices with their start and end apart: 24, of which 14 were waited for; matrix products, arithmetic and copies ran while one was open for 2% of the time, Pallas kernels for 12%

profile of v9, /device:TPU:0, one launch (start us, length us, event | category | flops | bytes accessed | tf_op | source)
XLA Modules:
  0.0 58.7 jit_solution(10696468250412384068)
XLA Ops:
  2.1 2.9 %collective-permute-start.25 = (s32[2,128]{1,0:T(2,128)S(1)}, s32[2,128]{1,0:T(2,128)S(1)}, u32[]{:S(2)}, u32[]{:S(2)}) collective-permute-start(s32[2,128]{1,0:T(2,128)S(1)} %shard_map.104.first), channel_id=1, source_target_pairs={{0,2},{1,3},{2,0},{3,1},{4,6},{5,7},{6,4},{7,5},{8,10},{9,11},{10,... | collective-permute-start | bytes 3080 | tf_op jit(solution)/shard_map/ppermute | solution.py:526
  5.0 2.1 %shard_map.106 = (bf16[128,4096]{1,0:T(8,128)(2,1)S(1)}, bf16[16,512]{1,0:T(8,128)(2,1)S(1)}, bf16[128,128]{1,0:T(8,128)(2,1)S(1)}) custom-call(s32[4]{0:T(128)} %ids.1, s32[1,128]{1,0:T(1,128)} %send.1, bf16[32,128]{1,0:T(8,128)(2,1)} %bitcast.5, bf16[512,1024]{1,0:T(8,128)(2,1)} %table.1, bf16[128,4096]{1,0:T(8,128)(2,1)} %qkvu.1), custom_call_target="tpu_custom_call" | custom-call | tf_op jit(solution)/shard_map/pallas_call | solution.py:583
  7.1 2.7 %collective-permute-start.26 = (s32[4,128]{1,0:T(4,128)S(1)}, s32[4,128]{1,0:T(4,128)S(1)}, u32[]{:S(2)}, u32[]{:S(2)}) collective-permute-start(s32[4,128]{1,0:T(4,128)S(1)} %shard_map.105.b0), channel_id=1, source_target_pairs={{0,4},{1,5},{2,6},{3,7},{4,0},{5,1},{6,2},{7,3},{8,12},{9,13},{10,... | collective-permute-start | bytes 6152 | tf_op jit(solution)/shard_map/ppermute | solution.py:526
  10.6 1.1 %collective-permute-done.26.b1 = s32[4,128]{1,0:T(4,128)S(1)} collective-permute-done((s32[4,128]{1,0:T(4,128)S(1)}, s32[4,128]{1,0:T(4,128)S(1)}, u32[]{:S(2)}, u32[]{:S(2)}) %collective-permute-start.26) | collective-permute-done | bytes 2080 | tf_op jit(solution)/shard_map/ppermute | solution.py:526
  11.7 1.3 %shard_map.107 = (bf16[136,512]{1,0:T(8,128)(2,1)S(1)}, bf16[136,512]{1,0:T(8,128)(2,1)S(1)}, bf16[136,512]{1,0:T(8,128)(2,1)S(1)}, bf16[136,512]{1,0:T(8,128)(2,1)S(1)}, bf16[128,128]{1,0:T(8,128)(2,1)S(1)}) custom-call(s32[10]{0:T(128)S(1)} %pad_add_fusion.meta, s32[4,128]{1,0:T(4,128)S(1)} %shard_map.105.b0, s32[4,128]{1,0:T(4,128)S(1)} %collective-permute-done.26.b1, ...), custom_call_target="tpu_custom_call" | custom-call | tf_op jit(solution)/shard_map/pallas_call | solution.py:597
  13.0 2.7 %collective-permute-start.27 = (bf16[136,512]{1,0:T(8,128)(2,1)S(1)}, bf16[136,512]{1,0:T(8,128)(2,1)S(1)}, u32[]{:S(2)}, u32[]{:S(2)}) collective-permute-start(bf16[136,512]{1,0:T(8,128)(2,1)S(1)} %get-tuple-element.141), channel_id=1, source_target_pairs={{0,4},{1,5},{2,6},{3,7},{4,0},{5,1},{6,2},{7,3},{8,12},{9,13},{10,... | collective-permute-start | bytes 417800 | tf_op jit(solution)/shard_map/ppermute | solution.py:526
  15.7 1.3 %collective-permute-start.29 = (bf16[136,512]{1,0:T(8,128)(2,1)S(1)}, bf16[136,512]{1,0:T(8,128)(2,1)S(1)}, u32[]{:S(2)}, u32[]{:S(2)}) collective-permute-start(bf16[136,512]{1,0:T(8,128)(2,1)S(1)} %get-tuple-element.155), channel_id=1, source_target_pairs={{0,2},{1,3},{2,0},{3,1},{4,6},{5,7},{6,4},{7,5},{8,10},{9,11},{10,... | collective-permute-start | bytes 417800 | tf_op jit(solution)/shard_map/ppermute | solution.py:526
  17.5 2.6 %shard_map.108 = (bf16[384,512]{1,0:T(8,128)(2,1)S(1)}, bf16[608,384]{1,0:T(8,128)(2,1)S(1)}, bf16[128,256]{1,0:T(8,128)(2,1)S(1)}, bf16[128,256]{1,0:T(8,128)(2...) custom-call(s32[10]{0:T(128)S(1)} %pad_add_fusion.meta, ...), custom_call_target="tpu_custom_call" | custom-call | tf_op jit(solution)/shard_map/pallas_call | solution.py:605
  20.0 5.1 %collective-permute-done.27.refs_4_ = bf16[136,512]{1,0:T(8,128)(2,1)S(1)} collective-permute-done((bf16[136,512]{1,0:T(8,128)(2,1)S(1)}, bf16[136,512]{1,0:T(8,128)(2,1)S(1)}, u32[]{:S(2)}, u32[]{:S(2)}) %collective-permute-start.27) | collective-permute-done | bytes 139296 | tf_op jit(solution)/shard_map/ppermute | solution.py:526
  27.2 1.8 %shard_map.109 = (bf16[384,512]{1,0:T(8,128)(2,1)S(1)}, bf16[384,384]{1,0:T(8,128)(2,1)S(1)}, f32[384,128]{1,0:T(8,128)S(1)}, f32[8,384]{1,0:T(8,128)S(1)}, bf16...) custom-call(s32[10]{0:T(128)S(1)} %pad_add_fusion.meta, ...), custom_call_target="tpu_custom_call" | custom-call | tf_op jit(solution)/shard_map/pallas_call | solution.py:622
  30.3 3.1 %collective-permute-start.35 = (f32[8,384]{1,0:T(8,128)S(1)}, f32[8,384]{1,0:T(8,128)S(1)}, u32[]{:S(2)}, u32[]{:S(2)}) collective-permute-start(f32[8,384]{1,0:T(8,128)S(1)} %stack.10.st0), channel_id=1, source_target_pairs={{0,6},{1,7},{2,4},{3,5},{4,2},{5,3},{6,0},{7,1},{8,14},{9,15},{10,... | collective-permute-start | bytes 36872 | tf_op jit(solution)/shard_map/ppermute | solution.py:526
  33.8 1.0 %collective-permute-start.37 = (f32[8,384]{1,0:T(8,128)S(1)}, f32[8,384]{1,0:T(8,128)S(1)}, u32[]{:S(2)}, u32[]{:S(2)}) collective-permute-start(f32[8,384]{1,0:T(8,128)S(1)} %stack.10.st0), channel_id=1, source_target_pairs={{0,2},{1,3},{2,0},{3,1},{4,6},{5,7},{6,4},{7,5},{8,10},{9,11},{10,... | collective-permute-start | bytes 36872 | tf_op jit(solution)/shard_map/ppermute | solution.py:526
  34.8 1.1 %collective-permute-done.35.st1 = f32[8,384]{1,0:T(8,128)S(1)} collective-permute-done((f32[8,384]{1,0:T(8,128)S(1)}, f32[8,384]{1,0:T(8,128)S(1)}, u32[]{:S(2)}, u32[]{:S(2)}) %collective-permute-start.35) | collective-permute-done | bytes 12320 | tf_op jit(solution)/shard_map/ppermute | solution.py:526
  35.9 2.1 %collective-permute-done.36.st2 = f32[8,384]{1,0:T(8,128)S(1)} collective-permute-done((f32[8,384]{1,0:T(8,128)S(1)}, f32[8,384]{1,0:T(8,128)S(1)}, u32[]{:S(2)}, u32[]{:S(2)}) %collective-permute-start.36) | collective-permute-done | bytes 12320 | tf_op jit(solution)/shard_map/ppermute | solution.py:526
  38.0 2.0 %shard_map.110 = (bf16[152,512]{1,0:T(8,128)(2,1)S(1)}, bf16[152,512]{1,0:T(8,128)(2,1)S(1)}, bf16[152,512]{1,0:T(8,128)(2,1)S(1)}, bf16[152,512]{1,0:T(8,128)(2,1)S(1)}, bf16[384,128]{1,0:T(8,128)(2,1)S(1)}) custom-call(s32[10]{0:T(128)S(1)} %pad_add_fusion.meta, bf16[384,512]{1,0:T(8,128)(2,1)S(1)} %get-tuple-element.158.compact, ...), custom_call_target="tpu_custom_call" | custom-call | tf_op jit(solution)/shard_map/pallas_call | solution.py:639
  40.0 2.1 %collective-permute-start.38 = (bf16[152,512]{1,0:T(8,128)(2,1)S(1)}, bf16[152,512]{1,0:T(8,128)(2,1)S(1)}, u32[]{:S(2)}, u32[]{:S(2)}) collective-permute-start(bf16[152,512]{1,0:T(8,128)(2,1)S(1)} %get-tuple-element.164), channel_id=1, source_target_pairs={{0,4},{1,5},{2,6},{3,7},{4,0},{5,1},{6,2},{7,3},{8,12},{9,13},{10,... | collective-permute-start | bytes 466952 | tf_op jit(solution)/shard_map/ppermute | solution.py:526
  42.7 1.7 %collective-permute-start.46 = (bf16[152,512]{1,0:T(8,128)(2,1)S(1)}, bf16[152,512]{1,0:T(8,128)(2,1)S(1)}, u32[]{:S(2)}, u32[]{:S(2)}) collective-permute-start(bf16[152,512]{1,0:T(8,128)(2,1)S(1)} %get-tuple-element.180), channel_id=1, source_target_pairs={{0,6},{1,7},{2,4},{3,5},{4,2},{5,3},{6,0},{7,1},{8,14},{9,15},{10,... | collective-permute-start | bytes 466952 | tf_op jit(solution)/shard_map/ppermute | solution.py:526
  44.6 1.5 %collective-permute-start.39 = (f32[40,128]{1,0:T(8,128)S(1)}, f32[40,128]{1,0:T(8,128)S(1)}, u32[]{:S(2)}, u32[]{:S(2)}) collective-permute-start(f32[40,128]{1,0:T(8,128)S(1)} %shard_map.111.refs_0_), channel_id=1, source_target_pairs={{0,16},{8,24},{16,0},{24,8},{1,17},{9,25},{17,1},{25,9},{2,18},{10... | collective-permute-start | bytes 61448 | tf_op jit(solution)/shard_map/ppermute | solution.py:526
  46.1 1.4 %collective-permute-start.40 = (f32[40,128]{1,0:T(8,128)S(1)}, f32[40,128]{1,0:T(8,128)S(1)}, u32[]{:S(2)}, u32[]{:S(2)}) collective-permute-start(f32[40,128]{1,0:T(8,128)S(1)} %shard_map.111.refs_0_), channel_id=1, source_target_pairs={{0,24},{8,16},{16,8},{24,0},{1,25},{9,17},{17,9},{25,1},{2,26},{10... | collective-permute-start | bytes 61448 | tf_op jit(solution)/shard_map/ppermute | solution.py:526
  48.4 1.5 %collective-permute-start.41 = (f32[40,128]{1,0:T(8,128)S(1)}, f32[40,128]{1,0:T(8,128)S(1)}, u32[]{:S(2)}, u32[]{:S(2)}) collective-permute-start(f32[40,128]{1,0:T(8,128)S(1)} %shard_map.111.refs_0_), channel_id=1, source_target_pairs={{0,8},{8,0},{16,24},{24,16},{1,9},{9,1},{17,25},{25,17},{2,10},{10... | collective-permute-start | bytes 61448 | tf_op jit(solution)/shard_map/ppermute | solution.py:526
  49.9 0.9 %collective-permute-done.40.refs_2_ = f32[40,128]{1,0:T(8,128)S(1)} collective-permute-done((f32[40,128]{1,0:T(8,128)S(1)}, f32[40,128]{1,0:T(8,128)S(1)}, u32[]{:S(2)}, u32[]{:S(2)}) %collective-permute-start.40) | collective-permute-done | bytes 20512 | tf_op jit(solution)/shard_map/ppermute | solution.py:526
  50.8 1.4 %collective-permute-done.41.refs_3_ = f32[40,128]{1,0:T(8,128)S(1)} collective-permute-done((f32[40,128]{1,0:T(8,128)S(1)}, f32[40,128]{1,0:T(8,128)S(1)}, u32[]{:S(2)}, u32[]{:S(2)}) %collective-permute-start.41) | collective-permute-done | bytes 20512 | tf_op jit(solution)/shard_map/ppermute | solution.py:526
  52.2 1.6 %shard_map.112 = (f32[128,256]{1,0:T(8,128)}, f32[8,128]{1,0:T(8,128)S(1)}, bf16[1152,1024]{1,0:T(8,128)(2,1)S(1)}) custom-call(s32[10]{0:T(128)S(1)} %pad_add_fusion.meta, bf16[128,256]{1,0:T(8,128)(2,1)S(1)} %get-tuple-element.165.even, bf16[128,256]{1,0:T(8,128)(2,1)S(1)} %get-tuple-element.166.odd, bf16[128,256]{1,0:T(8,128)(2,1)S(1)} %get-tuple-element.167.tile, ...), custom_call_target="tpu_custom_call" | custom-call | tf_op jit(solution)/shard_map/pallas_call | solution.py:649
  55.8 2.5 %shard_map.113 = (bf16[128,4096]{1,0:T(8,128)(2,1)}, bf16[128,1024]{1,0:T(8,128)(2,1)}) custom-call(s32[10]{0:T(128)S(1)} %pad_add_fusion.meta, bf16[1152,1024]{1,0:T(8,128)(2,1)S(1)} %get-tuple-element.176.kit, bf16[152,512]{1,0:T(8,128)(2,1)S(1)} %get-tuple-element.177.refs_0_, bf16[152,512]{1,0:T(8,128)(2,1)S(1)} %collective-permute-done.42.refs_1_, ...), custom_call_target="tpu_custom_call" | custom-call | tf_op jit(solution)/shard_map/pallas_call | solution.py:661
  (57 shorter events, 9.6 us)
Async XLA Ops:
  0.6 1.5 %collective-permute-start.24 = (s32[1,128]{1,0:T(1,128)}, s32[1,128]{1,0:T(1,128)S(1)}, u32[]{:S(2)}, u32[]{:S(2)}) collective-permute-start(s32[1,128]{1,0:T(1,128)} %block.1), channel_id=1, source_target_pairs={{0,1},{1,0},{2,3},{3,2},{4,5},{5,4},{6,7},{7,6},{8,9},{9,8},{10,11... | collective-permute-start | bytes 1544 | tf_op jit(solution)/shard_map/ppermute | solution.py:526
  2.1 5.0 %collective-permute-start.25 = (s32[2,128]{1,0:T(2,128)S(1)}, s32[2,128]{1,0:T(2,128)S(1)}, u32[]{:S(2)}, u32[]{:S(2)}) collective-permute-start(s32[2,128]{1,0:T(2,128)S(1)} %shard_map.104.first), channel_id=1, source_target_pairs={{0,2},{1,3},{2,0},{3,1},{4,6},{5,7},{6,4},{7,5},{8,10},{9,11},{10,... | collective-permute-start | bytes 3080 | tf_op jit(solution)/shard_map/ppermute | solution.py:526
  7.1 4.5 %collective-permute-start.26 = (s32[4,128]{1,0:T(4,128)S(1)}, s32[4,128]{1,0:T(4,128)S(1)}, u32[]{:S(2)}, u32[]{:S(2)}) collective-permute-start(s32[4,128]{1,0:T(4,128)S(1)} %shard_map.105.b0), channel_id=1, source_target_pairs={{0,4},{1,5},{2,6},{3,7},{4,0},{5,1},{6,2},{7,3},{8,12},{9,13},{10,... | collective-permute-start | bytes 6152 | tf_op jit(solution)/shard_map/ppermute | solution.py:526
  13.0 12.1 %collective-permute-start.27 = (bf16[136,512]{1,0:T(8,128)(2,1)S(1)}, bf16[136,512]{1,0:T(8,128)(2,1)S(1)}, u32[]{:S(2)}, u32[]{:S(2)}) collective-permute-start(bf16[136,512]{1,0:T(8,128)(2,1)S(1)} %get-tuple-element.141), channel_id=1, source_target_pairs={{0,4},{1,5},{2,6},{3,7},{4,0},{5,1},{6,2},{7,3},{8,12},{9,13},{10,... | collective-permute-start | bytes 417800 | tf_op jit(solution)/shard_map/ppermute | solution.py:526
  15.7 10.0 %collective-permute-start.29 = (bf16[136,512]{1,0:T(8,128)(2,1)S(1)}, bf16[136,512]{1,0:T(8,128)(2,1)S(1)}, u32[]{:S(2)}, u32[]{:S(2)}) collective-permute-start(bf16[136,512]{1,0:T(8,128)(2,1)S(1)} %get-tuple-element.155), channel_id=1, source_target_pairs={{0,2},{1,3},{2,0},{3,1},{4,6},{5,7},{6,4},{7,5},{8,10},{9,11},{10,... | collective-permute-start | bytes 417800 | tf_op jit(solution)/shard_map/ppermute | solution.py:526
  17.0 8.7 %collective-permute-start.32 = (bf16[136,512]{1,0:T(8,128)(2,1)S(1)}, bf16[136,512]{1,0:T(8,128)(2,1)S(1)}, u32[]{:S(2)}, u32[]{:S(2)}) collective-permute-start(bf16[136,512]{1,0:T(8,128)(2,1)S(1)} %get-tuple-element.157), channel_id=1, source_target_pairs={{0,6},{1,7},{2,4},{3,5},{4,2},{5,3},{6,0},{7,1},{8,14},{9,15},{10,... | collective-permute-start | bytes 417800 | tf_op jit(solution)/shard_map/ppermute | solution.py:526
  17.5 8.7 %collective-permute-start.28 = (bf16[136,512]{1,0:T(8,128)(2,1)S(1)}, bf16[136,512]{1,0:T(8,128)(2,1)S(1)}, u32[]{:S(2)}, u32[]{:S(2)}) collective-permute-start(bf16[136,512]{1,0:T(8,128)(2,1)S(1)} %get-tuple-element.154.refs_0_), channel_id=1, source_target_pairs={{0,1},{1,0},{2,3},{3,2},{4,5},{5,4},{6,7},{7,6},{8,9},{9,8},{10,11... | collective-permute-start | bytes 417800 | tf_op jit(solution)/shard_map/ppermute | solution.py:526
  25.1 1.4 %collective-permute-start.31 = (bf16[136,512]{1,0:T(8,128)(2,1)S(1)}, bf16[136,512]{1,0:T(8,128)(2,1)S(1)}, u32[]{:S(2)}, u32[]{:S(2)}) collective-permute-start(bf16[136,512]{1,0:T(8,128)(2,1)S(1)} %collective-permute-done.27.refs_4_), channel_id=1, source_target_pairs={{0,1},{1,0},{2,3},{3,2},{4,5},{5,4},{6,7},{7,6},{8,9},{9,8},{10,11... | collective-permute-start | bytes 417800 | tf_op jit(solution)/shard_map/ppermute | solution.py:526
  25.7 1.4 %collective-permute-start.30 = (bf16[136,512]{1,0:T(8,128)(2,1)S(1)}, bf16[136,512]{1,0:T(8,128)(2,1)S(1)}, u32[]{:S(2)}, u32[]{:S(2)}) collective-permute-start(bf16[136,512]{1,0:T(8,128)(2,1)S(1)} %collective-permute-done.29.refs_2_), channel_id=1, source_target_pairs={{0,1},{1,0},{2,3},{3,2},{4,5},{5,4},{6,7},{7,6},{8,9},{9,8},{10,11... | collective-permute-start | bytes 417800 | tf_op jit(solution)/shard_map/ppermute | solution.py:526
  25.7 1.6 %collective-permute-start.33 = (bf16[136,512]{1,0:T(8,128)(2,1)S(1)}, bf16[136,512]{1,0:T(8,128)(2,1)S(1)}, u32[]{:S(2)}, u32[]{:S(2)}) collective-permute-start(bf16[136,512]{1,0:T(8,128)(2,1)S(1)} %collective-permute-done.32.refs_6_), channel_id=1, source_target_pairs={{0,1},{1,0},{2,3},{3,2},{4,5},{5,4},{6,7},{7,6},{8,9},{9,8},{10,11... | collective-permute-start | bytes 417800 | tf_op jit(solution)/shard_map/ppermute | solution.py:526
  29.0 1.2 %collective-permute-start.34 = (f32[8,384]{1,0:T(8,128)S(1)}, f32[8,384]{1,0:T(8,128)S(1)}, u32[]{:S(2)}, u32[]{:S(2)}) collective-permute-start(f32[8,384]{1,0:T(8,128)S(1)} %get-tuple-element.162), channel_id=1, source_target_pairs={{0,1},{1,0},{2,3},{3,2},{4,5},{5,4},{6,7},{7,6},{8,9},{9,8},{10,11... | collective-permute-start | bytes 36872 | tf_op jit(solution)/shard_map/ppermute | solution.py:526
  30.3 5.6 %collective-permute-start.35 = (f32[8,384]{1,0:T(8,128)S(1)}, f32[8,384]{1,0:T(8,128)S(1)}, u32[]{:S(2)}, u32[]{:S(2)}) collective-permute-start(f32[8,384]{1,0:T(8,128)S(1)} %stack.10.st0), channel_id=1, source_target_pairs={{0,6},{1,7},{2,4},{3,5},{4,2},{5,3},{6,0},{7,1},{8,14},{9,15},{10,... | collective-permute-start | bytes 36872 | tf_op jit(solution)/shard_map/ppermute | solution.py:526
  33.4 4.6 %collective-permute-start.36 = (f32[8,384]{1,0:T(8,128)S(1)}, f32[8,384]{1,0:T(8,128)S(1)}, u32[]{:S(2)}, u32[]{:S(2)}) collective-permute-start(f32[8,384]{1,0:T(8,128)S(1)} %stack.10.st0), channel_id=1, source_target_pairs={{0,4},{1,5},{2,6},{3,7},{4,0},{5,1},{6,2},{7,3},{8,12},{9,13},{10,... | collective-permute-start | bytes 36872 | tf_op jit(solution)/shard_map/ppermute | solution.py:526
  33.8 4.2 %collective-permute-start.37 = (f32[8,384]{1,0:T(8,128)S(1)}, f32[8,384]{1,0:T(8,128)S(1)}, u32[]{:S(2)}, u32[]{:S(2)}) collective-permute-start(f32[8,384]{1,0:T(8,128)S(1)} %stack.10.st0), channel_id=1, source_target_pairs={{0,2},{1,3},{2,0},{3,1},{4,6},{5,7},{6,4},{7,5},{8,10},{9,11},{10,... | collective-permute-start | bytes 36872 | tf_op jit(solution)/shard_map/ppermute | solution.py:526
  40.0 13.8 %collective-permute-start.38 = (bf16[152,512]{1,0:T(8,128)(2,1)S(1)}, bf16[152,512]{1,0:T(8,128)(2,1)S(1)}, u32[]{:S(2)}, u32[]{:S(2)}) collective-permute-start(bf16[152,512]{1,0:T(8,128)(2,1)S(1)} %get-tuple-element.164), channel_id=1, source_target_pairs={{0,4},{1,5},{2,6},{3,7},{4,0},{5,1},{6,2},{7,3},{8,12},{9,13},{10,... | collective-permute-start | bytes 466952 | tf_op jit(solution)/shard_map/ppermute | solution.py:526
  42.1 11.9 %collective-permute-start.43 = (bf16[152,512]{1,0:T(8,128)(2,1)S(1)}, bf16[152,512]{1,0:T(8,128)(2,1)S(1)}, u32[]{:S(2)}, u32[]{:S(2)}) collective-permute-start(bf16[152,512]{1,0:T(8,128)(2,1)S(1)} %get-tuple-element.178), channel_id=1, source_target_pairs={{0,2},{1,3},{2,0},{3,1},{4,6},{5,7},{6,4},{7,5},{8,10},{9,11},{10,... | collective-permute-start | bytes 466952 | tf_op jit(solution)/shard_map/ppermute | solution.py:526
  42.7 11.7 %collective-permute-start.46 = (bf16[152,512]{1,0:T(8,128)(2,1)S(1)}, bf16[152,512]{1,0:T(8,128)(2,1)S(1)}, u32[]{:S(2)}, u32[]{:S(2)}) collective-permute-start(bf16[152,512]{1,0:T(8,128)(2,1)S(1)} %get-tuple-element.180), channel_id=1, source_target_pairs={{0,6},{1,7},{2,4},{3,5},{4,2},{5,3},{6,0},{7,1},{8,14},{9,15},{10,... | collective-permute-start | bytes 466952 | tf_op jit(solution)/shard_map/ppermute | solution.py:526
  44.6 3.8 %collective-permute-start.39 = (f32[40,128]{1,0:T(8,128)S(1)}, f32[40,128]{1,0:T(8,128)S(1)}, u32[]{:S(2)}, u32[]{:S(2)}) collective-permute-start(f32[40,128]{1,0:T(8,128)S(1)} %shard_map.111.refs_0_), channel_id=1, source_target_pairs={{0,16},{8,24},{16,0},{24,8},{1,17},{9,25},{17,1},{25,9},{2,18},{10... | collective-permute-start | bytes 61448 | tf_op jit(solution)/shard_map/ppermute | solution.py:526
  46.1 4.7 %collective-permute-start.40 = (f32[40,128]{1,0:T(8,128)S(1)}, f32[40,128]{1,0:T(8,128)S(1)}, u32[]{:S(2)}, u32[]{:S(2)}) collective-permute-start(f32[40,128]{1,0:T(8,128)S(1)} %shard_map.111.refs_0_), channel_id=1, source_target_pairs={{0,24},{8,16},{16,8},{24,0},{1,25},{9,17},{17,9},{25,1},{2,26},{10... | collective-permute-start | bytes 61448 | tf_op jit(solution)/shard_map/ppermute | solution.py:526
  48.4 3.8 %collective-permute-start.41 = (f32[40,128]{1,0:T(8,128)S(1)}, f32[40,128]{1,0:T(8,128)S(1)}, u32[]{:S(2)}, u32[]{:S(2)}) collective-permute-start(f32[40,128]{1,0:T(8,128)S(1)} %shard_map.111.refs_0_), channel_id=1, source_target_pairs={{0,8},{8,0},{16,24},{24,16},{1,9},{9,1},{17,25},{25,17},{2,10},{10... | collective-permute-start | bytes 61448 | tf_op jit(solution)/shard_map/ppermute | solution.py:526
  50.8 4.9 %collective-permute-start.42 = (bf16[152,512]{1,0:T(8,128)(2,1)S(1)}, bf16[152,512]{1,0:T(8,128)(2,1)S(1)}, u32[]{:S(2)}, u32[]{:S(2)}) collective-permute-start(bf16[152,512]{1,0:T(8,128)(2,1)S(1)} %get-tuple-element.177.refs_0_), channel_id=1, source_target_pairs={{0,1},{1,0},{2,3},{3,2},{4,5},{5,4},{6,7},{7,6},{8,9},{9,8},{10,11... | collective-permute-start | bytes 466952 | tf_op jit(solution)/shard_map/ppermute | solution.py:526
  53.8 1.8 %collective-permute-start.45 = (bf16[152,512]{1,0:T(8,128)(2,1)S(1)}, bf16[152,512]{1,0:T(8,128)(2,1)S(1)}, u32[]{:S(2)}, u32[]{:S(2)}) collective-permute-start(bf16[152,512]{1,0:T(8,128)(2,1)S(1)} %collective-permute-done.38.refs_4_), channel_id=1, source_target_pairs={{0,1},{1,0},{2,3},{3,2},{4,5},{5,4},{6,7},{7,6},{8,9},{9,8},{10,11... | collective-permute-start | bytes 466952 | tf_op jit(solution)/shard_map/ppermute | solution.py:526
  53.9 1.8 %collective-permute-start.44 = (bf16[152,512]{1,0:T(8,128)(2,1)S(1)}, bf16[152,512]{1,0:T(8,128)(2,1)S(1)}, u32[]{:S(2)}, u32[]{:S(2)}) collective-permute-start(bf16[152,512]{1,0:T(8,128)(2,1)S(1)} %collective-permute-done.43.refs_2_), channel_id=1, source_target_pairs={{0,1},{1,0},{2,3},{3,2},{4,5},{5,4},{6,7},{7,6},{8,9},{9,8},{10,11... | collective-permute-start | bytes 466952 | tf_op jit(solution)/shard_map/ppermute | solution.py:526
  54.4 1.4 %collective-permute-start.47 = (bf16[152,512]{1,0:T(8,128)(2,1)S(1)}, bf16[152,512]{1,0:T(8,128)(2,1)S(1)}, u32[]{:S(2)}, u32[]{:S(2)}) collective-permute-start(bf16[152,512]{1,0:T(8,128)(2,1)S(1)} %collective-permute-done.46.refs_6_), channel_id=1, source_target_pairs={{0,1},{1,0},{2,3},{3,2},{4,5},{5,4},{6,7},{7,6},{8,9},{9,8},{10,11... | collective-permute-start | bytes 466952 | tf_op jit(solution)/shard_map/ppermute | solution.py:526
  (8 other events, 61.7 us)
